TPU v7x, 32 devices: a whole 2x2x4 slice. The times are simulated.
32 devices in a mesh: ctx: 16 (over z, x, core), wa: 2 (over y).
Axes of the slice: x: 2, y: 2, z: 4, core: 2. Of those that a mesh axis runs over, the one named last changes fastest.
Arguments:
- tokens: bfloat16 [2, 1024, 2048], P(None, 'ctx'), may hold values from -6 to 6
- norm_in: bfloat16 [2048], P('ctx'), may hold values from 0.099609375 to 1.8984375
- query_weight: bfloat16 [2048, 3072], P('ctx', 'wa'), may hold values from -0.125 to 0.125
- latent_down: bfloat16 [2048, 576], P('ctx'), may hold values from -0.125 to 0.125
- latent_norm: bfloat16 [512], P('ctx'), may hold values from 0.099609375 to 1.8984375
- latent_up: bfloat16 [512, 4096], P('ctx', 'wa'), may hold values from -0.25 to 0.25
- output_weight: bfloat16 [2048, 2048], P('wa', 'ctx'), may hold values from -0.75 to 0.75
- norm_ffn: bfloat16 [2048], P('ctx'), may hold values from 0.099609375 to 1.8984375
- router_weight: bfloat16 [2048, 16], P('ctx'), may hold values from -0.0625 to 0.0625
- shared_gate: bfloat16 [2048, 2816], P('ctx', 'wa'), may hold values from -0.125 to 0.125
- shared_up: bfloat16 [2048, 2816], P('ctx', 'wa'), may hold values from -0.125 to 0.125
- shared_down: bfloat16 [2816, 2048], P('wa', 'ctx'), may hold values from -0.109375 to 0.109375
- expert_gate: bfloat16 [16, 2048, 1408], P('ctx', None, 'wa'), may hold values from -0.125 to 0.125
- expert_up: bfloat16 [16, 2048, 1408], P('ctx', None, 'wa'), may hold values from -0.125 to 0.125
- expert_down: bfloat16 [16, 1408, 2048], P('ctx', 'wa'), may hold values from -2.5 to 2.5
- routes: int32 [2, 1024, 6], P(None, 'ctx'), may hold values from 0 to 15, all different within a row; in each aligned block of 64 rows (0 to 63, 64 to 127, ..., all dimensions but the last counted through in order) at most 32 rows name the same one
- cotangent: bfloat16 [2, 1024, 2048], P(None, 'ctx'), may hold values from -6 to 6
Outputs:
- block_output: bfloat16 [2, 1024, 2048], P(None, 'ctx')
- tokens_gradient: float32 [2, 1024, 2048], P(None, 'ctx')
- norm_in_gradient: float32 [2048], P('ctx')
- query_weight_gradient: float32 [2048, 3072], P('ctx', 'wa')
- latent_down_gradient: float32 [2048, 576], P('ctx')
- latent_norm_gradient: float32 [512], P('ctx')
- latent_up_gradient: float32 [512, 4096], P('ctx', 'wa')
- output_weight_gradient: float32 [2048, 2048], P('wa', 'ctx')
- norm_ffn_gradient: float32 [2048], P('ctx')
- router_weight_gradient: float32 [2048, 16], P('ctx')
- shared_gate_gradient: float32 [2048, 2816], P('ctx', 'wa')
- shared_up_gradient: float32 [2048, 2816], P('ctx', 'wa')
- shared_down_gradient: float32 [2816, 2048], P('wa', 'ctx')
- expert_gate_gradient: float32 [16, 2048, 1408], P('ctx', None, 'wa')
- expert_up_gradient: float32 [16, 2048, 1408], P('ctx', None, 'wa')
- expert_down_gradient: float32 [16, 1408, 2048], P('ctx', 'wa')
Inputs may be any that keep to these rules, and one draw needn't show every extreme that they name: `routes`: each row names 6 different experts. In each aligned block of 64 rows (one sequence's positions on one index of ctx) no expert is named by more than 32 rows, and some block reaches 32.
All inputs are finite; a program needn't handle non-finite values.
Results may differ from a plain program's by a relative error of at most 0.028.
Values may be sent and summed in bfloat16 or wider, within the bound.
No kernel may reach another device: no remote copies, remote signals or barrier semaphores. Data moves between devices by JAX's collectives and lax.ppermute only.
A program may use at most 256 MiB of HBM per device.

v0:
```python
import jax
import jax.numpy as jnp
from jax import lax
from jax.sharding import PartitionSpec as P

DN = 128
DR = 64
DV = 128
R = 512
TOPK = 6


epsilon = 1e-06
highest = lax.Precision.HIGHEST


def shifted(value, axis, steps):
    count = lax.axis_size(axis)
    pairs = [(source, (source + steps) % count) for source in range(count)]
    return lax.ppermute(value, axis, pairs)


def root_norm(values, gain):
    inverse = lax.rsqrt(jnp.mean(values * values, axis=-1, keepdims=True) + epsilon)
    unit = values * inverse
    return (unit * gain, unit, inverse)


def root_norm_back(upstream, unit, inverse, gain):
    scaled = upstream * gain
    inner = jnp.mean(scaled * unit, axis=-1, keepdims=True)
    leading = tuple(range(upstream.ndim - 1))
    return (inverse * (scaled - unit * inner), jnp.sum(upstream * unit, axis=leading))


def rotary_tables(positions, width):
    half = width // 2
    frequency = 10000.0 ** (-jnp.arange(half, dtype=jnp.float32) * 2.0 / width)
    angle = positions.astype(jnp.float32)[:, None] * frequency[None, :]
    return (jnp.cos(angle), jnp.sin(angle))


def rotate(values, cosine, sine):
    half = values.shape[-1] // 2
    first = values[..., :half]
    second = values[..., half:]
    return jnp.concatenate(
        [first * cosine - second * sine, second * cosine + first * sine], axis=-1
    )


def silu_slope(values):
    sigmoid = jax.nn.sigmoid(values)
    return sigmoid * (1.0 + values * (1.0 - sigmoid))


def fetch_weights(
    norm_in,
    query_weight,
    latent_down,
    latent_norm,
    latent_up,
    output_weight,
    norm_ffn,
    router_weight,
    shared_gate,
    shared_up,
    shared_down,
):
    return (
        lax.all_gather(norm_in, "ctx", axis=0, tiled=True),
        lax.all_gather(query_weight, "ctx", axis=0, tiled=True),
        lax.all_gather(latent_down, "ctx", axis=0, tiled=True),
        lax.all_gather(latent_norm, "ctx", axis=0, tiled=True),
        lax.all_gather(latent_up, "ctx", axis=0, tiled=True),
        lax.all_gather(output_weight, "ctx", axis=1, tiled=True),
        lax.all_gather(norm_ffn, "ctx", axis=0, tiled=True),
        lax.all_gather(router_weight, "ctx", axis=0, tiled=True),
        lax.all_gather(shared_gate, "ctx", axis=0, tiled=True),
        lax.all_gather(shared_up, "ctx", axis=0, tiled=True),
        lax.all_gather(shared_down, "ctx", axis=1, tiled=True),
    )


def shards(
    tokens,
    norm_in,
    query_weight,
    latent_down,
    latent_norm,
    latent_up,
    output_weight,
    norm_ffn,
    router_weight,
    shared_gate,
    shared_up,
    shared_down,
    expert_gate,
    expert_up,
    expert_down,
    routes,
    cotangent,
):
    context_count = lax.axis_size("ctx")
    context_index = lax.axis_index("ctx")
    lead = (lax.axis_index("wa") == 0).astype(jnp.float32)
    sequences, block, width = tokens.shape
    local_experts = expert_gate.shape[0]
    experts = context_count * local_experts
    capacity = max(2, block * TOPK * 4 // (3 * experts))
    scale = (DN + DR) ** (-0.5)
    gathered = fetch_weights(
        norm_in,
        query_weight,
        latent_down,
        latent_norm,
        latent_up,
        output_weight,
        norm_ffn,
        router_weight,
        shared_gate,
        shared_up,
        shared_down,
    )
    (
        full_norm_in,
        full_query,
        full_down,
        full_latent_norm,
        full_up,
        full_output,
        full_norm_ffn,
        full_router,
        full_shared_gate,
        full_shared_up,
        full_shared_down,
    ) = gathered
    heads_here = full_up.shape[1] // (DN + DV)
    positions = context_index * block + jnp.arange(block)
    cosine, sine = rotary_tables(positions, DR)
    source = tokens.astype(jnp.float32)
    normed_in, unit_in, inverse_in = root_norm(source, full_norm_in.astype(jnp.float32))
    input_low = normed_in.astype(jnp.bfloat16)
    query_raw = jnp.dot(input_low, full_query, preferred_element_type=jnp.float32).reshape(
        sequences, block, heads_here, DN + DR
    )
    query_low = jnp.concatenate(
        [query_raw[..., :DN], rotate(query_raw[..., DN:], cosine[:, None, :], sine[:, None, :])],
        axis=-1,
    ).astype(jnp.bfloat16)
    up_view = full_up.reshape(R, heads_here, DN + DV)
    key_up = up_view[..., :DN]
    value_up = up_view[..., DN:]
    absorbed = jnp.einsum(
        "sbhn,rhn->shbr", query_low[..., :DN], key_up, preferred_element_type=jnp.float32
    )
    query_rows = jnp.concatenate(
        [absorbed.astype(jnp.bfloat16), jnp.transpose(query_low[..., DN:], (0, 2, 1, 3))], axis=-1
    )
    latent_raw = jnp.dot(input_low, full_down, preferred_element_type=jnp.float32)
    latent_scaled, latent_unit, latent_inverse = root_norm(
        latent_raw[..., :R], full_latent_norm.astype(jnp.float32)
    )
    key_rows = jnp.concatenate(
        [latent_scaled, rotate(latent_raw[..., R:], cosine, sine)], axis=-1
    ).astype(jnp.bfloat16)
    piece = lax.all_gather(key_rows, "ctx", axis=1, tiled=True)
    top = jnp.full((sequences, heads_here, block), -1e30, jnp.float32)
    scores = (
        jnp.einsum("shqc,skc->shqk", query_rows, piece, preferred_element_type=jnp.float32) * scale
    )
    key_positions = jnp.arange(piece.shape[1])
    allowed = positions[:, None] >= key_positions[None, :]
    scores = jnp.where(allowed, scores, -1e30)
    new_top = jnp.maximum(top, jnp.max(scores, axis=-1))
    weights = jnp.where(allowed, jnp.exp(scores - new_top[..., None]), 0.0)
    total = jnp.sum(weights, axis=-1)
    weights_high = weights.astype(jnp.bfloat16)
    weights_rest = (weights - weights_high.astype(jnp.float32)).astype(jnp.bfloat16)
    running = jnp.einsum(
        "shqk,skr->shqr", weights_high, piece[..., :R], preferred_element_type=jnp.float32
    )
    remainder = jnp.einsum(
        "shqk,skr->shqr", weights_rest, piece[..., :R], preferred_element_type=jnp.float32
    )
    top, total, running, remainder = (new_top, total, running, remainder)
    log_total = top + jnp.log(total)
    latent_out = (running / total[..., None]).astype(jnp.bfloat16)
    latent_exact = (running + remainder) / total[..., None]
    head_out = (
        jnp.einsum("shbr,rhv->sbhv", latent_out, value_up, preferred_element_type=jnp.float32)
        .astype(jnp.bfloat16)
        .reshape(sequences, block, heads_here * DV)
    )
    attention_part = jnp.dot(head_out, full_output, preferred_element_type=jnp.float32)
    hidden_in = source + lax.psum(attention_part, "wa")
    normed_ffn, unit_ffn, inverse_ffn = root_norm(hidden_in, full_norm_ffn.astype(jnp.float32))
    ffn_low = normed_ffn.astype(jnp.bfloat16)
    shares = jax.nn.softmax(
        jnp.dot(ffn_low, full_router, preferred_element_type=jnp.float32), axis=-1
    )
    shared_g = jnp.dot(ffn_low, full_shared_gate, preferred_element_type=jnp.float32)
    shared_u = jnp.dot(ffn_low, full_shared_up, preferred_element_type=jnp.float32)
    shared_silu = jax.nn.silu(shared_g)
    shared_activation = (shared_silu * shared_u).astype(jnp.bfloat16)
    shared_part = jnp.dot(shared_activation, full_shared_down, preferred_element_type=jnp.float32)
    expert_ids = jnp.arange(experts, dtype=jnp.int32)
    chosen = (
        (routes[..., None] == expert_ids)
        .astype(jnp.int32)
        .reshape(sequences, block * TOPK, experts)
    )
    earlier = jnp.cumsum(chosen, axis=1) - chosen
    slot_of = jnp.sum(earlier * chosen, axis=-1).reshape(sequences, block, TOPK)
    slot_ids = jnp.arange(capacity, dtype=jnp.int32)
    hit = (routes[None, :, :, :, None] == expert_ids[:, None, None, None, None]) & (
        slot_of[None, :, :, :, None] == slot_ids[None, None, None, None, :]
    )
    dispatch = jnp.transpose(jnp.any(hit, axis=3), (0, 1, 3, 2)).astype(jnp.float32)
    send = (
        jnp.einsum(
            "escb,sbd->escd",
            dispatch.astype(jnp.bfloat16),
            ffn_low,
            preferred_element_type=jnp.float32,
        )
        .astype(jnp.bfloat16)
        .reshape(experts, sequences * capacity, width)
    )
    slot_share = jnp.einsum("escb,sbe->esc", dispatch, shares, precision=highest)
    received = lax.all_to_all(send, "ctx", split_axis=0, concat_axis=0, tiled=True)
    count = received.shape[1]
    rows = received.reshape(context_count, local_experts, count, width)
    gate_pre = jnp.einsum("nesd,edf->nesf", rows, expert_gate, preferred_element_type=jnp.float32)
    up_pre = jnp.einsum("nesd,edf->nesf", rows, expert_up, preferred_element_type=jnp.float32)
    activation = (jax.nn.silu(gate_pre) * up_pre).astype(jnp.bfloat16)
    result = jnp.einsum(
        "nesf,efd->nesd", activation, expert_down, preferred_element_type=jnp.float32
    ).reshape(experts, count, width)
    returned = lax.all_to_all(result, "ctx", split_axis=0, concat_axis=0, tiled=True)
    hidden_units = gate_pre.shape[-1]
    returned, received, gate_keep, up_keep = (
        returned,
        received,
        gate_pre.reshape(experts, count, hidden_units),
        up_pre.reshape(experts, count, hidden_units),
    )
    returned = returned.reshape(experts, sequences, capacity, width)
    routed_part = jnp.einsum(
        "escb,escd->sbd", dispatch, returned * slot_share[..., None], precision=highest
    )
    output = hidden_in + lax.psum(shared_part + routed_part, "wa")
    gathered = fetch_weights(
        norm_in,
        query_weight,
        latent_down,
        latent_norm,
        latent_up,
        output_weight,
        norm_ffn,
        router_weight,
        shared_gate,
        shared_up,
        shared_down,
    )
    (
        full_norm_in,
        full_query,
        full_down,
        full_latent_norm,
        full_up,
        full_output,
        full_norm_ffn,
        full_router,
        full_shared_gate,
        full_shared_up,
        full_shared_down,
    ) = gathered
    up_view = full_up.reshape(R, heads_here, DN + DV)
    key_up = up_view[..., :DN]
    value_up = up_view[..., DN:]
    grad_y = cotangent.astype(jnp.float32)
    shared_grad = jnp.einsum(
        "sbd,fd->sbf", cotangent, full_shared_down, preferred_element_type=jnp.float32
    )
    shared_gate_grad = (shared_grad * shared_u * silu_slope(shared_g)).astype(jnp.bfloat16)
    shared_up_grad = (shared_grad * shared_silu).astype(jnp.bfloat16)
    grad_shared_down = jnp.einsum(
        "sbf,sbd->fd", shared_activation, cotangent, preferred_element_type=jnp.float32
    )
    grad_shared_gate = jnp.einsum(
        "sbd,sbf->df", ffn_low, shared_gate_grad, preferred_element_type=jnp.float32
    )
    grad_shared_up = jnp.einsum(
        "sbd,sbf->df", ffn_low, shared_up_grad, preferred_element_type=jnp.float32
    )
    ffn_grad = jnp.einsum(
        "sbf,df->sbd", shared_gate_grad, full_shared_gate, preferred_element_type=jnp.float32
    )
    ffn_grad = ffn_grad + jnp.einsum(
        "sbf,df->sbd", shared_up_grad, full_shared_up, preferred_element_type=jnp.float32
    )
    grad_at_slots = jnp.einsum("escb,sbd->escd", dispatch, grad_y, precision=highest)
    slot_grads = (
        (grad_at_slots * slot_share[..., None])
        .astype(jnp.bfloat16)
        .reshape(experts, sequences * capacity, width)
    )
    slot_dot = jnp.sum(returned * grad_at_slots, axis=-1)
    share_grad = jnp.einsum("escb,esc->sbe", dispatch, slot_dot, precision=highest)
    logit_grad = shares * (share_grad - jnp.sum(shares * share_grad, axis=-1, keepdims=True))
    grad_router = jnp.einsum(
        "sbd,sbe->de", ffn_low.astype(jnp.float32), logit_grad, precision=highest
    )
    ffn_grad = ffn_grad + jnp.einsum(
        "sbe,de->sbd", logit_grad, full_router.astype(jnp.float32), precision=highest
    )
    slot_back = lax.all_to_all(slot_grads, "ctx", split_axis=0, concat_axis=0, tiled=True).reshape(
        context_count, local_experts, -1, width
    )
    rows = received.reshape(context_count, local_experts, -1, width)
    gate_pre = gate_keep.reshape(context_count, local_experts, -1, gate_keep.shape[-1])
    up_pre = up_keep.reshape(context_count, local_experts, -1, up_keep.shape[-1])
    hidden_grad = jnp.einsum(
        "nesd,efd->nesf", slot_back, expert_down, preferred_element_type=jnp.float32
    )
    silu_gate = jax.nn.silu(gate_pre)
    gate_grad = (hidden_grad * up_pre * silu_slope(gate_pre)).astype(jnp.bfloat16)
    up_grad = (hidden_grad * silu_gate).astype(jnp.bfloat16)
    activation = (silu_gate * up_pre).astype(jnp.bfloat16)
    grad_expert_down = jnp.einsum(
        "nesf,nesd->efd", activation, slot_back, preferred_element_type=jnp.float32
    )
    grad_expert_gate = jnp.einsum(
        "nesd,nesf->edf", rows, gate_grad, preferred_element_type=jnp.float32
    )
    grad_expert_up = jnp.einsum("nesd,nesf->edf", rows, up_grad, preferred_element_type=jnp.float32)
    rows_grad = jnp.einsum(
        "nesf,edf->nesd", gate_grad, expert_gate, preferred_element_type=jnp.float32
    )
    rows_grad = rows_grad + jnp.einsum(
        "nesf,edf->nesd", up_grad, expert_up, preferred_element_type=jnp.float32
    )
    slot_grad = lax.all_to_all(
        rows_grad.reshape(experts, -1, width), "ctx", split_axis=0, concat_axis=0, tiled=True
    ).reshape(experts, sequences, capacity, width)
    ffn_grad = ffn_grad + jnp.einsum("escb,escd->sbd", dispatch, slot_grad, precision=highest)
    hidden_part, grad_norm_ffn = root_norm_back(
        ffn_grad, unit_ffn, inverse_ffn, full_norm_ffn.astype(jnp.float32)
    )
    grad_hidden = grad_y + lax.psum(hidden_part, "wa")
    attention_grad = grad_hidden.astype(jnp.bfloat16)
    grad_output = jnp.einsum(
        "sbk,sbd->kd", head_out, attention_grad, preferred_element_type=jnp.float32
    )
    head_grad = (
        jnp.einsum("sbd,kd->sbk", attention_grad, full_output, preferred_element_type=jnp.float32)
        .astype(jnp.bfloat16)
        .reshape(sequences, block, heads_here, DV)
    )
    grad_value_up = jnp.einsum(
        "shbr,sbhv->rhv", latent_out, head_grad, preferred_element_type=jnp.float32
    )
    latent_out_grad = jnp.einsum(
        "sbhv,rhv->shbr", head_grad, value_up, preferred_element_type=jnp.float32
    ).astype(jnp.bfloat16)
    row_dot = jnp.sum(latent_out_grad.astype(jnp.float32) * latent_exact, axis=-1)

    def turn_body(turn, carry):
        keys_here, key_grad, query_grad = carry
        source_index = (context_index + turn) % context_count
        key_positions = source_index * block + jnp.arange(block)
        allowed = positions[:, None] >= key_positions[None, :]
        scores = (
            jnp.einsum("shqc,skc->shqk", query_rows, keys_here, preferred_element_type=jnp.float32)
            * scale
        )
        weights = jnp.where(allowed[None, None], jnp.exp(scores - log_total[..., None]), 0.0)
        weight_grad = jnp.einsum(
            "shqr,skr->shqk",
            latent_out_grad,
            keys_here[..., :R],
            preferred_element_type=jnp.float32,
        )
        score_grad = (weights * (weight_grad - row_dot[..., None])).astype(jnp.bfloat16)
        query_grad = (
            query_grad
            + jnp.einsum(
                "shqk,skc->shqc", score_grad, keys_here, preferred_element_type=jnp.float32
            )
            * scale
        )
        key_part = (
            jnp.einsum("shqk,shqc->skc", score_grad, query_rows, preferred_element_type=jnp.float32)
            * scale
        )
        value_part = jnp.einsum(
            "shqk,shqr->skr",
            weights.astype(jnp.bfloat16),
            latent_out_grad,
            preferred_element_type=jnp.float32,
        )
        key_grad = key_grad + key_part + jnp.pad(value_part, ((0, 0), (0, 0), (0, DR)))
        keys_next = shifted(keys_here, "ctx", -1)
        grad_next = shifted(key_grad, "ctx", -1)
        return (keys_next, grad_next, query_grad)

    start_back = (
        key_rows,
        jnp.zeros((sequences, block, R + DR), jnp.float32),
        jnp.zeros((sequences, heads_here, block, R + DR), jnp.float32),
    )
    unused_keys, key_grad, query_grad = lax.fori_loop(0, context_count, turn_body, start_back)
    key_grad_total = lax.psum(key_grad, "wa")
    query_grad_low = query_grad.astype(jnp.bfloat16)
    absorbed_grad = query_grad_low[..., :R]
    rope_query_grad = jnp.transpose(query_grad_low[..., R:], (0, 2, 1, 3)).astype(jnp.float32)
    grad_key_up = jnp.einsum(
        "shbr,sbhn->rhn", absorbed_grad, query_low[..., :DN], preferred_element_type=jnp.float32
    )
    nope_grad = jnp.einsum(
        "shbr,rhn->sbhn", absorbed_grad, key_up, preferred_element_type=jnp.float32
    )
    rope_raw_grad = rotate(rope_query_grad, cosine[:, None, :], -sine[:, None, :])
    query_raw_grad = (
        jnp.concatenate([nope_grad, rope_raw_grad], axis=-1)
        .astype(jnp.bfloat16)
        .reshape(sequences, block, heads_here * (DN + DR))
    )
    grad_query = jnp.einsum(
        "sbd,sbk->dk", input_low, query_raw_grad, preferred_element_type=jnp.float32
    )
    input_part = jnp.einsum(
        "sbk,dk->sbd", query_raw_grad, full_query, preferred_element_type=jnp.float32
    )
    grad_latent_up = jnp.concatenate([grad_key_up, grad_value_up], axis=-1).reshape(
        R, heads_here * (DN + DV)
    )
    latent_grad, grad_latent_norm = root_norm_back(
        key_grad_total[..., :R], latent_unit, latent_inverse, full_latent_norm.astype(jnp.float32)
    )
    rope_key_grad = rotate(key_grad_total[..., R:], cosine, -sine)
    latent_raw_grad = jnp.concatenate([latent_grad, rope_key_grad], axis=-1).astype(jnp.bfloat16)
    grad_down = jnp.einsum(
        "sbd,sbc->dc", input_low, latent_raw_grad, preferred_element_type=jnp.float32
    )
    input_part = input_part + lead * jnp.einsum(
        "sbc,dc->sbd", latent_raw_grad, full_down, preferred_element_type=jnp.float32
    )
    source_part, grad_norm_in = root_norm_back(
        input_part, unit_in, inverse_in, full_norm_in.astype(jnp.float32)
    )
    summed = lax.psum((source_part, grad_norm_in, grad_norm_ffn, grad_router), "wa")
    tokens_gradient = grad_hidden + summed[0]
    reduced = (
        lax.psum_scatter(summed[1], "ctx", scatter_dimension=0, tiled=True),
        lax.psum_scatter(grad_query, "ctx", scatter_dimension=0, tiled=True),
        lax.psum_scatter(grad_down, "ctx", scatter_dimension=0, tiled=True),
        lax.psum_scatter(grad_latent_norm, "ctx", scatter_dimension=0, tiled=True),
        lax.psum_scatter(grad_latent_up, "ctx", scatter_dimension=0, tiled=True),
        lax.psum_scatter(grad_output, "ctx", scatter_dimension=1, tiled=True),
        lax.psum_scatter(summed[2], "ctx", scatter_dimension=0, tiled=True),
        lax.psum_scatter(summed[3], "ctx", scatter_dimension=0, tiled=True),
        lax.psum_scatter(grad_shared_gate, "ctx", scatter_dimension=0, tiled=True),
        lax.psum_scatter(grad_shared_up, "ctx", scatter_dimension=0, tiled=True),
        lax.psum_scatter(grad_shared_down, "ctx", scatter_dimension=1, tiled=True),
    )
    return (
        output.astype(jnp.bfloat16),
        tokens_gradient,
        reduced[0],
        reduced[1],
        reduced[2],
        reduced[3],
        reduced[4],
        reduced[5],
        reduced[6],
        reduced[7],
        reduced[8],
        reduced[9],
        reduced[10],
        grad_expert_gate,
        grad_expert_up,
        grad_expert_down,
    )


def solution(mesh):
    return jax.shard_map(
        shards,
        mesh=mesh,
        in_specs=(
            P(None, "ctx", None),
            P("ctx"),
            P("ctx", "wa"),
            P("ctx", None),
            P("ctx"),
            P("ctx", "wa"),
            P("wa", "ctx"),
            P("ctx"),
            P("ctx", None),
            P("ctx", "wa"),
            P("ctx", "wa"),
            P("wa", "ctx"),
            P("ctx", None, "wa"),
            P("ctx", None, "wa"),
            P("ctx", "wa", None),
            P(None, "ctx", None),
            P(None, "ctx", None),
        ),
        out_specs=(
            P(None, "ctx", None),
            P(None, "ctx", None),
            P("ctx"),
            P("ctx", "wa"),
            P("ctx", None),
            P("ctx"),
            P("ctx", "wa"),
            P("wa", "ctx"),
            P("ctx"),
            P("ctx", None),
            P("ctx", "wa"),
            P("ctx", "wa"),
            P("wa", "ctx"),
            P("ctx", None, "wa"),
            P("ctx", None, "wa"),
            P("ctx", "wa", None),
        ),
        check_vma=False,
    )
```

profile of v0, /device:TPU:16, one launch (start us, length us, event | category | flops | bytes accessed | tf_op | source)
XLA Modules:
  0.0 2265.0 jit_solution(11840866376719816594)
XLA Ops:
  9.5 16.0 all-gather
  28.4 24.7 %all-reduce.1 = bf16[512]{0:T(512)(128)(2,1)S(1)} all-reduce(bf16[512]{0:T(512)(128)(2,1)S(1)} %dynamic-update-slice), channel_id=1, replica_groups=mesh['ctx'=16,'wa'=2] {'ctx'}, use_global_device_ids=true, to_apply=%add.1 | all-reduce | flops 512 | bytes 2048
  62.5 32.0 %all-gather.13.cloned.1.call-done = bf16[512,2048]{1,0:T(8,128)(2,1)} async-done(((bf16[32,2048]{1,0:T(8,128)(2,1)}), bf16[512,2048]{1,0:T(8,128)(2,1)}) %all-gather.13.cloned.1.call-update) | async-done | bytes 2097168 | tf_op jit(solution)/shard_map/all_gather | solution.py:75
  98.5 60.3 %all-gather.11.cloned.1.call-done = bf16[2048,1536]{1,0:T(8,128)(2,1)} async-done(((bf16[128,1536]{1,0:T(8,128)(2,1)}), bf16[2048,1536]{1,0:T(8,128)(2,1)}) %all-gather.11.cloned.1.call-update) | async-done | bytes 6291472 | tf_op jit(solution)/shard_map/all_gather | solution.py:72
  158.7 4.7 fusion.22
  171.1 31.8 %all-gather.17.cloned.1.call-done = bf16[2,1024,576]{2,1,0:T(8,128)(2,1)} async-done(((bf16[2,64,576]{2,1,0:T(8,128)(2,1)}), bf16[2,1024,576]{2,1,0:T(8,128)(2,1)}) %all-gather.17.cloned.1.call-update) | async-done | bytes 2359312 | tf_op jit(solution)/shard_map/all_gather | solution.py:167
  215.0 41.8 %all-gather.19.cloned.1.call-done = bf16[1024,2048]{1,0:T(8,128)(2,1)} async-done(((bf16[1024,128]{1,0:T(8,128)(2,1)}), bf16[1024,2048]{1,0:T(8,128)(2,1)}) %all-gather.19.cloned.1.call-update) | async-done | bytes 4194320 | tf_op jit(solution)/shard_map/all_gather | solution.py:76
  265.4 14.9 all-gather.1
  280.8 19.3 all-reduce.13.cloned.1.call-done
  305.3 98.7 %all_to_all.20 = bf16[16,64,2048]{2,1,0:T(8,128)(2,1)S(1)} all-to-all(bf16[16,64,2048]{2,1,0:T(8,128)(2,1)S(1)} %bitcast.397), channel_id=1, replica_groups=mesh['ctx'=16,'wa'=2] {'ctx'}, dimensions={0} | all-to-all | bytes 8388608 | tf_op jit(solution)/shard_map/all_to_all | solution.py:231
  413.8 5.7 fusion.52
  419.5 5.1 all-to-all-start.1
  425.4 228.0 %all_gather.58 = bf16[2048,16]{0,1:T(8,128)(2,1)} all-gather(bf16[128,16]{0,1:T(8,128)(2,1)S(1)} %copy-done.72), channel_id=1, replica_groups=mesh['ctx'=16,'wa'=2] {'ctx'}, dimensions={0}, use_global_device_ids=true | all-gather | bytes 69632 | tf_op jit(solution)/shard_map/all_gather | solution.py:78
  657.2 7.3 fusion.17
  672.0 126.4 %all-to-all-done.2 = bf16[16,64,2048]{2,1,0:T(8,128)(2,1)} async-done(((bf16[16,64,2048]{2,1,0:T(8,128)(2,1)}), bf16[16,64,2048]{2,1,0:T(8,128)(2,1)}, u32[]{:S(2)}, u32[]{:S(2)}) %all-to-all-start.2) | async-done | bytes 4194336 | tf_op jit(solution)/shard_map/all_to_all | solution.py:318
  798.4 8.4 fusion.84
  810.4 5.8 convolution_add_fusion
  816.1 5.3 all-to-all-start.3
  822.6 4.6 fusion.24
  827.3 4.5 fusion.30
  831.8 159.5 %all-gather.21.cloned.1.call-done = bf16[2048,1408]{1,0:T(8,128)(2,1)} async-done(((bf16[128,1408]{1,0:T(8,128)(2,1)}), bf16[2048,1408]{1,0:T(8,128)(2,1)}) %all-gather.21.cloned.1.call-update) | async-done | bytes 5767184 | tf_op jit(solution)/shard_map/all_gather | solution.py:79
  991.3 4.9 multiply_convert_fusion.2
  1003.2 35.6 %all-to-all-done.3 = f32[16,64,2048]{2,1,0:T(8,128)} async-done(((f32[16,64,2048]{2,1,0:T(8,128)}), f32[16,64,2048]{2,1,0:T(8,128)}, u32[]{:S(2)}, u32[]{:S(2)}) %all-to-all-start.3) | async-done | bytes 8388640 | tf_op jit(solution)/shard_map/all_to_all | solution.py:344
  1038.7 7.8 multiply_reduce_fusion.1
  1051.7 34.9 %all-reduce.15.cloned.1.call-done = f32[2,64,2048]{2,1,0:T(8,128)} async-done(((f32[2,64,2048]{2,1,0:T(8,128)}), f32[2,64,2048]{2,1,0:T(8,128)}) %all-reduce.15.cloned.1.call-update) | async-done | bytes 1048592 | tf_op jit(solution)/shard_map/psum | solution.py:351
  1095.8 205.2 %while.20 = (s32[]{:T(128)}, bf16[2,64,576]{2,1,0:T(8,128)(2,1)S(1)}, f32[2,64,576]{2,1,0:T(8,128)S(1)}, f32[2,8,64,576]{3,2,1,0:T(8,128)}, s32[]{:T(128)}, /*in...) while((s32[]{:T(128)}, ...), condition=%wide.region_19.20_spmd.clone, body=%wide.region_18.19_spmd.clone.sunk | while | flops 363163776 | bytes 14243188 | solution.py:413
  1301.8 7.6 fusion.63
  1309.8 5.1 fusion.71
  1319.5 6.1 fusion.20
  1325.6 15.2 all-reduce.17.cloned.1.call-done
  1349.0 7.0 convolution_bitcast_fusion.4
  1356.1 7.1 convolution_bitcast_fusion.3
  1363.2 7.1 convolution_bitcast_fusion.2
  1376.0 5.4 copy.147
  1386.7 4.5 convolution_bitcast_fusion.6
  1392.1 6.5 convolution_bitcast_fusion.5
  1400.1 8.1 convolution_bitcast_fusion.8
  1408.2 5.1 convolution_bitcast_fusion.7
  1413.2 8.0 convolution_bitcast_fusion.9
  1421.2 45.3 %all-reduce.5 = (f32[2048]{0:T(1024)S(1)}, f32[512]{0:T(512)S(1)}, f32[2048]{0:T(1024)S(1)}) all-reduce(f32[2048]{0:T(1024)S(1)} %copy-done.61, f32[512]{0:T(512)S(1)} %get-tuple-element.343, f32[2048]{0:T(1024)S(1)} %copy-done.58), channel_id=2, replica_groups=mesh['ctx'=16,'wa'=2] {'ctx'}, use_global_device_ids=true, to_apply=%region_26.27.clone | all-reduce | flops 4608 | bytes 36864
  1467.2 5.7 all-reduce.6
  1477.2 115.7 %reduce-scatter.17.cloned.1.call-done = f32[128,1408]{1,0:T(8,128)} async-done(((f32[2048,1408]{1,0:T(8,128)}), f32[128,1408]{1,0:T(8,128)}) %reduce-scatter.17.cloned.1.call-update) | async-done | bytes 720912 | tf_op jit(solution)/shard_map/reduce_scatter | solution.py:464
  1592.9 130.6 %reduce-scatter.19.cloned.1.call-done = f32[128,1408]{1,0:T(8,128)} async-done(((f32[2048,1408]{1,0:T(8,128)}), f32[128,1408]{1,0:T(8,128)}) %reduce-scatter.19.cloned.1.call-update) | async-done | bytes 720912 | tf_op jit(solution)/shard_map/reduce_scatter | solution.py:465
  1723.5 131.2 %reduce-scatter.21.cloned.1.call-done = f32[1408,128]{1,0:T(8,128)} async-done(((f32[1408,2048]{1,0:T(8,128)}), f32[1408,128]{1,0:T(8,128)}) %reduce-scatter.21.cloned.1.call-update) | async-done | bytes 720912 | tf_op jit(solution)/shard_map/reduce_scatter | solution.py:466
  1854.7 76.0 %reduce-scatter.13.cloned.1.call-done = f32[32,2048]{1,0:T(8,128)} async-done(((f32[512,2048]{1,0:T(8,128)}), f32[32,2048]{1,0:T(8,128)}) %reduce-scatter.13.cloned.1.call-update) | async-done | bytes 262160 | tf_op jit(solution)/shard_map/reduce_scatter | solution.py:460
  1930.7 79.3 %reduce-scatter.11.cloned.1.call-done = f32[128,576]{0,1:T(8,128)} async-done(((f32[2048,576]{0,1:T(8,128)}), f32[128,576]{0,1:T(8,128)}) %reduce-scatter.11.cloned.1.call-update) | async-done | bytes 294928 | tf_op jit(solution)/shard_map/reduce_scatter | solution.py:458
  2010.0 109.4 %reduce-scatter.15.cloned.1.call-done = f32[1024,128]{1,0:T(8,128)} async-done(((f32[1024,2048]{1,0:T(8,128)}), f32[1024,128]{1,0:T(8,128)}) %reduce-scatter.15.cloned.1.call-update) | async-done | bytes 524304 | tf_op jit(solution)/shard_map/reduce_scatter | solution.py:461
  2119.4 138.3 %reduce-scatter.9.cloned.1.call-done = f32[128,1536]{1,0:T(8,128)} async-done(((f32[2048,1536]{1,0:T(8,128)}), f32[128,1536]{1,0:T(8,128)}) %reduce-scatter.9.cloned.1.call-update) | async-done | bytes 786448 | tf_op jit(solution)/shard_map/reduce_scatter | solution.py:457
  (523 shorter events, 334.4 us)
Async XLA Ops:
  7.2 48.0 %all-gather.15.cloned.1.call-start = ((), (), s32[]{:S(2)}) async-start(), calls=%async_computation.14 | async-start | bytes 2506752 | tf_op jit(solution)/shard_map/all_gather | solution.py:73
  7.9 86.6 %all-gather.13.cloned.1.call-start = ((), (), s32[]{:S(2)}) async-start(), calls=%async_computation.13 | async-start | bytes 2228224 | tf_op jit(solution)/shard_map/all_gather | solution.py:75
  8.7 150.1 %all-gather.11.cloned.1.call-start = ((), (), s32[]{:S(2)}) async-start(), calls=%async_computation.12 | async-start | bytes 6684672 | tf_op jit(solution)/shard_map/all_gather | solution.py:72
  9.4 193.4 %all-gather.17.cloned.1.call-start = ((), (), s32[]{:S(2)}) async-start(), calls=%async_computation.15 | async-start | bytes 2785280 | tf_op jit(solution)/shard_map/all_gather | solution.py:167
  59.6 197.2 %all-gather.19.cloned.1.call-start = ((), (), s32[]{:S(2)}) async-start(), calls=%async_computation.16 | async-start | bytes 4456448 | tf_op jit(solution)/shard_map/all_gather | solution.py:76
  60.2 239.9 %all-reduce.13.cloned.1.call-start = ((), (), s32[]{:S(2)}) async-start(), calls=%async_computation.17 | async-start | bytes 2097152 | tf_op jit(solution)/shard_map/psum | solution.py:196
  419.5 237.7 %all-to-all-start.1 = ((f32[16,64,2048]{2,1,0:T(8,128)}), f32[16,64,2048]{2,1,0:T(8,128)}, u32[]{:S(2)}, u32[]{:S(2)}) async-start(f32[16,64,2048]{2,1,0:T(8,128)} %fusion.52), calls=%async_computation.1 | async-start | bytes 16777216 | tf_op jit(solution)/shard_map/all_to_all | solution.py:240
  424.6 398.0 %all-gather.25.cloned.1.call-start = ((), (), s32[]{:S(2)}) async-start(), calls=%async_computation.20 | async-start | bytes 6127616 | tf_op jit(solution)/shard_map/all_gather | solution.py:81
  666.8 131.6 %all-to-all-start.2 = ((bf16[16,64,2048]{2,1,0:T(8,128)(2,1)}), bf16[16,64,2048]{2,1,0:T(8,128)(2,1)}, u32[]{:S(2)}, u32[]{:S(2)}) async-start(bf16[16,64,2048]{2,1,0:T(8,128)(2,1)} %bitcast.395), calls=%async_computation.2 | async-start | bytes 8388608 | tf_op jit(solution)/shard_map/all_to_all | solution.py:318
  671.3 156.0 %all-gather.23.cloned.1.call-start = ((), (), s32[]{:S(2)}) async-start(), calls=%async_computation.19 | async-start | bytes 6127616 | tf_op jit(solution)/shard_map/all_gather | solution.py:80
  816.1 222.6 %all-to-all-start.3 = ((f32[16,64,2048]{2,1,0:T(8,128)}), f32[16,64,2048]{2,1,0:T(8,128)}, u32[]{:S(2)}, u32[]{:S(2)}) async-start(f32[16,64,2048]{2,1,0:T(8,128)} %convolution_add_fusion), calls=%async_computation.3 | async-start | bytes 16777216 | tf_op jit(solution)/shard_map/all_to_all | solution.py:344
  821.4 169.9 %all-gather.21.cloned.1.call-start = ((), (), s32[]{:S(2)}) async-start(), calls=%async_computation.18 | async-start | bytes 6127616 | tf_op jit(solution)/shard_map/all_gather | solution.py:79
  822.1 264.5 %all-reduce.15.cloned.1.call-start = ((), (), s32[]{:S(2)}) async-start(), calls=%async_computation.21 | async-start | bytes 2097152 | tf_op jit(solution)/shard_map/psum | solution.py:351
  1047.8 293.0 %all-reduce.17.cloned.1.call-start = ((), (), s32[]{:S(2)}) async-start(), calls=%async_computation.22 | async-start | bytes 655360 | tf_op jit(solution)/shard_map/psum | solution.py:414
  1095.8 8.0 collective-permute-start
  1106.5 11.0 collective-permute-start
  1118.4 11.0 collective-permute-start
  1130.3 11.0 collective-permute-start
  1142.3 11.0 collective-permute-start
  1154.2 11.0 collective-permute-start
  1166.1 11.0 collective-permute-start
  1178.1 12.3 collective-permute-start
  1185.3 5.9 collective-permute-start.1
  1191.2 12.8 collective-permute-start
  1198.5 6.5 collective-permute-start.1
  1205.0 12.8 collective-permute-start
  1212.2 6.5 collective-permute-start.1
  1218.7 12.8 collective-permute-start
  1225.9 6.5 collective-permute-start.1
  1232.4 12.8 collective-permute-start
  1239.6 6.5 collective-permute-start.1
  1246.2 12.8 collective-permute-start
  1253.4 6.5 collective-permute-start.1
  1259.9 12.8 collective-permute-start
  1267.1 6.5 collective-permute-start.1
  1273.6 12.8 collective-permute-start
  1280.8 6.5 collective-permute-start.1
  1287.3 12.8 collective-permute-start
  1294.6 6.5 collective-permute-start.1
  1301.8 165.4 %reduce-scatter.23.cloned.1.call-start = ((), (), s32[]{:S(2)}) async-start(), calls=%async_computation.30 | async-start | bytes 139264 | tf_op jit(solution)/shard_map/reduce_scatter | solution.py:463
  1309.5 163.5 %all-reduce.19.cloned.1.call-start = ((), (), s32[]{:S(2)}) async-start(), calls=%async_computation.31 | async-start | bytes 4194304 | tf_op jit(solution)/shard_map/psum | solution.py:252
  1349.0 243.9 %reduce-scatter.17.cloned.1.call-start = ((), (), s32[]{:S(2)}) async-start(), calls=%async_computation.27 | async-start | bytes 12255232 | tf_op jit(solution)/shard_map/reduce_scatter | solution.py:464
  1356.0 367.5 %reduce-scatter.19.cloned.1.call-start = ((), (), s32[]{:S(2)}) async-start(), calls=%async_computation.28 | async-start | bytes 12255232 | tf_op jit(solution)/shard_map/reduce_scatter | solution.py:465
  1363.2 491.5 %reduce-scatter.21.cloned.1.call-start = ((), (), s32[]{:S(2)}) async-start(), calls=%async_computation.29 | async-start | bytes 12255232 | tf_op jit(solution)/shard_map/reduce_scatter | solution.py:466
  1370.4 560.3 %reduce-scatter.13.cloned.1.call-start = ((), (), s32[]{:S(2)}) async-start(), calls=%async_computation.25 | async-start | bytes 4456448 | tf_op jit(solution)/shard_map/reduce_scatter | solution.py:460
  1381.5 628.6 %reduce-scatter.11.cloned.1.call-start = ((), (), s32[]{:S(2)}) async-start(), calls=%async_computation.24 | async-start | bytes 5013504 | tf_op jit(solution)/shard_map/reduce_scatter | solution.py:458
  1385.3 734.2 %reduce-scatter.15.cloned.1.call-start = ((), (), s32[]{:S(2)}) async-start(), calls=%async_computation.26 | async-start | bytes 8912896 | tf_op jit(solution)/shard_map/reduce_scatter | solution.py:461
  1391.2 866.5 %reduce-scatter.9.cloned.1.call-start = ((), (), s32[]{:S(2)}) async-start(), calls=%async_computation.23 | async-start | bytes 13369344 | tf_op jit(solution)/shard_map/reduce_scatter | solution.py:457
  (91 other events, 2543.4 us)
Sparse Core Ops, SparseCore 0:
  10.2 42.9 all-gather.14
  55.3 39.1 all-gather.12
  96.8 61.8 all-gather.10
  161.4 41.3 all-gather.16
  204.9 51.9 all-gather.18
  260.9 39.1 all-reduce.12
  427.8 178.3 all-gather.24
  674.7 109.8 all-gather.22
  824.8 166.4 all-gather.20
  1048.0 38.6 all-reduce.14
  1301.9 38.8 all-reduce.16
  1344.4 51.2 reduce-scatter.22
  1398.7 63.0 all-reduce.18
  1466.9 126.0 reduce-scatter.16
  1597.4 126.0 reduce-scatter.18
  1728.6 126.0 reduce-scatter.20
  1859.0 71.6 reduce-scatter.12
  1935.5 74.5 reduce-scatter.10
  2014.7 104.7 reduce-scatter.14
  2123.9 133.7 reduce-scatter.8
where the time goes:
time: 2280 us; the launch traced here: 2260 us
  waiting for transfers between devices  1360 us (60%)
  blocking collectives  433 us (19%)
  matrix products  307 us (13%)
  starting transfers between devices  78.2 us (3%)
  local copies, waits for them, and re-layouts  40.7 us (2%)
  other arithmetic  29.7 us (1%)
    all_gather x1, blocking collectives, fetch_weights(): lax.all_gather(router_weight, 'ctx', axis=0, tiled=True)  228 us
    all_gather x1, waiting for transfers between devices, fetch_weights(): lax.all_gather(shared_gate, 'ctx', axis=0, tiled=True)  160 us
    reduce_scatter x1, waiting for transfers between devices, shards(): lax.psum_scatter(grad_query, 'ctx', scatter_dimension=0, tiled=True)  138 us
    reduce_scatter x1, waiting for transfers between devices, shards(): lax.psum_scatter(grad_shared_down, 'ctx', scatter_dimension=1, tiled=True)  131 us
    reduce_scatter x1, waiting for transfers between devices, shards(): lax.psum_scatter(grad_shared_up, 'ctx', scatter_dimension=0, tiled=True)  131 us
    all_to_all x1, waiting for transfers between devices, shards(): lax.all_to_all(slot_grads, 'ctx', split_axis=0, concat_axis=0, tiled=True)  126 us
    reduce_scatter x1, waiting for transfers between devices, shards(): lax.psum_scatter(grad_shared_gate, 'ctx', scatter_dimension=0, tiled=True)  116 us
    reduce_scatter x1, waiting for transfers between devices, shards(): lax.psum_scatter(grad_output, 'ctx', scatter_dimension=1, tiled=True)  109 us
  transfers between devices with their start and end apart: 55, of which 33 were waited for; matrix products, arithmetic and copies ran while one was open for 14% of the time, Pallas kernels for 0%

commit v1 on v0

--- a/solution.py
+++ b/solution.py
@@ -1,7 +1,7 @@
 import jax
 import jax.numpy as jnp
 from jax import lax
-from jax.sharding import PartitionSpec as P
+from jax.sharding import Mesh, PartitionSpec as P
 
 DN = 128
 DR = 64
@@ -485,46 +485,529 @@
     )
 
 
+CTX = ("z", "x", "c")
+
+
+def swap(value, axis):
+    return lax.ppermute(value, axis, [(0, 1), (1, 0)])
+
+
+def from_z(value, steps):
+    count = lax.axis_size("z")
+    return lax.ppermute(value, "z", [((i + steps) % count, i) for i in range(count)])
+
+
+def to_z(value, steps):
+    count = lax.axis_size("z")
+    return lax.ppermute(value, "z", [(i, (i + steps) % count) for i in range(count)])
+
+
+def trade(value, axes):
+    return lax.all_to_all(value, axes, split_axis=0, concat_axis=0, tiled=True)
+
+
+def add(left, right):
+    return left.astype(jnp.float32) + right.astype(jnp.float32)
+
+
+def low(value):
+    return value.astype(jnp.bfloat16)
+
+
+def dot(left, right):
+    return jnp.dot(left, right, preferred_element_type=jnp.float32)
+
+
+def dot_nt(left, right):
+    return lax.dot_general(
+        left, right, (((1,), (1,)), ((), ())), preferred_element_type=jnp.float32
+    )
+
+
+def dot_tn(left, right):
+    return lax.dot_general(
+        left, right, (((0,), (0,)), ((), ())), preferred_element_type=jnp.float32
+    )
+
+
+def by_own(value, axis_name, dim):
+    flipped = jnp.flip(value, axis=dim)
+    return jnp.where(lax.axis_index(axis_name) == 0, value, flipped)
+
+
+def gather_z(value):
+    count = lax.axis_size("z")
+    return trade(jnp.broadcast_to(value[None], (count,) + value.shape), "z")
+
+
+def gather_ctx(value):
+    slabs = gather_z(value)
+    slabs = by_own(jnp.stack([slabs, swap(slabs, "x")], axis=1), "x", 1)
+    slabs = by_own(jnp.stack([slabs, swap(slabs, "c")], axis=2), "c", 2)
+    return slabs.reshape((-1,) + value.shape)
+
+
+def gather_plane(rows):
+    half = rows.shape[0] // 2
+    over_x = swap(rows, "x")
+    over_y = swap(rows, "y")
+    both = jnp.concatenate([swap(over_y[:half], "x"), swap(over_x[half:], "y")], axis=0)
+    return jnp.stack([jnp.stack([rows, over_y]), jnp.stack([over_x, both])])
+
+
+def scatter_plane(rows):
+    half = rows.shape[2] // 2
+    lower, upper = (rows[:, :, :half], rows[:, :, half:])
+    lower = low(add(lower[0], swap(lower[1], "x")))
+    upper = low(add(upper[:, 0], swap(upper[:, 1], "y")))
+    lower = add(lower[0], swap(lower[1], "y"))
+    upper = add(upper[0], swap(upper[1], "x"))
+    return jnp.concatenate([lower, upper], axis=0)
+
+
+def gather_all(rows):
+    count = lax.axis_size("z")
+    slabs = jnp.concatenate([rows] + [from_z(rows, s) for s in range(1, count)], axis=0)
+    own = gather_plane(slabs)
+    return (own, swap(own, "c"))
+
+
+def scatter_all(own, other):
+    count = lax.axis_size("z")
+    own = low(add(own, swap(other, "c")))
+    slabs = scatter_plane(own)
+    block = slabs.shape[0] // count
+    sent = low(slabs)
+    total = slabs[:block]
+    for s in range(1, count):
+        total = total + to_z(sent[s * block : (s + 1) * block], s).astype(jnp.float32)
+    return total
+
+
+def sum_z(value):
+    return jnp.sum(trade(value, "z").astype(jnp.float32).reshape((lax.axis_size("z"), -1) + value.shape[1:]), axis=0)
+
+
+def both_halves(rows):
+    other = swap(rows, "y")
+    return by_own(jnp.stack([rows, other]), "y", 0)
+
+
+def dense_shards(
+    tokens,
+    norm_in,
+    query_weight,
+    latent_down,
+    latent_norm,
+    latent_up,
+    output_weight,
+    norm_ffn,
+    router_weight,
+    shared_gate,
+    shared_up,
+    shared_down,
+    expert_gate,
+    expert_up,
+    expert_down,
+    routes,
+    cotangent,
+):
+    zs = lax.axis_size("z")
+    z, x, c = (lax.axis_index("z"), lax.axis_index("x"), lax.axis_index("c"))
+    me = (z * 2 + x) * 2 + c
+    sequences, block, width = tokens.shape
+    count = 4 * zs
+    rows_here = width // count
+    slab = 4 * block
+    experts = router_weight.shape[1]
+    hidden_here = expert_gate.shape[2]
+    shared_here = shared_gate.shape[1] // count
+    used = hidden_here + shared_here
+    padded = -(-(used + experts) // 128) * 128
+    heads = latent_up.shape[1] // (4 * (DN + DV))
+    query_columns = heads * (DN + DR)
+    rank_rows = R // count
+    head_rows = heads * DV
+    scale = (DN + DR) ** (-0.5)
+
+    extra = jnp.zeros((rows_here, 1), jnp.bfloat16)
+    latent_column = jnp.pad(latent_norm, (0, rows_here - rank_rows))[:, None]
+    small = jnp.concatenate(
+        [
+            latent_down,
+            router_weight,
+            norm_in[:, None],
+            norm_ffn[:, None],
+            latent_column,
+            routes.reshape(sequences * block, TOPK).astype(jnp.bfloat16),
+        ],
+        axis=1,
+    )
+    small = jnp.pad(small, ((0, 0), (0, -small.shape[1] % 128)))
+    small = gather_ctx(small)
+    small_rows = small.reshape(width, -1)
+    at = R + DR
+    full_down = small_rows[:, :at]
+    full_router = small_rows[:, at : at + experts]
+    full_norm_in = small_rows[:, at + experts].astype(jnp.float32)
+    full_norm_ffn = small_rows[:, at + experts + 1].astype(jnp.float32)
+    full_latent_norm = small[:, :rank_rows, at + experts + 2].reshape(R).astype(jnp.float32)
+    all_routes = small[:, :, at + experts + 3 : at + experts + 3 + TOPK]
+
+    by_heads = jnp.transpose(query_weight.reshape(rows_here, 4, query_columns), (1, 0, 2))
+    query_here = gather_z(trade(by_heads, ("x", "c"))).reshape(width, query_columns)
+    up_part = jnp.transpose(
+        latent_up.reshape(rank_rows, 4, heads * (DN + DV)), (1, 0, 2)
+    ).reshape(4, -1, 128)
+    out_part = jnp.transpose(output_weight.reshape(4, heads, DV, rows_here), (0, 2, 1, 3)).reshape(
+        4, DV, heads * rows_here
+    )
+    up_columns = heads * (DN + DV) * rank_rows // DV
+    up_part = up_part.reshape(4, DV, up_columns)
+    by_heads = jnp.concatenate([up_part, out_part], axis=2)
+    up_out = gather_z(trade(by_heads, ("x", "c"))).reshape(count, DV, -1)
+    up_here = up_out[:, :, :up_columns].reshape(R, heads, DN + DV)
+    key_up = up_here[..., :DN]
+    value_up = up_here[..., DN:]
+    out_here = jnp.transpose(
+        up_out[:, :, up_columns:].reshape(count, DV, heads, rows_here), (2, 1, 0, 3)
+    ).reshape(head_rows, width)
+
+    shared_mine = jnp.concatenate(
+        [
+            shared_gate.T.reshape(count, shared_here, rows_here),
+            shared_up.T.reshape(count, shared_here, rows_here),
+            shared_down.reshape(count, shared_here, rows_here),
+        ],
+        axis=1,
+    )
+    shared_here_rows = jnp.transpose(trade(shared_mine, CTX), (1, 0, 2)).reshape(-1, width)
+    gate_rows = shared_here_rows[:shared_here]
+    up_rows = shared_here_rows[shared_here : 2 * shared_here]
+    down_rows = shared_here_rows[2 * shared_here :]
+    first = jnp.concatenate(
+        [
+            expert_gate[0],
+            gate_rows.T,
+            full_router,
+            jnp.zeros((width, padded - used - experts), jnp.bfloat16),
+            expert_up[0],
+            up_rows.T,
+            jnp.zeros((width, padded - used), jnp.bfloat16),
+        ],
+        axis=1,
+    )
+    second = jnp.concatenate(
+        [expert_down[0], down_rows, jnp.zeros((padded - used, width), jnp.bfloat16)], axis=0
+    )
+
+    mine = by_own(tokens, "y", 0)
+    line = jnp.stack([mine, swap(mine, "x")], axis=1)
+    line = jnp.stack([line, swap(line, "c")], axis=1)
+    source = line.reshape(sequences * slab, width).astype(jnp.float32)
+    grad_mine = by_own(cotangent, "y", 0)[0]
+    grads_own, grads_other = gather_all(grad_mine)
+
+    def places(turn):
+        columns = jnp.arange(2)
+        base = ((z + turn) % zs) * 4 + (x ^ columns[None, :]) * 2 + (c ^ columns[:, None])
+        return (base[:, :, None] * block + jnp.arange(block)).reshape(slab)
+
+    positions = places(0)
+    key_positions = jnp.concatenate([places(turn) for turn in range(zs)])
+    cosine, sine = rotary_tables(positions, DR)
+    normed, unit_in, inverse_in = root_norm(source, full_norm_in)
+    input_low = low(normed)
+    query_raw = dot(input_low, query_here).reshape(sequences, slab, heads, DN + DR)
+    query_low = low(
+        jnp.concatenate(
+            [
+                query_raw[..., :DN],
+                rotate(query_raw[..., DN:], cosine[:, None, :], sine[:, None, :]),
+            ],
+            axis=-1,
+        )
+    )
+    absorbed = jnp.einsum(
+        "sbhn,rhn->shbr", query_low[..., :DN], key_up, preferred_element_type=jnp.float32
+    )
+    query_rows = jnp.concatenate(
+        [low(absorbed), jnp.transpose(query_low[..., DN:], (0, 2, 1, 3))], axis=-1
+    )
+    latent_raw = dot(input_low, full_down).reshape(sequences, slab, R + DR)
+    latent_scaled, latent_unit, latent_inverse = root_norm(latent_raw[..., :R], full_latent_norm)
+    key_slab = low(
+        jnp.concatenate([latent_scaled, rotate(latent_raw[..., R:], cosine, sine)], axis=-1)
+    )
+    half_keys = key_slab[:, : slab // 2]
+    far = jnp.stack([from_z(half_keys, s) for s in range(1, zs)], axis=1)
+    far = jnp.stack([far, swap(far, "c")], axis=2).reshape(sequences, (zs - 1) * slab, R + DR)
+    keys = jnp.concatenate([key_slab, far], axis=1)
+
+    scores = (
+        jnp.einsum("shqc,skc->shqk", query_rows, keys, preferred_element_type=jnp.float32) * scale
+    )
+    allowed = positions[:, None] >= key_positions[None, :]
+    scores = jnp.where(allowed, scores, -1e30)
+    top = jnp.max(scores, axis=-1, keepdims=True)
+    weights = jnp.exp(scores - top)
+    prob = weights / jnp.sum(weights, axis=-1, keepdims=True)
+    prob_low = low(prob)
+    latent_out = low(
+        jnp.einsum("shqk,skr->shqr", prob_low, keys[..., :R], preferred_element_type=jnp.float32)
+    )
+    head_out = low(
+        jnp.einsum("shbr,rhv->sbhv", latent_out, value_up, preferred_element_type=jnp.float32)
+    ).reshape(sequences * slab, head_rows)
+
+    def scatter_slab(partial):
+        parts = partial.reshape(2, 2, 2, block, -1)
+        kept = low(add(parts[:, 0], swap(parts[:, 1], "c")))
+        return scatter_plane(jnp.transpose(kept, (1, 0, 2, 3)))
+
+    def gather_slab(rows):
+        plane = jnp.transpose(gather_plane(rows), (1, 0, 2, 3))
+        return jnp.stack([plane, swap(plane, "c")], axis=1).reshape(sequences * slab, -1)
+
+    attention = scatter_slab(low(dot(head_out, out_here)))
+    hidden_in = mine[0].astype(jnp.float32) + attention
+    normed_ffn, unit_ffn, inverse_ffn = root_norm(hidden_in, full_norm_ffn)
+    ffn_low = low(normed_ffn)
+    shares = jax.nn.softmax(dot(ffn_low, full_router), axis=-1)
+    ffn_own, ffn_other = gather_all(ffn_low)
+
+    relative = all_routes.reshape(zs, 2, 2, sequences, block, TOPK)
+    relative = by_own(by_own(by_own(relative, "x", 1), "c", 2), "y", 3)
+    relative = jnp.roll(relative, -z, axis=0)
+    routed = jnp.any(relative == me.astype(jnp.bfloat16), axis=-1)
+    routed = jnp.transpose(routed, (2, 1, 3, 0, 4)).reshape(2, -1).astype(jnp.float32)
+    column = jnp.arange(padded)
+    is_expert = (column < hidden_here)[None, :]
+    is_shared = ((column >= hidden_here) & (column < used))[None, :]
+    picked = (jnp.arange(experts) == me)[None, :]
+
+    def feed(rows, grads, named):
+        rows = rows.reshape(-1, width)
+        grads = grads.reshape(-1, width)
+        both = dot(rows, first)
+        gate = both[:, :padded]
+        up = both[:, padded:]
+        chances = jax.nn.softmax(gate[:, used : used + experts], axis=-1)
+        share = jnp.sum(jnp.where(picked, chances, 0.0), axis=-1) * named
+        factor = jnp.where(is_expert, share[:, None], jnp.where(is_shared, 1.0, 0.0))
+        sigmoid = jax.nn.sigmoid(gate)
+        silu = gate * sigmoid
+        slope = sigmoid * (1.0 + gate * (1.0 - sigmoid))
+        act = silu * up
+        back = dot_nt(grads, second)
+        gain = jnp.sum(jnp.where(is_expert, low(act).astype(jnp.float32) * back, 0.0), axis=-1)
+        back = back * factor
+        pre = jnp.concatenate([low(back * up * slope), low(back * silu)], axis=1)
+        act = low(act * factor)
+        return (act, pre, gain * named)
+
+    act_own, pre_own, gain_own = feed(ffn_own, grads_own, routed[0])
+    act_other, pre_other, gain_other = feed(ffn_other, grads_other, routed[1])
+    shape = (2, 2, zs * block, width)
+    ffn_grad = scatter_all(
+        low(dot_nt(pre_own, first)).reshape(shape), low(dot_nt(pre_other, first)).reshape(shape)
+    )
+    routed_sum = scatter_all(
+        low(dot(act_own, second)).reshape(shape), low(dot(act_other, second)).reshape(shape)
+    )
+    output = both_halves(low(hidden_in + routed_sum))
+
+    gains = jnp.stack([gain_own, gain_other]).reshape(2, 2, 2, zs, block)
+    gains = by_own(by_own(by_own(gains, "c", 0), "x", 1), "y", 2)
+    gains = jnp.roll(jnp.transpose(gains, (3, 1, 0, 2, 4)), z, axis=0)
+    gains = trade(gains.reshape(2 * count, block), CTX + ("y",))
+    share_grad = jnp.sum(gains.reshape(count, 2, block), axis=1).T
+    logit_grad = shares * (share_grad - jnp.sum(shares * share_grad, axis=-1, keepdims=True))
+
+    all_rows = jnp.concatenate([ffn_own.reshape(-1, width), ffn_other.reshape(-1, width)])
+    all_grads = jnp.concatenate([grads_own.reshape(-1, width), grads_other.reshape(-1, width)])
+    all_act = jnp.concatenate([act_own, act_other])
+    all_pre = jnp.concatenate([pre_own, pre_other])
+    grad_expert_down = dot_tn(all_act[:, :hidden_here], all_grads)[None]
+    grad_expert_gate = dot_tn(all_rows, all_pre[:, :hidden_here])[None]
+    grad_expert_up = dot_tn(all_rows, all_pre[:, padded : padded + hidden_here])[None]
+    shared_pre = jnp.concatenate(
+        [all_pre[:, hidden_here:used], all_pre[:, padded + hidden_here : padded + used]], axis=1
+    )
+    shared_back = jnp.concatenate(
+        [
+            low(dot_tn(shared_pre, all_rows)),
+            low(dot_tn(all_act[:, hidden_here:used], all_grads)),
+        ]
+    )
+    shared_back = trade(
+        jnp.transpose(shared_back.reshape(-1, count, rows_here), (1, 0, 2)), CTX
+    ).astype(jnp.float32)
+    grad_shared_gate = shared_back[:, :shared_here].reshape(-1, rows_here).T
+    grad_shared_up = shared_back[:, shared_here : 2 * shared_here].reshape(-1, rows_here).T
+    grad_shared_down = shared_back[:, 2 * shared_here :].reshape(-1, rows_here)
+
+    ffn_grad = ffn_grad + dot_nt(low(logit_grad), full_router)
+    grad_router = dot_tn(ffn_low, low(logit_grad))
+    hidden_part, grad_norm_ffn = root_norm_back(ffn_grad, unit_ffn, inverse_ffn, full_norm_ffn)
+    grad_hidden = grad_mine.astype(jnp.float32) + hidden_part
+
+    attention_grad = gather_slab(low(grad_hidden))
+    grad_out_here = dot_tn(head_out, attention_grad)
+    head_grad = low(dot_nt(attention_grad, out_here)).reshape(sequences, slab, heads, DV)
+    grad_value_up = jnp.einsum(
+        "shbr,sbhv->rhv", latent_out, head_grad, preferred_element_type=jnp.float32
+    )
+    latent_grad = low(
+        jnp.einsum("sbhv,rhv->shbr", head_grad, value_up, preferred_element_type=jnp.float32)
+    )
+    prob_grad = jnp.einsum(
+        "shqr,skr->shqk", latent_grad, keys[..., :R], preferred_element_type=jnp.float32
+    )
+    inner = jnp.sum(prob * prob_grad, axis=-1, keepdims=True)
+    score_grad = low(prob * (prob_grad - inner))
+    query_grad = low(
+        jnp.einsum("shqk,skc->shqc", score_grad, keys, preferred_element_type=jnp.float32) * scale
+    )
+    key_grad = (
+        jnp.einsum("shqk,shqc->skc", score_grad, query_rows, preferred_element_type=jnp.float32)
+        * scale
+    )
+    value_grad = jnp.einsum(
+        "shqk,shqr->skr", prob_low, latent_grad, preferred_element_type=jnp.float32
+    )
+    key_grad = low(key_grad + jnp.pad(value_grad, ((0, 0), (0, 0), (0, DR))))
+    key_grad = jnp.transpose(
+        key_grad.reshape(sequences, zs, 2, 2, block, R + DR), (2, 3, 0, 1, 4, 5)
+    ).reshape(2, 2, 2, zs * block, R + DR)
+    key_sum = scatter_all(key_grad[0], key_grad[1])
+
+    absorbed_grad = query_grad[..., :R]
+    rope_grad = jnp.transpose(query_grad[..., R:], (0, 2, 1, 3)).astype(jnp.float32)
+    grad_key_up = jnp.einsum(
+        "shbr,sbhn->rhn", absorbed_grad, query_low[..., :DN], preferred_element_type=jnp.float32
+    )
+    nope_grad = jnp.einsum(
+        "shbr,rhn->sbhn", absorbed_grad, key_up, preferred_element_type=jnp.float32
+    )
+    rope_raw = rotate(rope_grad, cosine[:, None, :], -sine[:, None, :])
+    query_raw_grad = low(jnp.concatenate([nope_grad, rope_raw], axis=-1)).reshape(
+        sequences * slab, query_columns
+    )
+    grad_query_here = dot_tn(input_low, query_raw_grad)
+    input_grad = scatter_slab(low(dot_nt(query_raw_grad, query_here)))
+
+    latent_back, grad_latent_norm = root_norm_back(
+        key_sum[:, :R], latent_unit[0, :block], latent_inverse[0, :block], full_latent_norm
+    )
+    rope_key = rotate(key_sum[:, R:], cosine[:block], -sine[:block])
+    latent_raw_grad = low(jnp.concatenate([latent_back, rope_key], axis=-1))
+    input_grad = input_grad + dot_nt(latent_raw_grad, full_down)
+    source_part, grad_norm_in = root_norm_back(
+        input_grad, unit_in[:block], inverse_in[:block], full_norm_in
+    )
+    tokens_gradient = both_halves(low(grad_hidden + source_part)).astype(jnp.float32)
+
+    slab_latent_grad = gather_slab(latent_raw_grad)
+    columns = lax.dynamic_index_in_dim(
+        input_low.reshape(sequences * slab, zs, 4, rows_here), x * 2 + c, 2, keepdims=False
+    ).reshape(sequences * slab, zs * rows_here)
+    grad_down = sum_z(low(dot_tn(columns, slab_latent_grad)))
+
+    grad_out_here = jnp.transpose(
+        grad_out_here.reshape(heads, DV, count, rows_here), (2, 1, 0, 3)
+    ).reshape(count * DV, heads * rows_here)
+    grad_out = trade(low(sum_z(low(grad_out_here))), ("x", "c"))
+    grad_output = jnp.transpose(
+        grad_out.reshape(4, DV, heads, rows_here), (0, 2, 1, 3)
+    ).reshape(-1, rows_here).astype(jnp.float32)
+    grad_up_here = jnp.concatenate([grad_key_up, grad_value_up], axis=-1).reshape(
+        count * DV, up_columns
+    )
+    both = jnp.concatenate([grad_query_here.reshape(width, query_columns), grad_up_here], axis=1)
+    both = trade(low(sum_z(low(both))), ("x", "c")).astype(jnp.float32).reshape(4, rows_here, -1)
+    grad_query = jnp.transpose(both[..., :query_columns], (1, 0, 2)).reshape(rows_here, -1)
+    grad_latent_up = jnp.transpose(
+        both[..., query_columns:].reshape(4, rank_rows, heads * (DN + DV)), (1, 0, 2)
+    ).reshape(rank_rows, -1)
+
+    small_grads = jnp.concatenate(
+        [
+            grad_router.T.reshape(experts, count, rows_here),
+            grad_norm_in.reshape(1, count, rows_here),
+            grad_norm_ffn.reshape(1, count, rows_here),
+            jnp.pad(
+                grad_latent_norm.reshape(1, count, rank_rows),
+                ((0, 0), (0, 0), (0, rows_here - rank_rows)),
+            ),
+        ]
+    )
+    small_grads = trade(jnp.transpose(small_grads, (1, 0, 2)), CTX)
+    small_grads = jnp.sum(small_grads, axis=0)
+    small_grads = small_grads + swap(small_grads, "y")
+    return (
+        output,
+        tokens_gradient,
+        small_grads[experts],
+        grad_query,
+        grad_down,
+        small_grads[experts + 2, :rank_rows],
+        grad_latent_up,
+        grad_output,
+        small_grads[experts + 1],
+        small_grads[:experts].T,
+        grad_shared_gate,
+        grad_shared_up,
+        grad_shared_down,
+        grad_expert_gate,
+        grad_expert_up,
+        grad_expert_down,
+    )
+
+
+IN_SPECS = (
+    (None, "ctx", None),
+    ("ctx",),
+    ("ctx", "wa"),
+    ("ctx", None),
+    ("ctx",),
+    ("ctx", "wa"),
+    ("wa", "ctx"),
+    ("ctx",),
+    ("ctx", None),
+    ("ctx", "wa"),
+    ("ctx", "wa"),
+    ("wa", "ctx"),
+    ("ctx", None, "wa"),
+    ("ctx", None, "wa"),
+    ("ctx", "wa", None),
+    (None, "ctx", None),
+    (None, "ctx", None),
+)
+OUT_SPECS = ((None, "ctx", None),) * 2 + IN_SPECS[1:15]
+
+
 def solution(mesh):
-    return jax.shard_map(
-        shards,
-        mesh=mesh,
-        in_specs=(
-            P(None, "ctx", None),
-            P("ctx"),
-            P("ctx", "wa"),
-            P("ctx", None),
-            P("ctx"),
-            P("ctx", "wa"),
-            P("wa", "ctx"),
-            P("ctx"),
-            P("ctx", None),
-            P("ctx", "wa"),
-            P("ctx", "wa"),
-            P("wa", "ctx"),
-            P("ctx", None, "wa"),
-            P("ctx", None, "wa"),
-            P("ctx", "wa", None),
-            P(None, "ctx", None),
-            P(None, "ctx", None),
-        ),
-        out_specs=(
-            P(None, "ctx", None),
-            P(None, "ctx", None),
-            P("ctx"),
-            P("ctx", "wa"),
-            P("ctx", None),
-            P("ctx"),
-            P("ctx", "wa"),
-            P("wa", "ctx"),
-            P("ctx"),
-            P("ctx", None),
-            P("ctx", "wa"),
-            P("ctx", "wa"),
-            P("wa", "ctx"),
-            P("ctx", None, "wa"),
-            P("ctx", None, "wa"),
-            P("ctx", "wa", None),
-        ),
-        check_vma=False,
-    )
+    count = mesh.shape["ctx"]
+
+    def run(*arguments):
+        experts = arguments[12].shape[0]
+        if experts > 4 * TOPK or experts != count or mesh.shape["wa"] != 2 or count % 8:
+            return jax.shard_map(
+                shards,
+                mesh=mesh,
+                in_specs=tuple(P(*spec) for spec in IN_SPECS),
+                out_specs=tuple(P(*spec) for spec in OUT_SPECS),
+                check_vma=False,
+            )(*arguments)
+        grid = Mesh(mesh.devices.reshape(count // 4, 2, 2, 2), ("z", "x", "c", "y"))
+        names = {"ctx": CTX, "wa": "y", None: None}
+        return jax.shard_map(
+            dense_shards,
+            mesh=grid,
+            in_specs=tuple(P(*[names[n] for n in spec]) for spec in IN_SPECS),
+            out_specs=tuple(P(*[names[n] for n in spec]) for spec in OUT_SPECS),
+            check_vma=False,
+        )(*arguments)
+
+    return run

time: 2280 us -> 903 us (0.40)
  waiting for transfers between devices: 1360 us -> 318 us
  blocking collectives: 433 us -> 0 us
  matrix products: 307 us -> 173 us
  local copies, waits for them, and re-layouts: 40.7 us -> 142 us
  other arithmetic: 29.7 us -> 114 us
  starting transfers between devices: 78.2 us -> 140 us
    reduce_scatter x8 -> x0, waiting for transfers between devices: 780 us -> none  [the longest x1 138 us: shards(): lax.psum_scatter(grad_query, 'ctx', scatter_dimension=0, tiled=True)]
    all_gather x8 -> x0, waiting for transfers between devices: 325 us -> none  [the longest x1 160 us: fetch_weights(): lax.all_gather(shared_gate, 'ctx', axis=0, tiled=True)]
    all_gather x3 -> x0, blocking collectives: 259 us -> none  [the longest x1 228 us: fetch_weights(): lax.all_gather(router_weight, 'ctx', axis=0, tiled=True)]
    ppermute x32 -> x71, waiting for transfers between devices: 15.8 us -> 244 us  [the longest x53 145 us: swap(): return lax.ppermute(value, axis, [(0, 1), (1, 0)])]
    dot_general x124 -> x37, matrix products: 305 us -> 173 us  [the longest x8 57.6 us: dot_nt(): lax.dot_general(left, right, (((1,), (1,)), ((), ())), preferred_element_...]
    all_to_all x1 -> x0, blocking collectives: 98.7 us -> none  [shards(): lax.all_to_all(send, 'ctx', split_axis=0, concat_axis=0, tiled=True)]
    all_to_all x3 -> x14, waiting for transfers between devices: 162 us -> 74 us  [trade(): return lax.all_to_all(value, axes, split_axis=0, concat_axis=0, tiled=True)]
    unnamed x2 -> x0, blocking collectives: 69.9 us -> none
  transfers between devices with their start and end apart: 55 -> 85, of which waited for: 33 -> 38; matrix products, arithmetic and copies ran while one was open for 14% -> 38% of each run, Pallas kernels for 0% -> 0%
where the time goes in v1:
time: 903 us; the launch traced here: 890 us
  waiting for transfers between devices  318 us (35%)
  matrix products  173 us (19%)
  local copies, waits for them, and re-layouts  142 us (16%)
  starting transfers between devices  140 us (16%)
  other arithmetic  114 us (13%)
    ppermute x53, waiting for transfers between devices, swap(): return lax.ppermute(value, axis, [(0, 1), (1, 0)])  145 us
    all_to_all x14, waiting for transfers between devices, trade(): return lax.all_to_all(value, axes, split_axis=0, concat_axis=0, tiled=True)  74 us
    all_to_all x14, starting transfers between devices, trade(): return lax.all_to_all(value, axes, split_axis=0, concat_axis=0, tiled=True)  72.5 us
    dot_general x8, matrix products, dot_nt(): lax.dot_general(left, right, (((1,), (1,)), ((), ())), preferred_element_...  57.6 us
    ppermute x9, waiting for transfers between devices, to_z(): lax.ppermute(value, 'z', [(i, (i + steps) % count) for i in range(count)])  56.9 us
    dot_general x9, matrix products, dot_tn(): lax.dot_general(left, right, (((0,), (0,)), ((), ())), preferred_element_...  53.6 us
    ppermute x53, starting transfers between devices, swap(): return lax.ppermute(value, axis, [(0, 1), (1, 0)])  47 us
    dot_general x8, matrix products, dot(): return jnp.dot(left, right, preferred_element_type=jnp.float32)  41.9 us
  transfers between devices with their start and end apart: 85, of which 38 were waited for; matrix products, arithmetic and copies ran while one was open for 38% of the time, Pallas kernels for 0%

profile of v1, /device:TPU:16, one launch (start us, length us, event | category | flops | bytes accessed | tf_op | source)
XLA Modules:
  0.0 889.8 jit_solution(8067927368933984426)
XLA Ops:
  8.6 5.3 all-to-all-done.3
  18.8 6.0 all-to-all-done
  25.6 5.2 all-to-all-start.2
  41.5 13.6 %all-to-all-done.2 = bf16[4,128,640]{2,1,0:T(8,128)(2,1)S(1)} async-done(((bf16[4,128,640]{2,1,0:T(8,128)(2,1)}), bf16[4,128,640]{2,1,0:T(8,128)(2,1)S(1)}, u32[]{:S(2)}, u32[]{:S(2)}) %all-to-all-start.2) | async-done | bytes 655392 | tf_op jit(solution)/shard_map/all_to_all | solution.py:506
  55.9 8.6 all-to-all-start.5
  67.2 24.1 %all-to-all-done.5 = bf16[16,264,128]{2,1,0:T(8,128)(2,1)S(1)} async-done(((bf16[16,264,128]{2,1,0:T(8,128)(2,1)}), bf16[16,264,128]{2,1,0:T(8,128)(2,1)S(1)}, u32[]{:S(2)}, u32[]{:S(2)}) %all-to-all-start.5) | async-done | bytes 1081376 | tf_op jit(solution)/shard_map/all_to_all | solution.py:506
  92.9 4.5 all-to-all-start.1
  112.7 15.1 %collective-permute-done.33 = bf16[256,2048]{1,0:T(8,128)(2,1)} collective-permute-done((bf16[256,2048]{1,0:T(8,128)(2,1)}, bf16[256,2048]{1,0:T(8,128)(2,1)}, u32[]{:S(2)}, u32[]{:S(2)}) %collective-permute-start.33) | collective-permute-done | bytes 1048608 | tf_op jit(solution)/shard_map/ppermute | solution.py:492
  141.5 5.3 all-to-all-start.4
  149.4 6.1 reshape.964
  169.0 11.2 %all-to-all-done.4 = bf16[4,4,128,384]{2,1,3,0:T(4,128)(2,1)} async-done(((bf16[4,4,128,384]{2,1,3,0:T(4,128)(2,1)}), bf16[4,4,128,384]{2,1,3,0:T(4,128)(2,1)}, u32[]{:S(2)}, u32[]{:S(2)}) %all-to-all-start.4) | async-done | bytes 1572896 | tf_op jit(solution)/shard_map/all_to_all | solution.py:506
  194.8 5.0 copy.335
  201.6 4.3 reshape_reshape.3
  217.8 4.3 collective-permute-start.5
  223.1 14.7 %collective-permute-done.4 = bf16[2,128,576]{1,2,0:T(8,128)(2,1)S(1)} collective-permute-done((bf16[2,128,576]{1,2,0:T(8,128)(2,1)S(1)}, bf16[2,128,576]{1,2,0:T(8,128)(2,1)S(1)}, u32[]{:S(2)}, u32[]{:S(2)}) %collective-permute-start.4) | collective-permute-done | bytes 294944 | tf_op jit(solution)/shard_map/ppermute | solution.py:497
  264.2 8.7 fusion.193
  292.9 15.7 %collective-permute-done.13 = bf16[64,2048]{1,0:T(8,128)(2,1)S(1)} collective-permute-done((bf16[64,2048]{1,0:T(8,128)(2,1)S(1)}, bf16[64,2048]{1,0:T(8,128)(2,1)S(1)}, u32[]{:S(2)}, u32[]{:S(2)}) %collective-permute-start.13) | collective-permute-done | bytes 262176 | tf_op jit(solution)/shard_map/ppermute | solution.py:497
  319.1 17.7 %collective-permute-done.16 = bf16[256,2048]{1,0:T(8,128)(2,1)S(1)} collective-permute-done((bf16[256,2048]{1,0:T(8,128)(2,1)S(1)}, bf16[256,2048]{1,0:T(8,128)(2,1)S(1)}, u32[]{:S(2)}, u32[]{:S(2)}) %collective-permute-start.16) | collective-permute-done | bytes 1048608 | tf_op jit(solution)/shard_map/ppermute | solution.py:492
  338.9 11.0 %collective-permute-done.18 = bf16[128,2048]{1,0:T(8,128)(2,1)S(1)} collective-permute-done((bf16[128,2048]{1,0:T(8,128)(2,1)S(1)}, bf16[128,2048]{1,0:T(8,128)(2,1)S(1)}, u32[]{:S(2)}, u32[]{:S(2)}) %collective-permute-start.18) | collective-permute-done | bytes 524320 | tf_op jit(solution)/shard_map/ppermute | solution.py:492
  367.3 11.7 %fusion.206 = f32[1024,1792]{1,0:T(8,128)S(1)} fusion(bf16[1024,2048]{1,0:T(8,128)(2,1)} %bitcast.66, bf16[2048,1792]{0,1:T(8,128)(2,1)} %broadcast_dynamic-update-slice_fusion), kind=kOutput, calls=%fused_computation.485 | convolution fusion | flops 7516192768 | bytes 18874368 | tf_op jit(solution)/shard_map/dot_general | solution.py:518
  380.0 13.4 %fusion.207 = f32[1024,1792]{1,0:T(8,128)S(1)} fusion(bf16[1024,2048]{1,0:T(8,128)(2,1)} %bitcast.81, bf16[2048,1792]{0,1:T(8,128)(2,1)} %broadcast_dynamic-update-slice_fusion), kind=kOutput, calls=%fused_computation.486 | convolution fusion | flops 7516192768 | bytes 18874368 | tf_op jit(solution)/shard_map/dot_general | solution.py:518
  398.3 17.2 %multiply_convert_fusion.4 = (bf16[1024,896]{1,0:T(8,128)(2,1)}, bf16[1024,896]{1,0:T(8,128)(2,1)}, f32[1024]{0:T(1024)S(1)}, f32[1024]{0:T(1024)S(1)}, bf16[102...) fusion(f32[1024,1792]{1,0:T(8,128)S(1)} %fusion.207, f32[1024]{0:T(1024)S(1)} %mul.569, ...), kind=kOutput, calls=%fused_computation.46 | convolution fusion | flops 3809474560 | bytes 34986112 | tf_op jit(solution)/shard_map/dot_general | solution.py:522
  415.5 13.2 %convolution_bitcast_fusion = f32[1,2048,704]{1,2,0:T(8,128)} fusion(bf16[1024,896]{1,0:T(8,128)(2,1)} %get-tuple-element.98, bf16[1024,896]{1,0:T(8,128)(2,1)} %get-tuple-element.97, bf16[1024,896]{1,0:T(8,128)(2,1)} %get-tuple-element.103, bf16[1024,896]{1,0:T(8,128)(2,1)} %get-tuple-element.104, bf16[1024,2048]{1,0:T(8,128)(2,1)} %bitcast.81, ...), kind=kOutput, calls=%fused_computation.54 | convolution fusion | flops 5933891584 | bytes 21495808 | tf_op jit(solution)/shard_map/dot_general | solution.py:528
  428.7 5.3 convolution_convert_fusion.6
  434.0 11.5 %convolution_convert_fusion = bf16[1024,2048]{1,0:T(8,128)(2,1)} fusion(bf16[2048,1792]{0,1:T(8,128)(2,1)} %broadcast_dynamic-update-slice_fusion, bf16[1024,896]{1,0:T(8,128)(2,1)S(1)} %copy-done.126, bf16[1024,896]{1,0:T(8,128)(2,1)S(1)} %copy-done.124), kind=kOutput, calls=%fused_computation.30 | convolution fusion | flops 7525629952 | bytes 15204352 | tf_op jit(solution)/shard_map/dot_general | solution.py:522
  445.6 6.4 convolution_convert_fusion.2
  452.0 10.2 %fusion.19 = f32[1,704,2048]{2,1,0:T(8,128)} fusion(bf16[1024,2048]{1,0:T(8,128)(2,1)} %bitcast.102, bf16[1024,2048]{1,0:T(8,128)(2,1)} %bitcast.100, bf16[1024,896]{1,0:T(8,128)(2,1)S(1)} %copy-done.54, bf16[1024,896]{1,0:T(8,128)(2,1)S(1)} %copy-done.122), kind=kOutput, calls=%fused_computation.53 | convolution fusion | flops 5928124416 | bytes 17825792 | tf_op jit(solution)/shard_map/dot_general | solution.py:528
  462.2 6.2 convolution_convert_fusion.3
  474.0 13.0 %convolution_convert_fusion.1 = bf16[1024,2048]{1,0:T(8,128)(2,1)} fusion(bf16[2048,1792]{0,1:T(8,128)(2,1)} %broadcast_dynamic-update-slice_fusion, bf16[1024,896]{1,0:T(8,128)(2,1)} %get-tuple-element.103, bf16[1024,896]{1,0:T(8,128)(2,1)} %get-tuple-element.104), kind=kOutput, calls=%fused_computation.31 | convolution fusion | flops 7525629952 | bytes 15204352 | tf_op jit(solution)/shard_map/dot_general | solution.py:522
  487.0 5.2 fusion.39
  492.6 12.2 %convolution_bitcast_fusion.1 = f32[1,2048,704]{1,2,0:T(8,128)} fusion(bf16[1024,896]{1,0:T(8,128)(2,1)S(1)} %copy-done.127, bf16[1024,896]{1,0:T(8,128)(2,1)S(1)} %copy-done.125, bf16[1024,896]{1,0:T(8,128)(2,1)S(1)} %copy-done.129, bf16[1024,896]{1,0:T(8,128)(2,1)S(1)} %copy-done.131, bf16[1024,2048]{1,0:T(8,128)(2,1)} %bitcast.81, ...), kind=kOutput, calls=%fused_computation.55 | convolution fusion | flops 5933891584 | bytes 21495808 | tf_op jit(solution)/shard_map/dot_general | solution.py:528
  506.0 6.4 all-to-all-start.13
  514.5 5.4 fusion.1
  527.5 23.7 %collective-permute-done.39 = bf16[2,128,2048]{2,1,0:T(8,128)(2,1)S(1)} collective-permute-done((bf16[2,128,2048]{2,1,0:T(8,128)(2,1)S(1)}, bf16[2,128,2048]{2,1,0:T(8,128)(2,1)S(1)}, u32[]{:S(2)}, u32[]{:S(2)}) %collective-permute-start.39) | collective-permute-done | bytes 1048608 | tf_op jit(solution)/shard_map/ppermute | solution.py:492
  556.5 10.5 %collective-permute-done.40 = bf16[128,2048]{1,0:T(8,128)(2,1)S(1)} collective-permute-done((bf16[128,2048]{1,0:T(8,128)(2,1)S(1)}, bf16[128,2048]{1,0:T(8,128)(2,1)S(1)}, u32[]{:S(2)}, u32[]{:S(2)}) %collective-permute-start.40) | collective-permute-done | bytes 524320 | tf_op jit(solution)/shard_map/ppermute | solution.py:492
  570.9 18.3 %collective-permute-done.22 = bf16[2,128,2048]{2,1,0:T(8,128)(2,1)S(1)} collective-permute-done((bf16[2,128,2048]{2,1,0:T(8,128)(2,1)S(1)}, bf16[2,128,2048]{2,1,0:T(8,128)(2,1)S(1)}, u32[]{:S(2)}, u32[]{:S(2)}) %collective-permute-start.22) | collective-permute-done | bytes 1048608 | tf_op jit(solution)/shard_map/ppermute | solution.py:492
  607.0 6.5 collective-permute-done.49
  646.5 4.6 copy.393
  678.1 6.3 all-to-all-start.11
  704.1 8.3 collective-permute-done.53
  744.4 6.2 all-to-all-start.7
  757.4 5.8 all-to-all-start.8
  770.4 50.1 %collective-permute-done.27 = bf16[64,2048]{1,0:T(8,128)(2,1)S(1)} collective-permute-done((bf16[64,2048]{1,0:T(8,128)(2,1)S(1)}, bf16[64,2048]{1,0:T(8,128)(2,1)S(1)}, u32[]{:S(2)}, u32[]{:S(2)}) %collective-permute-start.27) | collective-permute-done | bytes 262176 | tf_op jit(solution)/shard_map/ppermute | solution.py:502
  820.5 4.6 collective-permute-done.28
  834.7 8.9 %collective-permute-done.69 = bf16[32,576]{0,1:T(8,128)(2,1)S(1)} collective-permute-done((bf16[32,576]{0,1:T(8,128)(2,1)S(1)}, bf16[32,576]{0,1:T(8,128)(2,1)S(1)}, u32[]{:S(2)}, u32[]{:S(2)}) %collective-permute-start.69) | collective-permute-done | bytes 36896 | tf_op jit(solution)/shard_map/ppermute | solution.py:492
  855.8 5.9 all-to-all-start.10
  869.6 5.2 all-to-all-done.10
  880.3 6.9 all-to-all-done.9
  (717 shorter events, 390.9 us)
Async XLA Ops:
  25.6 29.4 %all-to-all-start.2 = ((bf16[4,128,640]{2,1,0:T(8,128)(2,1)}), bf16[4,128,640]{2,1,0:T(8,128)(2,1)S(1)}, u32[]{:S(2)}, u32[]{:S(2)}) async-start(bf16[4,128,640]{2,1,0:T(8,128)(2,1)} %broadcast_in_dim.198), calls=%async_computation.2 | async-start | bytes 1310720 | tf_op jit(solution)/shard_map/all_to_all | solution.py:506
  31.8 67.7 %collective-permute-start.30 = (bf16[64,2048]{1,0:T(8,128)(2,1)S(1)}, bf16[64,2048]{1,0:T(8,128)(2,1)S(1)}, u32[]{:S(2)}, u32[]{:S(2)}) collective-permute-start(bf16[64,2048]{1,0:T(8,128)(2,1)S(1)} %fusion.152), channel_id=1, source_target_pairs={{8,0},{16,8},{24,16},{0,24},{9,1},{17,9},{25,17},{1,25},{10,2},{18... | collective-permute-start | bytes 786440 | tf_op jit(solution)/shard_map/ppermute | solution.py:497
  32.5 67.0 %collective-permute-start.31 = (bf16[64,2048]{1,0:T(8,128)(2,1)S(1)}, bf16[64,2048]{1,0:T(8,128)(2,1)S(1)}, u32[]{:S(2)}, u32[]{:S(2)}) collective-permute-start(bf16[64,2048]{1,0:T(8,128)(2,1)S(1)} %fusion.152), channel_id=1, source_target_pairs={{16,0},{24,8},{0,16},{8,24},{17,1},{25,9},{1,17},{9,25},{18,2},{26... | collective-permute-start | bytes 786440 | tf_op jit(solution)/shard_map/ppermute | solution.py:497
  35.7 65.2 %collective-permute-start.32 = (bf16[64,2048]{1,0:T(8,128)(2,1)S(1)}, bf16[64,2048]{1,0:T(8,128)(2,1)}, u32[]{:S(2)}, u32[]{:S(2)}) collective-permute-start(bf16[64,2048]{1,0:T(8,128)(2,1)S(1)} %fusion.152), channel_id=1, source_target_pairs={{24,0},{0,8},{8,16},{16,24},{25,1},{1,9},{9,17},{17,25},{26,2},{2,... | collective-permute-start | bytes 786440 | tf_op jit(solution)/shard_map/ppermute | solution.py:497
  36.6 68.6 %collective-permute-start = (bf16[2,64,2048]{2,1,0:T(8,128)(2,1)}, bf16[2,64,2048]{2,1,0:T(8,128)(2,1)}, u32[]{:S(2)}, u32[]{:S(2)}) collective-permute-start(bf16[2,64,2048]{2,1,0:T(8,128)(2,1)} %reverse_select_fusion.4), channel_id=1, source_target_pairs={{0,4},{4,0},{1,5},{5,1},{2,6},{6,2},{3,7},{7,3},{8,12},{12,8},{9,1... | collective-permute-start | bytes 1572872 | tf_op jit(solution)/shard_map/ppermute | solution.py:492
  55.9 35.5 %all-to-all-start.5 = ((bf16[16,264,128]{2,1,0:T(8,128)(2,1)}), bf16[16,264,128]{2,1,0:T(8,128)(2,1)S(1)}, u32[]{:S(2)}, u32[]{:S(2)}) async-start(bf16[16,264,128]{2,1,0:T(8,128)(2,1)} %pad_maximum_fusion.26), calls=%async_computation.5 | async-start | bytes 2162688 | tf_op jit(solution)/shard_map/all_to_all | solution.py:506
  92.9 47.1 %all-to-all-start.1 = ((bf16[4,4,128,384]{2,3,1,0:T(8,128)(2,1)}), bf16[4,4,128,384]{2,3,1,0:T(8,128)(2,1)}, u32[]{:S(2)}, u32[]{:S(2)}) async-start(bf16[4,4,128,384]{2,3,1,0:T(8,128)(2,1)} %broadcast_in_dim.115), calls=%async_computation.1 | async-start | bytes 3145728 | tf_op jit(solution)/shard_map/all_to_all | solution.py:506
  103.2 24.5 %collective-permute-start.33 = (bf16[256,2048]{1,0:T(8,128)(2,1)}, bf16[256,2048]{1,0:T(8,128)(2,1)}, u32[]{:S(2)}, u32[]{:S(2)}) collective-permute-start(bf16[256,2048]{1,0:T(8,128)(2,1)} %get-tuple-element.129), channel_id=1, source_target_pairs={{0,1},{1,0},{2,3},{3,2},{4,5},{5,4},{6,7},{7,6},{8,9},{9,8},{10,11... | collective-permute-start | bytes 3145736 | tf_op jit(solution)/shard_map/ppermute | solution.py:492
  104.8 27.1 %collective-permute-start.34 = (bf16[256,2048]{1,0:T(8,128)(2,1)}, bf16[256,2048]{1,0:T(8,128)(2,1)}, u32[]{:S(2)}, u32[]{:S(2)}) collective-permute-start(bf16[256,2048]{1,0:T(8,128)(2,1)} %get-tuple-element.129), channel_id=1, source_target_pairs={{0,4},{4,0},{1,5},{5,1},{2,6},{6,2},{3,7},{7,3},{8,12},{12,8},{9,1... | collective-permute-start | bytes 3145736 | tf_op jit(solution)/shard_map/ppermute | solution.py:492
  107.3 30.7 %collective-permute-start.1 = (bf16[2,2,64,2048]{3,2,0,1:T(8,128)(2,1)}, bf16[2,2,64,2048]{3,2,0,1:T(8,128)(2,1)S(1)}, u32[]{:S(2)}, u32[]{:S(2)}) collective-permute-start(bf16[2,2,64,2048]{3,2,0,1:T(8,128)(2,1)} %get-tuple-element.135), channel_id=1, source_target_pairs={{0,2},{2,0},{1,3},{3,1},{4,6},{6,4},{5,7},{7,5},{8,10},{10,8},{9,1... | collective-permute-start | bytes 3145736 | tf_op jit(solution)/shard_map/ppermute | solution.py:492
  111.3 44.7 %collective-permute-start.2 = (bf16[4,128,640]{2,1,0:T(8,128)(2,1)}, bf16[4,128,640]{2,1,0:T(8,128)(2,1)}, u32[]{:S(2)}, u32[]{:S(2)}) collective-permute-start(bf16[4,128,640]{2,1,0:T(8,128)(2,1)} %copy-done.41), channel_id=1, source_target_pairs={{0,4},{4,0},{1,5},{5,1},{2,6},{6,2},{3,7},{7,3},{8,12},{12,8},{9,1... | collective-permute-start | bytes 1966088 | tf_op jit(solution)/shard_map/ppermute | solution.py:492
  129.7 29.2 %collective-permute-start.35 = (bf16[128,2048]{1,0:T(8,128)(2,1)}, bf16[128,2048]{1,0:T(8,128)(2,1)}, u32[]{:S(2)}, u32[]{:S(2)}) collective-permute-start(bf16[128,2048]{1,0:T(8,128)(2,1)} %slice.633), channel_id=1, source_target_pairs={{0,4},{4,0},{1,5},{5,1},{2,6},{6,2},{3,7},{7,3},{8,12},{12,8},{9,1... | collective-permute-start | bytes 1572872 | tf_op jit(solution)/shard_map/ppermute | solution.py:492
  133.7 25.1 %collective-permute-start.36 = (bf16[128,2048]{1,0:T(8,128)(2,1)}, bf16[128,2048]{1,0:T(8,128)(2,1)}, u32[]{:S(2)}, u32[]{:S(2)}) collective-permute-start(bf16[128,2048]{1,0:T(8,128)(2,1)} %slice.634), channel_id=1, source_target_pairs={{0,1},{1,0},{2,3},{3,2},{4,5},{5,4},{6,7},{7,6},{8,9},{9,8},{10,11... | collective-permute-start | bytes 1572872 | tf_op jit(solution)/shard_map/ppermute | solution.py:492
  141.5 38.7 %all-to-all-start.4 = ((bf16[4,4,128,384]{2,1,3,0:T(4,128)(2,1)}), bf16[4,4,128,384]{2,1,3,0:T(4,128)(2,1)}, u32[]{:S(2)}, u32[]{:S(2)}) async-start(bf16[4,4,128,384]{2,1,3,0:T(4,128)(2,1)} %broadcast_in_dim.199), calls=%async_computation.4 | async-start | bytes 3145728 | tf_op jit(solution)/shard_map/all_to_all | solution.py:506
  158.6 34.0 %collective-permute-start.3 = (bf16[4,2,128,640]{3,2,0,1:T(8,128)(2,1)}, bf16[4,2,128,640]{3,2,0,1:T(8,128)(2,1)}, u32[]{:S(2)}, u32[]{:S(2)}) collective-permute-start(bf16[4,2,128,640]{3,2,0,1:T(8,128)(2,1)} %reverse_select_fusion.1), channel_id=1, source_target_pairs={{0,2},{2,0},{1,3},{3,1},{4,6},{6,4},{5,7},{7,5},{8,10},{10,8},{9,1... | collective-permute-start | bytes 3932168 | tf_op jit(solution)/shard_map/ppermute | solution.py:492
  164.1 234.2 %collective-permute-start.37 = (bf16[2,2,256,2048]{3,2,1,0:T(8,128)(2,1)}, bf16[2,2,256,2048]{3,2,1,0:T(8,128)(2,1)}, u32[]{:S(2)}, u32[]{:S(2)}) collective-permute-start(bf16[2,2,256,2048]{3,2,1,0:T(8,128)(2,1)} %pad_maximum_fusion.5), channel_id=1, source_target_pairs={{0,2},{2,0},{1,3},{3,1},{4,6},{6,4},{5,7},{7,5},{8,10},{10,8},{9,1... | collective-permute-start | bytes 12582920 | tf_op jit(solution)/shard_map/ppermute | solution.py:492
  216.7 21.0 %collective-permute-start.4 = (bf16[2,128,576]{1,2,0:T(8,128)(2,1)S(1)}, bf16[2,128,576]{1,2,0:T(8,128)(2,1)S(1)}, u32[]{:S(2)}, u32[]{:S(2)}) collective-permute-start(bf16[2,128,576]{1,2,0:T(8,128)(2,1)S(1)} %pad_maximum_fusion.38), channel_id=1, source_target_pairs={{8,0},{16,8},{24,16},{0,24},{9,1},{17,9},{25,17},{1,25},{10,2},{18... | collective-permute-start | bytes 884744 | tf_op jit(solution)/shard_map/ppermute | solution.py:497
  217.8 24.2 %collective-permute-start.5 = (bf16[2,128,576]{1,2,0:T(8,128)(2,1)S(1)}, bf16[2,128,576]{1,2,0:T(8,128)(2,1)S(1)}, u32[]{:S(2)}, u32[]{:S(2)}) collective-permute-start(bf16[2,128,576]{1,2,0:T(8,128)(2,1)S(1)} %pad_maximum_fusion.38), channel_id=1, source_target_pairs={{16,0},{24,8},{0,16},{8,24},{17,1},{25,9},{1,17},{9,25},{18,2},{26... | collective-permute-start | bytes 884744 | tf_op jit(solution)/shard_map/ppermute | solution.py:497
  222.1 23.9 %collective-permute-start.6 = (bf16[2,128,576]{1,2,0:T(8,128)(2,1)S(1)}, bf16[2,128,576]{1,2,0:T(8,128)(2,1)S(1)}, u32[]{:S(2)}, u32[]{:S(2)}) collective-permute-start(bf16[2,128,576]{1,2,0:T(8,128)(2,1)S(1)} %pad_maximum_fusion.38), channel_id=1, source_target_pairs={{24,0},{0,8},{8,16},{16,24},{25,1},{1,9},{9,17},{17,25},{26,2},{2,... | collective-permute-start | bytes 884744 | tf_op jit(solution)/shard_map/ppermute | solution.py:497
  290.8 20.6 %collective-permute-start.14 = (bf16[64,2048]{1,0:T(8,128)(2,1)S(1)}, bf16[64,2048]{1,0:T(8,128)(2,1)S(1)}, u32[]{:S(2)}, u32[]{:S(2)}) collective-permute-start(bf16[64,2048]{1,0:T(8,128)(2,1)S(1)} %multiply_convert_fusion.9), channel_id=1, source_target_pairs={{16,0},{24,8},{0,16},{8,24},{17,1},{25,9},{1,17},{9,25},{18,2},{26... | collective-permute-start | bytes 786440 | tf_op jit(solution)/shard_map/ppermute | solution.py:497
  290.9 20.5 %collective-permute-start.15 = (bf16[64,2048]{1,0:T(8,128)(2,1)S(1)}, bf16[64,2048]{1,0:T(8,128)(2,1)S(1)}, u32[]{:S(2)}, u32[]{:S(2)}) collective-permute-start(bf16[64,2048]{1,0:T(8,128)(2,1)S(1)} %multiply_convert_fusion.9), channel_id=1, source_target_pairs={{24,0},{0,8},{8,16},{16,24},{25,1},{1,9},{9,17},{17,25},{26,2},{2,... | collective-permute-start | bytes 786440 | tf_op jit(solution)/shard_map/ppermute | solution.py:497
  311.6 25.1 %collective-permute-start.16 = (bf16[256,2048]{1,0:T(8,128)(2,1)S(1)}, bf16[256,2048]{1,0:T(8,128)(2,1)S(1)}, u32[]{:S(2)}, u32[]{:S(2)}) collective-permute-start(bf16[256,2048]{1,0:T(8,128)(2,1)S(1)} %get-tuple-element.131), channel_id=1, source_target_pairs={{0,1},{1,0},{2,3},{3,2},{4,5},{5,4},{6,7},{7,6},{8,9},{9,8},{10,11... | collective-permute-start | bytes 3145736 | tf_op jit(solution)/shard_map/ppermute | solution.py:492
  312.2 25.3 %collective-permute-start.17 = (bf16[256,2048]{1,0:T(8,128)(2,1)S(1)}, bf16[256,2048]{1,0:T(8,128)(2,1)S(1)}, u32[]{:S(2)}, u32[]{:S(2)}) collective-permute-start(bf16[256,2048]{1,0:T(8,128)(2,1)S(1)} %get-tuple-element.131), channel_id=1, source_target_pairs={{0,4},{4,0},{1,5},{5,1},{2,6},{6,2},{3,7},{7,3},{8,12},{12,8},{9,1... | collective-permute-start | bytes 3145736 | tf_op jit(solution)/shard_map/ppermute | solution.py:492
  353.0 27.0 %collective-permute-start.20 = (bf16[2,2,256,2048]{3,2,1,0:T(8,128)(2,1)}, bf16[2,2,256,2048]{3,2,1,0:T(8,128)(2,1)}, u32[]{:S(2)}, u32[]{:S(2)}) collective-permute-start(bf16[2,2,256,2048]{3,2,1,0:T(8,128)(2,1)} %pad_maximum_fusion.4), channel_id=1, source_target_pairs={{0,2},{2,0},{1,3},{3,1},{4,6},{6,4},{5,7},{7,5},{8,10},{10,8},{9,1... | collective-permute-start | bytes 12582920 | tf_op jit(solution)/shard_map/ppermute | solution.py:492
  468.4 46.2 %collective-permute-start.38 = (bf16[2,2,256,2048]{3,2,1,0:T(8,128)(2,1)}, bf16[2,2,256,2048]{3,2,1,0:T(8,128)(2,1)}, u32[]{:S(2)}, u32[]{:S(2)}) collective-permute-start(bf16[2,2,256,2048]{3,2,1,0:T(8,128)(2,1)} %bitcast.103), channel_id=1, source_target_pairs={{0,2},{2,0},{1,3},{3,1},{4,6},{6,4},{5,7},{7,5},{8,10},{10,8},{9,1... | collective-permute-start | bytes 12582920 | tf_op jit(solution)/shard_map/ppermute | solution.py:492
  469.8 36.2 %all-to-all-start.6 = ((f32[32,1,64]{2,1,0:T(1,128)}), f32[32,1,64]{2,1,0:T(1,128)S(1)}, u32[]{:S(2)}, u32[]{:S(2)}) async-start(f32[32,1,64]{2,1,0:T(1,128)} %bitcast.116), calls=%async_computation.6 | async-start | bytes 32768 | tf_op jit(solution)/shard_map/all_to_all | solution.py:506
  473.7 49.5 %collective-permute-start.21 = (bf16[2,2,256,2048]{3,2,1,0:T(8,128)(2,1)}, bf16[2,2,256,2048]{3,2,1,0:T(8,128)(2,1)}, u32[]{:S(2)}, u32[]{:S(2)}) collective-permute-start(bf16[2,2,256,2048]{3,2,1,0:T(8,128)(2,1)} %bitcast.701), channel_id=1, source_target_pairs={{0,2},{2,0},{1,3},{3,1},{4,6},{6,4},{5,7},{7,5},{8,10},{10,8},{9,1... | collective-permute-start | bytes 12582920 | tf_op jit(solution)/shard_map/ppermute | solution.py:492
  506.0 108.7 %all-to-all-start.13 = ((bf16[16,264,128]{2,1,0:T(8,128)(2,1)}), bf16[16,264,128]{2,1,0:T(8,128)(2,1)S(1)}, u32[]{:S(2)}, u32[]{:S(2)}) async-start(bf16[16,264,128]{2,1,0:T(8,128)(2,1)} %bitcast_bitcast_fusion), calls=%async_computation.13 | async-start | bytes 2162688 | tf_op jit(solution)/shard_map/all_to_all | solution.py:506
  520.1 31.1 %collective-permute-start.39 = (bf16[2,128,2048]{2,1,0:T(8,128)(2,1)S(1)}, bf16[2,128,2048]{2,1,0:T(8,128)(2,1)S(1)}, u32[]{:S(2)}, u32[]{:S(2)}) collective-permute-start(bf16[2,128,2048]{2,1,0:T(8,128)(2,1)S(1)} %slice_bitcast_fusion.9), channel_id=1, source_target_pairs={{0,4},{4,0},{1,5},{5,1},{2,6},{6,2},{3,7},{7,3},{8,12},{12,8},{9,1... | collective-permute-start | bytes 3145736 | tf_op jit(solution)/shard_map/ppermute | solution.py:492
  521.7 29.4 %collective-permute-start.42 = (bf16[2,128,2048]{2,1,0:T(8,128)(2,1)S(1)}, bf16[2,128,2048]{2,1,0:T(8,128)(2,1)S(1)}, u32[]{:S(2)}, u32[]{:S(2)}) collective-permute-start(bf16[2,128,2048]{2,1,0:T(8,128)(2,1)S(1)} %slice_bitcast_fusion.7), channel_id=1, source_target_pairs={{0,1},{1,0},{2,3},{3,2},{4,5},{5,4},{6,7},{7,6},{8,9},{9,8},{10,11... | collective-permute-start | bytes 3145736 | tf_op jit(solution)/shard_map/ppermute | solution.py:492
  555.0 34.2 %collective-permute-start.22 = (bf16[2,128,2048]{2,1,0:T(8,128)(2,1)S(1)}, bf16[2,128,2048]{2,1,0:T(8,128)(2,1)S(1)}, u32[]{:S(2)}, u32[]{:S(2)}) collective-permute-start(bf16[2,128,2048]{2,1,0:T(8,128)(2,1)S(1)} %slice_bitcast_fusion.13), channel_id=1, source_target_pairs={{0,4},{4,0},{1,5},{5,1},{2,6},{6,2},{3,7},{7,3},{8,12},{12,8},{9,1... | collective-permute-start | bytes 3145736 | tf_op jit(solution)/shard_map/ppermute | solution.py:492
  556.0 33.2 %collective-permute-start.25 = (bf16[2,128,2048]{2,1,0:T(8,128)(2,1)S(1)}, bf16[2,128,2048]{2,1,0:T(8,128)(2,1)S(1)}, u32[]{:S(2)}, u32[]{:S(2)}) collective-permute-start(bf16[2,128,2048]{2,1,0:T(8,128)(2,1)S(1)} %slice_bitcast_fusion.11), channel_id=1, source_target_pairs={{0,1},{1,0},{2,3},{3,2},{4,5},{5,4},{6,7},{7,6},{8,9},{9,8},{10,11... | collective-permute-start | bytes 3145736 | tf_op jit(solution)/shard_map/ppermute | solution.py:492
  567.2 23.8 %collective-permute-start.41 = (bf16[64,2048]{1,0:T(8,128)(2,1)S(1)}, bf16[64,2048]{1,0:T(8,128)(2,1)S(1)}, u32[]{:S(2)}, u32[]{:S(2)}) collective-permute-start(bf16[64,2048]{1,0:T(8,128)(2,1)S(1)} %slice.933), channel_id=1, source_target_pairs={{0,8},{8,16},{16,24},{24,0},{1,9},{9,17},{17,25},{25,1},{2,10},{10... | collective-permute-start | bytes 786440 | tf_op jit(solution)/shard_map/ppermute | solution.py:502
  568.8 22.2 %collective-permute-start.44 = (bf16[64,2048]{1,0:T(8,128)(2,1)S(1)}, bf16[64,2048]{1,0:T(8,128)(2,1)S(1)}, u32[]{:S(2)}, u32[]{:S(2)}) collective-permute-start(bf16[64,2048]{1,0:T(8,128)(2,1)S(1)} %get-tuple-element.144), channel_id=1, source_target_pairs={{0,16},{8,24},{16,0},{24,8},{1,17},{9,25},{17,1},{25,9},{2,18},{10... | collective-permute-start | bytes 786440 | tf_op jit(solution)/shard_map/ppermute | solution.py:502
  570.3 20.7 %collective-permute-start.45 = (bf16[64,2048]{1,0:T(8,128)(2,1)S(1)}, bf16[64,2048]{1,0:T(8,128)(2,1)S(1)}, u32[]{:S(2)}, u32[]{:S(2)}) collective-permute-start(bf16[64,2048]{1,0:T(8,128)(2,1)S(1)} %get-tuple-element.145), channel_id=1, source_target_pairs={{0,24},{8,0},{16,8},{24,16},{1,25},{9,1},{17,9},{25,17},{2,26},{10... | collective-permute-start | bytes 786440 | tf_op jit(solution)/shard_map/ppermute | solution.py:502
  596.1 27.8 %collective-permute-start.23 = (bf16[128,2048]{1,0:T(8,128)(2,1)}, bf16[128,2048]{1,0:T(8,128)(2,1)}, u32[]{:S(2)}, u32[]{:S(2)}) collective-permute-start(bf16[128,2048]{1,0:T(8,128)(2,1)} %slice_bitcast_fusion.24), channel_id=1, source_target_pairs={{0,1},{1,0},{2,3},{3,2},{4,5},{5,4},{6,7},{7,6},{8,9},{9,8},{10,11... | collective-permute-start | bytes 1572872 | tf_op jit(solution)/shard_map/ppermute | solution.py:492
  621.5 141.8 %collective-permute-start.26 = (bf16[128,2048]{1,0:T(8,128)(2,1)}, bf16[128,2048]{1,0:T(8,128)(2,1)}, u32[]{:S(2)}, u32[]{:S(2)}) collective-permute-start(bf16[128,2048]{1,0:T(8,128)(2,1)} %slice_bitcast_fusion.22), channel_id=1, source_target_pairs={{0,4},{4,0},{1,5},{5,1},{2,6},{6,2},{3,7},{7,3},{8,12},{12,8},{9,1... | collective-permute-start | bytes 1572872 | tf_op jit(solution)/shard_map/ppermute | solution.py:492
  626.0 144.3 %collective-permute-start.24 = (bf16[64,2048]{1,0:T(8,128)(2,1)}, bf16[64,2048]{1,0:T(8,128)(2,1)}, u32[]{:S(2)}, u32[]{:S(2)}) collective-permute-start(bf16[64,2048]{1,0:T(8,128)(2,1)} %slice.934), channel_id=1, source_target_pairs={{0,8},{8,16},{16,24},{24,0},{1,9},{9,17},{17,25},{25,1},{2,10},{10... | collective-permute-start | bytes 786440 | tf_op jit(solution)/shard_map/ppermute | solution.py:502
  654.2 36.7 %collective-permute-start.51 = (bf16[2,2,64,2048]{3,2,1,0:T(8,128)(2,1)}, bf16[2,2,64,2048]{3,2,1,0:T(8,128)(2,1)}, u32[]{:S(2)}, u32[]{:S(2)}) collective-permute-start(bf16[2,2,64,2048]{3,2,1,0:T(8,128)(2,1)} %slice_bitcast_fusion.5), channel_id=1, source_target_pairs={{0,2},{2,0},{1,3},{3,1},{4,6},{6,4},{5,7},{7,5},{8,10},{10,8},{9,1... | collective-permute-start | bytes 3145736 | tf_op jit(solution)/shard_map/ppermute | solution.py:492
  667.0 27.8 %collective-permute-start.56 = (bf16[2,2,256,576]{2,3,1,0:T(8,128)(2,1)}, bf16[2,2,256,576]{2,3,1,0:T(8,128)(2,1)}, u32[]{:S(2)}, u32[]{:S(2)}) collective-permute-start(bf16[2,2,256,576]{2,3,1,0:T(8,128)(2,1)} %copy.396), channel_id=1, source_target_pairs={{0,2},{2,0},{1,3},{3,1},{4,6},{6,4},{5,7},{7,5},{8,10},{10,8},{9,1... | collective-permute-start | bytes 3538952 | tf_op jit(solution)/shard_map/ppermute | solution.py:492
  678.1 48.0 %all-to-all-start.11 = ((bf16[4,512,256]{2,1,0:T(8,128)(2,1)}), bf16[4,512,256]{2,1,0:T(8,128)(2,1)}, u32[]{:S(2)}, u32[]{:S(2)}) async-start(bf16[4,512,256]{2,1,0:T(8,128)(2,1)} %convert_element_type.801), calls=%async_computation.11 | async-start | bytes 2097152 | tf_op jit(solution)/shard_map/all_to_all | solution.py:506
  757.4 98.3 %all-to-all-start.8 = ((bf16[4,512,512]{1,2,0:T(8,128)(2,1)}), bf16[4,512,512]{1,2,0:T(8,128)(2,1)S(1)}, u32[]{:S(2)}, u32[]{:S(2)}) async-start(bf16[4,512,512]{1,2,0:T(8,128)(2,1)} %pad_maximum_fusion.21), calls=%async_computation.8 | async-start | bytes 4194304 | tf_op jit(solution)/shard_map/all_to_all | solution.py:506
  764.7 55.8 %collective-permute-start.27 = (bf16[64,2048]{1,0:T(8,128)(2,1)S(1)}, bf16[64,2048]{1,0:T(8,128)(2,1)S(1)}, u32[]{:S(2)}, u32[]{:S(2)}) collective-permute-start(bf16[64,2048]{1,0:T(8,128)(2,1)S(1)} %get-tuple-element.146), channel_id=1, source_target_pairs={{0,16},{8,24},{16,0},{24,8},{1,17},{9,25},{17,1},{25,9},{2,18},{10... | collective-permute-start | bytes 786440 | tf_op jit(solution)/shard_map/ppermute | solution.py:502
  764.8 60.2 %collective-permute-start.28 = (bf16[64,2048]{1,0:T(8,128)(2,1)S(1)}, bf16[64,2048]{1,0:T(8,128)(2,1)S(1)}, u32[]{:S(2)}, u32[]{:S(2)}) collective-permute-start(bf16[64,2048]{1,0:T(8,128)(2,1)S(1)} %get-tuple-element.147), channel_id=1, source_target_pairs={{0,24},{8,0},{16,8},{24,16},{1,25},{9,1},{17,9},{25,17},{2,26},{10... | collective-permute-start | bytes 786440 | tf_op jit(solution)/shard_map/ppermute | solution.py:502
  769.1 64.1 %collective-permute-start.66 = (bf16[64,576]{0,1:T(8,128)(2,1)}, bf16[64,576]{0,1:T(8,128)(2,1)}, u32[]{:S(2)}, u32[]{:S(2)}) collective-permute-start(bf16[64,576]{0,1:T(8,128)(2,1)} %pad_maximum_fusion.40), channel_id=1, source_target_pairs={{0,1},{1,0},{2,3},{3,2},{4,5},{5,4},{6,7},{7,6},{8,9},{9,8},{10,11... | collective-permute-start | bytes 221192 | tf_op jit(solution)/shard_map/ppermute | solution.py:492
  769.7 61.8 %collective-permute-start.67 = (bf16[64,576]{0,1:T(8,128)(2,1)}, bf16[64,576]{0,1:T(8,128)(2,1)}, u32[]{:S(2)}, u32[]{:S(2)}) collective-permute-start(bf16[64,576]{0,1:T(8,128)(2,1)} %pad_maximum_fusion.40), channel_id=1, source_target_pairs={{0,4},{4,0},{1,5},{5,1},{2,6},{6,2},{3,7},{7,3},{8,12},{12,8},{9,1... | collective-permute-start | bytes 221192 | tf_op jit(solution)/shard_map/ppermute | solution.py:492
  828.0 33.7 %collective-permute-start.29 = (bf16[64,2048]{1,0:T(8,128)(2,1)}, bf16[64,2048]{1,0:T(8,128)(2,1)}, u32[]{:S(2)}, u32[]{:S(2)}) collective-permute-start(bf16[64,2048]{1,0:T(8,128)(2,1)} %get-tuple-element.143), channel_id=1, source_target_pairs={{0,1},{1,0},{2,3},{3,2},{4,5},{5,4},{6,7},{7,6},{8,9},{9,8},{10,11... | collective-permute-start | bytes 786440 | tf_op jit(solution)/shard_map/ppermute | solution.py:492
  855.8 19.1 %all-to-all-start.10 = ((bf16[4,128,576]{1,2,0:T(8,128)(2,1)}), bf16[4,128,576]{1,2,0:T(8,128)(2,1)S(1)}, u32[]{:S(2)}, u32[]{:S(2)}) async-start(bf16[4,128,576]{1,2,0:T(8,128)(2,1)} %bitcast.641), calls=%async_computation.10 | async-start | bytes 1179648 | tf_op jit(solution)/shard_map/all_to_all | solution.py:506
  (169 other events, 1827.9 us)

commit v2 on v1

--- a/solution.py
+++ b/solution.py
@@ -1,6 +1,11 @@
+from functools import partial
+
 import jax
 import jax.numpy as jnp
 from jax import lax
+from jax.experimental import pallas as pl
+from jax.experimental.layout import Layout, with_layout_constraint
+from jax.experimental.pallas import tpu as pltpu
 from jax.sharding import Mesh, PartitionSpec as P
 
 DN = 128
@@ -485,6 +490,464 @@
     )
 
 
+VMEM_LIMIT = 60 * 1024 * 1024
+TILE = 256
+
+
+def local_call(body, grid, in_specs, out_specs, out_shape, operands, after=()):
+    inputs = len(in_specs)
+
+    def run(*refs):
+        body(*refs[:inputs], *refs[inputs + len(after) :])
+
+    return pl.pallas_call(
+        run,
+        grid=grid,
+        in_specs=list(in_specs) + [pl.BlockSpec(memory_space=pl.ANY)] * len(after),
+        out_specs=out_specs,
+        out_shape=out_shape,
+        compiler_params=pltpu.CompilerParams(vmem_limit_bytes=VMEM_LIMIT),
+        cost_estimate=pl.CostEstimate(flops=1, bytes_accessed=1, transcendentals=0),
+    )(*operands, *after)
+
+
+def whole(array):
+    return pl.BlockSpec(array.shape, lambda *_: (0,) * array.ndim)
+
+
+def by_rows(array, rows=TILE):
+    return pl.BlockSpec((rows, array.shape[1]), lambda i: (i, 0))
+
+
+def by_first(array):
+    return pl.BlockSpec((1,) + array.shape[1:], lambda i: (i,) + (0,) * (array.ndim - 1))
+
+
+def shaped(shape, dtype=jnp.bfloat16):
+    return jax.ShapeDtypeStruct(shape, dtype)
+
+
+def mul(left, right):
+    return jnp.dot(left, right, preferred_element_type=jnp.float32)
+
+
+def mul_nt(left, right):
+    return lax.dot_general(
+        left, right, (((1,), (1,)), ((), ())), preferred_element_type=jnp.float32
+    )
+
+
+def mul_tn(left, right):
+    return lax.dot_general(
+        left, right, (((0,), (0,)), ((), ())), preferred_element_type=jnp.float32
+    )
+
+
+def glu_back(gate, up, grads):
+    sigmoid = 1.0 / (1.0 + jnp.exp(-gate))
+    silu = gate * sigmoid
+    slope = sigmoid * (1.0 + gate * (1.0 - sigmoid))
+    return (silu * up, grads * up * slope, grads * silu)
+
+
+def feed_body(
+    experts, rows, back, shared_back, gate_t, up_t, small_t, named, pick,
+    act_out, shared_act_out, gate_out, up_out, shared_out, gain_out,
+):
+    here = rows[...]
+    part = small_t.shape[0] // 3
+    small = mul_nt(here, small_t[...])
+    logits = small[:, 2 * part :]
+    ids = lax.broadcasted_iota(jnp.int32, logits.shape, 1)
+    logits = jnp.where(ids < experts, logits, -1e30)
+    chances = jnp.exp(logits - jnp.max(logits, axis=1, keepdims=True))
+    total = jnp.sum(chances, axis=1, keepdims=True)
+    named_here = named[...]
+    share = jnp.sum(chances * pick[...], axis=1, keepdims=True) / total * named_here
+    act, gate_grad, up_grad = glu_back(
+        small[:, :part], small[:, part : 2 * part], shared_back[...].astype(jnp.float32)
+    )
+    shared_act_out[...] = act.astype(jnp.bfloat16)
+    shared_out[:, :part] = gate_grad.astype(jnp.bfloat16)
+    shared_out[:, part:] = up_grad.astype(jnp.bfloat16)
+    grads = back[...].astype(jnp.float32)
+    act, gate_grad, up_grad = glu_back(mul_nt(here, gate_t[...]), mul_nt(here, up_t[...]), grads)
+    gain_out[...] = jnp.sum(act * grads, axis=1, keepdims=True) * named_here
+    act_out[...] = (act * share).astype(jnp.bfloat16)
+    gate_out[...] = (gate_grad * share).astype(jnp.bfloat16)
+    up_out[...] = (up_grad * share).astype(jnp.bfloat16)
+
+
+def feed_kernel(rows, back, shared_back, gate_t, up_t, small_t, named, pick, experts):
+    count = rows.shape[0]
+    hidden, part = (back.shape[1], shared_back.shape[1])
+    shapes = [shaped((count, s)) for s in (hidden, part, hidden, hidden, 2 * part)]
+    shapes.append(shaped((count, 1), jnp.float32))
+    return local_call(
+        partial(feed_body, experts),
+        (count // TILE,),
+        [
+            by_rows(rows),
+            by_rows(back),
+            by_rows(shared_back),
+            whole(gate_t),
+            whole(up_t),
+            whole(small_t),
+            by_rows(named),
+            whole(pick),
+        ],
+        [by_rows(s) for s in shapes],
+        shapes,
+        (rows, back, shared_back, gate_t, up_t, small_t, named, pick),
+    )
+
+
+def input_body(gate, up, shared, gate_t, up_t, small_t, gain, pick, out):
+    width = gate_t.shape[1]
+    used = shared.shape[1]
+    out[:, :width] = (
+        mul(gate[...], gate_t[...]) + mul(up[...], up_t[...]) + mul(shared[...], small_t[:used, :])
+    ).astype(jnp.bfloat16)
+    out[:, width:] = (gain[...] * pick[...]).astype(jnp.bfloat16)
+
+
+def input_kernel(gate, up, shared, gate_t, up_t, small_t, gain, pick, after=()):
+    count = gate.shape[0]
+    shape = shaped((count, gate_t.shape[1] + pick.shape[1]))
+    return local_call(
+        input_body,
+        (count // TILE,),
+        [by_rows(gate), by_rows(up), by_rows(shared)]
+        + [whole(gate_t), whole(up_t), whole(small_t), by_rows(gain), whole(pick)],
+        by_rows(shape),
+        shape,
+        (gate, up, shared, gate_t, up_t, small_t, gain, pick),
+        after,
+    )
+
+
+def result_body(act, shared_act, down, shared_down, out):
+    out[...] = (mul(act[...], down[...]) + mul(shared_act[...], shared_down[...])).astype(
+        jnp.bfloat16
+    )
+
+
+def result_kernel(act, shared_act, down, shared_down, after=()):
+    count = act.shape[0]
+    shape = shaped((count, down.shape[1]))
+    return local_call(
+        result_body,
+        (count // TILE,),
+        [by_rows(act), by_rows(shared_act), whole(down), whole(shared_down)],
+        by_rows(shape),
+        shape,
+        (act, shared_act, down, shared_down),
+        after,
+    )
+
+
+def weight_body(left_own, left_other, more_own, more_other, own, other, out, more_out):
+    here, there = (own[...], other[...])
+    out[...] = mul_tn(left_own[...], here) + mul_tn(left_other[...], there)
+    more_out[...] = (mul_tn(more_own[...], here) + mul_tn(more_other[...], there)).astype(
+        jnp.bfloat16
+    )
+
+
+def weight_kernel(lefts, mores, rights, side=0, part=128, after=()):
+    count, width = rights[0].shape
+    columns = lambda rows: pl.BlockSpec((rows, TILE), lambda i: (0, i))
+    hidden, more = (lefts[0].shape[1], part)
+    return local_call(
+        weight_body,
+        (width // TILE,),
+        [whole(a) for a in lefts]
+        + [pl.BlockSpec((count, part), lambda i: (0, side))] * 2
+        + [columns(count)] * 2,
+        [columns(hidden), columns(more)],
+        [shaped((hidden, width), jnp.float32), shaped((more, width))],
+        (*lefts, *mores, *rights),
+        after,
+    )
+
+
+def head_parts_of(query, heads, nope):
+    rope = query.shape[1] // heads - nope
+    return [
+        (
+            query[:, k * nope : (k + 1) * nope],
+            query[:, heads * nope + k * rope : heads * nope + (k + 1) * rope],
+        )
+        for k in range(heads)
+    ]
+
+
+def attend_body(
+    heads, scale, query, own, other, up, out_weight, spots, key_spots,
+    part_out, prob_out, absorbed_out, latent_out, head_out,
+):
+    rank = up.shape[0]
+    absorbed, ropes = ([], [])
+    for k, (nope, rope) in enumerate(head_parts_of(query[...], heads, DN)):
+        key_up = up[:, k * (DN + DV) : k * (DN + DV) + DN]
+        absorbed.append(mul_nt(nope, key_up).astype(jnp.bfloat16))
+        ropes.append(rope)
+    absorbed = jnp.concatenate(absorbed, axis=0)
+    rope = jnp.concatenate(ropes, axis=0)
+    absorbed_out[0] = absorbed
+    keys = [source[0, k] for source in (own, other) for k in range(2)]
+    scores = jnp.concatenate(
+        [mul_nt(absorbed, key[:, :rank]) + mul_nt(rope, key[:, rank:]) for key in keys], axis=1
+    )
+    allowed = spots[...] >= key_spots[...]
+    allowed = jnp.concatenate([allowed] * heads, axis=0)
+    scores = jnp.where(allowed, scores * scale, -1e30)
+    weights = jnp.exp(scores - jnp.max(scores, axis=1, keepdims=True))
+    prob = (weights / jnp.sum(weights, axis=1, keepdims=True)).astype(jnp.bfloat16)
+    prob_out[0] = prob
+    size = keys[0].shape[0]
+    latent = sum(
+        mul(prob[:, j * size : (j + 1) * size], key[:, :rank]) for j, key in enumerate(keys)
+    ).astype(jnp.bfloat16)
+    latent_out[0] = latent
+    rows = query.shape[0]
+    head = jnp.concatenate(
+        [
+            mul(
+                latent[k * rows : (k + 1) * rows],
+                up[:, k * (DN + DV) + DN : (k + 1) * (DN + DV)],
+            )
+            for k in range(heads)
+        ],
+        axis=1,
+    ).astype(jnp.bfloat16)
+    head_out[...] = head
+    part_out[...] = mul(head, out_weight[...]).astype(jnp.bfloat16)
+
+
+def attend_kernel(query, own, other, up, out_weight, spots, key_spots, heads, scale, after=()):
+    sequences = own.shape[0]
+    rows = query.shape[0] // sequences
+    key_count = 4 * own.shape[2]
+    rank = up.shape[0]
+    shapes = [
+        shaped((query.shape[0], out_weight.shape[1])),
+        shaped((sequences, heads * rows, key_count)),
+        shaped((sequences, heads * rows, rank)),
+        shaped((sequences, heads * rows, rank)),
+        shaped((query.shape[0], heads * DV)),
+    ]
+    return local_call(
+        partial(attend_body, heads, scale),
+        (sequences,),
+        [by_rows(query, rows), by_first(own), by_first(other)]
+        + [whole(a) for a in (up, out_weight, spots, key_spots)],
+        [
+            by_rows(shapes[0], rows),
+            by_first(shapes[1]),
+            by_first(shapes[2]),
+            by_first(shapes[3]),
+            by_rows(shapes[4], rows),
+        ],
+        shapes,
+        (query, own, other, up, out_weight, spots, key_spots),
+        after,
+    )
+
+
+def attend_back_body(
+    heads, scale, grads, query, own, other, up, out_weight, prob, absorbed, latent,
+    own_out, other_out, query_out, up_out,
+):
+    rank = up.shape[0]
+    rows = query.shape[0]
+    first = pl.program_id(0) == 0
+    grads_here = grads[...]
+    head_grad = mul_nt(grads_here, out_weight[...]).astype(jnp.bfloat16)
+    span = lambda k: slice(k * rows, (k + 1) * rows)
+    latent_grad = []
+    value_parts = []
+    for k in range(heads):
+        mine = head_grad[:, k * DV : (k + 1) * DV]
+        value_up = up[:, k * (DN + DV) + DN : (k + 1) * (DN + DV)]
+        latent_grad.append(mul_nt(mine, value_up).astype(jnp.bfloat16))
+        value_parts.append(mul_tn(latent[0, span(k)], mine))
+    latent_grad = jnp.concatenate(latent_grad, axis=0)
+    keys = [source[0, k] for source in (own, other) for k in range(2)]
+    size = keys[0].shape[0]
+    prob_here = prob[0]
+    prob_wide = prob_here.astype(jnp.float32)
+    prob_grad = jnp.concatenate([mul_nt(latent_grad, key[:, :rank]) for key in keys], axis=1)
+    inner = jnp.sum(prob_wide * prob_grad, axis=1, keepdims=True)
+    score_grad = (prob_wide * (prob_grad - inner)).astype(jnp.bfloat16)
+    absorbed_here = absorbed[0]
+    parts = head_parts_of(query[...], heads, DN)
+    rope = jnp.concatenate([part[1] for part in parts], axis=0)
+    wide = 0.0
+    narrow = 0.0
+    for j, key in enumerate(keys):
+        piece = score_grad[:, j * size : (j + 1) * size]
+        wide = wide + mul(piece, key[:, :rank])
+        narrow = narrow + mul(piece, key[:, rank:])
+        target = (own_out, other_out)[j // 2]
+        value = mul_tn(prob_here[:, j * size : (j + 1) * size], latent_grad)
+        target[0, j % 2, :, :rank] = (mul_tn(piece, absorbed_here) * scale + value).astype(
+            jnp.bfloat16
+        )
+        target[0, j % 2, :, rank:] = (mul_tn(piece, rope) * scale).astype(jnp.bfloat16)
+    wide = (wide * scale).astype(jnp.bfloat16)
+    narrow = narrow * scale
+    for k in range(heads):
+        start = k * (DN + DV)
+        key_part = mul_tn(wide[span(k)], parts[k][0])
+        up_out[:, start : start + DN] = (
+            jnp.where(first, 0.0, up_out[:, start : start + DN]) + key_part
+        )
+        up_out[:, start + DN : start + DN + DV] = (
+            jnp.where(first, 0.0, up_out[:, start + DN : start + DN + DV]) + value_parts[k]
+        )
+        query_out[:, k * DN : (k + 1) * DN] = mul(wide[span(k)], up[:, start : start + DN])
+        rope_size = narrow.shape[1]
+        at = heads * DN + k * rope_size
+        query_out[:, at : at + rope_size] = narrow[span(k)]
+
+
+def attend_back_kernel(
+    grads, query, own, other, up, out_weight, prob, absorbed, latent, heads, scale, after=()
+):
+    sequences = own.shape[0]
+    rows = query.shape[0] // sequences
+    shapes = [
+        shaped(own.shape),
+        shaped(own.shape),
+        shaped(query.shape, jnp.float32),
+        shaped(up.shape, jnp.float32),
+    ]
+    return local_call(
+        partial(attend_back_body, heads, scale),
+        (sequences,),
+        [by_rows(grads, rows), by_rows(query, rows), by_first(own), by_first(other)]
+        + [whole(up), whole(out_weight), by_first(prob), by_first(absorbed), by_first(latent)],
+        [by_first(own), by_first(own), by_rows(query, rows), whole(up)],
+        shapes,
+        (grads, query, own, other, up, out_weight, prob, absorbed, latent),
+        after,
+    )
+
+
+def heads_body(z, own, *refs):
+    query_out, up_out, out_out = refs[-3:]
+    count = (len(refs) - 3) // 2 + 1
+    above, below = (refs[: count - 1], refs[count - 1 : 2 * count - 2])
+    groups, rows, _ = own.shape
+    query_columns = query_out.shape[1]
+    up_blocks = up_out.shape[1] // 128
+    up_rows = rows // up_blocks
+    heads = out_out.shape[0] // rows
+    for s in range(count):
+        part = own[...] if s == 0 else above[s - 1][...] + below[count - s - 1][...]
+        place = lax.rem(z[0] + s, count)
+        for j in range(groups):
+            block = place * groups + j
+            start = pl.multiple_of(block * rows, rows)
+            query_out[pl.ds(start, rows), :] = part[j, :, :query_columns]
+            for k in range(up_blocks):
+                up_out[
+                    pl.ds(pl.multiple_of(block * up_rows, up_rows), up_rows),
+                    k * 128 : (k + 1) * 128,
+                ] = part[j, k * up_rows : (k + 1) * up_rows, query_columns : query_columns + 128]
+            for k in range(heads):
+                at = query_columns + 128 + k * rows
+                out_out[k * rows : (k + 1) * rows, pl.ds(start, rows)] = part[j, :, at : at + rows]
+
+
+def heads_kernel(z, own, above, below, query_columns, heads, up_columns):
+    count = len(above) + 1
+    groups, rows, _ = own.shape
+    width = count * groups * rows
+    up_rows = rows * 128 // up_columns
+    shapes = [
+        shaped((width, query_columns)),
+        shaped((count * groups * up_rows, up_columns)),
+        shaped((heads * rows, width)),
+    ]
+    return local_call(
+        heads_body,
+        (1,),
+        [pl.BlockSpec(memory_space=pltpu.SMEM)] + [whole(own)] * (2 * count - 1),
+        [whole(s) for s in shapes],
+        shapes,
+        (z, own, *above, *below),
+    )
+
+
+def out_grads_body(rows, head, grads, out):
+    heads = head.shape[1] // rows
+    total = mul_tn(head[...], grads[...]).astype(jnp.bfloat16)
+    for i in range(out.shape[0]):
+        for k in range(heads):
+            out[i, :, k * rows : (k + 1) * rows] = total[
+                k * rows : (k + 1) * rows, i * rows : (i + 1) * rows
+            ]
+
+
+def out_grads_kernel(head, grads, rows):
+    shape = shaped((grads.shape[1] // rows, rows, head.shape[1]))
+    return local_call(
+        partial(out_grads_body, rows),
+        (1,),
+        [whole(head), whole(grads)],
+        whole(shape),
+        shape,
+        (head, grads),
+    )
+
+
+def query_grads_body(rows, grads, source, up, out):
+    columns = grads.shape[1]
+    up_blocks = up.shape[1] // 128
+    up_rows = rows // up_blocks
+    here = grads[...]
+    for i in range(out.shape[0]):
+        out[i, :, :columns] = mul_tn(source[:, i * rows : (i + 1) * rows], here).astype(
+            jnp.bfloat16
+        )
+        for k in range(up_blocks):
+            out[i, k * up_rows : (k + 1) * up_rows, columns:] = up[
+                i * up_rows : (i + 1) * up_rows, k * 128 : (k + 1) * 128
+            ].astype(jnp.bfloat16)
+
+
+def query_grads_kernel(grads, source, up, rows, after=()):
+    shape = shaped((source.shape[1] // rows, rows, grads.shape[1] + 128))
+    return local_call(
+        partial(query_grads_body, rows),
+        (1,),
+        [whole(grads), whole(source), whole(up)],
+        whole(shape),
+        shape,
+        (grads, source, up),
+        after,
+    )
+
+
+def product_nt_body(left, right, out):
+    out[...] = mul_nt(left[...], right[...]).astype(jnp.bfloat16)
+
+
+def product_nt_kernel(left, right, after=()):
+    shape = shaped((left.shape[0], right.shape[0]))
+    return local_call(
+        product_nt_body,
+        (left.shape[0] // TILE,),
+        [by_rows(left), whole(right)],
+        by_rows(shape),
+        shape,
+        (left, right),
+        after,
+    )
+
+
 CTX = ("z", "x", "c")
 
 
@@ -535,57 +998,96 @@
     return jnp.where(lax.axis_index(axis_name) == 0, value, flipped)
 
 
-def gather_z(value):
+def tie(value, *others):
+    if not others:
+        return value
+    zero = sum(other[(0,) * other.ndim].astype(jnp.float32) for other in others) * 0.0
+    return value + zero.astype(value.dtype)
+
+
+def rows_first(value):
+    return with_layout_constraint(value, Layout(major_to_minor=tuple(range(value.ndim))))
+
+
+def put(parts, places):
+    whole = jnp.zeros((len(parts),) + parts[0].shape, parts[0].dtype)
+    for part, place in zip(parts, places):
+        whole = lax.dynamic_update_index_in_dim(whole, part, place, 0)
+    return rows_first(whole)
+
+
+def z_parts(value):
+    return [value] + [from_z(value, s) for s in range(1, lax.axis_size("z"))]
+
+
+def chain_z(value):
     count = lax.axis_size("z")
-    return trade(jnp.broadcast_to(value[None], (count,) + value.shape), "z")
-
-
-def gather_ctx(value):
-    slabs = gather_z(value)
-    slabs = by_own(jnp.stack([slabs, swap(slabs, "x")], axis=1), "x", 1)
-    slabs = by_own(jnp.stack([slabs, swap(slabs, "c")], axis=2), "c", 2)
-    return slabs.reshape((-1,) + value.shape)
-
-
-def gather_plane(rows):
+    above, below = ([value], [value])
+    for r in range(1, count):
+        down = [(i + 1, i) for i in range(count - r)]
+        up = [(i, i + 1) for i in range(r - 1, count - 1)]
+        above.append(lax.ppermute(above[-1], "z", down))
+        below.append(lax.ppermute(below[-1], "z", up))
+    return (above[1:], below[1:])
+
+
+def put_z(parts):
+    z = lax.axis_index("z")
+    count = len(parts)
+    return put(parts, [(z + s) % count for s in range(count)])
+
+
+def gather_plane(rows, axes=("x", "y"), gates=()):
     half = rows.shape[0] // 2
-    over_x = swap(rows, "x")
-    over_y = swap(rows, "y")
-    both = jnp.concatenate([swap(over_y[:half], "x"), swap(over_x[half:], "y")], axis=0)
-    return jnp.stack([jnp.stack([rows, over_y]), jnp.stack([over_x, both])])
-
-
-def scatter_plane(rows):
+    over_a = tie(swap(rows, axes[0]), *gates)
+    over_b = tie(swap(rows, axes[1]), *gates)
+    both = jnp.concatenate([swap(over_b[:half], axes[0]), swap(over_a[half:], axes[1])], axis=0)
+    return jnp.stack([jnp.stack([rows, over_b]), jnp.stack([over_a, both])])
+
+
+def plane_first(rows, axes=("x", "y"), gates=()):
     half = rows.shape[2] // 2
     lower, upper = (rows[:, :, :half], rows[:, :, half:])
-    lower = low(add(lower[0], swap(lower[1], "x")))
-    upper = low(add(upper[:, 0], swap(upper[:, 1], "y")))
-    lower = add(lower[0], swap(lower[1], "y"))
-    upper = add(upper[0], swap(upper[1], "x"))
+    lower = low(add(lower[0], tie(swap(lower[1], axes[0]), *gates)))
+    upper = low(add(upper[:, 0], tie(swap(upper[:, 1], axes[1]), *gates)))
+    return (lower, upper)
+
+
+def plane_second(lower, upper, axes=("x", "y"), gates=()):
+    lower = add(lower[0], tie(swap(lower[1], axes[1]), *gates))
+    upper = add(upper[0], tie(swap(upper[1], axes[0]), *gates))
     return jnp.concatenate([lower, upper], axis=0)
 
 
-def gather_all(rows):
+def scatter_plane(rows, axes=("x", "y")):
+    return plane_second(*plane_first(rows, axes), axes)
+
+
+def spread_z(rows):
+    return jnp.concatenate(z_parts(rows), axis=0)
+
+
+def fold_z(slabs, gates=()):
     count = lax.axis_size("z")
-    slabs = jnp.concatenate([rows] + [from_z(rows, s) for s in range(1, count)], axis=0)
-    own = gather_plane(slabs)
-    return (own, swap(own, "c"))
-
-
-def scatter_all(own, other):
-    count = lax.axis_size("z")
-    own = low(add(own, swap(other, "c")))
-    slabs = scatter_plane(own)
     block = slabs.shape[0] // count
     sent = low(slabs)
     total = slabs[:block]
     for s in range(1, count):
-        total = total + to_z(sent[s * block : (s + 1) * block], s).astype(jnp.float32)
+        part = tie(to_z(sent[s * block : (s + 1) * block], s), *gates)
+        total = total + part.astype(jnp.float32)
     return total
 
 
-def sum_z(value):
-    return jnp.sum(trade(value, "z").astype(jnp.float32).reshape((lax.axis_size("z"), -1) + value.shape[1:]), axis=0)
+def sum_z(value, gates=()):
+    count = lax.axis_size("z")
+    z = lax.axis_index("z")
+    parts = [
+        lax.dynamic_index_in_dim(value, (z + s) % count, 0, keepdims=False) for s in range(count)
+    ]
+    total = parts[0].astype(jnp.float32)
+    for s in range(1, count):
+        total = total + tie(to_z(parts[s], s), *gates).astype(jnp.float32)
+    return total
 
 
 def both_halves(rows):
@@ -620,17 +1122,14 @@
     rows_here = width // count
     slab = 4 * block
     experts = router_weight.shape[1]
-    hidden_here = expert_gate.shape[2]
     shared_here = shared_gate.shape[1] // count
-    used = hidden_here + shared_here
-    padded = -(-(used + experts) // 128) * 128
+    part = -(-max(shared_here, experts) // 128) * 128
     heads = latent_up.shape[1] // (4 * (DN + DV))
     query_columns = heads * (DN + DR)
     rank_rows = R // count
     head_rows = heads * DV
     scale = (DN + DR) ** (-0.5)
 
-    extra = jnp.zeros((rows_here, 1), jnp.bfloat16)
     latent_column = jnp.pad(latent_norm, (0, rows_here - rank_rows))[:, None]
     small = jnp.concatenate(
         [
@@ -643,35 +1142,99 @@
         ],
         axis=1,
     )
-    small = jnp.pad(small, ((0, 0), (0, -small.shape[1] % 128)))
-    small = gather_ctx(small)
-    small_rows = small.reshape(width, -1)
+    small = put_z(z_parts(jnp.pad(small, ((0, 0), (0, -small.shape[1] % 128)))))
     at = R + DR
-    full_down = small_rows[:, :at]
-    full_router = small_rows[:, at : at + experts]
-    full_norm_in = small_rows[:, at + experts].astype(jnp.float32)
-    full_norm_ffn = small_rows[:, at + experts + 1].astype(jnp.float32)
-    full_latent_norm = small[:, :rank_rows, at + experts + 2].reshape(R).astype(jnp.float32)
-    all_routes = small[:, :, at + experts + 3 : at + experts + 3 + TOPK]
-
-    by_heads = jnp.transpose(query_weight.reshape(rows_here, 4, query_columns), (1, 0, 2))
-    query_here = gather_z(trade(by_heads, ("x", "c"))).reshape(width, query_columns)
+    down_here = small[:, :, :at]
+    rest = small[:, :, at:]
+    down_here = down_here.reshape(-1, R + DR)
+    down_x = swap(down_here, "x")
+    down_pieces = (down_here, down_x, swap(down_here, "c"), swap(down_x, "c"))
+    own_gain = rest[:, :, experts].reshape(1, zs * rows_here).astype(jnp.float32)
+    rest = jnp.stack([rest, swap(rest, "x")], axis=1)
+    rest = jnp.stack([rest, swap(rest, "c")], axis=2)
+    rest = by_own(by_own(rest, "x", 1), "c", 2).reshape(count, rows_here, -1)
+    full_router = rest[:, :, :experts].reshape(width, experts)
+    full_norm_in = rest[:, :, experts].reshape(width).astype(jnp.float32)
+    full_norm_ffn = rest[:, :, experts + 1].reshape(width).astype(jnp.float32)
+    full_latent_norm = rest[:, :rank_rows, experts + 2].reshape(R).astype(jnp.float32)
+    all_routes = rest[:, :, experts + 3 : experts + 3 + TOPK]
+
+    up_columns = heads * (DN + DV)
     up_part = jnp.transpose(
-        latent_up.reshape(rank_rows, 4, heads * (DN + DV)), (1, 0, 2)
-    ).reshape(4, -1, 128)
+        latent_up.reshape(rank_rows, 4, up_columns // 128, 128), (1, 2, 0, 3)
+    ).reshape(4, rows_here, 128)
     out_part = jnp.transpose(output_weight.reshape(4, heads, DV, rows_here), (0, 2, 1, 3)).reshape(
         4, DV, heads * rows_here
     )
-    up_columns = heads * (DN + DV) * rank_rows // DV
-    up_part = up_part.reshape(4, DV, up_columns)
-    by_heads = jnp.concatenate([up_part, out_part], axis=2)
-    up_out = gather_z(trade(by_heads, ("x", "c"))).reshape(count, DV, -1)
-    up_here = up_out[:, :, :up_columns].reshape(R, heads, DN + DV)
-    key_up = up_here[..., :DN]
-    value_up = up_here[..., DN:]
-    out_here = jnp.transpose(
-        up_out[:, :, up_columns:].reshape(count, DV, heads, rows_here), (2, 1, 0, 3)
-    ).reshape(head_rows, width)
+    by_heads = query_weight.reshape(rows_here, 4, heads, DN + DR)
+    by_heads = jnp.concatenate(
+        [
+            by_heads[..., :DN].reshape(rows_here, 4, heads * DN),
+            by_heads[..., DN:].reshape(rows_here, 4, heads * DR),
+        ],
+        axis=2,
+    )
+    by_heads = jnp.transpose(by_heads, (1, 0, 2))
+    by_heads = trade(jnp.concatenate([by_heads, up_part, out_part], axis=2), ("x", "c"))
+    mine = by_own(tokens, "y", 0)
+    line = jnp.stack([mine, swap(mine, "x")], axis=1)
+    line = jnp.stack([line, swap(line, "c")], axis=1)
+    source = line.reshape(sequences * slab, width).astype(jnp.float32)
+    grad_mine = by_own(cotangent, "y", 0)[0]
+    grad_parts = z_parts(tie(grad_mine, small))
+    grads_own = gather_plane(jnp.concatenate(grad_parts))
+    grads_other = swap(grads_own, "c").reshape(-1, width)
+    grads_own = grads_own.reshape(-1, width)
+    gate_t, up_t, down = (expert_gate[0].T, expert_up[0].T, expert_down[0])
+    back_own = product_nt_kernel(grads_own, down)
+    back_other = product_nt_kernel(grads_other, down)
+    by_heads = tie(by_heads, grad_parts[-1])
+    above, below = chain_z(by_heads)
+    query_here, up_here, out_here = heads_kernel(
+        z[None], by_heads, above, below, query_columns, heads, up_columns
+    )
+
+    def places(turns):
+        two = jnp.arange(2)
+        base = (
+            ((z + turns[None, None, :]) % zs) * 4
+            + (x ^ two[None, :, None]) * 2
+            + (c ^ two[:, None, None])
+        )
+        return (base[..., None] * block + jnp.arange(block)).reshape(-1)
+
+    positions = places(jnp.arange(1))
+    key_positions = places(jnp.arange(zs))
+    cosine, sine = rotary_tables(positions, DR)
+    normed, unit_in, inverse_in = root_norm(source, full_norm_in)
+    input_low = low(normed)
+
+    own_rows = line[0].reshape(slab, width)
+    own_columns = jnp.concatenate(
+        [
+            lax.dynamic_slice_in_dim(own_rows, (4 * k + 2 * x + c) * rows_here, rows_here, 1)
+            for k in range(zs)
+        ],
+        axis=1,
+    ).astype(jnp.float32)
+    latent_part = dot(
+        low(own_columns * inverse_in[:slab] * own_gain), down_here
+    )
+    latent_part = low(latent_part).reshape(2, 2, block, R + DR)
+    latent_part = low(add(latent_part[0], swap(latent_part[1], "c")))
+    latent_raw = add(latent_part[0], swap(latent_part[1], "x"))
+    latent_scaled, latent_unit, latent_inverse = root_norm(latent_raw[:, :R], full_latent_norm)
+    key_own = low(
+        jnp.concatenate(
+            [latent_scaled, rotate(latent_raw[:, R:], cosine[:block], sine[:block])], axis=-1
+        )
+    )
+    plane = gather_plane(spread_z(key_own), ("y", "x"))
+    keys_own, keys_other = (plane, swap(plane, "c"))
+    query = dot(input_low, query_here)
+    rope = query[:, heads * DN :].reshape(sequences, slab, heads, DR)
+    rope = rotate(rope, cosine[:, None, :], sine[:, None, :]).reshape(sequences * slab, -1)
+    query_low = low(jnp.concatenate([query[:, : heads * DN], rope], axis=1))
 
     shared_mine = jnp.concatenate(
         [
@@ -681,163 +1244,110 @@
         ],
         axis=1,
     )
-    shared_here_rows = jnp.transpose(trade(shared_mine, CTX), (1, 0, 2)).reshape(-1, width)
-    gate_rows = shared_here_rows[:shared_here]
-    up_rows = shared_here_rows[shared_here : 2 * shared_here]
-    down_rows = shared_here_rows[2 * shared_here :]
-    first = jnp.concatenate(
+    shared_rows = trade(tie(shared_mine, query_low), CTX)
+    shared_rows = jnp.transpose(shared_rows, (1, 0, 2)).reshape(3, shared_here, width)
+    shared_rows = jnp.pad(shared_rows, ((0, 0), (0, part - shared_here), (0, 0)))
+    small_t = jnp.concatenate(
         [
-            expert_gate[0],
-            gate_rows.T,
-            full_router,
-            jnp.zeros((width, padded - used - experts), jnp.bfloat16),
-            expert_up[0],
-            up_rows.T,
-            jnp.zeros((width, padded - used), jnp.bfloat16),
-        ],
-        axis=1,
-    )
-    second = jnp.concatenate(
-        [expert_down[0], down_rows, jnp.zeros((padded - used, width), jnp.bfloat16)], axis=0
-    )
-
-    mine = by_own(tokens, "y", 0)
-    line = jnp.stack([mine, swap(mine, "x")], axis=1)
-    line = jnp.stack([line, swap(line, "c")], axis=1)
-    source = line.reshape(sequences * slab, width).astype(jnp.float32)
-    grad_mine = by_own(cotangent, "y", 0)[0]
-    grads_own, grads_other = gather_all(grad_mine)
-
-    def places(turn):
-        columns = jnp.arange(2)
-        base = ((z + turn) % zs) * 4 + (x ^ columns[None, :]) * 2 + (c ^ columns[:, None])
-        return (base[:, :, None] * block + jnp.arange(block)).reshape(slab)
-
-    positions = places(0)
-    key_positions = jnp.concatenate([places(turn) for turn in range(zs)])
-    cosine, sine = rotary_tables(positions, DR)
-    normed, unit_in, inverse_in = root_norm(source, full_norm_in)
-    input_low = low(normed)
-    query_raw = dot(input_low, query_here).reshape(sequences, slab, heads, DN + DR)
-    query_low = low(
-        jnp.concatenate(
-            [
-                query_raw[..., :DN],
-                rotate(query_raw[..., DN:], cosine[:, None, :], sine[:, None, :]),
-            ],
-            axis=-1,
-        )
-    )
-    absorbed = jnp.einsum(
-        "sbhn,rhn->shbr", query_low[..., :DN], key_up, preferred_element_type=jnp.float32
-    )
-    query_rows = jnp.concatenate(
-        [low(absorbed), jnp.transpose(query_low[..., DN:], (0, 2, 1, 3))], axis=-1
-    )
-    latent_raw = dot(input_low, full_down).reshape(sequences, slab, R + DR)
-    latent_scaled, latent_unit, latent_inverse = root_norm(latent_raw[..., :R], full_latent_norm)
-    key_slab = low(
-        jnp.concatenate([latent_scaled, rotate(latent_raw[..., R:], cosine, sine)], axis=-1)
-    )
-    half_keys = key_slab[:, : slab // 2]
-    far = jnp.stack([from_z(half_keys, s) for s in range(1, zs)], axis=1)
-    far = jnp.stack([far, swap(far, "c")], axis=2).reshape(sequences, (zs - 1) * slab, R + DR)
-    keys = jnp.concatenate([key_slab, far], axis=1)
-
-    scores = (
-        jnp.einsum("shqc,skc->shqk", query_rows, keys, preferred_element_type=jnp.float32) * scale
-    )
-    allowed = positions[:, None] >= key_positions[None, :]
-    scores = jnp.where(allowed, scores, -1e30)
-    top = jnp.max(scores, axis=-1, keepdims=True)
-    weights = jnp.exp(scores - top)
-    prob = weights / jnp.sum(weights, axis=-1, keepdims=True)
-    prob_low = low(prob)
-    latent_out = low(
-        jnp.einsum("shqk,skr->shqr", prob_low, keys[..., :R], preferred_element_type=jnp.float32)
-    )
-    head_out = low(
-        jnp.einsum("shbr,rhv->sbhv", latent_out, value_up, preferred_element_type=jnp.float32)
-    ).reshape(sequences * slab, head_rows)
+            shared_rows[0],
+            shared_rows[1],
+            jnp.pad(full_router.T, ((0, part - experts), (0, 0))),
+        ]
+    )
+    shared_down_t = shared_rows[2]
 
     def scatter_slab(partial):
         parts = partial.reshape(2, 2, 2, block, -1)
         kept = low(add(parts[:, 0], swap(parts[:, 1], "c")))
-        return scatter_plane(jnp.transpose(kept, (1, 0, 2, 3)))
-
-    def gather_slab(rows):
-        plane = jnp.transpose(gather_plane(rows), (1, 0, 2, 3))
+        return scatter_plane(kept, ("y", "x"))
+
+    def gather_slab(rows, gates=()):
+        plane = gather_plane(rows, ("y", "x"), gates)
         return jnp.stack([plane, swap(plane, "c")], axis=1).reshape(sequences * slab, -1)
 
-    attention = scatter_slab(low(dot(head_out, out_here)))
+    attention, prob, absorbed, latent_out, head_out = attend_kernel(
+        query_low,
+        keys_own,
+        keys_other,
+        up_here,
+        out_here,
+        positions[:, None],
+        key_positions[None, :],
+        heads,
+        scale,
+        (back_own, back_other) + down_pieces[1:],
+    )
+    attention = scatter_slab(attention)
     hidden_in = mine[0].astype(jnp.float32) + attention
     normed_ffn, unit_ffn, inverse_ffn = root_norm(hidden_in, full_norm_ffn)
     ffn_low = low(normed_ffn)
     shares = jax.nn.softmax(dot(ffn_low, full_router), axis=-1)
-    ffn_own, ffn_other = gather_all(ffn_low)
+    ffn_slabs = spread_z(ffn_low)
+    ffn_own = gather_plane(ffn_slabs, gates=(small_t,))
+    ffn_other = swap(ffn_own, "c").reshape(-1, width)
+    ffn_own = ffn_own.reshape(-1, width)
 
     relative = all_routes.reshape(zs, 2, 2, sequences, block, TOPK)
     relative = by_own(by_own(by_own(relative, "x", 1), "c", 2), "y", 3)
     relative = jnp.roll(relative, -z, axis=0)
     routed = jnp.any(relative == me.astype(jnp.bfloat16), axis=-1)
-    routed = jnp.transpose(routed, (2, 1, 3, 0, 4)).reshape(2, -1).astype(jnp.float32)
-    column = jnp.arange(padded)
-    is_expert = (column < hidden_here)[None, :]
-    is_shared = ((column >= hidden_here) & (column < used))[None, :]
-    picked = (jnp.arange(experts) == me)[None, :]
-
-    def feed(rows, grads, named):
-        rows = rows.reshape(-1, width)
-        grads = grads.reshape(-1, width)
-        both = dot(rows, first)
-        gate = both[:, :padded]
-        up = both[:, padded:]
-        chances = jax.nn.softmax(gate[:, used : used + experts], axis=-1)
-        share = jnp.sum(jnp.where(picked, chances, 0.0), axis=-1) * named
-        factor = jnp.where(is_expert, share[:, None], jnp.where(is_shared, 1.0, 0.0))
-        sigmoid = jax.nn.sigmoid(gate)
-        silu = gate * sigmoid
-        slope = sigmoid * (1.0 + gate * (1.0 - sigmoid))
-        act = silu * up
-        back = dot_nt(grads, second)
-        gain = jnp.sum(jnp.where(is_expert, low(act).astype(jnp.float32) * back, 0.0), axis=-1)
-        back = back * factor
-        pre = jnp.concatenate([low(back * up * slope), low(back * silu)], axis=1)
-        act = low(act * factor)
-        return (act, pre, gain * named)
-
-    act_own, pre_own, gain_own = feed(ffn_own, grads_own, routed[0])
-    act_other, pre_other, gain_other = feed(ffn_other, grads_other, routed[1])
-    shape = (2, 2, zs * block, width)
-    ffn_grad = scatter_all(
-        low(dot_nt(pre_own, first)).reshape(shape), low(dot_nt(pre_other, first)).reshape(shape)
-    )
-    routed_sum = scatter_all(
-        low(dot(act_own, second)).reshape(shape), low(dot(act_other, second)).reshape(shape)
-    )
-    output = both_halves(low(hidden_in + routed_sum))
-
-    gains = jnp.stack([gain_own, gain_other]).reshape(2, 2, 2, zs, block)
-    gains = by_own(by_own(by_own(gains, "c", 0), "x", 1), "y", 2)
-    gains = jnp.roll(jnp.transpose(gains, (3, 1, 0, 2, 4)), z, axis=0)
-    gains = trade(gains.reshape(2 * count, block), CTX + ("y",))
-    share_grad = jnp.sum(gains.reshape(count, 2, block), axis=1).T
+    routed = jnp.transpose(routed, (2, 1, 3, 0, 4)).reshape(2, -1, 1).astype(jnp.float32)
+    pick = (jnp.arange(part)[None, :] == me).astype(jnp.float32)
+
+    def feed(rows, grads, back, named):
+        shared_back = product_nt_kernel(grads, shared_down_t)
+        return feed_kernel(rows, back, shared_back, gate_t, up_t, small_t, named, pick, experts)
+
+    act_own, more_own, gate_own, up_own, pre_own, gain_own = feed(
+        ffn_own, grads_own, back_own, routed[0]
+    )
+    act_other, more_other, gate_other, up_other, pre_other, gain_other = feed(
+        ffn_other, grads_other, back_other, routed[1]
+    )
+    shape = (2, 2, zs * block, -1)
+    grad_other = input_kernel(
+        gate_other, up_other, pre_other, gate_t, up_t, small_t, gain_other, pick
+    )
+    grad_own = input_kernel(
+        gate_own, up_own, pre_own, gate_t, up_t, small_t, gain_own, pick, (grad_other,)
+    )
+    grad_own = low(add(grad_own, swap(grad_other, "c"))).reshape(shape)
+    sum_other = result_kernel(act_other, more_other, down, shared_down_t, (grad_own,))
+    sum_own = result_kernel(act_own, more_own, down, shared_down_t, (sum_other,))
+    lower, upper = plane_first(grad_own, gates=(sum_own,))
+    routed_own = low(add(tie(sum_own, lower), swap(sum_other, "c"))).reshape(shape)
+    grad_slab = plane_second(lower, upper, gates=(routed_own,))
+    grad_expert_down, shared_down_back = weight_kernel(
+        (act_own, act_other), (more_own, more_other), (grads_own, grads_other), 0, part, (grad_slab,)
+    )
+    ffn_grad = fold_z(grad_slab, (grad_expert_down,))
+    share_grad = ffn_grad[:, width : width + experts]
+    ffn_grad = ffn_grad[:, :width]
     logit_grad = shares * (share_grad - jnp.sum(shares * share_grad, axis=-1, keepdims=True))
-
-    all_rows = jnp.concatenate([ffn_own.reshape(-1, width), ffn_other.reshape(-1, width)])
-    all_grads = jnp.concatenate([grads_own.reshape(-1, width), grads_other.reshape(-1, width)])
-    all_act = jnp.concatenate([act_own, act_other])
-    all_pre = jnp.concatenate([pre_own, pre_other])
-    grad_expert_down = dot_tn(all_act[:, :hidden_here], all_grads)[None]
-    grad_expert_gate = dot_tn(all_rows, all_pre[:, :hidden_here])[None]
-    grad_expert_up = dot_tn(all_rows, all_pre[:, padded : padded + hidden_here])[None]
-    shared_pre = jnp.concatenate(
-        [all_pre[:, hidden_here:used], all_pre[:, padded + hidden_here : padded + used]], axis=1
-    )
+    ffn_grad = ffn_grad + dot_nt(low(logit_grad), full_router)
+    grad_router = dot_tn(ffn_low, low(logit_grad))
+    hidden_part, grad_norm_ffn = root_norm_back(ffn_grad, unit_ffn, inverse_ffn, full_norm_ffn)
+    grad_hidden = grad_mine.astype(jnp.float32) + hidden_part
+
+    hidden_low = low(grad_hidden)
+    grad_expert_gate, shared_gate_back = weight_kernel(
+        (gate_own, gate_other), (pre_own, pre_other), (ffn_own, ffn_other), 0, part, (hidden_low,)
+    )
+    grad_expert_up, shared_up_back = weight_kernel(
+        (up_own, up_other),
+        (pre_own, pre_other),
+        (ffn_own, ffn_other),
+        1,
+        part,
+        (grad_expert_gate,),
+    )
+    lower, upper = plane_first(tie(routed_own, grad_slab), gates=(grad_expert_gate,))
+    attention_grad = gather_slab(hidden_low, (grad_expert_gate,))
     shared_back = jnp.concatenate(
         [
-            low(dot_tn(shared_pre, all_rows)),
-            low(dot_tn(all_act[:, hidden_here:used], all_grads)),
+            shared_gate_back[:shared_here],
+            shared_up_back[:shared_here],
+            shared_down_back[:shared_here],
         ]
     )
     shared_back = trade(
@@ -847,88 +1357,71 @@
     grad_shared_up = shared_back[:, shared_here : 2 * shared_here].reshape(-1, rows_here).T
     grad_shared_down = shared_back[:, 2 * shared_here :].reshape(-1, rows_here)
 
-    ffn_grad = ffn_grad + dot_nt(low(logit_grad), full_router)
-    grad_router = dot_tn(ffn_low, low(logit_grad))
-    hidden_part, grad_norm_ffn = root_norm_back(ffn_grad, unit_ffn, inverse_ffn, full_norm_ffn)
-    grad_hidden = grad_mine.astype(jnp.float32) + hidden_part
-
-    attention_grad = gather_slab(low(grad_hidden))
-    grad_out_here = dot_tn(head_out, attention_grad)
-    head_grad = low(dot_nt(attention_grad, out_here)).reshape(sequences, slab, heads, DV)
-    grad_value_up = jnp.einsum(
-        "shbr,sbhv->rhv", latent_out, head_grad, preferred_element_type=jnp.float32
-    )
-    latent_grad = low(
-        jnp.einsum("sbhv,rhv->shbr", head_grad, value_up, preferred_element_type=jnp.float32)
-    )
-    prob_grad = jnp.einsum(
-        "shqr,skr->shqk", latent_grad, keys[..., :R], preferred_element_type=jnp.float32
-    )
-    inner = jnp.sum(prob * prob_grad, axis=-1, keepdims=True)
-    score_grad = low(prob * (prob_grad - inner))
-    query_grad = low(
-        jnp.einsum("shqk,skc->shqc", score_grad, keys, preferred_element_type=jnp.float32) * scale
-    )
-    key_grad = (
-        jnp.einsum("shqk,shqc->skc", score_grad, query_rows, preferred_element_type=jnp.float32)
-        * scale
-    )
-    value_grad = jnp.einsum(
-        "shqk,shqr->skr", prob_low, latent_grad, preferred_element_type=jnp.float32
-    )
-    key_grad = low(key_grad + jnp.pad(value_grad, ((0, 0), (0, 0), (0, DR))))
-    key_grad = jnp.transpose(
-        key_grad.reshape(sequences, zs, 2, 2, block, R + DR), (2, 3, 0, 1, 4, 5)
-    ).reshape(2, 2, 2, zs * block, R + DR)
-    key_sum = scatter_all(key_grad[0], key_grad[1])
-
-    absorbed_grad = query_grad[..., :R]
-    rope_grad = jnp.transpose(query_grad[..., R:], (0, 2, 1, 3)).astype(jnp.float32)
-    grad_key_up = jnp.einsum(
-        "shbr,sbhn->rhn", absorbed_grad, query_low[..., :DN], preferred_element_type=jnp.float32
-    )
-    nope_grad = jnp.einsum(
-        "shbr,rhn->sbhn", absorbed_grad, key_up, preferred_element_type=jnp.float32
-    )
-    rope_raw = rotate(rope_grad, cosine[:, None, :], -sine[:, None, :])
-    query_raw_grad = low(jnp.concatenate([nope_grad, rope_raw], axis=-1)).reshape(
-        sequences * slab, query_columns
-    )
-    grad_query_here = dot_tn(input_low, query_raw_grad)
-    input_grad = scatter_slab(low(dot_nt(query_raw_grad, query_here)))
+    grad_out_here = out_grads_kernel(head_out, attention_grad, rows_here)
+    key_own, key_other, query_grad, grad_up_here = attend_back_kernel(
+        attention_grad,
+        query_low,
+        keys_own,
+        keys_other,
+        up_here,
+        out_here,
+        prob,
+        absorbed,
+        latent_out,
+        heads,
+        scale,
+        (lower, upper, grad_out_here, grad_expert_up),
+    )
+    routed_slab = plane_second(lower, upper, gates=(key_own,))
+    key_sum = low(add(key_own, swap(key_other, "c")))
+    key_sum = fold_z(scatter_plane(key_sum, ("y", "x")))
+    rope = query_grad[:, heads * DN :].reshape(sequences, slab, heads, DR)
+    rope = rotate(rope, cosine[:, None, :], -sine[:, None, :]).reshape(sequences * slab, -1)
+    query_raw_grad = low(jnp.concatenate([query_grad[:, : heads * DN], rope], axis=1))
+    input_grad = scatter_slab(product_nt_kernel(query_raw_grad, query_here))
+    grad_heads = query_grads_kernel(query_raw_grad, input_low, grad_up_here, rows_here)
+    output = both_halves(low(hidden_in + fold_z(routed_slab, (grad_heads,))))
 
     latent_back, grad_latent_norm = root_norm_back(
-        key_sum[:, :R], latent_unit[0, :block], latent_inverse[0, :block], full_latent_norm
+        key_sum[:, :R], latent_unit, latent_inverse, full_latent_norm
     )
     rope_key = rotate(key_sum[:, R:], cosine[:block], -sine[:block])
     latent_raw_grad = low(jnp.concatenate([latent_back, rope_key], axis=-1))
-    input_grad = input_grad + dot_nt(latent_raw_grad, full_down)
+    latent_input = jnp.stack([dot_nt(latent_raw_grad, down) for down in down_pieces])
+    latent_input = latent_input.reshape(2, 2, block, zs, rows_here)
+    latent_input = by_own(by_own(latent_input, "c", 0), "x", 1)
+    input_grad = input_grad + jnp.transpose(latent_input, (2, 3, 1, 0, 4)).reshape(block, width)
     source_part, grad_norm_in = root_norm_back(
         input_grad, unit_in[:block], inverse_in[:block], full_norm_in
     )
     tokens_gradient = both_halves(low(grad_hidden + source_part)).astype(jnp.float32)
 
     slab_latent_grad = gather_slab(latent_raw_grad)
-    columns = lax.dynamic_index_in_dim(
-        input_low.reshape(sequences * slab, zs, 4, rows_here), x * 2 + c, 2, keepdims=False
-    ).reshape(sequences * slab, zs * rows_here)
-    grad_down = sum_z(low(dot_tn(columns, slab_latent_grad)))
-
-    grad_out_here = jnp.transpose(
-        grad_out_here.reshape(heads, DV, count, rows_here), (2, 1, 0, 3)
-    ).reshape(count * DV, heads * rows_here)
-    grad_out = trade(low(sum_z(low(grad_out_here))), ("x", "c"))
+    grad_down = low(dot_tn(input_low, slab_latent_grad)).reshape(zs, 4, rows_here, R + DR)
+    grad_down = sum_z(
+        lax.dynamic_index_in_dim(grad_down, x * 2 + c, 1, keepdims=False)
+    )
+
+    grad_out = trade(
+        low(sum_z(grad_out_here.reshape(zs, 4, rows_here, -1), (key_own,))), ("x", "c")
+    )
     grad_output = jnp.transpose(
         grad_out.reshape(4, DV, heads, rows_here), (0, 2, 1, 3)
     ).reshape(-1, rows_here).astype(jnp.float32)
-    grad_up_here = jnp.concatenate([grad_key_up, grad_value_up], axis=-1).reshape(
-        count * DV, up_columns
-    )
-    both = jnp.concatenate([grad_query_here.reshape(width, query_columns), grad_up_here], axis=1)
-    both = trade(low(sum_z(low(both))), ("x", "c")).astype(jnp.float32).reshape(4, rows_here, -1)
-    grad_query = jnp.transpose(both[..., :query_columns], (1, 0, 2)).reshape(rows_here, -1)
+    grad_heads = sum_z(
+        tie(grad_heads, key_sum).reshape(zs, 4, rows_here, -1), (slab_latent_grad,)
+    )
+    both = trade(low(grad_heads), ("x", "c")).astype(jnp.float32)
+    grad_query = jnp.transpose(both[..., :query_columns], (1, 0, 2))
+    grad_query = jnp.concatenate(
+        [
+            grad_query[..., : heads * DN].reshape(rows_here, 4, heads, DN),
+            grad_query[..., heads * DN :].reshape(rows_here, 4, heads, DR),
+        ],
+        axis=-1,
+    ).reshape(rows_here, -1)
     grad_latent_up = jnp.transpose(
-        both[..., query_columns:].reshape(4, rank_rows, heads * (DN + DV)), (1, 0, 2)
+        both[..., query_columns:].reshape(4, up_columns // 128, rank_rows, 128), (2, 0, 1, 3)
     ).reshape(rank_rows, -1)
 
     small_grads = jnp.concatenate(
@@ -959,9 +1452,9 @@
         grad_shared_gate,
         grad_shared_up,
         grad_shared_down,
-        grad_expert_gate,
-        grad_expert_up,
-        grad_expert_down,
+        grad_expert_gate.T[None],
+        grad_expert_up.T[None],
+        grad_expert_down[None],
     )
 
 

time: 903 us -> 807 us (0.89)
  Pallas kernels: 0 us -> 181 us
  matrix products: 173 us -> 14 us
  waiting for transfers between devices: 318 us -> 211 us
  local copies, waits for them, and re-layouts: 142 us -> 120 us
  between operations: 3.49 us -> 12.6 us
    pallas_call x0 -> x19, Pallas kernels: none -> 181 us  [local_call(): pl.pallas_call(run, grid=grid, in_specs=list(in_specs) + [pl.BlockSpec(me...]
    all_to_all x14 -> x6, waiting for transfers between devices: 74 us -> 7.51 us  [trade(): return lax.all_to_all(value, axes, split_axis=0, concat_axis=0, tiled=True)]
    dot_general x8 -> x5, matrix products: 57.6 us -> 5.12 us  [dot_nt(): lax.dot_general(left, right, (((1,), (1,)), ((), ())), preferred_element_...]
    dot_general x9 -> x2, matrix products: 53.6 us -> 4.7 us  [dot_tn(): lax.dot_general(left, right, (((0,), (0,)), ((), ())), preferred_element_...]
    ppermute x53 -> x62, waiting for transfers between devices: 145 us -> 100 us  [swap(): return lax.ppermute(value, axis, [(0, 1), (1, 0)])]
    all_to_all x14 -> x6, starting transfers between devices: 72.5 us -> 29.1 us  [trade(): return lax.all_to_all(value, axes, split_axis=0, concat_axis=0, tiled=True)]
    dot_general x8 -> x3, matrix products: 41.9 us -> 4.17 us  [dot(): return jnp.dot(left, right, preferred_element_type=jnp.float32)]
    ppermute x9 -> x18, starting transfers between devices: 9.03 us -> 29.5 us  [to_z(): lax.ppermute(value, 'z', [(i, (i + steps) % count) for i in range(count)])]
  transfers between devices with their start and end apart: 85 -> 104, of which waited for: 38 -> 45; matrix products, arithmetic and copies ran while one was open for 38% -> 26% of each run, Pallas kernels for 0% -> 16%
where the time goes in v2:
time: 807 us; the launch traced here: 794 us
  waiting for transfers between devices  211 us (26%)
  Pallas kernels  181 us (22%)
  starting transfers between devices  145 us (18%)
  local copies, waits for them, and re-layouts  120 us (15%)
  other arithmetic  110 us (14%)
  matrix products  14 us (2%)
  between operations  12.6 us (2%)
    pallas_call x19, Pallas kernels, local_call(): pl.pallas_call(run, grid=grid, in_specs=list(in_specs) + [pl.BlockSpec(me...  181 us
    ppermute x62, waiting for transfers between devices, swap(): return lax.ppermute(value, axis, [(0, 1), (1, 0)])  100 us
    ppermute x62, starting transfers between devices, swap(): return lax.ppermute(value, axis, [(0, 1), (1, 0)])  56.6 us
    ppermute x18, waiting for transfers between devices, to_z(): lax.ppermute(value, 'z', [(i, (i + steps) % count) for i in range(count)])  52.2 us
    ppermute x12, waiting for transfers between devices, from_z(): lax.ppermute(value, 'z', [((i + steps) % count, i) for i in range(count)])  48.9 us
    convert_element_type x19, other arithmetic, low(): return value.astype(jnp.bfloat16)  36.9 us
    ppermute x18, starting transfers between devices, to_z(): lax.ppermute(value, 'z', [(i, (i + steps) % count) for i in range(count)])  29.5 us
    all_to_all x6, starting transfers between devices, trade(): return lax.all_to_all(value, axes, split_axis=0, concat_axis=0, tiled=True)  29.1 us
  transfers between devices with their start and end apart: 104, of which 45 were waited for; matrix products, arithmetic and copies ran while one was open for 26% of the time, Pallas kernels for 16%

profile of v2, /device:TPU:16, one launch (start us, length us, event | category | flops | bytes accessed | tf_op | source)
XLA Modules:
  0.0 793.7 jit_solution(6814053768079057041)
XLA Ops:
  12.8 3.6 all-to-all-start
  31.1 11.2 %collective-permute-done.5 = bf16[4,128,64]{2,1,0:T(8,128)(2,1)} collective-permute-done((bf16[4,128,64]{2,1,0:T(8,128)(2,1)S(1)}, bf16[4,128,64]{2,1,0:T(8,128)(2,1)}, u32[]{:S(2)}, u32[]{:S(2)}) %collective-permute-start.5) | collective-permute-done | bytes 65568 | tf_op jit(solution)/shard_map/ppermute | solution.py:955
  44.0 6.6 collective-permute-done.24
  71.2 9.6 %collective-permute-done.26 = bf16[256,2048]{1,0:T(8,128)(2,1)} collective-permute-done((bf16[256,2048]{1,0:T(8,128)(2,1)}, bf16[256,2048]{1,0:T(8,128)(2,1)}, u32[]{:S(2)}, u32[]{:S(2)}) %collective-permute-start.26) | collective-permute-done | bytes 1048608 | tf_op jit(solution)/shard_map/ppermute | solution.py:955
  97.4 3.9 collective-permute-start.8
  101.3 4.6 collective-permute-done.28
  119.7 5.0 collective-permute-start.9
  133.5 11.6 %collective-permute-done.17 = bf16[64,576]{1,0:T(8,128)(2,1)S(1)} collective-permute-done((bf16[64,576]{1,0:T(8,128)(2,1)}, bf16[64,576]{1,0:T(8,128)(2,1)S(1)}, u32[]{:S(2)}, u32[]{:S(2)}) %collective-permute-start.17) | collective-permute-done | bytes 73760 | tf_op jit(solution)/shard_map/ppermute | solution.py:960
  150.9 3.6 collective-permute-done.19
  164.0 5.4 multiply_convert_fusion.1
  169.4 7.4 shard_map.289.refs_7_.refs_1_
  176.8 4.9 shard_map.288
  189.0 7.4 shard_map.290.refs_8_.refs_1_
  196.4 8.5 %shard_map.291 = (bf16[512,2048]{1,0:T(8,128)(2,1)}, bf16[2,512,1024]{2,1,0:T(8,128)(2,1)}, bf16[2,512,512]{2,1,0:T(8,128)(2,1)}, bf16[2,512,512]{2,1,0:T(8,128)(2,1)}, bf16[512,256]{1,0:T(8,128)(2,1)}) custom-call(bf16[512,384]{1,0:T(8,128)(2,1)} %pad_maximum_fusion.17.refs_0_.refs_1_, bf16[2,2,256,576]{3,2,1,0:T(8,128)(2,1)} %copy-done, ...), custom_call_target="tpu_custom_call" | custom-call | flops 1 | bytes 1 | tf_op jit(solution)/shard_map/pallas_call | solution.py:503
  216.3 6.1 all-to-all-start.1
  230.0 3.7 collective-permute-done.36
  235.7 4.4 collective-permute-start.41
  241.8 23.2 %collective-permute-done.41 = bf16[64,2048]{1,0:T(8,128)(2,1)S(1)} collective-permute-done((bf16[64,2048]{1,0:T(8,128)(2,1)S(1)}, bf16[64,2048]{1,0:T(8,128)(2,1)S(1)}, u32[]{:S(2)}, u32[]{:S(2)}) %collective-permute-start.41) | collective-permute-done | bytes 262176 | tf_op jit(solution)/shard_map/ppermute | solution.py:960
  265.0 3.9 collective-permute-done.39
  278.8 16.7 %collective-permute-done.42 = bf16[256,2048]{1,0:T(8,128)(2,1)} collective-permute-done((bf16[256,2048]{1,0:T(8,128)(2,1)}, bf16[256,2048]{1,0:T(8,128)(2,1)}, u32[]{:S(2)}, u32[]{:S(2)}) %collective-permute-start.42) | collective-permute-done | bytes 1048608 | tf_op jit(solution)/shard_map/ppermute | solution.py:955
  304.2 5.3 collective-permute-done.44
  318.8 4.8 shard_map.294.refs_2_
  323.6 16.2 %shard_map.295 = (bf16[1024,704]{1,0:T(8,128)(2,1)}, bf16[1024,128]{1,0:T(8,128)(2,1)}, bf16[1024,704]{1,0:T(8,128)(2,1)}, bf16[1024,704]{1,0:T(8,128)(2,1)}, bf...) custom-call(bf16[1024,2048]{1,0:T(8,128)(2,1)} %bitcast.91.refs_0_.refs_5_, bf16[1024,704]{1,0:T(8,128)(2,1)} %shard_map.290.refs_8_.refs_1_, ...), custom_call_target="tpu_custom_call" | custom-call | flops 1 | bytes 1 | tf_op jit(solution)/shard_map/pallas_call | solution.py:503
  339.7 12.9 %shard_map.296.refs_8_ = bf16[1024,2176]{1,0:T(8,128)(2,1)} custom-call(bf16[1024,704]{1,0:T(8,128)(2,1)} %get-tuple-element.58.refs_0_.refs_1_, bf16[1024,704]{1,0:T(8,128)(2,1)} %get-tuple-element.59.refs_1_, bf16[1024,256]{1,0:T(8,128)(2,1)} %get-tuple-element.60.refs_2_.refs_3_, bf16[704,2048]{1,0:T(8,128)(2,1)} %bitcast.529, ...), custom_call_target="tpu_custom_call" | custom-call | flops 1 | bytes 1 | tf_op jit(solution)/shard_map/pallas_call | solution.py:503
  354.4 4.8 shard_map.292.refs_2_
  359.2 16.1 %shard_map.293 = (bf16[1024,704]{1,0:T(8,128)(2,1)}, bf16[1024,128]{1,0:T(8,128)(2,1)}, bf16[1024,704]{1,0:T(8,128)(2,1)}, bf16[1024,704]{1,0:T(8,128)(2,1)}, bf...) custom-call(bf16[1024,2048]{1,0:T(8,128)(2,1)} %bitcast.82.refs_0_.refs_4_, bf16[1024,704]{1,0:T(8,128)(2,1)} %shard_map.289.refs_7_.refs_1_, ...), custom_call_target="tpu_custom_call" | custom-call | flops 1 | bytes 1 | tf_op jit(solution)/shard_map/pallas_call | solution.py:503
  375.4 13.3 %shard_map.297 = bf16[1024,2176]{1,0:T(8,128)(2,1)} custom-call(bf16[1024,704]{1,0:T(8,128)(2,1)} %get-tuple-element.54.refs_0_, bf16[1024,704]{1,0:T(8,128)(2,1)} %get-tuple-element.55.refs_1_.refs_0_, bf16[1024,256]{1,0:T(8,128)(2,1)} %get-tuple-element.56.refs_2_, bf16[704,2048]{1,0:T(8,128)(2,1)} %bitcast.531, bf16[704,2048]{1,0:T(8,128)(2,1)} %bitcast.535, ...), custom_call_target="tpu_custom_call" | custom-call | flops 1 | bytes 1 | tf_op jit(solution)/shard_map/pallas_call | solution.py:503
  388.7 6.8 add_convert_fusion
  395.5 8.1 %shard_map.298.refs_4_ = bf16[1024,2048]{1,0:T(8,128)(2,1)} custom-call(bf16[1024,704]{1,0:T(8,128)(2,1)} %get-tuple-element.52.refs_0_.refs_1_, bf16[1024,128]{1,0:T(8,128)(2,1)} %get-tuple-element.53.refs_1_.refs_3_, bf16[704,2048]{1,0:T(8,128)(2,1)} %bitcast.526, bf16[128,2048]{1,0:T(8,128)(2,1)} %get-tuple-element.207.refs_1_.refs_3_, ...), custom_call_target="tpu_custom_call" | custom-call | flops 1 | bytes 1 | tf_op jit(solution)/shard_map/pallas_call | solution.py:503
  413.3 8.1 %shard_map.299 = bf16[1024,2048]{1,0:T(8,128)(2,1)} custom-call(bf16[1024,704]{1,0:T(8,128)(2,1)} %get-tuple-element.50.refs_0_, bf16[1024,128]{1,0:T(8,128)(2,1)} %get-tuple-element.51.refs_1_.refs_2_, bf16[704,2048]{1,0:T(8,128)(2,1)} %bitcast.527, bf16[128,2048]{1,0:T(8,128)(2,1)} %get-tuple-element.207.refs_1_.refs_3_, bf16[1024,2048]{1,0:T(8,128)(2,1)} %shard_map.298.refs_4_), custom_call_target="tpu_custom_call" | custom-call | flops 1 | bytes 1 | tf_op jit(solution)/shard_map/pallas_call | solution.py:503
  423.3 12.2 %collective-permute-done.48 = bf16[2,128,2176]{2,1,0:T(8,128)(2,1)S(1)} collective-permute-done((bf16[2,128,2176]{2,1,0:T(8,128)(2,1)}, bf16[2,128,2176]{2,1,0:T(8,128)(2,1)S(1)}, u32[]{:S(2)}, u32[]{:S(2)}) %collective-permute-start.48) | collective-permute-done | bytes 1114144 | tf_op jit(solution)/shard_map/ppermute | solution.py:955
  443.0 4.2 add_convert_fusion.1
  448.4 5.4 collective-permute-done.50
  464.9 14.2 %shard_map.300 = (f32[704,2048]{1,0:T(8,128)}, bf16[128,2048]{1,0:T(8,128)(2,1)}) custom-call(bf16[1024,704]{1,0:T(8,128)(2,1)} %get-tuple-element.50.refs_0_, bf16[1024,704]{1,0:T(8,128)(2,1)} %get-tuple-element.52.refs_0_.refs_1_, bf16[1024,128]{1,0:T(8,128)(2,1)} %get-tuple-element.51.refs_1_.refs_2_, ...), custom_call_target="tpu_custom_call" | custom-call | flops 1 | bytes 1 | tf_op jit(solution)/shard_map/pallas_call | solution.py:503
  494.5 14.0 %shard_map.301 = (f32[704,2048]{1,0:T(8,128)}, bf16[128,2048]{1,0:T(8,128)(2,1)}) custom-call(bf16[1024,704]{1,0:T(8,128)(2,1)} %get-tuple-element.54.refs_0_, bf16[1024,704]{1,0:T(8,128)(2,1)} %get-tuple-element.58.refs_0_.refs_1_, bf16[1024,256]{1,0:T(8,128)(2,1)} %get-tuple-element.56.refs_2_, bf16[1024,256]{1,0:T(8,128)(2,1)} %get-tuple-element.60.refs_2_.refs_3_, ...), custom_call_target="tpu_custom_call" | custom-call | flops 1 | bytes 1 | tf_op jit(solution)/shard_map/pallas_call | solution.py:503
  508.5 14.0 %shard_map.303 = (f32[704,2048]{1,0:T(8,128)}, bf16[128,2048]{1,0:T(8,128)(2,1)}) custom-call(bf16[1024,704]{1,0:T(8,128)(2,1)} %get-tuple-element.55.refs_1_.refs_0_, bf16[1024,704]{1,0:T(8,128)(2,1)} %get-tuple-element.59.refs_1_, bf16[1024,256]{1,0:T(8,128)(2,1)} %get-tuple-element.56.refs_2_, bf16[1024,256]{1,0:T(8,128)(2,1)} %get-tuple-element.60.refs_2_.refs_3_, ...), custom_call_target="tpu_custom_call" | custom-call | flops 1 | bytes 1 | tf_op jit(solution)/shard_map/pallas_call | solution.py:503
  550.8 13.8 %shard_map.304 = (bf16[2,2,256,576]{3,2,1,0:T(8,128)(2,1)}, bf16[2,2,256,576]{3,2,1,0:T(8,128)(2,1)}, f32[512,384]{1,0:T(8,128)}, f32[512,512]{1,0:T(8,128)}) custom-call(bf16[512,2048]{1,0:T(8,128)(2,1)} %bitcast.541, bf16[512,384]{1,0:T(8,128)(2,1)} %pad_maximum_fusion.17.refs_0_.refs_1_, bf16[2,2,256,576]{3,2,1,0:T(8,128)(2,1)} %copy-done, ...), custom_call_target="tpu_custom_call" | custom-call | flops 1 | bytes 1 | tf_op jit(solution)/shard_map/pallas_call | solution.py:503
  569.2 4.8 collective-permute-start.96
  580.1 4.7 collective-permute-done.97
  584.8 5.8 collective-permute-done.96
  603.7 5.6 all-to-all-start.5
  611.0 4.0 shard_map.306
  615.1 4.7 shard_map.305
  621.8 13.7 %collective-permute-done.67 = bf16[64,2048]{1,0:T(8,128)(2,1)} collective-permute-done((bf16[64,2048]{1,0:T(8,128)(2,1)}, bf16[64,2048]{1,0:T(8,128)(2,1)}, u32[]{:S(2)}, u32[]{:S(2)}) %collective-permute-start.67) | collective-permute-done | bytes 262176 | tf_op jit(solution)/shard_map/ppermute | solution.py:965
  706.5 6.9 all-to-all-start.2
  743.8 5.1 reshape.810
  754.5 19.1 %collective-permute-done.91 = bf16[4,128,512]{1,2,0:T(8,128)(2,1)} collective-permute-done((bf16[4,128,512]{1,2,0:T(8,128)(2,1)}, bf16[4,128,512]{1,2,0:T(8,128)(2,1)}, u32[]{:S(2)}, u32[]{:S(2)}) %collective-permute-start.91) | collective-permute-done | bytes 524320 | tf_op jit(solution)/shard_map/ppermute | solution.py:965
  783.2 7.5 all-to-all-done.3
  (669 shorter events, 373.5 us)
Async XLA Ops:
  12.8 57.5 %all-to-all-start = ((bf16[4,128,768]{2,1,0:T(8,128)(2,1)}), bf16[4,128,768]{2,1,0:T(8,128)(2,1)S(1)}, u32[]{:S(2)}, u32[]{:S(2)}) async-start(bf16[4,128,768]{2,1,0:T(8,128)(2,1)} %pad_maximum_fusion.10), calls=%async_computation | async-start | bytes 1572864 | tf_op jit(solution)/shard_map/all_to_all | solution.py:969
  17.3 40.5 %collective-permute-start = (bf16[2,64,2048]{2,1,0:T(8,128)(2,1)}, bf16[2,64,2048]{2,1,0:T(8,128)(2,1)}, u32[]{:S(2)}, u32[]{:S(2)}) collective-permute-start(bf16[2,64,2048]{2,1,0:T(8,128)(2,1)} %reverse_select_fusion.5), channel_id=1, source_target_pairs={{0,4},{4,0},{1,5},{5,1},{2,6},{6,2},{3,7},{7,3},{8,12},{12,8},{9,1... | collective-permute-start | bytes 1572872 | tf_op jit(solution)/shard_map/ppermute | solution.py:955
  28.1 22.5 %collective-permute-start.24 = (bf16[64,2048]{1,0:T(8,128)(2,1)S(1)}, bf16[64,2048]{1,0:T(8,128)(2,1)}, u32[]{:S(2)}, u32[]{:S(2)}) collective-permute-start(bf16[64,2048]{1,0:T(8,128)(2,1)S(1)} %add_bitcast_fusion), channel_id=1, source_target_pairs={{8,0},{16,8},{24,16},{0,24},{9,1},{17,9},{25,17},{1,25},{10,2},{18... | collective-permute-start | bytes 786440 | tf_op jit(solution)/shard_map/ppermute | solution.py:960
  30.4 22.4 %collective-permute-start.7 = (bf16[64,2048]{1,0:T(8,128)(2,1)S(1)}, bf16[64,2048]{1,0:T(8,128)(2,1)S(1)}, u32[]{:S(2)}, u32[]{:S(2)}) collective-permute-start(bf16[64,2048]{1,0:T(8,128)(2,1)S(1)} %add_bitcast_fusion), channel_id=1, source_target_pairs={{24,0},{0,8},{8,16},{16,24},{25,1},{1,9},{9,17},{17,25},{26,2},{2,... | collective-permute-start | bytes 786440 | tf_op jit(solution)/shard_map/ppermute | solution.py:960
  55.4 25.4 %collective-permute-start.26 = (bf16[256,2048]{1,0:T(8,128)(2,1)}, bf16[256,2048]{1,0:T(8,128)(2,1)}, u32[]{:S(2)}, u32[]{:S(2)}) collective-permute-start(bf16[256,2048]{1,0:T(8,128)(2,1)} %get-tuple-element.221), channel_id=1, source_target_pairs={{0,1},{1,0},{2,3},{3,2},{4,5},{5,4},{6,7},{7,6},{8,9},{9,8},{10,11... | collective-permute-start | bytes 3145736 | tf_op jit(solution)/shard_map/ppermute | solution.py:955
  56.9 26.4 %collective-permute-start.27 = (bf16[256,2048]{1,0:T(8,128)(2,1)}, bf16[256,2048]{1,0:T(8,128)(2,1)}, u32[]{:S(2)}, u32[]{:S(2)}) collective-permute-start(bf16[256,2048]{1,0:T(8,128)(2,1)} %get-tuple-element.221), channel_id=1, source_target_pairs={{0,4},{4,0},{1,5},{5,1},{2,6},{6,2},{3,7},{7,3},{8,12},{12,8},{9,1... | collective-permute-start | bytes 3145736 | tf_op jit(solution)/shard_map/ppermute | solution.py:955
  60.0 26.5 %collective-permute-start.1 = (bf16[2,2,64,2048]{3,2,0,1:T(8,128)(2,1)}, bf16[2,2,64,2048]{3,2,0,1:T(8,128)(2,1)S(1)}, u32[]{:S(2)}, u32[]{:S(2)}) collective-permute-start(bf16[2,2,64,2048]{3,2,0,1:T(8,128)(2,1)} %get-tuple-element.227), channel_id=1, source_target_pairs={{0,2},{2,0},{1,3},{3,1},{4,6},{6,4},{5,7},{7,5},{8,10},{10,8},{9,1... | collective-permute-start | bytes 3145736 | tf_op jit(solution)/shard_map/ppermute | solution.py:955
  61.8 51.8 %collective-permute-start.32 = (bf16[512,576]{0,1:T(8,128)(2,1)}, bf16[512,576]{0,1:T(8,128)(2,1)}, u32[]{:S(2)}, u32[]{:S(2)}) collective-permute-start(bf16[512,576]{0,1:T(8,128)(2,1)} %copy.438), channel_id=1, source_target_pairs={{0,2},{2,0},{1,3},{3,1},{4,6},{6,4},{5,7},{7,5},{8,10},{10,8},{9,1... | collective-permute-start | bytes 1769480 | tf_op jit(solution)/shard_map/ppermute | solution.py:955
  62.3 35.1 %collective-permute-start.31 = (bf16[512,576]{0,1:T(8,128)(2,1)}, bf16[512,576]{0,1:T(8,128)(2,1)}, u32[]{:S(2)}, u32[]{:S(2)}) collective-permute-start(bf16[512,576]{0,1:T(8,128)(2,1)} %copy.438), channel_id=1, source_target_pairs={{0,4},{4,0},{1,5},{5,1},{2,6},{6,2},{3,7},{7,3},{8,12},{12,8},{9,1... | collective-permute-start | bytes 1769480 | tf_op jit(solution)/shard_map/ppermute | solution.py:955
  82.7 23.2 %collective-permute-start.28 = (bf16[128,2048]{1,0:T(8,128)(2,1)}, bf16[128,2048]{1,0:T(8,128)(2,1)}, u32[]{:S(2)}, u32[]{:S(2)}) collective-permute-start(bf16[128,2048]{1,0:T(8,128)(2,1)} %slice.648), channel_id=1, source_target_pairs={{0,4},{4,0},{1,5},{5,1},{2,6},{6,2},{3,7},{7,3},{8,12},{12,8},{9,1... | collective-permute-start | bytes 1572872 | tf_op jit(solution)/shard_map/ppermute | solution.py:955
  95.4 22.3 %collective-permute-start.11 = (bf16[4,128,768]{2,1,0:T(8,128)(2,1)S(1)}, bf16[4,128,768]{2,1,0:T(8,128)(2,1)}, u32[]{:S(2)}, u32[]{:S(2)}) collective-permute-start(bf16[4,128,768]{2,1,0:T(8,128)(2,1)S(1)} %copy-done.20), channel_id=1, source_target_pairs={{0,8},{8,16},{16,24},{1,9},{9,17},{17,25},{2,10},{10,18},{18,26},{... | collective-permute-start | bytes 2359304 | tf_op jit(solution)/shard_map/ppermute | solution.py:1030
  97.4 22.3 %collective-permute-start.8 = (bf16[4,128,768]{2,1,0:T(8,128)(2,1)S(1)}, bf16[4,128,768]{2,1,0:T(8,128)(2,1)}, u32[]{:S(2)}, u32[]{:S(2)}) collective-permute-start(bf16[4,128,768]{2,1,0:T(8,128)(2,1)S(1)} %copy-done.20), channel_id=1, source_target_pairs={{8,0},{16,8},{24,16},{9,1},{17,9},{25,17},{10,2},{18,10},{26,18},{... | collective-permute-start | bytes 2359304 | tf_op jit(solution)/shard_map/ppermute | solution.py:1029
  111.9 77.2 %collective-permute-start.30 = (bf16[2,2,256,2048]{3,2,1,0:T(8,128)(2,1)}, bf16[2,2,256,2048]{3,2,1,0:T(8,128)(2,1)}, u32[]{:S(2)}, u32[]{:S(2)}) collective-permute-start(bf16[2,2,256,2048]{3,2,1,0:T(8,128)(2,1)} %pad_maximum_fusion), channel_id=1, source_target_pairs={{0,2},{2,0},{1,3},{3,1},{4,6},{6,4},{5,7},{7,5},{8,10},{10,8},{9,1... | collective-permute-start | bytes 12582920 | tf_op jit(solution)/shard_map/ppermute | solution.py:955
  117.7 39.3 %collective-permute-start.12 = (bf16[4,128,768]{2,1,0:T(8,128)(2,1)}, bf16[4,128,768]{2,1,0:T(8,128)(2,1)}, u32[]{:S(2)}, u32[]{:S(2)}) collective-permute-start(bf16[4,128,768]{2,1,0:T(8,128)(2,1)} %collective-permute-done.11.refs_5_), channel_id=1, source_target_pairs={{8,16},{16,24},{9,17},{17,25},{10,18},{18,26},{11,19},{19,27},{12,... | collective-permute-start | bytes 2359304 | tf_op jit(solution)/shard_map/ppermute | solution.py:1030
  119.7 39.5 %collective-permute-start.9 = (bf16[4,128,768]{2,1,0:T(8,128)(2,1)}, bf16[4,128,768]{2,1,0:T(8,128)(2,1)S(1)}, u32[]{:S(2)}, u32[]{:S(2)}) collective-permute-start(bf16[4,128,768]{2,1,0:T(8,128)(2,1)} %collective-permute-done.8.refs_2_), channel_id=1, source_target_pairs={{8,0},{16,8},{9,1},{17,9},{10,2},{18,10},{11,3},{19,11},{12,4},{20... | collective-permute-start | bytes 2359304 | tf_op jit(solution)/shard_map/ppermute | solution.py:1029
  164.0 22.7 %collective-permute-start.23 = (bf16[2,2,256,576]{2,3,1,0:T(8,128)(2,1)}, bf16[2,2,256,576]{2,3,1,0:T(8,128)(2,1)}, u32[]{:S(2)}, u32[]{:S(2)}) collective-permute-start(bf16[2,2,256,576]{2,3,1,0:T(8,128)(2,1)} %copy.437), channel_id=1, source_target_pairs={{0,2},{2,0},{1,3},{3,1},{4,6},{6,4},{5,7},{7,5},{8,10},{10,8},{9,1... | collective-permute-start | bytes 3538952 | tf_op jit(solution)/shard_map/ppermute | solution.py:955
  216.3 57.2 %all-to-all-start.1 = ((bf16[16,264,128]{2,1,0:T(8,128)(2,1)}), bf16[16,264,128]{2,1,0:T(8,128)(2,1)S(1)}, u32[]{:S(2)}, u32[]{:S(2)}) async-start(bf16[16,264,128]{2,1,0:T(8,128)(2,1)} %maximum_add_fusion), calls=%async_computation.1 | async-start | bytes 2162688 | tf_op jit(solution)/shard_map/all_to_all | solution.py:969
  235.7 29.3 %collective-permute-start.41 = (bf16[64,2048]{1,0:T(8,128)(2,1)S(1)}, bf16[64,2048]{1,0:T(8,128)(2,1)S(1)}, u32[]{:S(2)}, u32[]{:S(2)}) collective-permute-start(bf16[64,2048]{1,0:T(8,128)(2,1)S(1)} %multiply_convert_fusion.2), channel_id=1, source_target_pairs={{24,0},{0,8},{8,16},{16,24},{25,1},{1,9},{9,17},{17,25},{26,2},{2,... | collective-permute-start | bytes 786440 | tf_op jit(solution)/shard_map/ppermute | solution.py:960
  240.1 24.9 %collective-permute-start.40 = (bf16[64,2048]{1,0:T(8,128)(2,1)S(1)}, bf16[64,2048]{1,0:T(8,128)(2,1)S(1)}, u32[]{:S(2)}, u32[]{:S(2)}) collective-permute-start(bf16[64,2048]{1,0:T(8,128)(2,1)S(1)} %multiply_convert_fusion.2), channel_id=1, source_target_pairs={{16,0},{24,8},{0,16},{8,24},{17,1},{25,9},{1,17},{9,25},{18,2},{26... | collective-permute-start | bytes 786440 | tf_op jit(solution)/shard_map/ppermute | solution.py:960
  240.1 28.8 %collective-permute-start.39 = (bf16[64,2048]{1,0:T(8,128)(2,1)S(1)}, bf16[64,2048]{1,0:T(8,128)(2,1)S(1)}, u32[]{:S(2)}, u32[]{:S(2)}) collective-permute-start(bf16[64,2048]{1,0:T(8,128)(2,1)S(1)} %multiply_convert_fusion.2), channel_id=1, source_target_pairs={{8,0},{16,8},{24,16},{0,24},{9,1},{17,9},{25,17},{1,25},{10,2},{18... | collective-permute-start | bytes 786440 | tf_op jit(solution)/shard_map/ppermute | solution.py:960
  270.5 25.0 %collective-permute-start.42 = (bf16[256,2048]{1,0:T(8,128)(2,1)}, bf16[256,2048]{1,0:T(8,128)(2,1)}, u32[]{:S(2)}, u32[]{:S(2)}) collective-permute-start(bf16[256,2048]{1,0:T(8,128)(2,1)} %get-tuple-element.217), channel_id=1, source_target_pairs={{0,1},{1,0},{2,3},{3,2},{4,5},{5,4},{6,7},{7,6},{8,9},{9,8},{10,11... | collective-permute-start | bytes 3145736 | tf_op jit(solution)/shard_map/ppermute | solution.py:955
  272.0 26.4 %collective-permute-start.43 = (bf16[256,2048]{1,0:T(8,128)(2,1)}, bf16[256,2048]{1,0:T(8,128)(2,1)}, u32[]{:S(2)}, u32[]{:S(2)}) collective-permute-start(bf16[256,2048]{1,0:T(8,128)(2,1)} %get-tuple-element.217), channel_id=1, source_target_pairs={{0,4},{4,0},{1,5},{5,1},{2,6},{6,2},{3,7},{7,3},{8,12},{12,8},{9,1... | collective-permute-start | bytes 3145736 | tf_op jit(solution)/shard_map/ppermute | solution.py:955
  352.7 36.1 %collective-permute-start.47 = (bf16[1024,2176]{1,0:T(8,128)(2,1)}, bf16[1024,2176]{1,0:T(8,128)(2,1)}, u32[]{:S(2)}, u32[]{:S(2)}) collective-permute-start(bf16[1024,2176]{1,0:T(8,128)(2,1)} %shard_map.296.refs_8_), channel_id=1, source_target_pairs={{0,2},{2,0},{1,3},{3,1},{4,6},{6,4},{5,7},{7,5},{8,10},{10,8},{9,1... | collective-permute-start | bytes 13369352 | tf_op jit(solution)/shard_map/ppermute | solution.py:955
  403.6 39.4 %collective-permute-start.49 = (bf16[1024,2048]{1,0:T(8,128)(2,1)}, bf16[1024,2048]{1,0:T(8,128)(2,1)}, u32[]{:S(2)}, u32[]{:S(2)}) collective-permute-start(bf16[1024,2048]{1,0:T(8,128)(2,1)} %shard_map.298.refs_4_), channel_id=1, source_target_pairs={{0,2},{2,0},{1,3},{3,1},{4,6},{6,4},{5,7},{7,5},{8,10},{10,8},{9,1... | collective-permute-start | bytes 12582920 | tf_op jit(solution)/shard_map/ppermute | solution.py:955
  408.4 27.1 %collective-permute-start.48 = (bf16[2,128,2176]{2,1,0:T(8,128)(2,1)}, bf16[2,128,2176]{2,1,0:T(8,128)(2,1)S(1)}, u32[]{:S(2)}, u32[]{:S(2)}) collective-permute-start(bf16[2,128,2176]{2,1,0:T(8,128)(2,1)} %slice_bitcast_fusion.2), channel_id=1, source_target_pairs={{0,4},{4,0},{1,5},{5,1},{2,6},{6,2},{3,7},{7,3},{8,12},{12,8},{9,1... | collective-permute-start | bytes 3342344 | tf_op jit(solution)/shard_map/ppermute | solution.py:955
  408.9 26.9 %collective-permute-start.52 = (bf16[2,128,2176]{2,1,0:T(8,128)(2,1)}, bf16[2,128,2176]{2,1,0:T(8,128)(2,1)}, u32[]{:S(2)}, u32[]{:S(2)}) collective-permute-start(bf16[2,128,2176]{2,1,0:T(8,128)(2,1)} %slice_bitcast_fusion), channel_id=1, source_target_pairs={{0,1},{1,0},{2,3},{3,2},{4,5},{5,4},{6,7},{7,6},{8,9},{9,8},{10,11... | collective-permute-start | bytes 3342344 | tf_op jit(solution)/shard_map/ppermute | solution.py:955
  460.0 23.2 %collective-permute-start.54 = (bf16[64,2176]{1,0:T(8,128)(2,1)S(1)}, bf16[64,2176]{1,0:T(8,128)(2,1)S(1)}, u32[]{:S(2)}, u32[]{:S(2)}) collective-permute-start(bf16[64,2176]{1,0:T(8,128)(2,1)S(1)} %get-tuple-element.200), channel_id=1, source_target_pairs={{0,8},{8,16},{16,24},{24,0},{1,9},{9,17},{17,25},{25,1},{2,10},{10... | collective-permute-start | bytes 835592 | tf_op jit(solution)/shard_map/ppermute | solution.py:965
  462.6 22.0 %collective-permute-start.55 = (bf16[64,2176]{1,0:T(8,128)(2,1)S(1)}, bf16[64,2176]{1,0:T(8,128)(2,1)}, u32[]{:S(2)}, u32[]{:S(2)}) collective-permute-start(bf16[64,2176]{1,0:T(8,128)(2,1)S(1)} %get-tuple-element.202), channel_id=1, source_target_pairs={{0,16},{8,24},{16,0},{24,8},{1,17},{9,25},{17,1},{25,9},{2,18},{10... | collective-permute-start | bytes 835592 | tf_op jit(solution)/shard_map/ppermute | solution.py:965
  488.0 39.7 %collective-permute-start.59 = (bf16[64,2048]{1,0:T(8,128)(2,1)S(1)}, bf16[64,2048]{1,0:T(8,128)(2,1)S(1)}, u32[]{:S(2)}, u32[]{:S(2)}) collective-permute-start(bf16[64,2048]{1,0:T(8,128)(2,1)S(1)} %get-tuple-element.178.refs_6_), channel_id=1, source_target_pairs={{0,1},{1,0},{2,3},{3,2},{4,5},{5,4},{6,7},{7,6},{8,9},{9,8},{10,11... | collective-permute-start | bytes 786440 | tf_op jit(solution)/shard_map/ppermute | solution.py:955
  491.5 43.8 %collective-permute-start.63 = (bf16[2,128,2048]{2,1,0:T(8,128)(2,1)}, bf16[2,128,2048]{2,1,0:T(8,128)(2,1)S(1)}, u32[]{:S(2)}, u32[]{:S(2)}) collective-permute-start(bf16[2,128,2048]{2,1,0:T(8,128)(2,1)} %slice_bitcast_fusion.4), channel_id=1, source_target_pairs={{0,1},{1,0},{2,3},{3,2},{4,5},{5,4},{6,7},{7,6},{8,9},{9,8},{10,11... | collective-permute-start | bytes 3145736 | tf_op jit(solution)/shard_map/ppermute | solution.py:955
  492.3 43.9 %collective-permute-start.51 = (bf16[2,128,2048]{2,1,0:T(8,128)(2,1)}, bf16[2,128,2048]{2,1,0:T(8,128)(2,1)}, u32[]{:S(2)}, u32[]{:S(2)}) collective-permute-start(bf16[2,128,2048]{2,1,0:T(8,128)(2,1)} %slice_bitcast_fusion.6), channel_id=1, source_target_pairs={{0,4},{4,0},{1,5},{5,1},{2,6},{6,2},{3,7},{7,3},{8,12},{12,8},{9,1... | collective-permute-start | bytes 3145736 | tf_op jit(solution)/shard_map/ppermute | solution.py:955
  493.5 35.4 %collective-permute-start.58 = (bf16[64,2048]{1,0:T(8,128)(2,1)S(1)}, bf16[64,2048]{1,0:T(8,128)(2,1)}, u32[]{:S(2)}, u32[]{:S(2)}) collective-permute-start(bf16[64,2048]{1,0:T(8,128)(2,1)S(1)} %get-tuple-element.178.refs_6_), channel_id=1, source_target_pairs={{0,4},{4,0},{1,5},{5,1},{2,6},{6,2},{3,7},{7,3},{8,12},{12,8},{9,1... | collective-permute-start | bytes 786440 | tf_op jit(solution)/shard_map/ppermute | solution.py:955
  540.8 33.2 %collective-permute-start.65 = (bf16[128,2048]{1,0:T(8,128)(2,1)}, bf16[128,2048]{1,0:T(8,128)(2,1)}, u32[]{:S(2)}, u32[]{:S(2)}) collective-permute-start(bf16[128,2048]{1,0:T(8,128)(2,1)} %slice_bitcast_fusion.15), channel_id=1, source_target_pairs={{0,4},{4,0},{1,5},{5,1},{2,6},{6,2},{3,7},{7,3},{8,12},{12,8},{9,1... | collective-permute-start | bytes 1572872 | tf_op jit(solution)/shard_map/ppermute | solution.py:955
  542.6 32.8 %collective-permute-start.57 = (bf16[128,2048]{1,0:T(8,128)(2,1)}, bf16[128,2048]{1,0:T(8,128)(2,1)}, u32[]{:S(2)}, u32[]{:S(2)}) collective-permute-start(bf16[128,2048]{1,0:T(8,128)(2,1)} %slice_bitcast_fusion.17), channel_id=1, source_target_pairs={{0,1},{1,0},{2,3},{3,2},{4,5},{5,4},{6,7},{7,6},{8,9},{9,8},{10,11... | collective-permute-start | bytes 1572872 | tf_op jit(solution)/shard_map/ppermute | solution.py:955
  569.2 21.5 %collective-permute-start.96 = (bf16[4,128,256]{2,1,0:T(8,128)(2,1)S(1)}, bf16[4,128,256]{2,1,0:T(8,128)(2,1)}, u32[]{:S(2)}, u32[]{:S(2)}) collective-permute-start(bf16[4,128,256]{2,1,0:T(8,128)(2,1)S(1)} %get-tuple-element.211), channel_id=1, source_target_pairs={{0,16},{8,24},{16,0},{24,8},{1,17},{9,25},{17,1},{25,9},{2,18},{10... | collective-permute-start | bytes 786440 | tf_op jit(solution)/shard_map/ppermute | solution.py:965
  596.5 25.3 %collective-permute-start.64 = (bf16[64,2048]{1,0:T(8,128)(2,1)}, bf16[64,2048]{1,0:T(8,128)(2,1)}, u32[]{:S(2)}, u32[]{:S(2)}) collective-permute-start(bf16[64,2048]{1,0:T(8,128)(2,1)} %slice.958), channel_id=1, source_target_pairs={{0,8},{8,16},{16,24},{24,0},{1,9},{9,17},{17,25},{25,1},{2,10},{10... | collective-permute-start | bytes 786440 | tf_op jit(solution)/shard_map/ppermute | solution.py:965
  598.1 23.7 %collective-permute-start.66 = (bf16[64,2048]{1,0:T(8,128)(2,1)}, bf16[64,2048]{1,0:T(8,128)(2,1)}, u32[]{:S(2)}, u32[]{:S(2)}) collective-permute-start(bf16[64,2048]{1,0:T(8,128)(2,1)} %get-tuple-element.230), channel_id=1, source_target_pairs={{0,16},{8,24},{16,0},{24,8},{1,17},{9,25},{17,1},{25,9},{2,18},{10... | collective-permute-start | bytes 786440 | tf_op jit(solution)/shard_map/ppermute | solution.py:965
  600.1 35.5 %collective-permute-start.67 = (bf16[64,2048]{1,0:T(8,128)(2,1)}, bf16[64,2048]{1,0:T(8,128)(2,1)}, u32[]{:S(2)}, u32[]{:S(2)}) collective-permute-start(bf16[64,2048]{1,0:T(8,128)(2,1)} %get-tuple-element.231), channel_id=1, source_target_pairs={{0,24},{8,0},{16,8},{24,16},{1,25},{9,1},{17,9},{25,17},{2,26},{10... | collective-permute-start | bytes 786440 | tf_op jit(solution)/shard_map/ppermute | solution.py:965
  603.7 43.6 %all-to-all-start.5 = ((bf16[16,264,128]{2,1,0:T(8,128)(2,1)}), bf16[16,264,128]{2,1,0:T(8,128)(2,1)S(1)}, u32[]{:S(2)}, u32[]{:S(2)}) async-start(bf16[16,264,128]{2,1,0:T(8,128)(2,1)} %bitcast_bitcast_fusion), calls=%async_computation.5 | async-start | bytes 2162688 | tf_op jit(solution)/shard_map/all_to_all | solution.py:969
  690.5 33.2 %collective-permute-start.86 = (bf16[64,576]{1,0:T(8,128)(2,1)S(1)}, bf16[64,576]{1,0:T(8,128)(2,1)}, u32[]{:S(2)}, u32[]{:S(2)}) collective-permute-start(bf16[64,576]{1,0:T(8,128)(2,1)S(1)} %pad_maximum_fusion.25), channel_id=1, source_target_pairs={{0,1},{1,0},{2,3},{3,2},{4,5},{5,4},{6,7},{7,6},{8,9},{9,8},{10,11... | collective-permute-start | bytes 221192 | tf_op jit(solution)/shard_map/ppermute | solution.py:955
  691.7 34.2 %collective-permute-start.85 = (bf16[64,576]{1,0:T(8,128)(2,1)S(1)}, bf16[64,576]{1,0:T(8,128)(2,1)}, u32[]{:S(2)}, u32[]{:S(2)}) collective-permute-start(bf16[64,576]{1,0:T(8,128)(2,1)S(1)} %pad_maximum_fusion.25), channel_id=1, source_target_pairs={{0,4},{4,0},{1,5},{5,1},{2,6},{6,2},{3,7},{7,3},{8,12},{12,8},{9,1... | collective-permute-start | bytes 221192 | tf_op jit(solution)/shard_map/ppermute | solution.py:955
  706.5 27.0 %all-to-all-start.2 = ((f32[16,19,128]{2,1,0:T(8,128)}), f32[16,19,128]{2,1,0:T(8,128)}, u32[]{:S(2)}, u32[]{:S(2)}) async-start(f32[16,19,128]{2,1,0:T(8,128)} %fusion.58), calls=%async_computation.2 | async-start | bytes 393216 | tf_op jit(solution)/shard_map/all_to_all | solution.py:969
  720.7 32.3 %collective-permute-start.90 = (bf16[4,128,512]{1,2,0:T(8,128)(2,1)}, bf16[4,128,512]{1,2,0:T(8,128)(2,1)}, u32[]{:S(2)}, u32[]{:S(2)}) collective-permute-start(bf16[4,128,512]{1,2,0:T(8,128)(2,1)} %bitcast.184), channel_id=1, source_target_pairs={{0,16},{8,24},{16,0},{24,8},{1,17},{9,25},{17,1},{25,9},{2,18},{10... | collective-permute-start | bytes 1572872 | tf_op jit(solution)/shard_map/ppermute | solution.py:965
  720.9 52.7 %collective-permute-start.91 = (bf16[4,128,512]{1,2,0:T(8,128)(2,1)}, bf16[4,128,512]{1,2,0:T(8,128)(2,1)}, u32[]{:S(2)}, u32[]{:S(2)}) collective-permute-start(bf16[4,128,512]{1,2,0:T(8,128)(2,1)} %bitcast.185), channel_id=1, source_target_pairs={{0,24},{8,0},{16,8},{24,16},{1,25},{9,1},{17,9},{25,17},{2,26},{10... | collective-permute-start | bytes 1572872 | tf_op jit(solution)/shard_map/ppermute | solution.py:965
  728.8 47.0 %collective-permute-start.84 = (bf16[4,128,512]{1,2,0:T(8,128)(2,1)}, bf16[4,128,512]{1,2,0:T(8,128)(2,1)}, u32[]{:S(2)}, u32[]{:S(2)}) collective-permute-start(bf16[4,128,512]{1,2,0:T(8,128)(2,1)} %bitcast.171), channel_id=1, source_target_pairs={{0,8},{8,16},{16,24},{24,0},{1,9},{9,17},{17,25},{25,1},{2,10},{10... | collective-permute-start | bytes 1572872 | tf_op jit(solution)/shard_map/ppermute | solution.py:965
  750.9 31.4 %collective-permute-start.94 = (bf16[128,576]{0,1:T(8,128)(2,1)S(1)}, bf16[128,576]{0,1:T(8,128)(2,1)S(1)}, u32[]{:S(2)}, u32[]{:S(2)}) collective-permute-start(bf16[128,576]{0,1:T(8,128)(2,1)S(1)} %bitcast.602), channel_id=1, source_target_pairs={{0,24},{8,0},{16,8},{24,16},{1,25},{9,1},{17,9},{25,17},{2,26},{10... | collective-permute-start | bytes 442376 | tf_op jit(solution)/shard_map/ppermute | solution.py:965
  751.5 30.8 %collective-permute-start.92 = (bf16[128,576]{0,1:T(8,128)(2,1)S(1)}, bf16[128,576]{0,1:T(8,128)(2,1)S(1)}, u32[]{:S(2)}, u32[]{:S(2)}) collective-permute-start(bf16[128,576]{0,1:T(8,128)(2,1)S(1)} %bitcast.601), channel_id=1, source_target_pairs={{0,8},{8,16},{16,24},{24,0},{1,9},{9,17},{17,25},{25,1},{2,10},{10... | collective-permute-start | bytes 442376 | tf_op jit(solution)/shard_map/ppermute | solution.py:965
  753.0 29.4 %collective-permute-start.93 = (bf16[128,576]{0,1:T(8,128)(2,1)S(1)}, bf16[128,576]{0,1:T(8,128)(2,1)S(1)}, u32[]{:S(2)}, u32[]{:S(2)}) collective-permute-start(bf16[128,576]{0,1:T(8,128)(2,1)S(1)} %bitcast.600), channel_id=1, source_target_pairs={{0,16},{8,24},{16,0},{24,8},{1,17},{9,25},{17,1},{25,9},{2,18},{10... | collective-permute-start | bytes 442376 | tf_op jit(solution)/shard_map/ppermute | solution.py:965
  (140 other events, 1550.5 us)

commit v3 on v2

--- a/solution.py
+++ b/solution.py
@@ -684,7 +684,7 @@
 
 def attend_body(
     heads, scale, query, own, other, up, out_weight, spots, key_spots,
-    part_out, prob_out, absorbed_out, latent_out, head_out,
+    kept_out, sent_out, prob_out, absorbed_out, latent_out, head_out,
 ):
     rank = up.shape[0]
     absorbed, ropes = ([], [])
@@ -722,7 +722,9 @@
         axis=1,
     ).astype(jnp.bfloat16)
     head_out[...] = head
-    part_out[...] = mul(head, out_weight[...]).astype(jnp.bfloat16)
+    total = mul(head, out_weight[...]).astype(jnp.bfloat16)
+    kept_out[0] = total[: rows // 2]
+    sent_out[0] = total[rows // 2 :]
 
 
 def attend_kernel(query, own, other, up, out_weight, spots, key_spots, heads, scale, after=()):
@@ -731,7 +733,8 @@
     key_count = 4 * own.shape[2]
     rank = up.shape[0]
     shapes = [
-        shaped((query.shape[0], out_weight.shape[1])),
+        shaped((sequences, rows // 2, out_weight.shape[1])),
+        shaped((sequences, rows // 2, out_weight.shape[1])),
         shaped((sequences, heads * rows, key_count)),
         shaped((sequences, heads * rows, rank)),
         shaped((sequences, heads * rows, rank)),
@@ -742,13 +745,7 @@
         (sequences,),
         [by_rows(query, rows), by_first(own), by_first(other)]
         + [whole(a) for a in (up, out_weight, spots, key_spots)],
-        [
-            by_rows(shapes[0], rows),
-            by_first(shapes[1]),
-            by_first(shapes[2]),
-            by_first(shapes[3]),
-            by_rows(shapes[4], rows),
-        ],
+        [by_first(shape) for shape in shapes[:5]] + [by_rows(shapes[5], rows)],
         shapes,
         (query, own, other, up, out_weight, spots, key_spots),
         after,
@@ -835,35 +832,28 @@
     )
 
 
-def heads_body(z, own, *refs):
-    query_out, up_out, out_out = refs[-3:]
-    count = (len(refs) - 3) // 2 + 1
-    above, below = (refs[: count - 1], refs[count - 1 : 2 * count - 2])
-    groups, rows, _ = own.shape
+def heads_body(parts, *refs):
+    query_out, up_out, out_out = refs
+    count, groups, rows, _ = parts.shape
     query_columns = query_out.shape[1]
     up_blocks = up_out.shape[1] // 128
     up_rows = rows // up_blocks
     heads = out_out.shape[0] // rows
-    for s in range(count):
-        part = own[...] if s == 0 else above[s - 1][...] + below[count - s - 1][...]
-        place = lax.rem(z[0] + s, count)
-        for j in range(groups):
-            block = place * groups + j
-            start = pl.multiple_of(block * rows, rows)
-            query_out[pl.ds(start, rows), :] = part[j, :, :query_columns]
-            for k in range(up_blocks):
-                up_out[
-                    pl.ds(pl.multiple_of(block * up_rows, up_rows), up_rows),
-                    k * 128 : (k + 1) * 128,
-                ] = part[j, k * up_rows : (k + 1) * up_rows, query_columns : query_columns + 128]
-            for k in range(heads):
-                at = query_columns + 128 + k * rows
-                out_out[k * rows : (k + 1) * rows, pl.ds(start, rows)] = part[j, :, at : at + rows]
-
-
-def heads_kernel(z, own, above, below, query_columns, heads, up_columns):
-    count = len(above) + 1
-    groups, rows, _ = own.shape
+    for block in range(count * groups):
+        here = parts[block // groups, block % groups]
+        span = slice(block * rows, (block + 1) * rows)
+        query_out[span, :] = here[:, :query_columns]
+        for k in range(up_blocks):
+            up_out[block * up_rows : (block + 1) * up_rows, k * 128 : (k + 1) * 128] = here[
+                k * up_rows : (k + 1) * up_rows, query_columns : query_columns + 128
+            ]
+        for k in range(heads):
+            at = query_columns + 128 + k * rows
+            out_out[k * rows : (k + 1) * rows, span] = here[:, at : at + rows]
+
+
+def heads_kernel(parts, query_columns, heads, up_columns, after=()):
+    count, groups, rows, _ = parts.shape
     width = count * groups * rows
     up_rows = rows * 128 // up_columns
     shapes = [
@@ -874,60 +864,210 @@
     return local_call(
         heads_body,
         (1,),
-        [pl.BlockSpec(memory_space=pltpu.SMEM)] + [whole(own)] * (2 * count - 1),
+        [whole(parts)],
         [whole(s) for s in shapes],
         shapes,
-        (z, own, *above, *below),
-    )
-
-
-def out_grads_body(rows, head, grads, out):
+        (parts,),
+        after,
+    )
+
+
+SCALAR = pl.BlockSpec(memory_space=pltpu.SMEM)
+
+
+def out_grads_body(rows, z, head, grads, *outs):
     heads = head.shape[1] // rows
-    total = mul_tn(head[...], grads[...]).astype(jnp.bfloat16)
-    for i in range(out.shape[0]):
-        for k in range(heads):
-            out[i, :, k * rows : (k + 1) * rows] = total[
-                k * rows : (k + 1) * rows, i * rows : (i + 1) * rows
-            ]
-
-
-def out_grads_kernel(head, grads, rows):
-    shape = shaped((grads.shape[1] // rows, rows, head.shape[1]))
+    for s, out in enumerate(outs):
+        size = out.shape[0] * rows
+        start = pl.multiple_of(lax.rem(z[0] + s, len(outs)) * size, size)
+        total = mul_tn(head[...], grads[:, pl.ds(start, size)]).astype(jnp.bfloat16)
+        for j in range(out.shape[0]):
+            for k in range(heads):
+                out[j, :, k * rows : (k + 1) * rows] = total[
+                    k * rows : (k + 1) * rows, j * rows : (j + 1) * rows
+                ]
+
+
+def out_grads_kernel(z, count, head, grads, rows):
+    shapes = [shaped((grads.shape[1] // (rows * count), rows, head.shape[1]))] * count
     return local_call(
         partial(out_grads_body, rows),
         (1,),
-        [whole(head), whole(grads)],
-        whole(shape),
-        shape,
-        (head, grads),
-    )
-
-
-def query_grads_body(rows, grads, source, up, out):
+        [SCALAR, whole(head), whole(grads)],
+        [whole(s) for s in shapes],
+        shapes,
+        (z, head, grads),
+    )
+
+
+def query_grads_body(rows, z, grads, source, up, *outs):
     columns = grads.shape[1]
     up_blocks = up.shape[1] // 128
     up_rows = rows // up_blocks
     here = grads[...]
-    for i in range(out.shape[0]):
-        out[i, :, :columns] = mul_tn(source[:, i * rows : (i + 1) * rows], here).astype(
-            jnp.bfloat16
-        )
-        for k in range(up_blocks):
-            out[i, k * up_rows : (k + 1) * up_rows, columns:] = up[
-                i * up_rows : (i + 1) * up_rows, k * 128 : (k + 1) * 128
-            ].astype(jnp.bfloat16)
-
-
-def query_grads_kernel(grads, source, up, rows, after=()):
-    shape = shaped((source.shape[1] // rows, rows, grads.shape[1] + 128))
+    for s, out in enumerate(outs):
+        groups = out.shape[0]
+        place = lax.rem(z[0] + s, len(outs))
+        start = pl.multiple_of(place * groups * rows, groups * rows)
+        total = mul_tn(source[:, pl.ds(start, groups * rows)], here).astype(jnp.bfloat16)
+        start = pl.multiple_of(place * groups * up_rows, groups * up_rows)
+        more = up[pl.ds(start, groups * up_rows), :].astype(jnp.bfloat16)
+        for j in range(groups):
+            out[j, :, :columns] = total[j * rows : (j + 1) * rows]
+            for k in range(up_blocks):
+                out[j, k * up_rows : (k + 1) * up_rows, columns:] = more[
+                    j * up_rows : (j + 1) * up_rows, k * 128 : (k + 1) * 128
+                ]
+
+
+def query_grads_kernel(z, count, grads, source, up, rows, after=()):
+    shapes = [shaped((source.shape[1] // (rows * count), rows, grads.shape[1] + 128))] * count
     return local_call(
         partial(query_grads_body, rows),
         (1,),
-        [whole(grads), whole(source), whole(up)],
-        whole(shape),
-        shape,
-        (grads, source, up),
+        [SCALAR, whole(grads), whole(source), whole(up)],
+        [whole(s) for s in shapes],
+        shapes,
+        (z, grads, source, up),
         after,
+    )
+
+
+def latent_grads_body(z, place, source, grads, *outs):
+    rows = outs[0].shape[0]
+    here = grads[...]
+    for s, out in enumerate(outs):
+        block = 4 * lax.rem(z[0] + s, len(outs)) + place[0]
+        start = pl.multiple_of(block * rows, rows)
+        out[...] = mul_tn(source[:, pl.ds(start, rows)], here).astype(jnp.bfloat16)
+
+
+def latent_grads_kernel(z, place, count, source, grads, rows):
+    shapes = [shaped((rows, grads.shape[1]))] * count
+    return local_call(
+        latent_grads_body,
+        (1,),
+        [SCALAR, SCALAR, whole(source), whole(grads)],
+        [whole(s) for s in shapes],
+        shapes,
+        (z, place, source, grads),
+    )
+
+
+def split_product_body(left, right, kept_out, sent_out):
+    total = mul_nt(left[...], right[...]).astype(jnp.bfloat16)
+    half = total.shape[0] // 2
+    kept_out[0] = total[:half]
+    sent_out[0] = total[half:]
+
+
+def split_product_kernel(left, right, sequences):
+    rows = left.shape[0] // sequences
+    shapes = [shaped((sequences, rows // 2, right.shape[0]))] * 2
+    return local_call(
+        split_product_body,
+        (sequences,),
+        [by_rows(left, rows), whole(right)],
+        [by_first(s) for s in shapes],
+        shapes,
+        (left, right),
+    )
+
+
+def core_fold_body(*refs):
+    for k in range(4):
+        total = refs[k][0, 0].astype(jnp.float32) + refs[4 + k][0, 0].astype(jnp.float32)
+        refs[8 + k][0] = total.astype(jnp.bfloat16)
+
+
+def core_fold_kernel(own, received, after=()):
+    half, width = (own.shape[2] // 2, own.shape[3])
+    block = (1, 1, half, width)
+    specs = [
+        pl.BlockSpec(block, lambda k: (0, k, 0, 0)),
+        pl.BlockSpec(block, lambda k: (1, k, 0, 0)),
+        pl.BlockSpec(block, lambda k: (k, 0, 1, 0)),
+        pl.BlockSpec(block, lambda k: (k, 1, 1, 0)),
+    ]
+    shapes = [shaped((2, half, width))] * 4
+    return local_call(
+        core_fold_body,
+        (2,),
+        specs + specs,
+        [by_first(s) for s in shapes],
+        shapes,
+        (own,) * 4 + (received,) * 4,
+        after,
+    )
+
+
+def plane_fold_body(lower, lower_got, upper, upper_got, *outs):
+    for k, (left, right) in enumerate(((lower, lower_got), (upper, upper_got))):
+        for j in range(2):
+            total = left[j].astype(jnp.float32) + right[j].astype(jnp.float32)
+            outs[2 * k + j][...] = total.astype(jnp.bfloat16)
+
+
+def plane_fold_kernel(lower, lower_got, upper, upper_got, after=()):
+    _, rows, width = lower.shape
+    tile = max(16, rows // 2)
+    spec = pl.BlockSpec((2, tile, width), lambda i: (0, i, 0))
+    shapes = [shaped((rows, width))] * 4
+    return local_call(
+        plane_fold_body,
+        (rows // tile,),
+        [spec] * 4,
+        [by_rows(s, tile) for s in shapes],
+        shapes,
+        (lower, lower_got, upper, upper_got),
+        after,
+    )
+
+
+def slab_fold_body(lower, lower_got, upper, upper_got, own_out, *outs):
+    half = lower.shape[0]
+    count = len(outs) + 1
+    block = 2 * half // count
+    for k, (left, right) in enumerate(((lower, lower_got), (upper, upper_got))):
+        total = left[...].astype(jnp.float32) + right[...].astype(jnp.float32)
+        if count == 1:
+            own_out[k * half : (k + 1) * half, :] = total
+            continue
+        for j in range(half // block):
+            here = total[j * block : (j + 1) * block]
+            s = k * (half // block) + j
+            if s == 0:
+                own_out[...] = here
+            else:
+                outs[s - 1][...] = here.astype(jnp.bfloat16)
+
+
+def slab_fold_kernel(lower, lower_got, upper, upper_got, count, after=()):
+    half, width = lower.shape
+    block = 2 * half // count
+    shapes = [shaped((block, width), jnp.float32)] + [shaped((block, width))] * (count - 1)
+    return local_call(
+        slab_fold_body,
+        (1,),
+        [whole(lower)] * 4,
+        [whole(s) for s in shapes],
+        shapes,
+        (lower, lower_got, upper, upper_got),
+        after,
+    )
+
+
+def z_fold_body(*refs):
+    total = refs[0][...].astype(jnp.float32)
+    for ref in refs[1:-1]:
+        total = total + ref[...].astype(jnp.float32)
+    refs[-1][...] = total.astype(refs[-1].dtype)
+
+
+def z_fold_kernel(parts, dtype, after=()):
+    shape = shaped(parts[0].shape, dtype)
+    return local_call(
+        z_fold_body, (1,), [whole(p) for p in parts], whole(shape), shape, tuple(parts), after
     )
 
 
@@ -948,6 +1088,21 @@
     )
 
 
+def join_body(*refs):
+    out = refs[-1]
+    rows = refs[0].shape[0]
+    for s, ref in enumerate(refs[:-1]):
+        out[s * rows : (s + 1) * rows, :] = ref[...]
+
+
+def join_kernel(parts, after=()):
+    rows, width = parts[0].shape
+    shape = shaped((len(parts) * rows, width), parts[0].dtype)
+    return local_call(
+        join_body, (1,), [whole(p) for p in parts], whole(shape), shape, tuple(parts), after
+    )
+
+
 CTX = ("z", "x", "c")
 
 
@@ -1018,17 +1173,6 @@
 
 def z_parts(value):
     return [value] + [from_z(value, s) for s in range(1, lax.axis_size("z"))]
-
-
-def chain_z(value):
-    count = lax.axis_size("z")
-    above, below = ([value], [value])
-    for r in range(1, count):
-        down = [(i + 1, i) for i in range(count - r)]
-        up = [(i, i + 1) for i in range(r - 1, count - 1)]
-        above.append(lax.ppermute(above[-1], "z", down))
-        below.append(lax.ppermute(below[-1], "z", up))
-    return (above[1:], below[1:])
 
 
 def put_z(parts):
@@ -1045,49 +1189,27 @@
     return jnp.stack([jnp.stack([rows, over_b]), jnp.stack([over_a, both])])
 
 
-def plane_first(rows, axes=("x", "y"), gates=()):
-    half = rows.shape[2] // 2
-    lower, upper = (rows[:, :, :half], rows[:, :, half:])
-    lower = low(add(lower[0], tie(swap(lower[1], axes[0]), *gates)))
-    upper = low(add(upper[:, 0], tie(swap(upper[:, 1], axes[1]), *gates)))
-    return (lower, upper)
-
-
-def plane_second(lower, upper, axes=("x", "y"), gates=()):
-    lower = add(lower[0], tie(swap(lower[1], axes[1]), *gates))
-    upper = add(upper[0], tie(swap(upper[1], axes[0]), *gates))
-    return jnp.concatenate([lower, upper], axis=0)
-
-
-def scatter_plane(rows, axes=("x", "y")):
-    return plane_second(*plane_first(rows, axes), axes)
+def fold_first(pieces, axes, after=()):
+    lower, lower_sent, upper, upper_sent = pieces
+    return plane_fold_kernel(
+        lower, swap(lower_sent, axes[0]), upper, swap(upper_sent, axes[1]), after
+    )
+
+
+def fold_second(pieces, axes, count, after=()):
+    lower, lower_sent, upper, upper_sent = pieces
+    return slab_fold_kernel(
+        lower, swap(lower_sent, axes[1]), upper, swap(upper_sent, axes[0]), count, after
+    )
+
+
+def fold_z(parts, dtype=jnp.float32, after=()):
+    received = [to_z(part, s + 1) for s, part in enumerate(parts[1:])]
+    return z_fold_kernel([parts[0]] + received, dtype, after)
 
 
 def spread_z(rows):
     return jnp.concatenate(z_parts(rows), axis=0)
-
-
-def fold_z(slabs, gates=()):
-    count = lax.axis_size("z")
-    block = slabs.shape[0] // count
-    sent = low(slabs)
-    total = slabs[:block]
-    for s in range(1, count):
-        part = tie(to_z(sent[s * block : (s + 1) * block], s), *gates)
-        total = total + part.astype(jnp.float32)
-    return total
-
-
-def sum_z(value, gates=()):
-    count = lax.axis_size("z")
-    z = lax.axis_index("z")
-    parts = [
-        lax.dynamic_index_in_dim(value, (z + s) % count, 0, keepdims=False) for s in range(count)
-    ]
-    total = parts[0].astype(jnp.float32)
-    for s in range(1, count):
-        total = total + tie(to_z(parts[s], s), *gates).astype(jnp.float32)
-    return total
 
 
 def both_halves(rows):
@@ -1175,23 +1297,52 @@
         axis=2,
     )
     by_heads = jnp.transpose(by_heads, (1, 0, 2))
-    by_heads = trade(jnp.concatenate([by_heads, up_part, out_part], axis=2), ("x", "c"))
+    by_heads = jnp.concatenate([by_heads, up_part, out_part], axis=2)
+    mine_at = 2 * x + c
+    for_group = [
+        lax.dynamic_index_in_dim(by_heads, mine_at ^ k, 0, keepdims=False) for k in range(4)
+    ]
+    by_heads = put(
+        [
+            for_group[0],
+            swap(for_group[1], "c"),
+            swap(for_group[2], "x"),
+            lax.ppermute(for_group[3], ("x", "c"), [(k, 3 - k) for k in range(4)]),
+        ],
+        [mine_at ^ k for k in range(4)],
+    )
     mine = by_own(tokens, "y", 0)
     line = jnp.stack([mine, swap(mine, "x")], axis=1)
     line = jnp.stack([line, swap(line, "c")], axis=1)
     source = line.reshape(sequences * slab, width).astype(jnp.float32)
     grad_mine = by_own(cotangent, "y", 0)[0]
-    grad_parts = z_parts(tie(grad_mine, small))
-    grads_own = gather_plane(jnp.concatenate(grad_parts))
-    grads_other = swap(grads_own, "c").reshape(-1, width)
-    grads_own = grads_own.reshape(-1, width)
+    grad_parts = z_parts(grad_mine)
     gate_t, up_t, down = (expert_gate[0].T, expert_up[0].T, expert_down[0])
-    back_own = product_nt_kernel(grads_own, down)
-    back_other = product_nt_kernel(grads_other, down)
-    by_heads = tie(by_heads, grad_parts[-1])
-    above, below = chain_z(by_heads)
+    shared_mine = jnp.concatenate(
+        [
+            shared_gate.T.reshape(count, shared_here, rows_here),
+            shared_up.T.reshape(count, shared_here, rows_here),
+            shared_down.reshape(count, shared_here, rows_here),
+        ],
+        axis=1,
+    )
+    shared_rows = trade(shared_mine, CTX)
+    shared_rows = jnp.transpose(shared_rows, (1, 0, 2)).reshape(3, shared_here, width)
+    shared_rows = jnp.pad(shared_rows, ((0, 0), (0, part - shared_here), (0, 0)))
+    small_t = jnp.concatenate(
+        [
+            shared_rows[0],
+            shared_rows[1],
+            jnp.pad(full_router.T, ((0, part - experts), (0, 0))),
+        ]
+    )
+    shared_down_t = shared_rows[2]
+
     query_here, up_here, out_here = heads_kernel(
-        z[None], by_heads, above, below, query_columns, heads, up_columns
+        lax.all_gather(by_heads, "z", axis=0),
+        query_columns,
+        heads,
+        up_columns,
     )
 
     def places(turns):
@@ -1231,41 +1382,24 @@
     )
     plane = gather_plane(spread_z(key_own), ("y", "x"))
     keys_own, keys_other = (plane, swap(plane, "c"))
+    grads_own = gather_plane(jnp.concatenate(grad_parts), gates=(plane,))
+    grads_other = swap(grads_own, "c").reshape(-1, width)
+    grads_own = grads_own.reshape(-1, width)
     query = dot(input_low, query_here)
     rope = query[:, heads * DN :].reshape(sequences, slab, heads, DR)
     rope = rotate(rope, cosine[:, None, :], sine[:, None, :]).reshape(sequences * slab, -1)
     query_low = low(jnp.concatenate([query[:, : heads * DN], rope], axis=1))
 
-    shared_mine = jnp.concatenate(
-        [
-            shared_gate.T.reshape(count, shared_here, rows_here),
-            shared_up.T.reshape(count, shared_here, rows_here),
-            shared_down.reshape(count, shared_here, rows_here),
-        ],
-        axis=1,
-    )
-    shared_rows = trade(tie(shared_mine, query_low), CTX)
-    shared_rows = jnp.transpose(shared_rows, (1, 0, 2)).reshape(3, shared_here, width)
-    shared_rows = jnp.pad(shared_rows, ((0, 0), (0, part - shared_here), (0, 0)))
-    small_t = jnp.concatenate(
-        [
-            shared_rows[0],
-            shared_rows[1],
-            jnp.pad(full_router.T, ((0, part - experts), (0, 0))),
-        ]
-    )
-    shared_down_t = shared_rows[2]
-
-    def scatter_slab(partial):
-        parts = partial.reshape(2, 2, 2, block, -1)
-        kept = low(add(parts[:, 0], swap(parts[:, 1], "c")))
-        return scatter_plane(kept, ("y", "x"))
-
-    def gather_slab(rows, gates=()):
-        plane = gather_plane(rows, ("y", "x"), gates)
+    def scatter_slab(kept, sent):
+        shape = (2, 2, block, width)
+        pieces = core_fold_kernel(kept.reshape(shape), swap(sent, "c").reshape(shape))
+        return fold_second(fold_first(pieces, ("y", "x")), ("y", "x"), 1)[0]
+
+    def gather_slab(rows):
+        plane = gather_plane(rows, ("y", "x"))
         return jnp.stack([plane, swap(plane, "c")], axis=1).reshape(sequences * slab, -1)
 
-    attention, prob, absorbed, latent_out, head_out = attend_kernel(
+    kept, sent, prob, absorbed, latent_out, head_out = attend_kernel(
         query_low,
         keys_own,
         keys_other,
@@ -1275,15 +1409,20 @@
         key_positions[None, :],
         heads,
         scale,
-        (back_own, back_other) + down_pieces[1:],
-    )
-    attention = scatter_slab(attention)
+        down_pieces[1:],
+    )
+    attention = scatter_slab(kept, sent)
     hidden_in = mine[0].astype(jnp.float32) + attention
     normed_ffn, unit_ffn, inverse_ffn = root_norm(hidden_in, full_norm_ffn)
     ffn_low = low(normed_ffn)
     shares = jax.nn.softmax(dot(ffn_low, full_router), axis=-1)
-    ffn_slabs = spread_z(ffn_low)
-    ffn_own = gather_plane(ffn_slabs, gates=(small_t,))
+    ffn_parts = z_parts(ffn_low)
+    back_own = product_nt_kernel(grads_own, down, (ffn_low,))
+    back_other = product_nt_kernel(grads_other, down, (back_own,))
+    shared_own = product_nt_kernel(grads_own, shared_down_t, (back_other,))
+    shared_other = product_nt_kernel(grads_other, shared_down_t, (shared_own,))
+    ffn_slabs = join_kernel(ffn_parts, (shared_other,))
+    ffn_own = gather_plane(ffn_slabs)
     ffn_other = swap(ffn_own, "c").reshape(-1, width)
     ffn_own = ffn_own.reshape(-1, width)
 
@@ -1294,33 +1433,48 @@
     routed = jnp.transpose(routed, (2, 1, 3, 0, 4)).reshape(2, -1, 1).astype(jnp.float32)
     pick = (jnp.arange(part)[None, :] == me).astype(jnp.float32)
 
-    def feed(rows, grads, back, named):
-        shared_back = product_nt_kernel(grads, shared_down_t)
+    def feed(rows, back, shared_back, named):
         return feed_kernel(rows, back, shared_back, gate_t, up_t, small_t, named, pick, experts)
 
     act_own, more_own, gate_own, up_own, pre_own, gain_own = feed(
-        ffn_own, grads_own, back_own, routed[0]
+        ffn_own, back_own, shared_own, routed[0]
     )
     act_other, more_other, gate_other, up_other, pre_other, gain_other = feed(
-        ffn_other, grads_other, back_other, routed[1]
-    )
-    shape = (2, 2, zs * block, -1)
+        ffn_other, back_other, shared_other, routed[1]
+    )
+    shape = (2, 2, zs * block, width + part)
     grad_other = input_kernel(
         gate_other, up_other, pre_other, gate_t, up_t, small_t, gain_other, pick
     )
     grad_own = input_kernel(
         gate_own, up_own, pre_own, gate_t, up_t, small_t, gain_own, pick, (grad_other,)
     )
-    grad_own = low(add(grad_own, swap(grad_other, "c"))).reshape(shape)
-    sum_other = result_kernel(act_other, more_other, down, shared_down_t, (grad_own,))
+    pieces = core_fold_kernel(grad_own.reshape(shape), swap(grad_other, "c").reshape(shape))
+    both_axes = ("x", "y")
+    sum_other = result_kernel(act_other, more_other, down, shared_down_t, pieces)
     sum_own = result_kernel(act_own, more_own, down, shared_down_t, (sum_other,))
-    lower, upper = plane_first(grad_own, gates=(sum_own,))
-    routed_own = low(add(tie(sum_own, lower), swap(sum_other, "c"))).reshape(shape)
-    grad_slab = plane_second(lower, upper, gates=(routed_own,))
+    grad_expert_up, shared_up_back = weight_kernel(
+        (up_own, up_other), (pre_own, pre_other), (ffn_own, ffn_other), 1, part, (sum_own,)
+    )
+    pieces = fold_first(pieces, both_axes, (grad_expert_up,))
+    shape = (2, 2, zs * block, width)
     grad_expert_down, shared_down_back = weight_kernel(
-        (act_own, act_other), (more_own, more_other), (grads_own, grads_other), 0, part, (grad_slab,)
-    )
-    ffn_grad = fold_z(grad_slab, (grad_expert_down,))
+        (act_own, act_other), (more_own, more_other), (grads_own, grads_other), 0, part, pieces
+    )
+    grad_slab = fold_second(pieces, both_axes, zs, (grad_expert_down,))
+    routed_pieces = core_fold_kernel(
+        sum_own.reshape(shape), swap(sum_other, "c").reshape(shape), grad_slab
+    )
+    grad_expert_gate, shared_gate_back = weight_kernel(
+        (gate_own, gate_other),
+        (pre_own, pre_other),
+        (ffn_own, ffn_other),
+        0,
+        part,
+        tuple(routed_pieces),
+    )
+    routed_pieces = fold_first(routed_pieces, both_axes, (grad_expert_gate,))
+    ffn_grad = fold_z(grad_slab, jnp.float32, routed_pieces)
     share_grad = ffn_grad[:, width : width + experts]
     ffn_grad = ffn_grad[:, :width]
     logit_grad = shares * (share_grad - jnp.sum(shares * share_grad, axis=-1, keepdims=True))
@@ -1330,19 +1484,7 @@
     grad_hidden = grad_mine.astype(jnp.float32) + hidden_part
 
     hidden_low = low(grad_hidden)
-    grad_expert_gate, shared_gate_back = weight_kernel(
-        (gate_own, gate_other), (pre_own, pre_other), (ffn_own, ffn_other), 0, part, (hidden_low,)
-    )
-    grad_expert_up, shared_up_back = weight_kernel(
-        (up_own, up_other),
-        (pre_own, pre_other),
-        (ffn_own, ffn_other),
-        1,
-        part,
-        (grad_expert_gate,),
-    )
-    lower, upper = plane_first(tie(routed_own, grad_slab), gates=(grad_expert_gate,))
-    attention_grad = gather_slab(hidden_low, (grad_expert_gate,))
+    attention_grad = gather_slab(hidden_low)
     shared_back = jnp.concatenate(
         [
             shared_gate_back[:shared_here],
@@ -1352,12 +1494,10 @@
     )
     shared_back = trade(
         jnp.transpose(shared_back.reshape(-1, count, rows_here), (1, 0, 2)), CTX
-    ).astype(jnp.float32)
-    grad_shared_gate = shared_back[:, :shared_here].reshape(-1, rows_here).T
-    grad_shared_up = shared_back[:, shared_here : 2 * shared_here].reshape(-1, rows_here).T
-    grad_shared_down = shared_back[:, 2 * shared_here :].reshape(-1, rows_here)
-
-    grad_out_here = out_grads_kernel(head_out, attention_grad, rows_here)
+    )
+    zero = jnp.zeros((1,), jnp.int32)
+    (out_grads,) = out_grads_kernel(zero, 1, head_out, attention_grad, rows_here)
+    grad_out = lax.psum_scatter(out_grads, "z", scatter_dimension=0, tiled=True)
     key_own, key_other, query_grad, grad_up_here = attend_back_kernel(
         attention_grad,
         query_low,
@@ -1370,23 +1510,39 @@
         latent_out,
         heads,
         scale,
-        (lower, upper, grad_out_here, grad_expert_up),
-    )
-    routed_slab = plane_second(lower, upper, gates=(key_own,))
-    key_sum = low(add(key_own, swap(key_other, "c")))
-    key_sum = fold_z(scatter_plane(key_sum, ("y", "x")))
+        (out_grads,),
+    )
+    shape = (2, 2, zs * block, R + DR)
+    routed_slab = fold_second(routed_pieces, both_axes, zs, (key_own,))
+    key_pieces = core_fold_kernel(key_own, swap(key_other, "c"), routed_slab)
+    key_slab = fold_second(fold_first(key_pieces, ("y", "x")), ("y", "x"), zs)
+    key_sum = fold_z(key_slab)
     rope = query_grad[:, heads * DN :].reshape(sequences, slab, heads, DR)
     rope = rotate(rope, cosine[:, None, :], -sine[:, None, :]).reshape(sequences * slab, -1)
     query_raw_grad = low(jnp.concatenate([query_grad[:, : heads * DN], rope], axis=1))
-    input_grad = scatter_slab(product_nt_kernel(query_raw_grad, query_here))
-    grad_heads = query_grads_kernel(query_raw_grad, input_low, grad_up_here, rows_here)
-    output = both_halves(low(hidden_in + fold_z(routed_slab, (grad_heads,))))
+    input_grad = scatter_slab(*split_product_kernel(query_raw_grad, query_here, sequences))
+    (query_grads,) = query_grads_kernel(
+        zero, 1, query_raw_grad, input_low, grad_up_here, rows_here
+    )
+    grad_heads = lax.psum_scatter(query_grads, "z", scatter_dimension=0, tiled=True)
+    output = both_halves(low(hidden_in + fold_z(routed_slab, jnp.float32, (key_sum,))))
+    shared_back = tie(shared_back, key_sum).astype(jnp.float32)
+    grad_shared_gate = shared_back[:, :shared_here].reshape(-1, rows_here).T
+    grad_shared_up = shared_back[:, shared_here : 2 * shared_here].reshape(-1, rows_here).T
+    grad_shared_down = shared_back[:, 2 * shared_here :].reshape(-1, rows_here)
+
 
     latent_back, grad_latent_norm = root_norm_back(
         key_sum[:, :R], latent_unit, latent_inverse, full_latent_norm
     )
     rope_key = rotate(key_sum[:, R:], cosine[:block], -sine[:block])
     latent_raw_grad = low(jnp.concatenate([latent_back, rope_key], axis=-1))
+    slab_latent_grad = gather_slab(latent_raw_grad)
+    down_grads = latent_grads_kernel(
+        z[None], (2 * x + c)[None], zs, input_low, slab_latent_grad, rows_here
+    )
+    grad_down = fold_z(down_grads)
+    latent_raw_grad = tie(latent_raw_grad, down_grads[0])
     latent_input = jnp.stack([dot_nt(latent_raw_grad, down) for down in down_pieces])
     latent_input = latent_input.reshape(2, 2, block, zs, rows_here)
     latent_input = by_own(by_own(latent_input, "c", 0), "x", 1)
@@ -1396,22 +1552,11 @@
     )
     tokens_gradient = both_halves(low(grad_hidden + source_part)).astype(jnp.float32)
 
-    slab_latent_grad = gather_slab(latent_raw_grad)
-    grad_down = low(dot_tn(input_low, slab_latent_grad)).reshape(zs, 4, rows_here, R + DR)
-    grad_down = sum_z(
-        lax.dynamic_index_in_dim(grad_down, x * 2 + c, 1, keepdims=False)
-    )
-
-    grad_out = trade(
-        low(sum_z(grad_out_here.reshape(zs, 4, rows_here, -1), (key_own,))), ("x", "c")
-    )
+    both = trade(jnp.concatenate([grad_heads, grad_out], axis=2), ("x", "c")).astype(jnp.float32)
+    out_at = both.shape[2] - head_rows
     grad_output = jnp.transpose(
-        grad_out.reshape(4, DV, heads, rows_here), (0, 2, 1, 3)
-    ).reshape(-1, rows_here).astype(jnp.float32)
-    grad_heads = sum_z(
-        tie(grad_heads, key_sum).reshape(zs, 4, rows_here, -1), (slab_latent_grad,)
-    )
-    both = trade(low(grad_heads), ("x", "c")).astype(jnp.float32)
+        both[..., out_at:].reshape(4, DV, heads, rows_here), (0, 2, 1, 3)
+    ).reshape(-1, rows_here)
     grad_query = jnp.transpose(both[..., :query_columns], (1, 0, 2))
     grad_query = jnp.concatenate(
         [
@@ -1421,7 +1566,7 @@
         axis=-1,
     ).reshape(rows_here, -1)
     grad_latent_up = jnp.transpose(
-        both[..., query_columns:].reshape(4, up_columns // 128, rank_rows, 128), (2, 0, 1, 3)
+        both[..., query_columns:out_at].reshape(4, up_columns // 128, rank_rows, 128), (2, 0, 1, 3)
     ).reshape(rank_rows, -1)
 
     small_grads = jnp.concatenate(

time: 807 us -> 742 us (0.919)
  Pallas kernels: 181 us -> 236 us
  other arithmetic: 110 us -> 69 us
  starting transfers between devices: 145 us -> 114 us
  waiting for transfers between devices: 211 us -> 182 us
  local copies, waits for them, and re-layouts: 120 us -> 101 us
    pallas_call x19 -> x40, Pallas kernels: 181 us -> 236 us  [local_call(): pl.pallas_call(run, grid=grid, in_specs=list(in_specs) + [pl.BlockSpec(me...]
    ppermute x12, waiting for transfers between devices: 48.9 us -> 13.5 us  [from_z(): lax.ppermute(value, 'z', [((i + steps) % count, i) for i in range(count)])]
    convert_element_type x19 -> x5, other arithmetic: 36.9 us -> 6.43 us  [low(): return value.astype(jnp.bfloat16)]
    ppermute x62 -> x64, waiting for transfers between devices: 100 us -> 125 us  [swap(): return lax.ppermute(value, axis, [(0, 1), (1, 0)])]
    ppermute x18 -> x12, waiting for transfers between devices: 52.2 us -> 33.4 us  [to_z(): lax.ppermute(value, 'z', [(i, (i + steps) % count) for i in range(count)])]
    ppermute x6 -> x1, starting transfers between devices: 16.8 us -> 0.01 us  [dense_shards(): lax.ppermute(for_group[3], ('x', 'c'), [(k, 3 - k) for k in range(4)])]
    squeeze x23 -> x2, local copies, waits for them, and re-layouts: 18.5 us -> 1.8 us  [the longest x1 0.97 us: dense_shards(): shared_rows[0]]
    slice x14 -> x3, local copies, waits for them, and re-layouts: 12.2 us -> 2.9 us  [tie(): other[(0,) * other.ndim].astype(jnp.float32)]
  transfers between devices with their start and end apart: 104 -> 96, of which waited for: 45 -> 41; matrix products, arithmetic and copies ran while one was open for 26% -> 19% of each run, Pallas kernels for 16% -> 23%
where the time goes in v3:
time: 742 us; the launch traced here: 729 us
  Pallas kernels  236 us (32%)
  waiting for transfers between devices  182 us (25%)
  starting transfers between devices  114 us (15%)
  local copies, waits for them, and re-layouts  101 us (14%)
  other arithmetic  69 us (9%)
  between operations  18 us (2%)
  matrix products  10.3 us (1%)
    pallas_call x40, Pallas kernels, local_call(): pl.pallas_call(run, grid=grid, in_specs=list(in_specs) + [pl.BlockSpec(me...  236 us
    ppermute x64, waiting for transfers between devices, swap(): return lax.ppermute(value, axis, [(0, 1), (1, 0)])  125 us
    ppermute x64, starting transfers between devices, swap(): return lax.ppermute(value, axis, [(0, 1), (1, 0)])  50.9 us
    ppermute x12, waiting for transfers between devices, to_z(): lax.ppermute(value, 'z', [(i, (i + steps) % count) for i in range(count)])  33.4 us
    unnamed x196, local copies, waits for them, and re-layouts  25.1 us
    ppermute x12, starting transfers between devices, to_z(): lax.ppermute(value, 'z', [(i, (i + steps) % count) for i in range(count)])  21.5 us
    all_to_all x4, starting transfers between devices, trade(): return lax.all_to_all(value, axes, split_axis=0, concat_axis=0, tiled=True)  21.1 us
    ppermute x12, starting transfers between devices, from_z(): lax.ppermute(value, 'z', [((i + steps) % count, i) for i in range(count)])  19.8 us
  transfers between devices with their start and end apart: 96, of which 41 were waited for; matrix products, arithmetic and copies ran while one was open for 19% of the time, Pallas kernels for 23%

profile of v3, /device:TPU:16, one launch (start us, length us, event | category | flops | bytes accessed | tf_op | source)
XLA Modules:
  0.0 728.9 jit_solution(2918249957372256886)
XLA Ops:
  22.5 6.4 all-to-all-start
  37.7 8.8 %collective-permute-done.2 = bf16[128,640]{1,0:T(8,128)(2,1)} collective-permute-done((bf16[128,640]{1,0:T(8,128)(2,1)}, bf16[128,640]{1,0:T(8,128)(2,1)}, u32[]{:S(2)}, u32[]{:S(2)}) %collective-permute-start.2) | collective-permute-done | bytes 163872 | tf_op jit(solution)/shard_map/ppermute | solution.py:1115
  46.5 6.5 collective-permute-start.31
  58.0 5.4 collective-permute-done
  68.3 4.7 collective-permute-done.5
  92.1 6.4 collective-permute-done.20
  125.5 18.6 %collective-permute-done.15 = bf16[256,576]{1,0:T(8,128)(2,1)} collective-permute-done((bf16[256,576]{1,0:T(8,128)(2,1)}, bf16[256,576]{1,0:T(8,128)(2,1)}, u32[]{:S(2)}, u32[]{:S(2)}) %collective-permute-start.15) | collective-permute-done | bytes 294944 | tf_op jit(solution)/shard_map/ppermute | solution.py:1110
  179.1 3.1 copy.295.refs_2_.refs_3_
  182.2 3.8 shard_map.288
  190.5 8.8 %shard_map.289 = (bf16[2,128,2048]{2,1,0:T(8,128)(2,1)}, bf16[2,128,2048]{2,1,0:T(8,128)(2,1)}, bf16[2,512,1024]{2,1,0:T(8,128)(2,1)}, bf16[2,512,512]{2,1,0:T(8...) custom-call(bf16[512,384]{1,0:T(8,128)(2,1)} %pad_maximum_fusion.17.refs_0_.refs_1_, ...), custom_call_target="tpu_custom_call" | custom-call | flops 1 | bytes 1 | tf_op jit(solution)/shard_map/pallas_call | solution.py:503
  207.6 7.1 collective-permute-done.24.refs_1_
  234.6 7.4 %shard_map.293.refs_2_.refs_1_ = bf16[1024,704]{1,0:T(8,128)(2,1)} custom-call(bf16[1024,2048]{1,0:T(8,128)(2,1)} %bitcast.68.refs_0_.refs_4_, bf16[704,2048]{1,0:T(8,128)(2,1)} %bitcast.308, bf16[64,2048]{1,0:T(8,128)(2,1)} %copy-done.7), custom_call_target="tpu_custom_call" | custom-call | flops 1 | bytes 1 | tf_op jit(solution)/shard_map/pallas_call | solution.py:503
  242.0 7.4 %shard_map.294.refs_2_.refs_1_ = bf16[1024,704]{1,0:T(8,128)(2,1)} custom-call(bf16[1024,2048]{1,0:T(8,128)(2,1)} %bitcast.60.refs_0_.refs_5_, bf16[704,2048]{1,0:T(8,128)(2,1)} %bitcast.309, bf16[1024,704]{1,0:T(8,128)(2,1)} %shard_map.293.refs_2_.refs_1_), custom_call_target="tpu_custom_call" | custom-call | flops 1 | bytes 1 | tf_op jit(solution)/shard_map/pallas_call | solution.py:503
  249.4 4.8 shard_map.295.refs_2_
  254.2 4.8 shard_map.296.refs_4_.refs_2_
  264.9 20.4 %collective-permute-done.40 = bf16[256,2048]{1,0:T(8,128)(2,1)S(1)} collective-permute-done((bf16[256,2048]{1,0:T(8,128)(2,1)}, bf16[256,2048]{1,0:T(8,128)(2,1)S(1)}, u32[]{:S(2)}, u32[]{:S(2)}) %collective-permute-start.40) | collective-permute-done | bytes 1048608 | tf_op jit(solution)/shard_map/ppermute | solution.py:1110
  288.8 8.6 %collective-permute-done.42 = bf16[128,2048]{1,0:T(8,128)(2,1)S(1)} collective-permute-done((bf16[128,2048]{1,0:T(8,128)(2,1)S(1)}, bf16[128,2048]{1,0:T(8,128)(2,1)S(1)}, u32[]{:S(2)}, u32[]{:S(2)}) %collective-permute-start.42) | collective-permute-done | bytes 524320 | tf_op jit(solution)/shard_map/ppermute | solution.py:1110
  304.0 3.5 collective-permute-done.43
  307.6 16.1 %shard_map.299 = (bf16[1024,704]{1,0:T(8,128)(2,1)}, bf16[1024,128]{1,0:T(8,128)(2,1)}, bf16[1024,704]{1,0:T(8,128)(2,1)}, bf16[1024,704]{1,0:T(8,128)(2,1)}, bf...) custom-call(bf16[1024,2048]{1,0:T(8,128)(2,1)} %bitcast.85.refs_0_.refs_5_, bf16[1024,704]{1,0:T(8,128)(2,1)} %shard_map.294.refs_2_.refs_1_, ...), custom_call_target="tpu_custom_call" | custom-call | flops 1 | bytes 1 | tf_op jit(solution)/shard_map/pallas_call | solution.py:503
  323.7 12.9 %shard_map.300.refs_8_ = bf16[1024,2176]{1,0:T(8,128)(2,1)} custom-call(bf16[1024,704]{1,0:T(8,128)(2,1)} %get-tuple-element.126.refs_0_.refs_1_, bf16[1024,704]{1,0:T(8,128)(2,1)} %get-tuple-element.127.refs_1_, bf16[1024,256]{1,0:T(8,128)(2,1)} %get-tuple-element.128.refs_2_.refs_3_, bf16[704,2048]{1,0:T(8,128)(2,1)} %bitcast.301, ...), custom_call_target="tpu_custom_call" | custom-call | flops 1 | bytes 1 | tf_op jit(solution)/shard_map/pallas_call | solution.py:503
  338.1 16.1 %shard_map.298 = (bf16[1024,704]{1,0:T(8,128)(2,1)}, bf16[1024,128]{1,0:T(8,128)(2,1)}, bf16[1024,704]{1,0:T(8,128)(2,1)}, bf16[1024,704]{1,0:T(8,128)(2,1)}, bf...) custom-call(bf16[1024,2048]{1,0:T(8,128)(2,1)} %bitcast.76.refs_0_.refs_4_, bf16[1024,704]{1,0:T(8,128)(2,1)} %shard_map.293.refs_2_.refs_1_, ...), custom_call_target="tpu_custom_call" | custom-call | flops 1 | bytes 1 | tf_op jit(solution)/shard_map/pallas_call | solution.py:503
  354.2 13.1 %shard_map.301 = bf16[1024,2176]{1,0:T(8,128)(2,1)} custom-call(bf16[1024,704]{1,0:T(8,128)(2,1)} %get-tuple-element.122.refs_0_, bf16[1024,704]{1,0:T(8,128)(2,1)} %get-tuple-element.123.refs_1_.refs_0_, bf16[1024,256]{1,0:T(8,128)(2,1)} %get-tuple-element.124.refs_2_, bf16[704,2048]{1,0:T(8,128)(2,1)} %bitcast.303, bf16[704,2048]{1,0:T(8,128)(2,1)} %bitcast.307, ...), custom_call_target="tpu_custom_call" | custom-call | flops 1 | bytes 1 | tf_op jit(solution)/shard_map/pallas_call | solution.py:503
  367.4 5.4 shard_map.302
  372.8 8.1 %shard_map.303.refs_4_ = bf16[1024,2048]{1,0:T(8,128)(2,1)} custom-call(bf16[1024,704]{1,0:T(8,128)(2,1)} %get-tuple-element.120.refs_0_.refs_1_, bf16[1024,128]{1,0:T(8,128)(2,1)} %get-tuple-element.121.refs_1_.refs_3_, bf16[704,2048]{1,0:T(8,128)(2,1)} %bitcast.310, bf16[128,2048]{1,0:T(8,128)(2,1)} %get-tuple-element.305.refs_1_.refs_3_, ...), custom_call_target="tpu_custom_call" | custom-call | flops 1 | bytes 1 | tf_op jit(solution)/shard_map/pallas_call | solution.py:503
  383.2 8.1 %shard_map.304.refs_6_ = bf16[1024,2048]{1,0:T(8,128)(2,1)} custom-call(bf16[1024,704]{1,0:T(8,128)(2,1)} %get-tuple-element.118.refs_0_, bf16[1024,128]{1,0:T(8,128)(2,1)} %get-tuple-element.119.refs_1_.refs_2_, bf16[704,2048]{1,0:T(8,128)(2,1)} %bitcast.311, bf16[128,2048]{1,0:T(8,128)(2,1)} %get-tuple-element.305.refs_1_.refs_3_, ...), custom_call_target="tpu_custom_call" | custom-call | flops 1 | bytes 1 | tf_op jit(solution)/shard_map/pallas_call | solution.py:503
  391.3 14.0 %shard_map.305 = (f32[704,2048]{1,0:T(8,128)}, bf16[128,2048]{1,0:T(8,128)(2,1)}) custom-call(bf16[1024,704]{1,0:T(8,128)(2,1)} %get-tuple-element.123.refs_1_.refs_0_, bf16[1024,704]{1,0:T(8,128)(2,1)} %get-tuple-element.127.refs_1_, bf16[1024,256]{1,0:T(8,128)(2,1)} %get-tuple-element.124.refs_2_, bf16[1024,256]{1,0:T(8,128)(2,1)} %get-tuple-element.128.refs_2_.refs_3_, ...), custom_call_target="tpu_custom_call" | custom-call | flops 1 | bytes 1 | tf_op jit(solution)/shard_map/pallas_call | solution.py:503
  409.7 3.4 shard_map.306
  415.2 14.0 %shard_map.307 = (f32[704,2048]{1,0:T(8,128)}, bf16[128,2048]{1,0:T(8,128)(2,1)}) custom-call(bf16[1024,704]{1,0:T(8,128)(2,1)} %get-tuple-element.118.refs_0_, bf16[1024,704]{1,0:T(8,128)(2,1)} %get-tuple-element.120.refs_0_.refs_1_, bf16[1024,128]{1,0:T(8,128)(2,1)} %get-tuple-element.119.refs_1_.refs_2_, ...), custom_call_target="tpu_custom_call" | custom-call | flops 1 | bytes 1 | tf_op jit(solution)/shard_map/pallas_call | solution.py:503
  433.0 5.2 shard_map.309
  444.8 14.2 %shard_map.310 = (f32[704,2048]{1,0:T(8,128)}, bf16[128,2048]{1,0:T(8,128)(2,1)}) custom-call(bf16[1024,704]{1,0:T(8,128)(2,1)} %get-tuple-element.122.refs_0_, bf16[1024,704]{1,0:T(8,128)(2,1)} %get-tuple-element.126.refs_0_.refs_1_, bf16[1024,256]{1,0:T(8,128)(2,1)} %get-tuple-element.124.refs_2_, bf16[1024,256]{1,0:T(8,128)(2,1)} %get-tuple-element.128.refs_2_.refs_3_, ...), custom_call_target="tpu_custom_call" | custom-call | flops 1 | bytes 1 | tf_op jit(solution)/shard_map/pallas_call | solution.py:503
  462.9 3.3 shard_map.311
  474.5 4.4 collective-permute-done.58
  491.0 3.4 shard_map.313.refs_9_
  494.4 13.7 %shard_map.314 = (bf16[2,2,256,576]{3,2,1,0:T(8,128)(2,1)}, bf16[2,2,256,576]{3,2,1,0:T(8,128)(2,1)}, f32[512,384]{1,0:T(8,128)}, f32[512,512]{1,0:T(8,128)}) custom-call(bf16[512,2048]{1,0:T(8,128)(2,1)} %bitcast.313, bf16[512,384]{1,0:T(8,128)(2,1)} %pad_maximum_fusion.17.refs_0_.refs_1_, bf16[2,2,256,576]{3,2,1,0:T(8,128)(2,1)} %copy-done, ...), custom_call_target="tpu_custom_call" | custom-call | flops 1 | bytes 1 | tf_op jit(solution)/shard_map/pallas_call | solution.py:503
  512.5 4.0 shard_map.321
  518.8 12.2 %collective-permute-done.52.refs_1_ = bf16[128,2048]{1,0:T(8,128)(2,1)S(1)} collective-permute-done((bf16[128,2048]{1,0:T(8,128)(2,1)}, bf16[128,2048]{1,0:T(8,128)(2,1)S(1)}, u32[]{:S(2)}, u32[]{:S(2)}) %collective-permute-start.52) | collective-permute-done | bytes 524320 | tf_op jit(solution)/shard_map/ppermute | solution.py:1110
  545.7 5.4 all-to-all-start.3
  565.6 4.9 collective-permute-start.70
  578.6 3.1 collective-permute-done.70.refs_1_
  594.7 4.6 shard_map.326
  612.8 8.8 %collective-permute-done.63.refs_2_ = bf16[64,2048]{1,0:T(8,128)(2,1)} collective-permute-done((bf16[64,2048]{1,0:T(8,128)(2,1)}, bf16[64,2048]{1,0:T(8,128)(2,1)}, u32[]{:S(2)}, u32[]{:S(2)}) %collective-permute-start.63) | collective-permute-done | bytes 262176 | tf_op jit(solution)/shard_map/ppermute | solution.py:1120
  621.6 21.1 %collective-permute-done.64.refs_3_ = bf16[64,2048]{1,0:T(8,128)(2,1)} collective-permute-done((bf16[64,2048]{1,0:T(8,128)(2,1)}, bf16[64,2048]{1,0:T(8,128)(2,1)}, u32[]{:S(2)}, u32[]{:S(2)}) %collective-permute-start.64) | collective-permute-done | bytes 262176 | tf_op jit(solution)/shard_map/ppermute | solution.py:1120
  645.8 3.1 shard_map.325
  657.1 5.6 collective-permute-start.87
  663.9 3.6 rev.49
  682.7 5.8 all-to-all-start.1
  702.8 3.5 all-to-all-start.2
  708.0 10.0 %all-to-all-done.2 = bf16[4,128,768]{2,1,0:T(8,128)(2,1)S(1)} async-done(((bf16[4,128,768]{2,1,0:T(8,128)(2,1)}), bf16[4,128,768]{2,1,0:T(8,128)(2,1)S(1)}, u32[]{:S(2)}, u32[]{:S(2)}) %all-to-all-start.2) | async-done | bytes 786464 | tf_op jit(solution)/shard_map/all_to_all | solution.py:1124
  (619 shorter events, 323.1 us)
Async XLA Ops:
  13.2 40.8 %collective-permute-start.3 = (bf16[128,640]{1,0:T(8,128)(2,1)}, bf16[128,640]{1,0:T(8,128)(2,1)}, u32[]{:S(2)}, u32[]{:S(2)}) collective-permute-start(bf16[128,640]{1,0:T(8,128)(2,1)} %pad.21), channel_id=1, source_target_pairs={{16,0},{24,8},{0,16},{8,24},{17,1},{25,9},{1,17},{9,25},{18,2},{26... | collective-permute-start | bytes 491528 | tf_op jit(solution)/shard_map/ppermute | solution.py:1115
  13.2 33.3 %collective-permute-start.2 = (bf16[128,640]{1,0:T(8,128)(2,1)}, bf16[128,640]{1,0:T(8,128)(2,1)}, u32[]{:S(2)}, u32[]{:S(2)}) collective-permute-start(bf16[128,640]{1,0:T(8,128)(2,1)} %pad.21), channel_id=1, source_target_pairs={{8,0},{16,8},{24,16},{0,24},{9,1},{17,9},{25,17},{1,25},{10,2},{18... | collective-permute-start | bytes 491528 | tf_op jit(solution)/shard_map/ppermute | solution.py:1115
  16.2 39.5 %collective-permute-start.4 = (bf16[128,640]{1,0:T(8,128)(2,1)}, bf16[128,640]{1,0:T(8,128)(2,1)}, u32[]{:S(2)}, u32[]{:S(2)}) collective-permute-start(bf16[128,640]{1,0:T(8,128)(2,1)} %pad.21), channel_id=1, source_target_pairs={{24,0},{0,8},{8,16},{16,24},{25,1},{1,9},{9,17},{17,25},{26,2},{2,... | collective-permute-start | bytes 491528 | tf_op jit(solution)/shard_map/ppermute | solution.py:1115
  17.4 55.7 %collective-permute-start.33 = (bf16[64,2048]{1,0:T(8,128)(2,1)S(1)}, bf16[64,2048]{1,0:T(8,128)(2,1)}, u32[]{:S(2)}, u32[]{:S(2)}) collective-permute-start(bf16[64,2048]{1,0:T(8,128)(2,1)S(1)} %fusion.9), channel_id=1, source_target_pairs={{24,0},{0,8},{8,16},{16,24},{25,1},{1,9},{9,17},{17,25},{26,2},{2,... | collective-permute-start | bytes 786440 | tf_op jit(solution)/shard_map/ppermute | solution.py:1115
  20.1 54.4 %collective-permute-start.32 = (bf16[64,2048]{1,0:T(8,128)(2,1)S(1)}, bf16[64,2048]{1,0:T(8,128)(2,1)}, u32[]{:S(2)}, u32[]{:S(2)}) collective-permute-start(bf16[64,2048]{1,0:T(8,128)(2,1)S(1)} %fusion.9), channel_id=1, source_target_pairs={{16,0},{24,8},{0,16},{8,24},{17,1},{25,9},{1,17},{9,25},{18,2},{26... | collective-permute-start | bytes 786440 | tf_op jit(solution)/shard_map/ppermute | solution.py:1115
  22.5 197.0 %all-to-all-start = ((bf16[16,264,128]{2,1,0:T(8,128)(2,1)}), bf16[16,264,128]{2,1,0:T(8,128)(2,1)}, u32[]{:S(2)}, u32[]{:S(2)}) async-start(bf16[16,264,128]{2,1,0:T(8,128)(2,1)} %pad_maximum_fusion.5), calls=%async_computation | async-start | bytes 2162688 | tf_op jit(solution)/shard_map/all_to_all | solution.py:1124
  28.9 153.3 %all-gather.3.cloned.1.call-start = ((), (), s32[]{:S(2)}) async-start(), calls=%async_computation.8 | async-start | bytes 3932160 | tf_op jit(solution)/shard_map/all_gather | solution.py:1342
  46.5 28.5 %collective-permute-start.31 = (bf16[64,2048]{1,0:T(8,128)(2,1)S(1)}, bf16[64,2048]{1,0:T(8,128)(2,1)}, u32[]{:S(2)}, u32[]{:S(2)}) collective-permute-start(bf16[64,2048]{1,0:T(8,128)(2,1)S(1)} %fusion.9), channel_id=1, source_target_pairs={{8,0},{16,8},{24,16},{0,24},{9,1},{17,9},{25,17},{1,25},{10,2},{18... | collective-permute-start | bytes 786440 | tf_op jit(solution)/shard_map/ppermute | solution.py:1115
  73.0 32.8 %collective-permute-start.9 = (bf16[128,768]{1,0:T(8,128)(2,1)}, bf16[128,768]{1,0:T(8,128)(2,1)}, u32[]{:S(2)}, u32[]{:S(2)}) collective-permute-start(bf16[128,768]{1,0:T(8,128)(2,1)} %get-tuple-element.316), channel_id=1, source_target_pairs={{0,6},{2,4},{4,2},{6,0},{1,7},{3,5},{5,3},{7,1},{8,14},{10,12},{12... | collective-permute-start | bytes 589832 | tf_op jit(solution)/shard_map/ppermute | solution.py:1310
  73.1 31.1 %collective-permute-start.8 = (bf16[128,768]{1,0:T(8,128)(2,1)}, bf16[128,768]{1,0:T(8,128)(2,1)}, u32[]{:S(2)}, u32[]{:S(2)}) collective-permute-start(bf16[128,768]{1,0:T(8,128)(2,1)} %get-tuple-element.317), channel_id=1, source_target_pairs={{0,4},{4,0},{1,5},{5,1},{2,6},{6,2},{3,7},{7,3},{8,12},{12,8},{9,1... | collective-permute-start | bytes 589832 | tf_op jit(solution)/shard_map/ppermute | solution.py:1110
  74.5 41.5 %collective-permute-start.21 = (bf16[512,576]{0,1:T(8,128)(2,1)}, bf16[512,576]{0,1:T(8,128)(2,1)}, u32[]{:S(2)}, u32[]{:S(2)}) collective-permute-start(bf16[512,576]{0,1:T(8,128)(2,1)} %copy.293), channel_id=1, source_target_pairs={{0,2},{2,0},{1,3},{3,1},{4,6},{6,4},{5,7},{7,5},{8,10},{10,8},{9,1... | collective-permute-start | bytes 1769480 | tf_op jit(solution)/shard_map/ppermute | solution.py:1110
  77.8 20.7 %collective-permute-start.20 = (bf16[512,576]{0,1:T(8,128)(2,1)}, bf16[512,576]{0,1:T(8,128)(2,1)S(1)}, u32[]{:S(2)}, u32[]{:S(2)}) collective-permute-start(bf16[512,576]{0,1:T(8,128)(2,1)} %copy.293), channel_id=1, source_target_pairs={{0,4},{4,0},{1,5},{5,1},{2,6},{6,2},{3,7},{7,3},{8,12},{12,8},{9,1... | collective-permute-start | bytes 1769480 | tf_op jit(solution)/shard_map/ppermute | solution.py:1110
  99.4 50.1 %collective-permute-start.34 = (bf16[256,2048]{1,0:T(8,128)(2,1)}, bf16[256,2048]{1,0:T(8,128)(2,1)S(1)}, u32[]{:S(2)}, u32[]{:S(2)}) collective-permute-start(bf16[256,2048]{1,0:T(8,128)(2,1)} %get-tuple-element.309), channel_id=1, source_target_pairs={{0,1},{1,0},{2,3},{3,2},{4,5},{5,4},{6,7},{7,6},{8,9},{9,8},{10,11... | collective-permute-start | bytes 3145736 | tf_op jit(solution)/shard_map/ppermute | solution.py:1110
  100.9 21.4 %collective-permute-start.22 = (bf16[512,576]{0,1:T(8,128)(2,1)}, bf16[512,576]{0,1:T(8,128)(2,1)}, u32[]{:S(2)}, u32[]{:S(2)}) collective-permute-start(bf16[512,576]{0,1:T(8,128)(2,1)} %copy-done.22), channel_id=1, source_target_pairs={{0,2},{2,0},{1,3},{3,1},{4,6},{6,4},{5,7},{7,5},{8,10},{10,8},{9,1... | collective-permute-start | bytes 1769480 | tf_op jit(solution)/shard_map/ppermute | solution.py:1110
  111.2 589.6 %reduce-scatter.5.cloned.1.call-start = ((), (), s32[]{:S(2)}) async-start(), calls=%async_computation.7 | async-start | bytes 1310720 | tf_op jit(solution)/shard_map/reduce_scatter | solution.py:1500
  112.0 40.1 %collective-permute-start.35 = (bf16[256,2048]{1,0:T(8,128)(2,1)}, bf16[256,2048]{1,0:T(8,128)(2,1)}, u32[]{:S(2)}, u32[]{:S(2)}) collective-permute-start(bf16[256,2048]{1,0:T(8,128)(2,1)} %get-tuple-element.309), channel_id=1, source_target_pairs={{0,4},{4,0},{1,5},{5,1},{2,6},{6,2},{3,7},{7,3},{8,12},{12,8},{9,1... | collective-permute-start | bytes 3145736 | tf_op jit(solution)/shard_map/ppermute | solution.py:1110
  116.0 28.1 %collective-permute-start.15 = (bf16[256,576]{1,0:T(8,128)(2,1)}, bf16[256,576]{1,0:T(8,128)(2,1)}, u32[]{:S(2)}, u32[]{:S(2)}) collective-permute-start(bf16[256,576]{1,0:T(8,128)(2,1)} %pad_maximum_fusion.19), channel_id=1, source_target_pairs={{0,4},{4,0},{1,5},{5,1},{2,6},{6,2},{3,7},{7,3},{8,12},{12,8},{9,1... | collective-permute-start | bytes 884744 | tf_op jit(solution)/shard_map/ppermute | solution.py:1110
  116.0 31.5 %collective-permute-start.16 = (bf16[256,576]{1,0:T(8,128)(2,1)}, bf16[256,576]{1,0:T(8,128)(2,1)}, u32[]{:S(2)}, u32[]{:S(2)}) collective-permute-start(bf16[256,576]{1,0:T(8,128)(2,1)} %pad_maximum_fusion.19), channel_id=1, source_target_pairs={{0,1},{1,0},{2,3},{3,2},{4,5},{5,4},{6,7},{7,6},{8,9},{9,8},{10,11... | collective-permute-start | bytes 884744 | tf_op jit(solution)/shard_map/ppermute | solution.py:1110
  171.5 70.6 %collective-permute-start.38 = (bf16[2,2,256,2048]{3,2,1,0:T(8,128)(2,1)}, bf16[2,2,256,2048]{3,2,1,0:T(8,128)(2,1)}, u32[]{:S(2)}, u32[]{:S(2)}) collective-permute-start(bf16[2,2,256,2048]{3,2,1,0:T(8,128)(2,1)} %pad_maximum_fusion), channel_id=1, source_target_pairs={{0,2},{2,0},{1,3},{3,1},{4,6},{6,4},{5,7},{7,5},{8,10},{10,8},{9,1... | collective-permute-start | bytes 12582920 | tf_op jit(solution)/shard_map/ppermute | solution.py:1110
  228.0 31.0 %collective-permute-start.30 = (bf16[64,2048]{1,0:T(8,128)(2,1)S(1)}, bf16[64,2048]{1,0:T(8,128)(2,1)S(1)}, u32[]{:S(2)}, u32[]{:S(2)}) collective-permute-start(bf16[64,2048]{1,0:T(8,128)(2,1)S(1)} %multiply_convert_fusion.1.refs_2_.refs_0_), channel_id=1, source_target_pairs={{24,0},{0,8},{8,16},{16,24},{25,1},{1,9},{9,17},{17,25},{26,2},{2,... | collective-permute-start | bytes 786440 | tf_op jit(solution)/shard_map/ppermute | solution.py:1115
  230.9 28.1 %collective-permute-start.29 = (bf16[64,2048]{1,0:T(8,128)(2,1)S(1)}, bf16[64,2048]{1,0:T(8,128)(2,1)S(1)}, u32[]{:S(2)}, u32[]{:S(2)}) collective-permute-start(bf16[64,2048]{1,0:T(8,128)(2,1)S(1)} %multiply_convert_fusion.1.refs_2_.refs_0_), channel_id=1, source_target_pairs={{16,0},{24,8},{0,16},{8,24},{17,1},{25,9},{1,17},{9,25},{18,2},{26... | collective-permute-start | bytes 786440 | tf_op jit(solution)/shard_map/ppermute | solution.py:1115
  230.9 28.1 %collective-permute-start.28 = (bf16[64,2048]{1,0:T(8,128)(2,1)S(1)}, bf16[64,2048]{1,0:T(8,128)(2,1)S(1)}, u32[]{:S(2)}, u32[]{:S(2)}) collective-permute-start(bf16[64,2048]{1,0:T(8,128)(2,1)S(1)} %multiply_convert_fusion.1.refs_2_.refs_0_), channel_id=1, source_target_pairs={{8,0},{16,8},{24,16},{0,24},{9,1},{17,9},{25,17},{1,25},{10,2},{18... | collective-permute-start | bytes 786440 | tf_op jit(solution)/shard_map/ppermute | solution.py:1115
  262.7 22.5 %collective-permute-start.40 = (bf16[256,2048]{1,0:T(8,128)(2,1)}, bf16[256,2048]{1,0:T(8,128)(2,1)S(1)}, u32[]{:S(2)}, u32[]{:S(2)}) collective-permute-start(bf16[256,2048]{1,0:T(8,128)(2,1)} %shard_map.297), channel_id=1, source_target_pairs={{0,4},{4,0},{1,5},{5,1},{2,6},{6,2},{3,7},{7,3},{8,12},{12,8},{9,1... | collective-permute-start | bytes 3145736 | tf_op jit(solution)/shard_map/ppermute | solution.py:1110
  263.9 24.0 %collective-permute-start.39 = (bf16[256,2048]{1,0:T(8,128)(2,1)}, bf16[256,2048]{1,0:T(8,128)(2,1)S(1)}, u32[]{:S(2)}, u32[]{:S(2)}) collective-permute-start(bf16[256,2048]{1,0:T(8,128)(2,1)} %shard_map.297), channel_id=1, source_target_pairs={{0,1},{1,0},{2,3},{3,2},{4,5},{5,4},{6,7},{7,6},{8,9},{9,8},{10,11... | collective-permute-start | bytes 3145736 | tf_op jit(solution)/shard_map/ppermute | solution.py:1110
  336.7 30.7 %collective-permute-start.44 = (bf16[1024,2176]{1,0:T(8,128)(2,1)}, bf16[1024,2176]{1,0:T(8,128)(2,1)}, u32[]{:S(2)}, u32[]{:S(2)}) collective-permute-start(bf16[1024,2176]{1,0:T(8,128)(2,1)} %shard_map.300.refs_8_), channel_id=1, source_target_pairs={{0,2},{2,0},{1,3},{3,1},{4,6},{6,4},{5,7},{7,5},{8,10},{10,8},{9,1... | collective-permute-start | bytes 13369352 | tf_op jit(solution)/shard_map/ppermute | solution.py:1110
  380.9 52.1 %collective-permute-start.45 = (bf16[1024,2048]{1,0:T(8,128)(2,1)}, bf16[1024,2048]{1,0:T(8,128)(2,1)}, u32[]{:S(2)}, u32[]{:S(2)}) collective-permute-start(bf16[1024,2048]{1,0:T(8,128)(2,1)} %shard_map.303.refs_4_), channel_id=1, source_target_pairs={{0,2},{2,0},{1,3},{3,1},{4,6},{6,4},{5,7},{7,5},{8,10},{10,8},{9,1... | collective-permute-start | bytes 12582920 | tf_op jit(solution)/shard_map/ppermute | solution.py:1110
  381.3 26.8 %collective-permute-start.46 = (bf16[2,128,2176]{2,1,0:T(8,128)(2,1)}, bf16[2,128,2176]{2,1,0:T(8,128)(2,1)S(1)}, u32[]{:S(2)}, u32[]{:S(2)}) collective-permute-start(bf16[2,128,2176]{2,1,0:T(8,128)(2,1)} %get-tuple-element.131.refs_5_), channel_id=1, source_target_pairs={{0,4},{4,0},{1,5},{5,1},{2,6},{6,2},{3,7},{7,3},{8,12},{12,8},{9,1... | collective-permute-start | bytes 3342344 | tf_op jit(solution)/shard_map/ppermute | solution.py:1110
  382.1 26.5 %collective-permute-start.47 = (bf16[2,128,2176]{2,1,0:T(8,128)(2,1)}, bf16[2,128,2176]{2,1,0:T(8,128)(2,1)S(1)}, u32[]{:S(2)}, u32[]{:S(2)}) collective-permute-start(bf16[2,128,2176]{2,1,0:T(8,128)(2,1)} %get-tuple-element.133.refs_7_), channel_id=1, source_target_pairs={{0,1},{1,0},{2,3},{3,2},{4,5},{5,4},{6,7},{7,6},{8,9},{9,8},{10,11... | collective-permute-start | bytes 3342344 | tf_op jit(solution)/shard_map/ppermute | solution.py:1110
  438.2 23.8 %collective-permute-start.50 = (bf16[2,128,2048]{2,1,0:T(8,128)(2,1)}, bf16[2,128,2048]{2,1,0:T(8,128)(2,1)S(1)}, u32[]{:S(2)}, u32[]{:S(2)}) collective-permute-start(bf16[2,128,2048]{2,1,0:T(8,128)(2,1)} %get-tuple-element.145.refs_7_), channel_id=1, source_target_pairs={{0,4},{4,0},{1,5},{5,1},{2,6},{6,2},{3,7},{7,3},{8,12},{12,8},{9,1... | collective-permute-start | bytes 3145736 | tf_op jit(solution)/shard_map/ppermute | solution.py:1110
  439.2 23.5 %collective-permute-start.51 = (bf16[2,128,2048]{2,1,0:T(8,128)(2,1)}, bf16[2,128,2048]{2,1,0:T(8,128)(2,1)}, u32[]{:S(2)}, u32[]{:S(2)}) collective-permute-start(bf16[2,128,2048]{2,1,0:T(8,128)(2,1)} %get-tuple-element.147.refs_9_), channel_id=1, source_target_pairs={{0,1},{1,0},{2,3},{3,2},{4,5},{5,4},{6,7},{7,6},{8,9},{9,8},{10,11... | collective-permute-start | bytes 3145736 | tf_op jit(solution)/shard_map/ppermute | solution.py:1110
  440.2 26.0 %collective-permute-start.54 = (bf16[64,2176]{1,0:T(8,128)(2,1)}, bf16[64,2176]{1,0:T(8,128)(2,1)S(1)}, u32[]{:S(2)}, u32[]{:S(2)}) collective-permute-start(bf16[64,2176]{1,0:T(8,128)(2,1)} %get-tuple-element.141.refs_9_), channel_id=1, source_target_pairs={{0,8},{8,16},{16,24},{24,0},{1,9},{9,17},{17,25},{25,1},{2,10},{10... | collective-permute-start | bytes 835592 | tf_op jit(solution)/shard_map/ppermute | solution.py:1120
  440.4 25.8 %collective-permute-start.55 = (bf16[64,2176]{1,0:T(8,128)(2,1)}, bf16[64,2176]{1,0:T(8,128)(2,1)}, u32[]{:S(2)}, u32[]{:S(2)}) collective-permute-start(bf16[64,2176]{1,0:T(8,128)(2,1)} %get-tuple-element.142.refs_10_), channel_id=1, source_target_pairs={{0,16},{8,24},{16,0},{24,8},{1,17},{9,25},{17,1},{25,9},{2,18},{10... | collective-permute-start | bytes 835592 | tf_op jit(solution)/shard_map/ppermute | solution.py:1120
  443.4 22.9 %collective-permute-start.56 = (bf16[64,2176]{1,0:T(8,128)(2,1)}, bf16[64,2176]{1,0:T(8,128)(2,1)}, u32[]{:S(2)}, u32[]{:S(2)}) collective-permute-start(bf16[64,2176]{1,0:T(8,128)(2,1)} %get-tuple-element.143.refs_11_), channel_id=1, source_target_pairs={{0,24},{8,0},{16,8},{24,16},{1,25},{9,1},{17,9},{25,17},{2,26},{10... | collective-permute-start | bytes 835592 | tf_op jit(solution)/shard_map/ppermute | solution.py:1120
  510.6 24.5 %collective-permute-start.65 = (bf16[2,2,256,576]{2,3,1,0:T(8,128)(2,1)}, bf16[2,2,256,576]{2,3,1,0:T(8,128)(2,1)}, u32[]{:S(2)}, u32[]{:S(2)}) collective-permute-start(bf16[2,2,256,576]{2,3,1,0:T(8,128)(2,1)} %copy.312), channel_id=1, source_target_pairs={{0,2},{2,0},{1,3},{3,1},{4,6},{6,4},{5,7},{7,5},{8,10},{10,8},{9,1... | collective-permute-start | bytes 3538952 | tf_op jit(solution)/shard_map/ppermute | solution.py:1110
  516.4 40.4 %collective-permute-start.74 = (bf16[2,128,2048]{2,1,0:T(8,128)(2,1)}, bf16[2,128,2048]{2,1,0:T(8,128)(2,1)S(1)}, u32[]{:S(2)}, u32[]{:S(2)}) collective-permute-start(bf16[2,128,2048]{2,1,0:T(8,128)(2,1)} %get-tuple-element.177), channel_id=1, source_target_pairs={{0,2},{2,0},{1,3},{3,1},{4,6},{6,4},{5,7},{7,5},{8,10},{10,8},{9,1... | collective-permute-start | bytes 3145736 | tf_op jit(solution)/shard_map/ppermute | solution.py:1110
  545.7 65.8 %all-to-all-start.3 = ((bf16[16,264,128]{2,1,0:T(8,128)(2,1)}), bf16[16,264,128]{2,1,0:T(8,128)(2,1)}, u32[]{:S(2)}, u32[]{:S(2)}) async-start(bf16[16,264,128]{2,1,0:T(8,128)(2,1)} %bitcast_bitcast_fusion), calls=%async_computation.5 | async-start | bytes 2162688 | tf_op jit(solution)/shard_map/all_to_all | solution.py:1124
  551.0 149.7 %reduce-scatter.3.cloned.1.call-start = ((), (), s32[]{:S(2)}) async-start(), calls=%async_computation.6 | async-start | bytes 2621440 | tf_op jit(solution)/shard_map/reduce_scatter | solution.py:1527
  576.1 23.2 %collective-permute-start.77 = (bf16[32,2048]{1,0:T(8,128)(2,1)}, bf16[32,2048]{1,0:T(8,128)(2,1)S(1)}, u32[]{:S(2)}, u32[]{:S(2)}) collective-permute-start(bf16[32,2048]{1,0:T(8,128)(2,1)} %get-tuple-element.183), channel_id=1, source_target_pairs={{0,4},{4,0},{1,5},{5,1},{2,6},{6,2},{3,7},{7,3},{8,12},{12,8},{9,1... | collective-permute-start | bytes 393224 | tf_op jit(solution)/shard_map/ppermute | solution.py:1110
  577.7 23.3 %collective-permute-start.78 = (bf16[32,2048]{1,0:T(8,128)(2,1)}, bf16[32,2048]{1,0:T(8,128)(2,1)S(1)}, u32[]{:S(2)}, u32[]{:S(2)}) collective-permute-start(bf16[32,2048]{1,0:T(8,128)(2,1)} %get-tuple-element.185), channel_id=1, source_target_pairs={{0,1},{1,0},{2,3},{3,2},{4,5},{5,4},{6,7},{7,6},{8,9},{9,8},{10,11... | collective-permute-start | bytes 393224 | tf_op jit(solution)/shard_map/ppermute | solution.py:1110
  588.2 17.7 %collective-permute-start.80 = (bf16[64,576]{1,0:T(8,128)(2,1)S(1)}, bf16[64,576]{1,0:T(8,128)(2,1)S(1)}, u32[]{:S(2)}, u32[]{:S(2)}) collective-permute-start(bf16[64,576]{1,0:T(8,128)(2,1)S(1)} %pad_maximum_fusion.25), channel_id=1, source_target_pairs={{0,1},{1,0},{2,3},{3,2},{4,5},{5,4},{6,7},{7,6},{8,9},{9,8},{10,11... | collective-permute-start | bytes 221192 | tf_op jit(solution)/shard_map/ppermute | solution.py:1110
  589.2 17.3 %collective-permute-start.79 = (bf16[64,576]{1,0:T(8,128)(2,1)S(1)}, bf16[64,576]{1,0:T(8,128)(2,1)S(1)}, u32[]{:S(2)}, u32[]{:S(2)}) collective-permute-start(bf16[64,576]{1,0:T(8,128)(2,1)S(1)} %pad_maximum_fusion.25), channel_id=1, source_target_pairs={{0,4},{4,0},{1,5},{5,1},{2,6},{6,2},{3,7},{7,3},{8,12},{12,8},{9,1... | collective-permute-start | bytes 221192 | tf_op jit(solution)/shard_map/ppermute | solution.py:1110
  592.4 20.4 %collective-permute-start.62 = (bf16[64,2048]{1,0:T(8,128)(2,1)}, bf16[64,2048]{1,0:T(8,128)(2,1)}, u32[]{:S(2)}, u32[]{:S(2)}) collective-permute-start(bf16[64,2048]{1,0:T(8,128)(2,1)} %get-tuple-element.159.refs_9_), channel_id=1, source_target_pairs={{0,8},{8,16},{16,24},{24,0},{1,9},{9,17},{17,25},{25,1},{2,10},{10... | collective-permute-start | bytes 786440 | tf_op jit(solution)/shard_map/ppermute | solution.py:1120
  599.3 22.2 %collective-permute-start.63 = (bf16[64,2048]{1,0:T(8,128)(2,1)}, bf16[64,2048]{1,0:T(8,128)(2,1)}, u32[]{:S(2)}, u32[]{:S(2)}) collective-permute-start(bf16[64,2048]{1,0:T(8,128)(2,1)} %get-tuple-element.160.refs_10_), channel_id=1, source_target_pairs={{0,16},{8,24},{16,0},{24,8},{1,17},{9,25},{17,1},{25,9},{2,18},{10... | collective-permute-start | bytes 786440 | tf_op jit(solution)/shard_map/ppermute | solution.py:1120
  601.0 41.7 %collective-permute-start.64 = (bf16[64,2048]{1,0:T(8,128)(2,1)}, bf16[64,2048]{1,0:T(8,128)(2,1)}, u32[]{:S(2)}, u32[]{:S(2)}) collective-permute-start(bf16[64,2048]{1,0:T(8,128)(2,1)} %get-tuple-element.161.refs_11_), channel_id=1, source_target_pairs={{0,24},{8,0},{16,8},{24,16},{1,25},{9,1},{17,9},{25,17},{2,26},{10... | collective-permute-start | bytes 786440 | tf_op jit(solution)/shard_map/ppermute | solution.py:1120
  611.4 33.4 %collective-permute-start.83 = (bf16[2,2,64,576]{3,2,1,0:T(8,128)(2,1)}, bf16[2,2,64,576]{3,2,1,0:T(8,128)(2,1)S(1)}, u32[]{:S(2)}, u32[]{:S(2)}) collective-permute-start(bf16[2,2,64,576]{3,2,1,0:T(8,128)(2,1)} %get-tuple-element.329), channel_id=1, source_target_pairs={{0,2},{2,0},{1,3},{3,1},{4,6},{6,4},{5,7},{7,5},{8,10},{10,8},{9,1... | collective-permute-start | bytes 884744 | tf_op jit(solution)/shard_map/ppermute | solution.py:1110
  657.1 32.9 %collective-permute-start.86 = (bf16[128,576]{1,0:T(8,128)(2,1)}, bf16[128,576]{1,0:T(8,128)(2,1)}, u32[]{:S(2)}, u32[]{:S(2)}) collective-permute-start(bf16[128,576]{1,0:T(8,128)(2,1)} %get-tuple-element.188), channel_id=1, source_target_pairs={{0,8},{8,16},{16,24},{24,0},{1,9},{9,17},{17,25},{25,1},{2,10},{10... | collective-permute-start | bytes 442376 | tf_op jit(solution)/shard_map/ppermute | solution.py:1120
  657.1 32.8 %collective-permute-start.87 = (bf16[128,576]{1,0:T(8,128)(2,1)}, bf16[128,576]{1,0:T(8,128)(2,1)}, u32[]{:S(2)}, u32[]{:S(2)}) collective-permute-start(bf16[128,576]{1,0:T(8,128)(2,1)} %get-tuple-element.189), channel_id=1, source_target_pairs={{0,16},{8,24},{16,0},{24,8},{1,17},{9,25},{17,1},{25,9},{2,18},{10... | collective-permute-start | bytes 442376 | tf_op jit(solution)/shard_map/ppermute | solution.py:1120
  662.7 27.3 %collective-permute-start.88 = (bf16[128,576]{1,0:T(8,128)(2,1)}, bf16[128,576]{1,0:T(8,128)(2,1)}, u32[]{:S(2)}, u32[]{:S(2)}) collective-permute-start(bf16[128,576]{1,0:T(8,128)(2,1)} %get-tuple-element.190), channel_id=1, source_target_pairs={{0,24},{8,0},{16,8},{24,16},{1,25},{9,1},{17,9},{25,17},{2,26},{10... | collective-permute-start | bytes 442376 | tf_op jit(solution)/shard_map/ppermute | solution.py:1120
  (141 other events, 1391.7 us)
Sparse Core Ops, SparseCore 0:
  111.3 62.2 all-gather.2
  518.9 24.8 reduce-scatter.4
  599.4 55.5 reduce-scatter.2

commit v4 on v3

--- a/solution.py
+++ b/solution.py
@@ -900,36 +900,30 @@
     )
 
 
-def query_grads_body(rows, z, grads, source, up, *outs):
+def query_grads_body(rows, grads, source, up, more, out):
     columns = grads.shape[1]
     up_blocks = up.shape[1] // 128
     up_rows = rows // up_blocks
     here = grads[...]
-    for s, out in enumerate(outs):
-        groups = out.shape[0]
-        place = lax.rem(z[0] + s, len(outs))
-        start = pl.multiple_of(place * groups * rows, groups * rows)
-        total = mul_tn(source[:, pl.ds(start, groups * rows)], here).astype(jnp.bfloat16)
-        start = pl.multiple_of(place * groups * up_rows, groups * up_rows)
-        more = up[pl.ds(start, groups * up_rows), :].astype(jnp.bfloat16)
-        for j in range(groups):
-            out[j, :, :columns] = total[j * rows : (j + 1) * rows]
-            for k in range(up_blocks):
-                out[j, k * up_rows : (k + 1) * up_rows, columns:] = more[
-                    j * up_rows : (j + 1) * up_rows, k * 128 : (k + 1) * 128
-                ]
-
-
-def query_grads_kernel(z, count, grads, source, up, rows, after=()):
-    shapes = [shaped((source.shape[1] // (rows * count), rows, grads.shape[1] + 128))] * count
+    for i in range(out.shape[0]):
+        span = slice(i * rows, (i + 1) * rows)
+        out[i, :, :columns] = mul_tn(source[:, span], here).astype(jnp.bfloat16)
+        for k in range(up_blocks):
+            out[i, k * up_rows : (k + 1) * up_rows, columns : columns + 128] = up[
+                i * up_rows : (i + 1) * up_rows, k * 128 : (k + 1) * 128
+            ].astype(jnp.bfloat16)
+        out[i, :, columns + 128 :] = more[i]
+
+
+def query_grads_kernel(grads, source, up, more, rows):
+    shape = shaped((source.shape[1] // rows, rows, grads.shape[1] + 128 + more.shape[2]))
     return local_call(
         partial(query_grads_body, rows),
         (1,),
-        [SCALAR, whole(grads), whole(source), whole(up)],
-        [whole(s) for s in shapes],
-        shapes,
-        (z, grads, source, up),
-        after,
+        [whole(grads), whole(source), whole(up), whole(more)],
+        whole(shape),
+        shape,
+        (grads, source, up, more),
     )
 
 
@@ -961,7 +955,7 @@
     sent_out[0] = total[half:]
 
 
-def split_product_kernel(left, right, sequences):
+def split_product_kernel(left, right, sequences, after=()):
     rows = left.shape[0] // sequences
     shapes = [shaped((sequences, rows // 2, right.shape[0]))] * 2
     return local_call(
@@ -971,6 +965,7 @@
         [by_first(s) for s in shapes],
         shapes,
         (left, right),
+        after,
     )
 
 
@@ -1090,17 +1085,44 @@
 
 def join_body(*refs):
     out = refs[-1]
-    rows = refs[0].shape[0]
-    for s, ref in enumerate(refs[:-1]):
-        out[s * rows : (s + 1) * rows, :] = ref[...]
-
-
-def join_kernel(parts, after=()):
-    rows, width = parts[0].shape
-    shape = shaped((len(parts) * rows, width), parts[0].dtype)
+    at = 0
+    for ref in refs[:-1]:
+        out[at : at + ref.shape[0], :] = ref[...]
+        at += ref.shape[0]
+
+
+def join_kernel(parts, after=(), more=()):
+    parts = list(parts) + list(more)
+    shape = shaped((sum(p.shape[0] for p in parts), parts[0].shape[1]), parts[0].dtype)
     return local_call(
         join_body, (1,), [whole(p) for p in parts], whole(shape), shape, tuple(parts), after
     )
+
+
+def reorder_body(places, *refs):
+    del places
+    out = refs[-1]
+    rows = refs[0].shape[1]
+    for s in range(4):
+        out[s * rows : (s + 1) * rows, :] = refs[s][0]
+
+
+def reorder_kernel(places, blocks, after):
+    _, rows, width = blocks.shape
+    count = places.shape[0]
+    step = lambda s: pl.BlockSpec((1, rows, width), lambda i, places: (places[4 * i + s], 0, 0))
+    return pl.pallas_call(
+        lambda places, a, b, c, d, dep, out: reorder_body(places, a, b, c, d, out),
+        grid_spec=pltpu.PrefetchScalarGridSpec(
+            num_scalar_prefetch=1,
+            grid=(count // 4,),
+            in_specs=[step(s) for s in range(4)] + [pl.BlockSpec(memory_space=pl.ANY)],
+            out_specs=pl.BlockSpec((4 * rows, width), lambda i, places: (i, 0)),
+        ),
+        out_shape=shaped((count * rows, width)),
+        compiler_params=pltpu.CompilerParams(vmem_limit_bytes=VMEM_LIMIT),
+        cost_estimate=pl.CostEstimate(flops=1, bytes_accessed=1, transcendentals=0),
+    )(places, *[blocks] * 4, after)
 
 
 CTX = ("z", "x", "c")
@@ -1264,7 +1286,38 @@
         ],
         axis=1,
     )
-    small = put_z(z_parts(jnp.pad(small, ((0, 0), (0, -small.shape[1] % 128)))))
+    small_parts = z_parts(jnp.pad(small, ((0, 0), (0, -small.shape[1] % 128))))
+    up_columns = heads * (DN + DV)
+    up_part = jnp.transpose(
+        latent_up.reshape(rank_rows, 4, up_columns // 128, 128), (1, 2, 0, 3)
+    ).reshape(4, rows_here, 128)
+    out_part = jnp.transpose(output_weight.reshape(4, heads, DV, rows_here), (0, 2, 1, 3)).reshape(
+        4, DV, heads * rows_here
+    )
+    by_heads = query_weight.reshape(rows_here, 4, heads, DN + DR)
+    by_heads = jnp.concatenate(
+        [
+            by_heads[..., :DN].reshape(rows_here, 4, heads * DN),
+            by_heads[..., DN:].reshape(rows_here, 4, heads * DR),
+        ],
+        axis=2,
+    )
+    by_heads = jnp.transpose(by_heads, (1, 0, 2))
+    by_heads = jnp.concatenate([by_heads, up_part, out_part], axis=2)
+    mine_at = 2 * x + c
+    for_group = [
+        lax.dynamic_index_in_dim(by_heads, mine_at ^ k, 0, keepdims=False) for k in range(4)
+    ]
+    by_heads = put(
+        [
+            for_group[0],
+            swap(for_group[1], "c"),
+            swap(for_group[2], "x"),
+            lax.ppermute(for_group[3], ("x", "c"), [(k, 3 - k) for k in range(4)]),
+        ],
+        [mine_at ^ k for k in range(4)],
+    )
+    small = put_z([tie(part, by_heads) for part in small_parts])
     at = R + DR
     down_here = small[:, :, :at]
     rest = small[:, :, at:]
@@ -1281,63 +1334,19 @@
     full_latent_norm = rest[:, :rank_rows, experts + 2].reshape(R).astype(jnp.float32)
     all_routes = rest[:, :, experts + 3 : experts + 3 + TOPK]
 
-    up_columns = heads * (DN + DV)
-    up_part = jnp.transpose(
-        latent_up.reshape(rank_rows, 4, up_columns // 128, 128), (1, 2, 0, 3)
-    ).reshape(4, rows_here, 128)
-    out_part = jnp.transpose(output_weight.reshape(4, heads, DV, rows_here), (0, 2, 1, 3)).reshape(
-        4, DV, heads * rows_here
-    )
-    by_heads = query_weight.reshape(rows_here, 4, heads, DN + DR)
-    by_heads = jnp.concatenate(
-        [
-            by_heads[..., :DN].reshape(rows_here, 4, heads * DN),
-            by_heads[..., DN:].reshape(rows_here, 4, heads * DR),
-        ],
-        axis=2,
-    )
-    by_heads = jnp.transpose(by_heads, (1, 0, 2))
-    by_heads = jnp.concatenate([by_heads, up_part, out_part], axis=2)
-    mine_at = 2 * x + c
-    for_group = [
-        lax.dynamic_index_in_dim(by_heads, mine_at ^ k, 0, keepdims=False) for k in range(4)
-    ]
-    by_heads = put(
-        [
-            for_group[0],
-            swap(for_group[1], "c"),
-            swap(for_group[2], "x"),
-            lax.ppermute(for_group[3], ("x", "c"), [(k, 3 - k) for k in range(4)]),
-        ],
-        [mine_at ^ k for k in range(4)],
-    )
     mine = by_own(tokens, "y", 0)
     line = jnp.stack([mine, swap(mine, "x")], axis=1)
     line = jnp.stack([line, swap(line, "c")], axis=1)
     source = line.reshape(sequences * slab, width).astype(jnp.float32)
     grad_mine = by_own(cotangent, "y", 0)[0]
-    grad_parts = z_parts(grad_mine)
+    all_grads = lax.all_gather(tie(grad_mine, by_heads), CTX + ("y",), axis=0)
+    one = jnp.arange(2)
+    order = (
+        (((z + jnp.arange(zs)) % zs)[None, None, None, :] * 2 + (x ^ one)[None, :, None, None]) * 2
+        + (c ^ one)[:, None, None, None]
+    ) * 2 + (lax.axis_index("y") ^ one)[None, None, :, None]
+    order = order.reshape(-1).astype(jnp.int32)
     gate_t, up_t, down = (expert_gate[0].T, expert_up[0].T, expert_down[0])
-    shared_mine = jnp.concatenate(
-        [
-            shared_gate.T.reshape(count, shared_here, rows_here),
-            shared_up.T.reshape(count, shared_here, rows_here),
-            shared_down.reshape(count, shared_here, rows_here),
-        ],
-        axis=1,
-    )
-    shared_rows = trade(shared_mine, CTX)
-    shared_rows = jnp.transpose(shared_rows, (1, 0, 2)).reshape(3, shared_here, width)
-    shared_rows = jnp.pad(shared_rows, ((0, 0), (0, part - shared_here), (0, 0)))
-    small_t = jnp.concatenate(
-        [
-            shared_rows[0],
-            shared_rows[1],
-            jnp.pad(full_router.T, ((0, part - experts), (0, 0))),
-        ]
-    )
-    shared_down_t = shared_rows[2]
-
     query_here, up_here, out_here = heads_kernel(
         lax.all_gather(by_heads, "z", axis=0),
         query_columns,
@@ -1382,18 +1391,36 @@
     )
     plane = gather_plane(spread_z(key_own), ("y", "x"))
     keys_own, keys_other = (plane, swap(plane, "c"))
-    grads_own = gather_plane(jnp.concatenate(grad_parts), gates=(plane,))
-    grads_other = swap(grads_own, "c").reshape(-1, width)
-    grads_own = grads_own.reshape(-1, width)
     query = dot(input_low, query_here)
     rope = query[:, heads * DN :].reshape(sequences, slab, heads, DR)
     rope = rotate(rope, cosine[:, None, :], sine[:, None, :]).reshape(sequences * slab, -1)
     query_low = low(jnp.concatenate([query[:, : heads * DN], rope], axis=1))
 
-    def scatter_slab(kept, sent):
+    shared_mine = jnp.concatenate(
+        [
+            shared_gate.T.reshape(count, shared_here, rows_here),
+            shared_up.T.reshape(count, shared_here, rows_here),
+            shared_down.reshape(count, shared_here, rows_here),
+        ],
+        axis=1,
+    )
+    shared_rows = trade(tie(shared_mine, query_low), CTX)
+    shared_got = shared_rows
+    shared_rows = jnp.transpose(shared_rows, (1, 0, 2)).reshape(3, shared_here, width)
+    shared_rows = jnp.pad(shared_rows, ((0, 0), (0, part - shared_here), (0, 0)))
+    small_t = jnp.concatenate(
+        [
+            shared_rows[0],
+            shared_rows[1],
+            jnp.pad(full_router.T, ((0, part - experts), (0, 0))),
+        ]
+    )
+    shared_down_t = shared_rows[2]
+
+    def scatter_slab(kept, sent, after=()):
         shape = (2, 2, block, width)
         pieces = core_fold_kernel(kept.reshape(shape), swap(sent, "c").reshape(shape))
-        return fold_second(fold_first(pieces, ("y", "x")), ("y", "x"), 1)[0]
+        return fold_second(fold_first(pieces, ("y", "x"), after), ("y", "x"), 1)[0]
 
     def gather_slab(rows):
         plane = gather_plane(rows, ("y", "x"))
@@ -1416,15 +1443,23 @@
     normed_ffn, unit_ffn, inverse_ffn = root_norm(hidden_in, full_norm_ffn)
     ffn_low = low(normed_ffn)
     shares = jax.nn.softmax(dot(ffn_low, full_router), axis=-1)
+    half_places = order.shape[0] // 2
+    grads_own = reorder_kernel(order[:half_places], all_grads, ffn_low)
+    grads_other = reorder_kernel(order[half_places:], all_grads, ffn_low)
     ffn_parts = z_parts(ffn_low)
-    back_own = product_nt_kernel(grads_own, down, (ffn_low,))
+    back_own = product_nt_kernel(grads_own, down)
     back_other = product_nt_kernel(grads_other, down, (back_own,))
-    shared_own = product_nt_kernel(grads_own, shared_down_t, (back_other,))
+    ffn_slabs = join_kernel(ffn_parts, (shared_got, back_other))
+    shared_own = product_nt_kernel(grads_own, shared_down_t, (ffn_slabs,))
     shared_other = product_nt_kernel(grads_other, shared_down_t, (shared_own,))
-    ffn_slabs = join_kernel(ffn_parts, (shared_other,))
-    ffn_own = gather_plane(ffn_slabs)
+    half = ffn_slabs.shape[0] // 2
+    over_x, over_y = (swap(ffn_slabs, "x"), swap(ffn_slabs, "y"))
+    ffn_own = join_kernel(
+        [ffn_slabs, over_y, over_x],
+        (shared_other,),
+        [swap(over_y[:half], "x"), swap(over_x[half:], "y")],
+    )
     ffn_other = swap(ffn_own, "c").reshape(-1, width)
-    ffn_own = ffn_own.reshape(-1, width)
 
     relative = all_routes.reshape(zs, 2, 2, sequences, block, TOPK)
     relative = by_own(by_own(by_own(relative, "x", 1), "c", 2), "y", 3)
@@ -1497,7 +1532,6 @@
     )
     zero = jnp.zeros((1,), jnp.int32)
     (out_grads,) = out_grads_kernel(zero, 1, head_out, attention_grad, rows_here)
-    grad_out = lax.psum_scatter(out_grads, "z", scatter_dimension=0, tiled=True)
     key_own, key_other, query_grad, grad_up_here = attend_back_kernel(
         attention_grad,
         query_low,
@@ -1512,26 +1546,20 @@
         scale,
         (out_grads,),
     )
-    shape = (2, 2, zs * block, R + DR)
-    routed_slab = fold_second(routed_pieces, both_axes, zs, (key_own,))
-    key_pieces = core_fold_kernel(key_own, swap(key_other, "c"), routed_slab)
-    key_slab = fold_second(fold_first(key_pieces, ("y", "x")), ("y", "x"), zs)
-    key_sum = fold_z(key_slab)
     rope = query_grad[:, heads * DN :].reshape(sequences, slab, heads, DR)
     rope = rotate(rope, cosine[:, None, :], -sine[:, None, :]).reshape(sequences * slab, -1)
     query_raw_grad = low(jnp.concatenate([query_grad[:, : heads * DN], rope], axis=1))
-    input_grad = scatter_slab(*split_product_kernel(query_raw_grad, query_here, sequences))
-    (query_grads,) = query_grads_kernel(
-        zero, 1, query_raw_grad, input_low, grad_up_here, rows_here
+    query_grads = query_grads_kernel(
+        query_raw_grad, input_low, grad_up_here, out_grads, rows_here
     )
     grad_heads = lax.psum_scatter(query_grads, "z", scatter_dimension=0, tiled=True)
-    output = both_halves(low(hidden_in + fold_z(routed_slab, jnp.float32, (key_sum,))))
-    shared_back = tie(shared_back, key_sum).astype(jnp.float32)
-    grad_shared_gate = shared_back[:, :shared_here].reshape(-1, rows_here).T
-    grad_shared_up = shared_back[:, shared_here : 2 * shared_here].reshape(-1, rows_here).T
-    grad_shared_down = shared_back[:, 2 * shared_here :].reshape(-1, rows_here)
-
-
+    key_pieces = core_fold_kernel(key_own, swap(key_other, "c"), (query_grads, shared_back))
+    input_grad = scatter_slab(
+        *split_product_kernel(query_raw_grad, query_here, sequences, (query_grads,))
+    )
+    key_slab = fold_second(fold_first(key_pieces, ("y", "x")), ("y", "x"), zs)
+    key_sum = fold_z(key_slab)
+    routed_slab = fold_second(routed_pieces, both_axes, zs, (key_sum,))
     latent_back, grad_latent_norm = root_norm_back(
         key_sum[:, :R], latent_unit, latent_inverse, full_latent_norm
     )
@@ -1543,6 +1571,13 @@
     )
     grad_down = fold_z(down_grads)
     latent_raw_grad = tie(latent_raw_grad, down_grads[0])
+    shared_back = shared_back.astype(jnp.float32)
+    grad_shared_gate = shared_back[:, :shared_here].reshape(-1, rows_here).T
+    grad_shared_up = shared_back[:, shared_here : 2 * shared_here].reshape(-1, rows_here).T
+    grad_shared_down = shared_back[:, 2 * shared_here :].reshape(-1, rows_here)
+
+
+    output = both_halves(low(hidden_in + fold_z(routed_slab, jnp.float32, (grad_down,))))
     latent_input = jnp.stack([dot_nt(latent_raw_grad, down) for down in down_pieces])
     latent_input = latent_input.reshape(2, 2, block, zs, rows_here)
     latent_input = by_own(by_own(latent_input, "c", 0), "x", 1)
@@ -1552,7 +1587,8 @@
     )
     tokens_gradient = both_halves(low(grad_hidden + source_part)).astype(jnp.float32)
 
-    both = trade(jnp.concatenate([grad_heads, grad_out], axis=2), ("x", "c")).astype(jnp.float32)
+    traded = trade(grad_heads, ("x", "c"))
+    both = traded.astype(jnp.float32)
     out_at = both.shape[2] - head_rows
     grad_output = jnp.transpose(
         both[..., out_at:].reshape(4, DV, heads, rows_here), (0, 2, 1, 3)

time: 742 us -> 690 us (0.930)
  local copies, waits for them, and re-layouts: 101 us -> 77.1 us
  other arithmetic: 69 us -> 48.5 us
  Pallas kernels: 236 us -> 251 us
  starting transfers between devices: 114 us -> 102 us
  waiting for transfers between devices: 182 us -> 171 us
    ppermute x12 -> x9, waiting for transfers between devices: 13.5 us -> 31.7 us  [from_z(): lax.ppermute(value, 'z', [((i + steps) % count, i) for i in range(count)])]
    ppermute x12, waiting for transfers between devices: 33.4 us -> 15.6 us  [to_z(): lax.ppermute(value, 'z', [(i, (i + steps) % count) for i in range(count)])]
    another operation x22 -> x11, other arithmetic: 16.9 us -> 1.67 us  [gather_plane(): return jnp.stack([jnp.stack([rows, over_b]), jnp.stack([over_a, both])])]
    ppermute x64 -> x59, waiting for transfers between devices: 125 us -> 113 us  [swap(): return lax.ppermute(value, axis, [(0, 1), (1, 0)])]
    pallas_call x0 -> x2, Pallas kernels: none -> 10.7 us  [reorder_kernel(): pl.pallas_call(lambda places, a, b, c, d, dep, out: reorder_body(places,...]
    ppermute x12 -> x9, starting transfers between devices: 19.8 us -> 9.33 us  [from_z(): lax.ppermute(value, 'z', [((i + steps) % count, i) for i in range(count)])]
    dynamic_update_slice x7 -> x3, local copies, waits for them, and re-layouts: 7.7 us -> 0.06 us  [put(): whole = lax.dynamic_update_index_in_dim(whole, part, place, 0)]
    pallas_call x40 -> x41, Pallas kernels: 236 us -> 241 us  [local_call(): pl.pallas_call(run, grid=grid, in_specs=list(in_specs) + [pl.BlockSpec(me...]
  transfers between devices with their start and end apart: 96 -> 88, of which waited for: 41 -> 36; matrix products, arithmetic and copies ran while one was open for 19% -> 16% of each run, Pallas kernels for 23% -> 28%
where the time goes in v4:
time: 690 us; the launch traced here: 678 us
  Pallas kernels  251 us (36%)
  waiting for transfers between devices  171 us (25%)
  starting transfers between devices  102 us (15%)
  local copies, waits for them, and re-layouts  77.1 us (11%)
  other arithmetic  48.5 us (7%)
  between operations  18 us (3%)
  matrix products  11 us (2%)
    pallas_call x41, Pallas kernels, local_call(): pl.pallas_call(run, grid=grid, in_specs=list(in_specs) + [pl.BlockSpec(me...  241 us
    ppermute x59, waiting for transfers between devices, swap(): return lax.ppermute(value, axis, [(0, 1), (1, 0)])  113 us
    ppermute x59, starting transfers between devices, swap(): return lax.ppermute(value, axis, [(0, 1), (1, 0)])  52.3 us
    ppermute x9, waiting for transfers between devices, from_z(): lax.ppermute(value, 'z', [((i + steps) % count, i) for i in range(count)])  31.7 us
    all_to_all x4, starting transfers between devices, trade(): return lax.all_to_all(value, axes, split_axis=0, concat_axis=0, tiled=True)  23.4 us
    unnamed x192, local copies, waits for them, and re-layouts  21.3 us
    ppermute x12, waiting for transfers between devices, to_z(): lax.ppermute(value, 'z', [(i, (i + steps) % count) for i in range(count)])  15.6 us
    ppermute x12, starting transfers between devices, to_z(): lax.ppermute(value, 'z', [(i, (i + steps) % count) for i in range(count)])  14.8 us
  transfers between devices with their start and end apart: 88, of which 36 were waited for; matrix products, arithmetic and copies ran while one was open for 16% of the time, Pallas kernels for 28%

profile of v4, /device:TPU:16, one launch (start us, length us, event | category | flops | bytes accessed | tf_op | source)
XLA Modules:
  0.0 678.2 jit_solution(63840394938078819)
XLA Ops:
  12.9 9.3 %collective-permute-done.3 = bf16[128,768]{1,0:T(8,128)(2,1)S(1)} collective-permute-done((bf16[128,768]{1,0:T(8,128)(2,1)S(1)}, bf16[128,768]{1,0:T(8,128)(2,1)S(1)}, u32[]{:S(2)}, u32[]{:S(2)}) %collective-permute-start.3) | collective-permute-done | bytes 196640 | tf_op jit(solution)/shard_map/ppermute | solution.py:1132
  34.0 20.6 %collective-permute-done.5 = bf16[128,640]{1,0:T(8,128)(2,1)} collective-permute-done((bf16[128,640]{1,0:T(8,128)(2,1)S(1)}, bf16[128,640]{1,0:T(8,128)(2,1)}, u32[]{:S(2)}, u32[]{:S(2)}) %collective-permute-start.5) | collective-permute-done | bytes 163872 | tf_op jit(solution)/shard_map/ppermute | solution.py:1137
  56.5 5.3 collective-permute-done.7
  67.3 3.9 collective-permute-done.8
  84.3 7.1 %collective-permute-done.11 = bf16[64,576]{1,0:T(8,128)(2,1)S(1)} collective-permute-done((bf16[64,576]{1,0:T(8,128)(2,1)S(1)}, bf16[64,576]{1,0:T(8,128)(2,1)S(1)}, u32[]{:S(2)}, u32[]{:S(2)}) %collective-permute-start.11) | collective-permute-done | bytes 73760 | tf_op jit(solution)/shard_map/ppermute | solution.py:1132
  95.2 5.8 collective-permute-done.14
  135.6 3.8 shard_map.288
  143.6 8.9 %shard_map.289 = (bf16[2,128,2048]{2,1,0:T(8,128)(2,1)}, bf16[2,128,2048]{2,1,0:T(8,128)(2,1)}, bf16[2,512,1024]{2,1,0:T(8,128)(2,1)}, bf16[2,512,512]{2,1,0:T(8...) custom-call(bf16[512,384]{1,0:T(8,128)(2,1)} %pad_maximum_fusion.12.refs_0_.refs_1_, ...), custom_call_target="tpu_custom_call" | custom-call | flops 1 | bytes 1 | tf_op jit(solution)/shard_map/pallas_call | solution.py:503
  155.8 8.1 %all-to-all-start = ((bf16[16,264,128]{2,1,0:T(8,128)(2,1)}), bf16[16,264,128]{2,1,0:T(8,128)(2,1)S(1)}, u32[]{:S(2)}, u32[]{:S(2)}) async-start(bf16[16,264,128]{2,1,0:T(8,128)(2,1)} %maximum_add_fusion), calls=%async_computation | async-start | bytes 2162688 | tf_op jit(solution)/shard_map/all_to_all | solution.py:1146
  170.5 5.5 collective-permute-done.24.refs_1_
  183.8 5.5 collective-permute-done.26.refs_1_
  198.6 5.4 shard_map.294.refs_0_.refs_4_
  203.9 7.4 %shard_map.295.refs_2_.refs_1_ = bf16[1024,704]{1,0:T(8,128)(2,1)} custom-call(bf16[1024,2048]{1,0:T(8,128)(2,1)} %shard_map.294.refs_0_.refs_4_, bf16[704,2048]{1,0:T(8,128)(2,1)} %bitcast.281), custom_call_target="tpu_custom_call" | custom-call | flops 1 | bytes 1 | tf_op jit(solution)/shard_map/pallas_call | solution.py:503
  211.3 5.4 shard_map.293.refs_0_.refs_5_
  216.7 7.4 %shard_map.296.refs_5_.refs_1_ = bf16[1024,704]{1,0:T(8,128)(2,1)} custom-call(bf16[1024,2048]{1,0:T(8,128)(2,1)} %shard_map.293.refs_0_.refs_5_, bf16[704,2048]{1,0:T(8,128)(2,1)} %bitcast.282, bf16[1024,704]{1,0:T(8,128)(2,1)} %shard_map.295.refs_2_.refs_1_), custom_call_target="tpu_custom_call" | custom-call | flops 1 | bytes 1 | tf_op jit(solution)/shard_map/pallas_call | solution.py:503
  231.3 21.0 %collective-permute-done.32.refs_2_ = bf16[256,2048]{1,0:T(8,128)(2,1)S(1)} collective-permute-done((bf16[256,2048]{1,0:T(8,128)(2,1)}, bf16[256,2048]{1,0:T(8,128)(2,1)S(1)}, u32[]{:S(2)}, u32[]{:S(2)}) %collective-permute-start.32) | collective-permute-done | bytes 1048608 | tf_op jit(solution)/shard_map/ppermute | solution.py:1132
  257.4 4.8 shard_map.298.refs_2_
  262.2 4.8 shard_map.299.refs_5_.refs_2_
  267.0 4.4 shard_map.300.refs_0_.refs_4_
  275.4 3.6 collective-permute-done.35.refs_0_.refs_5_
  279.0 16.2 %shard_map.302 = (bf16[1024,704]{1,0:T(8,128)(2,1)}, bf16[1024,128]{1,0:T(8,128)(2,1)}, bf16[1024,704]{1,0:T(8,128)(2,1)}, bf16[1024,704]{1,0:T(8,128)(2,1)}, bf...) custom-call(bf16[1024,2048]{1,0:T(8,128)(2,1)} %collective-permute-done.35.refs_0_.refs_5_, ...), custom_call_target="tpu_custom_call" | custom-call | flops 1 | bytes 1 | tf_op jit(solution)/shard_map/pallas_call | solution.py:503
  295.1 12.9 %shard_map.303.refs_8_ = bf16[1024,2176]{1,0:T(8,128)(2,1)} custom-call(bf16[1024,704]{1,0:T(8,128)(2,1)} %get-tuple-element.126.refs_0_.refs_1_, bf16[1024,704]{1,0:T(8,128)(2,1)} %get-tuple-element.127.refs_1_, bf16[1024,256]{1,0:T(8,128)(2,1)} %get-tuple-element.128.refs_2_.refs_3_, bf16[704,2048]{1,0:T(8,128)(2,1)} %bitcast.274, ...), custom_call_target="tpu_custom_call" | custom-call | flops 1 | bytes 1 | tf_op jit(solution)/shard_map/pallas_call | solution.py:503
  309.5 16.3 %shard_map.301 = (bf16[1024,704]{1,0:T(8,128)(2,1)}, bf16[1024,128]{1,0:T(8,128)(2,1)}, bf16[1024,704]{1,0:T(8,128)(2,1)}, bf16[1024,704]{1,0:T(8,128)(2,1)}, bf...) custom-call(bf16[1024,2048]{1,0:T(8,128)(2,1)} %shard_map.300.refs_0_.refs_4_, bf16[1024,704]{1,0:T(8,128)(2,1)} %shard_map.295.refs_2_.refs_1_, ...), custom_call_target="tpu_custom_call" | custom-call | flops 1 | bytes 1 | tf_op jit(solution)/shard_map/pallas_call | solution.py:503
  325.8 12.9 %shard_map.304 = bf16[1024,2176]{1,0:T(8,128)(2,1)} custom-call(bf16[1024,704]{1,0:T(8,128)(2,1)} %get-tuple-element.122.refs_0_, bf16[1024,704]{1,0:T(8,128)(2,1)} %get-tuple-element.123.refs_1_.refs_0_, bf16[1024,256]{1,0:T(8,128)(2,1)} %get-tuple-element.124.refs_2_, bf16[704,2048]{1,0:T(8,128)(2,1)} %bitcast.276, bf16[704,2048]{1,0:T(8,128)(2,1)} %bitcast.280, ...), custom_call_target="tpu_custom_call" | custom-call | flops 1 | bytes 1 | tf_op jit(solution)/shard_map/pallas_call | solution.py:503
  338.7 5.3 shard_map.305
  344.1 8.1 %shard_map.306.refs_4_ = bf16[1024,2048]{1,0:T(8,128)(2,1)} custom-call(bf16[1024,704]{1,0:T(8,128)(2,1)} %get-tuple-element.120.refs_0_.refs_1_, bf16[1024,128]{1,0:T(8,128)(2,1)} %get-tuple-element.121.refs_1_.refs_3_, bf16[704,2048]{1,0:T(8,128)(2,1)} %bitcast.283, bf16[128,2048]{1,0:T(8,128)(2,1)} %get-tuple-element.307.refs_1_.refs_3_, ...), custom_call_target="tpu_custom_call" | custom-call | flops 1 | bytes 1 | tf_op jit(solution)/shard_map/pallas_call | solution.py:503
  354.9 8.1 %shard_map.307.refs_6_ = bf16[1024,2048]{1,0:T(8,128)(2,1)} custom-call(bf16[1024,704]{1,0:T(8,128)(2,1)} %get-tuple-element.118.refs_0_, bf16[1024,128]{1,0:T(8,128)(2,1)} %get-tuple-element.119.refs_1_.refs_2_, bf16[704,2048]{1,0:T(8,128)(2,1)} %bitcast.284, bf16[128,2048]{1,0:T(8,128)(2,1)} %get-tuple-element.307.refs_1_.refs_3_, ...), custom_call_target="tpu_custom_call" | custom-call | flops 1 | bytes 1 | tf_op jit(solution)/shard_map/pallas_call | solution.py:503
  363.0 14.0 %shard_map.308 = (f32[704,2048]{1,0:T(8,128)}, bf16[128,2048]{1,0:T(8,128)(2,1)}) custom-call(bf16[1024,704]{1,0:T(8,128)(2,1)} %get-tuple-element.123.refs_1_.refs_0_, bf16[1024,704]{1,0:T(8,128)(2,1)} %get-tuple-element.127.refs_1_, bf16[1024,256]{1,0:T(8,128)(2,1)} %get-tuple-element.124.refs_2_, bf16[1024,256]{1,0:T(8,128)(2,1)} %get-tuple-element.128.refs_2_.refs_3_, ...), custom_call_target="tpu_custom_call" | custom-call | flops 1 | bytes 1 | tf_op jit(solution)/shard_map/pallas_call | solution.py:503
  381.3 3.4 shard_map.309
  387.5 14.0 %shard_map.310 = (f32[704,2048]{1,0:T(8,128)}, bf16[128,2048]{1,0:T(8,128)(2,1)}) custom-call(bf16[1024,704]{1,0:T(8,128)(2,1)} %get-tuple-element.118.refs_0_, bf16[1024,704]{1,0:T(8,128)(2,1)} %get-tuple-element.120.refs_0_.refs_1_, bf16[1024,128]{1,0:T(8,128)(2,1)} %get-tuple-element.119.refs_1_.refs_2_, ...), custom_call_target="tpu_custom_call" | custom-call | flops 1 | bytes 1 | tf_op jit(solution)/shard_map/pallas_call | solution.py:503
  405.3 5.3 shard_map.312
  416.7 14.0 %shard_map.313 = (f32[704,2048]{1,0:T(8,128)}, bf16[128,2048]{1,0:T(8,128)(2,1)}) custom-call(bf16[1024,704]{1,0:T(8,128)(2,1)} %get-tuple-element.122.refs_0_, bf16[1024,704]{1,0:T(8,128)(2,1)} %get-tuple-element.126.refs_0_.refs_1_, bf16[1024,256]{1,0:T(8,128)(2,1)} %get-tuple-element.124.refs_2_, bf16[1024,256]{1,0:T(8,128)(2,1)} %get-tuple-element.128.refs_2_.refs_3_, ...), custom_call_target="tpu_custom_call" | custom-call | flops 1 | bytes 1 | tf_op jit(solution)/shard_map/pallas_call | solution.py:503
  430.7 3.6 collective-permute-done.42.refs_1_
  447.3 4.8 collective-permute-done.50
  461.6 5.2 all-to-all-start.1
  469.8 3.4 shard_map.316.refs_9_.refs_3_
  473.2 13.9 %shard_map.317 = (bf16[2,2,256,576]{3,2,1,0:T(8,128)(2,1)}, bf16[2,2,256,576]{3,2,1,0:T(8,128)(2,1)}, f32[512,384]{1,0:T(8,128)}, f32[512,512]{1,0:T(8,128)}) custom-call(bf16[512,2048]{1,0:T(8,128)(2,1)} %bitcast.286, bf16[512,384]{1,0:T(8,128)(2,1)} %pad_maximum_fusion.12.refs_0_.refs_1_, bf16[2,2,256,576]{3,2,1,0:T(8,128)(2,1)} %copy-done, ...), custom_call_target="tpu_custom_call" | custom-call | flops 1 | bytes 1 | tf_op jit(solution)/shard_map/pallas_call | solution.py:503
  499.2 5.4 shard_map.318.refs_8_.refs_2_
  513.7 7.3 %collective-permute-done.55.refs_1_ = bf16[2,128,576]{2,1,0:T(8,128)(2,1)S(1)} collective-permute-done((bf16[2,128,576]{2,1,0:T(8,128)(2,1)}, bf16[2,128,576]{2,1,0:T(8,128)(2,1)S(1)}, u32[]{:S(2)}, u32[]{:S(2)}) %collective-permute-start.55) | collective-permute-done | bytes 294944 | tf_op jit(solution)/shard_map/ppermute | solution.py:1132
  527.0 3.5 collective-permute-done.57.refs_1_
  538.2 4.0 shard_map.327
  558.0 7.3 %collective-permute-done.68 = bf16[32,576]{1,0:T(8,128)(2,1)S(1)} collective-permute-done((bf16[32,576]{1,0:T(8,128)(2,1)S(1)}, bf16[32,576]{1,0:T(8,128)(2,1)S(1)}, u32[]{:S(2)}, u32[]{:S(2)}) %collective-permute-start.68) | collective-permute-done | bytes 36896 | tf_op jit(solution)/shard_map/ppermute | solution.py:1132
  566.5 3.9 collective-permute-done.67
  610.7 6.6 all-to-all-start.2
  617.2 12.2 %collective-permute-done.70.refs_1_ = bf16[128,576]{1,0:T(8,128)(2,1)S(1)} collective-permute-done((bf16[128,576]{1,0:T(8,128)(2,1)}, bf16[128,576]{1,0:T(8,128)(2,1)S(1)}, u32[]{:S(2)}, u32[]{:S(2)}) %collective-permute-start.70) | collective-permute-done | bytes 147488 | tf_op jit(solution)/shard_map/ppermute | solution.py:1142
  646.2 4.2 collective-permute-done.80
  652.1 3.5 all-to-all-start.3
  656.6 10.7 %all-to-all-done.3 = bf16[4,128,768]{2,1,0:T(8,128)(2,1)S(1)} async-done(((bf16[4,128,768]{2,1,0:T(8,128)(2,1)}), bf16[4,128,768]{2,1,0:T(8,128)(2,1)S(1)}, u32[]{:S(2)}, u32[]{:S(2)}) %all-to-all-start.3) | async-done | bytes 786464 | tf_op jit(solution)/shard_map/all_to_all | solution.py:1146
  (596 shorter events, 282.3 us)
Async XLA Ops:
  7.2 128.4 %all-gather.6.cloned.1.call-start = ((), (), s32[]{:S(2)}) async-start(), calls=%async_computation.7 | async-start | bytes 3932160 | tf_op jit(solution)/shard_map/all_gather | solution.py:1351
  10.7 11.5 %collective-permute-start.4 = (bf16[128,768]{1,0:T(8,128)(2,1)S(1)}, bf16[128,768]{1,0:T(8,128)(2,1)S(1)}, u32[]{:S(2)}, u32[]{:S(2)}) collective-permute-start(bf16[128,768]{1,0:T(8,128)(2,1)S(1)} %get-tuple-element.316), channel_id=1, source_target_pairs={{0,6},{2,4},{4,2},{6,0},{1,7},{3,5},{5,3},{7,1},{8,14},{10,12},{12... | collective-permute-start | bytes 589832 | tf_op jit(solution)/shard_map/ppermute | solution.py:1316
  23.2 175.4 %all-gather.4.cloned.1.call-start = ((), (), s32[]{:S(2)}) async-start(), calls=%async_computation.5 | async-start | bytes 8650752 | tf_op jit(solution)/shard_map/all_gather | solution.py:1342
  27.0 28.5 %collective-permute-start.6 = (bf16[128,640]{1,0:T(8,128)(2,1)S(1)}, bf16[128,640]{1,0:T(8,128)(2,1)}, u32[]{:S(2)}, u32[]{:S(2)}) collective-permute-start(bf16[128,640]{1,0:T(8,128)(2,1)S(1)} %pad.21), channel_id=1, source_target_pairs={{16,0},{24,8},{0,16},{8,24},{17,1},{25,9},{1,17},{9,25},{18,2},{26... | collective-permute-start | bytes 491528 | tf_op jit(solution)/shard_map/ppermute | solution.py:1137
  27.2 27.4 %collective-permute-start.5 = (bf16[128,640]{1,0:T(8,128)(2,1)S(1)}, bf16[128,640]{1,0:T(8,128)(2,1)}, u32[]{:S(2)}, u32[]{:S(2)}) collective-permute-start(bf16[128,640]{1,0:T(8,128)(2,1)S(1)} %pad.21), channel_id=1, source_target_pairs={{8,0},{16,8},{24,16},{0,24},{9,1},{17,9},{25,17},{1,25},{10,2},{18... | collective-permute-start | bytes 491528 | tf_op jit(solution)/shard_map/ppermute | solution.py:1137
  30.1 31.7 %collective-permute-start.7 = (bf16[128,640]{1,0:T(8,128)(2,1)S(1)}, bf16[128,640]{1,0:T(8,128)(2,1)}, u32[]{:S(2)}, u32[]{:S(2)}) collective-permute-start(bf16[128,640]{1,0:T(8,128)(2,1)S(1)} %pad.21), channel_id=1, source_target_pairs={{24,0},{0,8},{8,16},{16,24},{25,1},{1,9},{9,17},{17,25},{26,2},{2,... | collective-permute-start | bytes 491528 | tf_op jit(solution)/shard_map/ppermute | solution.py:1137
  30.2 32.5 %collective-permute-start = (bf16[2,64,2048]{2,1,0:T(8,128)(2,1)S(1)}, bf16[2,64,2048]{2,1,0:T(8,128)(2,1)}, u32[]{:S(2)}, u32[]{:S(2)}) collective-permute-start(bf16[2,64,2048]{2,1,0:T(8,128)(2,1)S(1)} %reverse_select_fusion.5), channel_id=1, source_target_pairs={{0,4},{4,0},{1,5},{5,1},{2,6},{6,2},{3,7},{7,3},{8,12},{12,8},{9,1... | collective-permute-start | bytes 1572872 | tf_op jit(solution)/shard_map/ppermute | solution.py:1132
  65.1 11.1 %collective-permute-start.1 = (bf16[2,2,64,2048]{3,2,0,1:T(8,128)(2,1)}, bf16[2,2,64,2048]{3,2,0,1:T(8,128)(2,1)S(1)}, u32[]{:S(2)}, u32[]{:S(2)}) collective-permute-start(bf16[2,2,64,2048]{3,2,0,1:T(8,128)(2,1)} %get-tuple-element.315), channel_id=1, source_target_pairs={{0,2},{2,0},{1,3},{3,1},{4,6},{6,4},{5,7},{7,5},{8,10},{10,8},{9,1... | collective-permute-start | bytes 3145736 | tf_op jit(solution)/shard_map/ppermute | solution.py:1132
  73.7 34.8 %collective-permute-start.20 = (bf16[512,576]{0,1:T(8,128)(2,1)}, bf16[512,576]{0,1:T(8,128)(2,1)}, u32[]{:S(2)}, u32[]{:S(2)}) collective-permute-start(bf16[512,576]{0,1:T(8,128)(2,1)} %copy.292), channel_id=1, source_target_pairs={{0,4},{4,0},{1,5},{5,1},{2,6},{6,2},{3,7},{7,3},{8,12},{12,8},{9,1... | collective-permute-start | bytes 1769480 | tf_op jit(solution)/shard_map/ppermute | solution.py:1132
  108.5 16.4 %collective-permute-start.21 = (bf16[512,576]{0,1:T(8,128)(2,1)}, bf16[512,576]{0,1:T(8,128)(2,1)}, u32[]{:S(2)}, u32[]{:S(2)}) collective-permute-start(bf16[512,576]{0,1:T(8,128)(2,1)} %copy.292), channel_id=1, source_target_pairs={{0,2},{2,0},{1,3},{3,1},{4,6},{6,4},{5,7},{7,5},{8,10},{10,8},{9,1... | collective-permute-start | bytes 1769480 | tf_op jit(solution)/shard_map/ppermute | solution.py:1132
  108.5 18.5 %collective-permute-start.22 = (bf16[512,576]{0,1:T(8,128)(2,1)}, bf16[512,576]{0,1:T(8,128)(2,1)}, u32[]{:S(2)}, u32[]{:S(2)}) collective-permute-start(bf16[512,576]{0,1:T(8,128)(2,1)} %collective-permute-done.20), channel_id=1, source_target_pairs={{0,2},{2,0},{1,3},{3,1},{4,6},{6,4},{5,7},{7,5},{8,10},{10,8},{9,1... | collective-permute-start | bytes 1769480 | tf_op jit(solution)/shard_map/ppermute | solution.py:1132
  152.5 11.4 %collective-permute-start.23 = (bf16[2,128,2048]{2,1,0:T(8,128)(2,1)}, bf16[2,128,2048]{2,1,0:T(8,128)(2,1)S(1)}, u32[]{:S(2)}, u32[]{:S(2)}) collective-permute-start(bf16[2,128,2048]{2,1,0:T(8,128)(2,1)} %get-tuple-element.109), channel_id=1, source_target_pairs={{0,2},{2,0},{1,3},{3,1},{4,6},{6,4},{5,7},{7,5},{8,10},{10,8},{9,1... | collective-permute-start | bytes 3145736 | tf_op jit(solution)/shard_map/ppermute | solution.py:1132
  155.8 68.4 %all-to-all-start = ((bf16[16,264,128]{2,1,0:T(8,128)(2,1)}), bf16[16,264,128]{2,1,0:T(8,128)(2,1)S(1)}, u32[]{:S(2)}, u32[]{:S(2)}) async-start(bf16[16,264,128]{2,1,0:T(8,128)(2,1)} %maximum_add_fusion), calls=%async_computation | async-start | bytes 2162688 | tf_op jit(solution)/shard_map/all_to_all | solution.py:1146
  193.3 30.8 %collective-permute-start.30 = (bf16[64,2048]{1,0:T(8,128)(2,1)S(1)}, bf16[64,2048]{1,0:T(8,128)(2,1)S(1)}, u32[]{:S(2)}, u32[]{:S(2)}) collective-permute-start(bf16[64,2048]{1,0:T(8,128)(2,1)S(1)} %multiply_convert_fusion.1.dep.refs_0_), channel_id=1, source_target_pairs={{24,0},{0,8},{8,16},{16,24},{25,1},{1,9},{9,17},{17,25},{26,2},{2,... | collective-permute-start | bytes 786440 | tf_op jit(solution)/shard_map/ppermute | solution.py:1137
  195.1 29.0 %collective-permute-start.29 = (bf16[64,2048]{1,0:T(8,128)(2,1)S(1)}, bf16[64,2048]{1,0:T(8,128)(2,1)S(1)}, u32[]{:S(2)}, u32[]{:S(2)}) collective-permute-start(bf16[64,2048]{1,0:T(8,128)(2,1)S(1)} %multiply_convert_fusion.1.dep.refs_0_), channel_id=1, source_target_pairs={{16,0},{24,8},{0,16},{8,24},{17,1},{25,9},{1,17},{9,25},{18,2},{26... | collective-permute-start | bytes 786440 | tf_op jit(solution)/shard_map/ppermute | solution.py:1137
  195.1 29.0 %collective-permute-start.28 = (bf16[64,2048]{1,0:T(8,128)(2,1)S(1)}, bf16[64,2048]{1,0:T(8,128)(2,1)S(1)}, u32[]{:S(2)}, u32[]{:S(2)}) collective-permute-start(bf16[64,2048]{1,0:T(8,128)(2,1)S(1)} %multiply_convert_fusion.1.dep.refs_0_), channel_id=1, source_target_pairs={{8,0},{16,8},{24,16},{0,24},{9,1},{17,9},{25,17},{1,25},{10,2},{18... | collective-permute-start | bytes 786440 | tf_op jit(solution)/shard_map/ppermute | solution.py:1137
  228.2 24.1 %collective-permute-start.32 = (bf16[256,2048]{1,0:T(8,128)(2,1)}, bf16[256,2048]{1,0:T(8,128)(2,1)S(1)}, u32[]{:S(2)}, u32[]{:S(2)}) collective-permute-start(bf16[256,2048]{1,0:T(8,128)(2,1)} %shard_map.297.refs_2_.refs_0_), channel_id=1, source_target_pairs={{0,4},{4,0},{1,5},{5,1},{2,6},{6,2},{3,7},{7,3},{8,12},{12,8},{9,1... | collective-permute-start | bytes 3145736 | tf_op jit(solution)/shard_map/ppermute | solution.py:1132
  230.5 23.6 %collective-permute-start.31 = (bf16[256,2048]{1,0:T(8,128)(2,1)}, bf16[256,2048]{1,0:T(8,128)(2,1)S(1)}, u32[]{:S(2)}, u32[]{:S(2)}) collective-permute-start(bf16[256,2048]{1,0:T(8,128)(2,1)} %shard_map.297.refs_2_.refs_0_), channel_id=1, source_target_pairs={{0,1},{1,0},{2,3},{3,2},{4,5},{5,4},{6,7},{7,6},{8,9},{9,8},{10,11... | collective-permute-start | bytes 3145736 | tf_op jit(solution)/shard_map/ppermute | solution.py:1132
  253.2 13.8 %collective-permute-start.34 = (bf16[128,2048]{1,0:T(8,128)(2,1)}, bf16[128,2048]{1,0:T(8,128)(2,1)}, u32[]{:S(2)}, u32[]{:S(2)}) collective-permute-start(bf16[128,2048]{1,0:T(8,128)(2,1)} %slice.348), channel_id=1, source_target_pairs={{0,1},{1,0},{2,3},{3,2},{4,5},{5,4},{6,7},{7,6},{8,9},{9,8},{10,11... | collective-permute-start | bytes 1572872 | tf_op jit(solution)/shard_map/ppermute | solution.py:1132
  255.1 12.0 %collective-permute-start.33 = (bf16[128,2048]{1,0:T(8,128)(2,1)}, bf16[128,2048]{1,0:T(8,128)(2,1)}, u32[]{:S(2)}, u32[]{:S(2)}) collective-permute-start(bf16[128,2048]{1,0:T(8,128)(2,1)} %slice.347), channel_id=1, source_target_pairs={{0,4},{4,0},{1,5},{5,1},{2,6},{6,2},{3,7},{7,3},{8,12},{12,8},{9,1... | collective-permute-start | bytes 1572872 | tf_op jit(solution)/shard_map/ppermute | solution.py:1132
  308.1 30.7 %collective-permute-start.36 = (bf16[1024,2176]{1,0:T(8,128)(2,1)}, bf16[1024,2176]{1,0:T(8,128)(2,1)}, u32[]{:S(2)}, u32[]{:S(2)}) collective-permute-start(bf16[1024,2176]{1,0:T(8,128)(2,1)} %shard_map.303.refs_8_), channel_id=1, source_target_pairs={{0,2},{2,0},{1,3},{3,1},{4,6},{6,4},{5,7},{7,5},{8,10},{10,8},{9,1... | collective-permute-start | bytes 13369352 | tf_op jit(solution)/shard_map/ppermute | solution.py:1132
  352.2 53.1 %collective-permute-start.37 = (bf16[1024,2048]{1,0:T(8,128)(2,1)}, bf16[1024,2048]{1,0:T(8,128)(2,1)}, u32[]{:S(2)}, u32[]{:S(2)}) collective-permute-start(bf16[1024,2048]{1,0:T(8,128)(2,1)} %shard_map.306.refs_4_), channel_id=1, source_target_pairs={{0,2},{2,0},{1,3},{3,1},{4,6},{6,4},{5,7},{7,5},{8,10},{10,8},{9,1... | collective-permute-start | bytes 12582920 | tf_op jit(solution)/shard_map/ppermute | solution.py:1132
  352.6 26.8 %collective-permute-start.38 = (bf16[2,128,2176]{2,1,0:T(8,128)(2,1)}, bf16[2,128,2176]{2,1,0:T(8,128)(2,1)S(1)}, u32[]{:S(2)}, u32[]{:S(2)}) collective-permute-start(bf16[2,128,2176]{2,1,0:T(8,128)(2,1)} %get-tuple-element.131.refs_5_), channel_id=1, source_target_pairs={{0,4},{4,0},{1,5},{5,1},{2,6},{6,2},{3,7},{7,3},{8,12},{12,8},{9,1... | collective-permute-start | bytes 3342344 | tf_op jit(solution)/shard_map/ppermute | solution.py:1132
  353.8 26.5 %collective-permute-start.39 = (bf16[2,128,2176]{2,1,0:T(8,128)(2,1)}, bf16[2,128,2176]{2,1,0:T(8,128)(2,1)S(1)}, u32[]{:S(2)}, u32[]{:S(2)}) collective-permute-start(bf16[2,128,2176]{2,1,0:T(8,128)(2,1)} %get-tuple-element.133.refs_7_), channel_id=1, source_target_pairs={{0,1},{1,0},{2,3},{3,2},{4,5},{5,4},{6,7},{7,6},{8,9},{9,8},{10,11... | collective-permute-start | bytes 3342344 | tf_op jit(solution)/shard_map/ppermute | solution.py:1132
  384.7 16.8 %collective-permute-start.40 = (bf16[128,2176]{1,0:T(8,128)(2,1)}, bf16[128,2176]{1,0:T(8,128)(2,1)S(1)}, u32[]{:S(2)}, u32[]{:S(2)}) collective-permute-start(bf16[128,2176]{1,0:T(8,128)(2,1)} %get-tuple-element.136.refs_7_), channel_id=1, source_target_pairs={{0,1},{1,0},{2,3},{3,2},{4,5},{5,4},{6,7},{7,6},{8,9},{9,8},{10,11... | collective-permute-start | bytes 1671176 | tf_op jit(solution)/shard_map/ppermute | solution.py:1132
  386.1 15.4 %collective-permute-start.41 = (bf16[128,2176]{1,0:T(8,128)(2,1)}, bf16[128,2176]{1,0:T(8,128)(2,1)S(1)}, u32[]{:S(2)}, u32[]{:S(2)}) collective-permute-start(bf16[128,2176]{1,0:T(8,128)(2,1)} %get-tuple-element.138.refs_9_), channel_id=1, source_target_pairs={{0,4},{4,0},{1,5},{5,1},{2,6},{6,2},{3,7},{7,3},{8,12},{12,8},{9,1... | collective-permute-start | bytes 1671176 | tf_op jit(solution)/shard_map/ppermute | solution.py:1132
  410.5 23.7 %collective-permute-start.42 = (bf16[2,128,2048]{2,1,0:T(8,128)(2,1)}, bf16[2,128,2048]{2,1,0:T(8,128)(2,1)S(1)}, u32[]{:S(2)}, u32[]{:S(2)}) collective-permute-start(bf16[2,128,2048]{2,1,0:T(8,128)(2,1)} %get-tuple-element.145.refs_7_), channel_id=1, source_target_pairs={{0,4},{4,0},{1,5},{5,1},{2,6},{6,2},{3,7},{7,3},{8,12},{12,8},{9,1... | collective-permute-start | bytes 3145736 | tf_op jit(solution)/shard_map/ppermute | solution.py:1132
  411.2 23.7 %collective-permute-start.43 = (bf16[2,128,2048]{2,1,0:T(8,128)(2,1)}, bf16[2,128,2048]{2,1,0:T(8,128)(2,1)S(1)}, u32[]{:S(2)}, u32[]{:S(2)}) collective-permute-start(bf16[2,128,2048]{2,1,0:T(8,128)(2,1)} %get-tuple-element.147.refs_9_), channel_id=1, source_target_pairs={{0,1},{1,0},{2,3},{3,2},{4,5},{5,4},{6,7},{7,6},{8,9},{9,8},{10,11... | collective-permute-start | bytes 3145736 | tf_op jit(solution)/shard_map/ppermute | solution.py:1132
  411.8 27.5 %collective-permute-start.46 = (bf16[64,2176]{1,0:T(8,128)(2,1)}, bf16[64,2176]{1,0:T(8,128)(2,1)}, u32[]{:S(2)}, u32[]{:S(2)}) collective-permute-start(bf16[64,2176]{1,0:T(8,128)(2,1)} %get-tuple-element.141.refs_9_), channel_id=1, source_target_pairs={{0,8},{8,16},{16,24},{24,0},{1,9},{9,17},{17,25},{25,1},{2,10},{10... | collective-permute-start | bytes 835592 | tf_op jit(solution)/shard_map/ppermute | solution.py:1142
  412.3 27.0 %collective-permute-start.47 = (bf16[64,2176]{1,0:T(8,128)(2,1)}, bf16[64,2176]{1,0:T(8,128)(2,1)}, u32[]{:S(2)}, u32[]{:S(2)}) collective-permute-start(bf16[64,2176]{1,0:T(8,128)(2,1)} %get-tuple-element.142.refs_10_), channel_id=1, source_target_pairs={{0,16},{8,24},{16,0},{24,8},{1,17},{9,25},{17,1},{25,9},{2,18},{10... | collective-permute-start | bytes 835592 | tf_op jit(solution)/shard_map/ppermute | solution.py:1142
  415.0 24.4 %collective-permute-start.48 = (bf16[64,2176]{1,0:T(8,128)(2,1)}, bf16[64,2176]{1,0:T(8,128)(2,1)}, u32[]{:S(2)}, u32[]{:S(2)}) collective-permute-start(bf16[64,2176]{1,0:T(8,128)(2,1)} %get-tuple-element.143.refs_11_), channel_id=1, source_target_pairs={{0,24},{8,0},{16,8},{24,16},{1,25},{9,1},{17,9},{25,17},{2,26},{10... | collective-permute-start | bytes 835592 | tf_op jit(solution)/shard_map/ppermute | solution.py:1142
  461.6 45.3 %all-to-all-start.1 = ((bf16[16,264,128]{2,1,0:T(8,128)(2,1)}), bf16[16,264,128]{2,1,0:T(8,128)(2,1)S(1)}, u32[]{:S(2)}, u32[]{:S(2)}) async-start(bf16[16,264,128]{2,1,0:T(8,128)(2,1)} %bitcast_bitcast_fusion), calls=%async_computation.1 | async-start | bytes 2162688 | tf_op jit(solution)/shard_map/all_to_all | solution.py:1146
  466.8 185.3 %reduce-scatter.2.cloned.1.call-start = ((), (), s32[]{:S(2)}) async-start(), calls=%async_computation.6 | async-start | bytes 3932160 | tf_op jit(solution)/shard_map/reduce_scatter | solution.py:1555
  488.8 15.8 %collective-permute-start.54 = (bf16[2,2,256,576]{2,3,1,0:T(8,128)(2,1)S(1)}, bf16[2,2,256,576]{2,3,1,0:T(8,128)(2,1)}, u32[]{:S(2)}, u32[]{:S(2)}) collective-permute-start(bf16[2,2,256,576]{2,3,1,0:T(8,128)(2,1)S(1)} %copy.311), channel_id=1, source_target_pairs={{0,2},{2,0},{1,3},{3,1},{4,6},{6,4},{5,7},{7,5},{8,10},{10,8},{9,1... | collective-permute-start | bytes 3538952 | tf_op jit(solution)/shard_map/ppermute | solution.py:1132
  548.7 35.7 %collective-permute-start.44 = (bf16[128,2048]{1,0:T(8,128)(2,1)}, bf16[128,2048]{1,0:T(8,128)(2,1)}, u32[]{:S(2)}, u32[]{:S(2)}) collective-permute-start(bf16[128,2048]{1,0:T(8,128)(2,1)} %get-tuple-element.150.refs_5_), channel_id=1, source_target_pairs={{0,1},{1,0},{2,3},{3,2},{4,5},{5,4},{6,7},{7,6},{8,9},{9,8},{10,11... | collective-permute-start | bytes 1572872 | tf_op jit(solution)/shard_map/ppermute | solution.py:1132
  550.2 34.2 %collective-permute-start.45 = (bf16[128,2048]{1,0:T(8,128)(2,1)}, bf16[128,2048]{1,0:T(8,128)(2,1)}, u32[]{:S(2)}, u32[]{:S(2)}) collective-permute-start(bf16[128,2048]{1,0:T(8,128)(2,1)} %get-tuple-element.152.refs_7_), channel_id=1, source_target_pairs={{0,4},{4,0},{1,5},{5,1},{2,6},{6,2},{3,7},{7,3},{8,12},{12,8},{9,1... | collective-permute-start | bytes 1572872 | tf_op jit(solution)/shard_map/ppermute | solution.py:1132
  555.4 17.0 %collective-permute-start.75 = (bf16[2,32,2048]{2,1,0:T(8,128)(2,1)}, bf16[2,32,2048]{2,1,0:T(8,128)(2,1)S(1)}, u32[]{:S(2)}, u32[]{:S(2)}) collective-permute-start(bf16[2,32,2048]{2,1,0:T(8,128)(2,1)} %get-tuple-element.187), channel_id=1, source_target_pairs={{0,1},{1,0},{2,3},{3,2},{4,5},{5,4},{6,7},{7,6},{8,9},{9,8},{10,11... | collective-permute-start | bytes 786440 | tf_op jit(solution)/shard_map/ppermute | solution.py:1132
  556.4 14.0 %collective-permute-start.67 = (bf16[32,576]{1,0:T(8,128)(2,1)S(1)}, bf16[32,576]{1,0:T(8,128)(2,1)S(1)}, u32[]{:S(2)}, u32[]{:S(2)}) collective-permute-start(bf16[32,576]{1,0:T(8,128)(2,1)S(1)} %slice.363), channel_id=1, source_target_pairs={{0,1},{1,0},{2,3},{3,2},{4,5},{5,4},{6,7},{7,6},{8,9},{9,8},{10,11... | collective-permute-start | bytes 110600 | tf_op jit(solution)/shard_map/ppermute | solution.py:1132
  571.4 21.2 %collective-permute-start.69 = (bf16[2,2,64,576]{3,2,1,0:T(8,128)(2,1)}, bf16[2,2,64,576]{3,2,1,0:T(8,128)(2,1)}, u32[]{:S(2)}, u32[]{:S(2)}) collective-permute-start(bf16[2,2,64,576]{3,2,1,0:T(8,128)(2,1)} %get-tuple-element.327), channel_id=1, source_target_pairs={{0,2},{2,0},{1,3},{3,1},{4,6},{6,4},{5,7},{7,5},{8,10},{10,8},{9,1... | collective-permute-start | bytes 884744 | tf_op jit(solution)/shard_map/ppermute | solution.py:1132
  587.1 51.0 %collective-permute-start.62 = (bf16[64,2048]{1,0:T(8,128)(2,1)}, bf16[64,2048]{1,0:T(8,128)(2,1)S(1)}, u32[]{:S(2)}, u32[]{:S(2)}) collective-permute-start(bf16[64,2048]{1,0:T(8,128)(2,1)} %get-tuple-element.177), channel_id=1, source_target_pairs={{0,8},{8,16},{16,24},{24,0},{1,9},{9,17},{17,25},{25,1},{2,10},{10... | collective-permute-start | bytes 786440 | tf_op jit(solution)/shard_map/ppermute | solution.py:1142
  588.5 49.6 %collective-permute-start.63 = (bf16[64,2048]{1,0:T(8,128)(2,1)}, bf16[64,2048]{1,0:T(8,128)(2,1)}, u32[]{:S(2)}, u32[]{:S(2)}) collective-permute-start(bf16[64,2048]{1,0:T(8,128)(2,1)} %get-tuple-element.178), channel_id=1, source_target_pairs={{0,16},{8,24},{16,0},{24,8},{1,17},{9,25},{17,1},{25,9},{2,18},{10... | collective-permute-start | bytes 786440 | tf_op jit(solution)/shard_map/ppermute | solution.py:1142
  590.0 48.1 %collective-permute-start.64 = (bf16[64,2048]{1,0:T(8,128)(2,1)}, bf16[64,2048]{1,0:T(8,128)(2,1)}, u32[]{:S(2)}, u32[]{:S(2)}) collective-permute-start(bf16[64,2048]{1,0:T(8,128)(2,1)} %get-tuple-element.179), channel_id=1, source_target_pairs={{0,24},{8,0},{16,8},{24,16},{1,25},{9,1},{17,9},{25,17},{2,26},{10... | collective-permute-start | bytes 786440 | tf_op jit(solution)/shard_map/ppermute | solution.py:1142
  604.0 25.5 %collective-permute-start.70 = (bf16[128,576]{1,0:T(8,128)(2,1)}, bf16[128,576]{1,0:T(8,128)(2,1)S(1)}, u32[]{:S(2)}, u32[]{:S(2)}) collective-permute-start(bf16[128,576]{1,0:T(8,128)(2,1)} %get-tuple-element.181), channel_id=1, source_target_pairs={{0,8},{8,16},{16,24},{24,0},{1,9},{9,17},{17,25},{25,1},{2,10},{10... | collective-permute-start | bytes 442376 | tf_op jit(solution)/shard_map/ppermute | solution.py:1142
  604.0 26.7 %collective-permute-start.71 = (bf16[128,576]{1,0:T(8,128)(2,1)}, bf16[128,576]{1,0:T(8,128)(2,1)}, u32[]{:S(2)}, u32[]{:S(2)}) collective-permute-start(bf16[128,576]{1,0:T(8,128)(2,1)} %get-tuple-element.182), channel_id=1, source_target_pairs={{0,16},{8,24},{16,0},{24,8},{1,17},{9,25},{17,1},{25,9},{2,18},{10... | collective-permute-start | bytes 442376 | tf_op jit(solution)/shard_map/ppermute | solution.py:1142
  610.7 34.0 %all-to-all-start.2 = ((f32[16,19,128]{2,1,0:T(8,128)}), f32[16,19,128]{2,1,0:T(8,128)S(1)}, u32[]{:S(2)}, u32[]{:S(2)}) async-start(f32[16,19,128]{2,1,0:T(8,128)} %fusion.18), calls=%async_computation.2 | async-start | bytes 393216 | tf_op jit(solution)/shard_map/all_to_all | solution.py:1146
  630.8 13.8 %collective-permute-start.79 = (bf16[64,2048]{1,0:T(8,128)(2,1)S(1)}, bf16[64,2048]{1,0:T(8,128)(2,1)S(1)}, u32[]{:S(2)}, u32[]{:S(2)}) collective-permute-start(bf16[64,2048]{1,0:T(8,128)(2,1)S(1)} %add_convert_fusion), channel_id=1, source_target_pairs={{0,1},{1,0},{2,3},{3,2},{4,5},{5,4},{6,7},{7,6},{8,9},{9,8},{10,11... | collective-permute-start | bytes 786440 | tf_op jit(solution)/shard_map/ppermute | solution.py:1132
  643.0 12.7 %collective-permute-start.73 = (bf16[64,2048]{1,0:T(8,128)(2,1)S(1)}, bf16[64,2048]{1,0:T(8,128)(2,1)S(1)}, u32[]{:S(2)}, u32[]{:S(2)}) collective-permute-start(bf16[64,2048]{1,0:T(8,128)(2,1)S(1)} %add_convert_fusion.1), channel_id=1, source_target_pairs={{0,1},{1,0},{2,3},{3,2},{4,5},{5,4},{6,7},{7,6},{8,9},{9,8},{10,11... | collective-permute-start | bytes 786440 | tf_op jit(solution)/shard_map/ppermute | solution.py:1132
  652.1 15.1 %all-to-all-start.3 = ((bf16[4,128,768]{2,1,0:T(8,128)(2,1)}), bf16[4,128,768]{2,1,0:T(8,128)(2,1)S(1)}, u32[]{:S(2)}, u32[]{:S(2)}) async-start(bf16[4,128,768]{2,1,0:T(8,128)(2,1)} %reduce-scatter.2.cloned.1.call-done), calls=%async_computation.4 | async-start | bytes 1572864 | tf_op jit(solution)/shard_map/all_to_all | solution.py:1146
  (133 other events, 1103.3 us)
Sparse Core Ops, SparseCore 0:
  23.3 71.0 all-gather.5
  97.4 90.5 all-gather.3
  538.3 62.3 reduce-scatter.1

commit v5 on v4

--- a/solution.py
+++ b/solution.py
@@ -578,7 +578,7 @@
     up_out[...] = (up_grad * share).astype(jnp.bfloat16)
 
 
-def feed_kernel(rows, back, shared_back, gate_t, up_t, small_t, named, pick, experts):
+def feed_kernel(rows, back, shared_back, gate_t, up_t, small_t, named, pick, experts, after=()):
     count = rows.shape[0]
     hidden, part = (back.shape[1], shared_back.shape[1])
     shapes = [shaped((count, s)) for s in (hidden, part, hidden, hidden, 2 * part)]
@@ -599,6 +599,7 @@
         [by_rows(s) for s in shapes],
         shapes,
         (rows, back, shared_back, gate_t, up_t, small_t, named, pick),
+        after,
     )
 
 
@@ -1468,14 +1469,16 @@
     routed = jnp.transpose(routed, (2, 1, 3, 0, 4)).reshape(2, -1, 1).astype(jnp.float32)
     pick = (jnp.arange(part)[None, :] == me).astype(jnp.float32)
 
-    def feed(rows, back, shared_back, named):
-        return feed_kernel(rows, back, shared_back, gate_t, up_t, small_t, named, pick, experts)
+    def feed(rows, back, shared_back, named, after=()):
+        return feed_kernel(
+            rows, back, shared_back, gate_t, up_t, small_t, named, pick, experts, after
+        )
 
     act_own, more_own, gate_own, up_own, pre_own, gain_own = feed(
         ffn_own, back_own, shared_own, routed[0]
     )
     act_other, more_other, gate_other, up_other, pre_other, gain_other = feed(
-        ffn_other, back_other, shared_other, routed[1]
+        ffn_other, back_other, shared_other, routed[1], (act_own,)
     )
     shape = (2, 2, zs * block, width + part)
     grad_other = input_kernel(
@@ -1569,7 +1572,6 @@
     down_grads = latent_grads_kernel(
         z[None], (2 * x + c)[None], zs, input_low, slab_latent_grad, rows_here
     )
-    grad_down = fold_z(down_grads)
     latent_raw_grad = tie(latent_raw_grad, down_grads[0])
     shared_back = shared_back.astype(jnp.float32)
     grad_shared_gate = shared_back[:, :shared_here].reshape(-1, rows_here).T
@@ -1577,7 +1579,7 @@
     grad_shared_down = shared_back[:, 2 * shared_here :].reshape(-1, rows_here)
 
 
-    output = both_halves(low(hidden_in + fold_z(routed_slab, jnp.float32, (grad_down,))))
+    output = both_halves(low(hidden_in + fold_z(routed_slab, jnp.float32, (down_grads[0],))))
     latent_input = jnp.stack([dot_nt(latent_raw_grad, down) for down in down_pieces])
     latent_input = latent_input.reshape(2, 2, block, zs, rows_here)
     latent_input = by_own(by_own(latent_input, "c", 0), "x", 1)
@@ -1587,8 +1589,17 @@
     )
     tokens_gradient = both_halves(low(grad_hidden + source_part)).astype(jnp.float32)
 
-    traded = trade(grad_heads, ("x", "c"))
+    group = by_own(by_own(grad_heads.reshape((2, 2) + grad_heads.shape[1:]), "x", 0), "c", 1)
+    crossed = lax.ppermute(group[1, 1], ("x", "c"), [(k, 3 - k) for k in range(4)])
+    traded = jnp.stack(
+        [
+            jnp.stack([group[0, 0], swap(group[0, 1], "c")]),
+            jnp.stack([swap(group[1, 0], "x"), crossed]),
+        ]
+    )
+    traded = by_own(by_own(traded, "x", 0), "c", 1).reshape(grad_heads.shape)
     both = traded.astype(jnp.float32)
+    grad_down = fold_z(down_grads, jnp.float32, (traded,))
     out_at = both.shape[2] - head_rows
     grad_output = jnp.transpose(
         both[..., out_at:].reshape(4, DV, heads, rows_here), (0, 2, 1, 3)

time: 690 us -> 682 us (0.988)
  waiting for transfers between devices: 171 us -> 156 us
    ppermute x12, waiting for transfers between devices: 15.6 us -> 6.57 us  [to_z(): lax.ppermute(value, 'z', [(i, (i + steps) % count) for i in range(count)])]
    ppermute x59 -> x61, waiting for transfers between devices: 113 us -> 106 us  [swap(): return lax.ppermute(value, axis, [(0, 1), (1, 0)])]
    all_to_all x4 -> x3, starting transfers between devices: 23.4 us -> 18.2 us  [trade(): return lax.all_to_all(value, axes, split_axis=0, concat_axis=0, tiled=True)]
    ppermute x59 -> x61, starting transfers between devices: 52.3 us -> 55.8 us  [swap(): return lax.ppermute(value, axis, [(0, 1), (1, 0)])]
    unnamed x192 -> x200, local copies, waits for them, and re-layouts: 21.3 us -> 22.9 us
  transfers between devices with their start and end apart: 88 -> 90, of which waited for: 36 -> 36; matrix products, arithmetic and copies ran while one was open for 16% -> 16% of each run, Pallas kernels for 28% -> 28%
where the time goes in v5:
time: 682 us; the launch traced here: 670 us
  Pallas kernels  251 us (37%)
  waiting for transfers between devices  156 us (23%)
  starting transfers between devices  104 us (15%)
  local copies, waits for them, and re-layouts  78.6 us (12%)
  other arithmetic  50.5 us (7%)
  between operations  18 us (3%)
  matrix products  11 us (2%)
    pallas_call x41, Pallas kernels, local_call(): pl.pallas_call(run, grid=grid, in_specs=list(in_specs) + [pl.BlockSpec(me...  241 us
    ppermute x61, waiting for transfers between devices, swap(): return lax.ppermute(value, axis, [(0, 1), (1, 0)])  106 us
    ppermute x61, starting transfers between devices, swap(): return lax.ppermute(value, axis, [(0, 1), (1, 0)])  55.8 us
    ppermute x9, waiting for transfers between devices, from_z(): lax.ppermute(value, 'z', [((i + steps) % count, i) for i in range(count)])  31.7 us
    unnamed x200, local copies, waits for them, and re-layouts  22.9 us
    ppermute x12, starting transfers between devices, to_z(): lax.ppermute(value, 'z', [(i, (i + steps) % count) for i in range(count)])  18.8 us
    all_to_all x3, starting transfers between devices, trade(): return lax.all_to_all(value, axes, split_axis=0, concat_axis=0, tiled=True)  18.2 us
  transfers between devices with their start and end apart: 90, of which 36 were waited for; matrix products, arithmetic and copies ran while one was open for 16% of the time, Pallas kernels for 28%

profile of v5, /device:TPU:16, one launch (start us, length us, event | category | flops | bytes accessed | tf_op | source)
XLA Modules:
  0.0 669.6 jit_solution(3104201249087645048)
XLA Ops:
  12.9 9.3 %collective-permute-done.3 = bf16[128,768]{1,0:T(8,128)(2,1)S(1)} collective-permute-done((bf16[128,768]{1,0:T(8,128)(2,1)S(1)}, bf16[128,768]{1,0:T(8,128)(2,1)S(1)}, u32[]{:S(2)}, u32[]{:S(2)}) %collective-permute-start.3) | collective-permute-done | bytes 196640 | tf_op jit(solution)/shard_map/ppermute | solution.py:1133
  34.0 20.6 %collective-permute-done.5 = bf16[128,640]{1,0:T(8,128)(2,1)} collective-permute-done((bf16[128,640]{1,0:T(8,128)(2,1)S(1)}, bf16[128,640]{1,0:T(8,128)(2,1)}, u32[]{:S(2)}, u32[]{:S(2)}) %collective-permute-start.5) | collective-permute-done | bytes 163872 | tf_op jit(solution)/shard_map/ppermute | solution.py:1138
  56.5 5.3 collective-permute-done.7
  67.3 3.9 collective-permute-done.8
  84.3 7.1 %collective-permute-done.11 = bf16[64,576]{1,0:T(8,128)(2,1)S(1)} collective-permute-done((bf16[64,576]{1,0:T(8,128)(2,1)S(1)}, bf16[64,576]{1,0:T(8,128)(2,1)S(1)}, u32[]{:S(2)}, u32[]{:S(2)}) %collective-permute-start.11) | collective-permute-done | bytes 73760 | tf_op jit(solution)/shard_map/ppermute | solution.py:1133
  95.2 5.8 collective-permute-done.14
  135.6 3.8 shard_map.288
  143.6 8.9 %shard_map.289 = (bf16[2,128,2048]{2,1,0:T(8,128)(2,1)}, bf16[2,128,2048]{2,1,0:T(8,128)(2,1)}, bf16[2,512,1024]{2,1,0:T(8,128)(2,1)}, bf16[2,512,512]{2,1,0:T(8...) custom-call(bf16[512,384]{1,0:T(8,128)(2,1)} %pad_maximum_fusion.13.refs_0_.refs_1_, ...), custom_call_target="tpu_custom_call" | custom-call | flops 1 | bytes 1 | tf_op jit(solution)/shard_map/pallas_call | solution.py:503
  155.7 8.1 %all-to-all-start = ((bf16[16,264,128]{2,1,0:T(8,128)(2,1)}), bf16[16,264,128]{2,1,0:T(8,128)(2,1)S(1)}, u32[]{:S(2)}, u32[]{:S(2)}) async-start(bf16[16,264,128]{2,1,0:T(8,128)(2,1)} %maximum_add_fusion), calls=%async_computation | async-start | bytes 2162688 | tf_op jit(solution)/shard_map/all_to_all | solution.py:1147
  170.4 5.5 collective-permute-done.24.refs_1_
  183.7 5.5 collective-permute-done.26.refs_1_
  198.5 5.4 shard_map.294.refs_0_.refs_4_
  203.9 7.4 %shard_map.295.refs_2_.refs_1_ = bf16[1024,704]{1,0:T(8,128)(2,1)} custom-call(bf16[1024,2048]{1,0:T(8,128)(2,1)} %shard_map.294.refs_0_.refs_4_, bf16[704,2048]{1,0:T(8,128)(2,1)} %bitcast.299), custom_call_target="tpu_custom_call" | custom-call | flops 1 | bytes 1 | tf_op jit(solution)/shard_map/pallas_call | solution.py:503
  211.3 5.4 shard_map.293.refs_0_.refs_5_
  216.6 7.4 %shard_map.296.refs_5_.refs_1_ = bf16[1024,704]{1,0:T(8,128)(2,1)} custom-call(bf16[1024,2048]{1,0:T(8,128)(2,1)} %shard_map.293.refs_0_.refs_5_, bf16[704,2048]{1,0:T(8,128)(2,1)} %bitcast.300, bf16[1024,704]{1,0:T(8,128)(2,1)} %shard_map.295.refs_2_.refs_1_), custom_call_target="tpu_custom_call" | custom-call | flops 1 | bytes 1 | tf_op jit(solution)/shard_map/pallas_call | solution.py:503
  231.3 21.0 %collective-permute-done.32.refs_2_ = bf16[256,2048]{1,0:T(8,128)(2,1)S(1)} collective-permute-done((bf16[256,2048]{1,0:T(8,128)(2,1)}, bf16[256,2048]{1,0:T(8,128)(2,1)S(1)}, u32[]{:S(2)}, u32[]{:S(2)}) %collective-permute-start.32) | collective-permute-done | bytes 1048608 | tf_op jit(solution)/shard_map/ppermute | solution.py:1133
  257.4 4.8 shard_map.298.refs_2_
  262.2 4.8 shard_map.299.refs_5_.refs_2_
  267.0 4.4 shard_map.300.refs_0_.refs_4_
  276.6 16.1 %shard_map.301 = (bf16[1024,704]{1,0:T(8,128)(2,1)}, bf16[1024,128]{1,0:T(8,128)(2,1)}, bf16[1024,704]{1,0:T(8,128)(2,1)}, bf16[1024,704]{1,0:T(8,128)(2,1)}, bf...) custom-call(bf16[1024,2048]{1,0:T(8,128)(2,1)} %shard_map.300.refs_0_.refs_4_, bf16[1024,704]{1,0:T(8,128)(2,1)} %shard_map.295.refs_2_.refs_1_, ...), custom_call_target="tpu_custom_call" | custom-call | flops 1 | bytes 1 | tf_op jit(solution)/shard_map/pallas_call | solution.py:503
  292.8 16.2 %shard_map.302 = (bf16[1024,704]{1,0:T(8,128)(2,1)}, bf16[1024,128]{1,0:T(8,128)(2,1)}, bf16[1024,704]{1,0:T(8,128)(2,1)}, bf16[1024,704]{1,0:T(8,128)(2,1)}, bf...) custom-call(bf16[1024,2048]{1,0:T(8,128)(2,1)} %collective-permute-done.35.refs_0_.refs_5_, ...), custom_call_target="tpu_custom_call" | custom-call | flops 1 | bytes 1 | tf_op jit(solution)/shard_map/pallas_call | solution.py:503
  309.0 13.1 %shard_map.303.refs_8_ = bf16[1024,2176]{1,0:T(8,128)(2,1)} custom-call(bf16[1024,704]{1,0:T(8,128)(2,1)} %get-tuple-element.126.refs_0_.refs_1_, bf16[1024,704]{1,0:T(8,128)(2,1)} %get-tuple-element.127.refs_1_, bf16[1024,256]{1,0:T(8,128)(2,1)} %get-tuple-element.128.refs_2_.refs_3_, bf16[704,2048]{1,0:T(8,128)(2,1)} %bitcast.293, ...), custom_call_target="tpu_custom_call" | custom-call | flops 1 | bytes 1 | tf_op jit(solution)/shard_map/pallas_call | solution.py:503
  322.6 12.9 %shard_map.304 = bf16[1024,2176]{1,0:T(8,128)(2,1)} custom-call(bf16[1024,704]{1,0:T(8,128)(2,1)} %get-tuple-element.122.refs_0_, bf16[1024,704]{1,0:T(8,128)(2,1)} %get-tuple-element.123.refs_1_.refs_0_, bf16[1024,256]{1,0:T(8,128)(2,1)} %get-tuple-element.124.refs_2_, bf16[704,2048]{1,0:T(8,128)(2,1)} %bitcast.294, bf16[704,2048]{1,0:T(8,128)(2,1)} %bitcast.298, ...), custom_call_target="tpu_custom_call" | custom-call | flops 1 | bytes 1 | tf_op jit(solution)/shard_map/pallas_call | solution.py:503
  335.5 5.5 shard_map.305
  341.0 8.1 %shard_map.306.refs_4_ = bf16[1024,2048]{1,0:T(8,128)(2,1)} custom-call(bf16[1024,704]{1,0:T(8,128)(2,1)} %get-tuple-element.120.refs_0_.refs_1_, bf16[1024,128]{1,0:T(8,128)(2,1)} %get-tuple-element.121.refs_1_.refs_3_, bf16[704,2048]{1,0:T(8,128)(2,1)} %bitcast.301, bf16[128,2048]{1,0:T(8,128)(2,1)} %get-tuple-element.307.refs_1_.refs_3_, ...), custom_call_target="tpu_custom_call" | custom-call | flops 1 | bytes 1 | tf_op jit(solution)/shard_map/pallas_call | solution.py:503
  351.4 8.1 %shard_map.307.refs_6_ = bf16[1024,2048]{1,0:T(8,128)(2,1)} custom-call(bf16[1024,704]{1,0:T(8,128)(2,1)} %get-tuple-element.118.refs_8_.refs_0_, bf16[1024,128]{1,0:T(8,128)(2,1)} %get-tuple-element.119.refs_1_.refs_2_, bf16[704,2048]{1,0:T(8,128)(2,1)} %bitcast.302, bf16[128,2048]{1,0:T(8,128)(2,1)} %get-tuple-element.307.refs_1_.refs_3_, ...), custom_call_target="tpu_custom_call" | custom-call | flops 1 | bytes 1 | tf_op jit(solution)/shard_map/pallas_call | solution.py:503
  359.5 14.0 %shard_map.308 = (f32[704,2048]{1,0:T(8,128)}, bf16[128,2048]{1,0:T(8,128)(2,1)}) custom-call(bf16[1024,704]{1,0:T(8,128)(2,1)} %get-tuple-element.123.refs_1_.refs_0_, bf16[1024,704]{1,0:T(8,128)(2,1)} %get-tuple-element.127.refs_1_, bf16[1024,256]{1,0:T(8,128)(2,1)} %get-tuple-element.124.refs_2_, bf16[1024,256]{1,0:T(8,128)(2,1)} %get-tuple-element.128.refs_2_.refs_3_, ...), custom_call_target="tpu_custom_call" | custom-call | flops 1 | bytes 1 | tf_op jit(solution)/shard_map/pallas_call | solution.py:503
  378.1 3.4 shard_map.309
  384.4 14.0 %shard_map.310 = (f32[704,2048]{1,0:T(8,128)}, bf16[128,2048]{1,0:T(8,128)(2,1)}) custom-call(bf16[1024,704]{1,0:T(8,128)(2,1)} %get-tuple-element.118.refs_8_.refs_0_, bf16[1024,704]{1,0:T(8,128)(2,1)} %get-tuple-element.120.refs_0_.refs_1_, bf16[1024,128]{1,0:T(8,128)(2,1)} %get-tuple-element.119.refs_1_.refs_2_, ...), custom_call_target="tpu_custom_call" | custom-call | flops 1 | bytes 1 | tf_op jit(solution)/shard_map/pallas_call | solution.py:503
  402.1 5.2 shard_map.312
  413.5 14.0 %shard_map.313 = (f32[704,2048]{1,0:T(8,128)}, bf16[128,2048]{1,0:T(8,128)(2,1)}) custom-call(bf16[1024,704]{1,0:T(8,128)(2,1)} %get-tuple-element.122.refs_0_, bf16[1024,704]{1,0:T(8,128)(2,1)} %get-tuple-element.126.refs_0_.refs_1_, bf16[1024,256]{1,0:T(8,128)(2,1)} %get-tuple-element.124.refs_2_, bf16[1024,256]{1,0:T(8,128)(2,1)} %get-tuple-element.128.refs_2_.refs_3_, ...), custom_call_target="tpu_custom_call" | custom-call | flops 1 | bytes 1 | tf_op jit(solution)/shard_map/pallas_call | solution.py:503
  427.6 3.9 collective-permute-done.42.refs_1_
  433.1 3.3 shard_map.314
  444.5 4.7 collective-permute-done.50
  458.6 5.0 all-to-all-start.1
  466.6 3.4 shard_map.316.refs_9_.refs_3_
  470.0 13.9 %shard_map.317 = (bf16[2,2,256,576]{3,2,1,0:T(8,128)(2,1)}, bf16[2,2,256,576]{3,2,1,0:T(8,128)(2,1)}, f32[512,384]{1,0:T(8,128)}, f32[512,512]{1,0:T(8,128)}) custom-call(bf16[512,2048]{1,0:T(8,128)(2,1)} %bitcast.304, bf16[512,384]{1,0:T(8,128)(2,1)} %pad_maximum_fusion.13.refs_0_.refs_1_, bf16[2,2,256,576]{3,2,1,0:T(8,128)(2,1)} %copy-done, ...), custom_call_target="tpu_custom_call" | custom-call | flops 1 | bytes 1 | tf_op jit(solution)/shard_map/pallas_call | solution.py:503
  495.9 5.3 shard_map.318.refs_8_.refs_2_
  510.8 7.0 %collective-permute-done.55.refs_1_ = bf16[2,128,576]{2,1,0:T(8,128)(2,1)S(1)} collective-permute-done((bf16[2,128,576]{2,1,0:T(8,128)(2,1)}, bf16[2,128,576]{2,1,0:T(8,128)(2,1)S(1)}, u32[]{:S(2)}, u32[]{:S(2)}) %collective-permute-start.55) | collective-permute-done | bytes 294944 | tf_op jit(solution)/shard_map/ppermute | solution.py:1133
  524.0 3.7 collective-permute-done.57.refs_1_
  535.3 4.0 shard_map.326
  555.1 7.1 %collective-permute-done.68 = bf16[32,576]{1,0:T(8,128)(2,1)S(1)} collective-permute-done((bf16[32,576]{1,0:T(8,128)(2,1)S(1)}, bf16[32,576]{1,0:T(8,128)(2,1)S(1)}, u32[]{:S(2)}, u32[]{:S(2)}) %collective-permute-start.68) | collective-permute-done | bytes 36896 | tf_op jit(solution)/shard_map/ppermute | solution.py:1133
  563.6 3.9 collective-permute-done.67
  591.7 3.1 shard_map.324
  608.2 4.6 collective-permute-done.64.refs_3_
  622.3 5.1 all-to-all-start.2
  628.6 6.6 all-to-all-done.2
  644.3 4.9 collective-permute-done.80
  (619 shorter events, 287.1 us)
Async XLA Ops:
  7.2 128.4 %all-gather.6.cloned.1.call-start = ((), (), s32[]{:S(2)}) async-start(), calls=%async_computation.6 | async-start | bytes 3932160 | tf_op jit(solution)/shard_map/all_gather | solution.py:1352
  10.7 11.5 %collective-permute-start.4 = (bf16[128,768]{1,0:T(8,128)(2,1)S(1)}, bf16[128,768]{1,0:T(8,128)(2,1)S(1)}, u32[]{:S(2)}, u32[]{:S(2)}) collective-permute-start(bf16[128,768]{1,0:T(8,128)(2,1)S(1)} %get-tuple-element.320), channel_id=1, source_target_pairs={{0,6},{2,4},{4,2},{6,0},{1,7},{3,5},{5,3},{7,1},{8,14},{10,12},{12... | collective-permute-start | bytes 589832 | tf_op jit(solution)/shard_map/ppermute | solution.py:1317
  23.2 175.4 %all-gather.4.cloned.1.call-start = ((), (), s32[]{:S(2)}) async-start(), calls=%async_computation.4 | async-start | bytes 8650752 | tf_op jit(solution)/shard_map/all_gather | solution.py:1343
  27.0 28.5 %collective-permute-start.6 = (bf16[128,640]{1,0:T(8,128)(2,1)S(1)}, bf16[128,640]{1,0:T(8,128)(2,1)}, u32[]{:S(2)}, u32[]{:S(2)}) collective-permute-start(bf16[128,640]{1,0:T(8,128)(2,1)S(1)} %pad.21), channel_id=1, source_target_pairs={{16,0},{24,8},{0,16},{8,24},{17,1},{25,9},{1,17},{9,25},{18,2},{26... | collective-permute-start | bytes 491528 | tf_op jit(solution)/shard_map/ppermute | solution.py:1138
  27.2 27.4 %collective-permute-start.5 = (bf16[128,640]{1,0:T(8,128)(2,1)S(1)}, bf16[128,640]{1,0:T(8,128)(2,1)}, u32[]{:S(2)}, u32[]{:S(2)}) collective-permute-start(bf16[128,640]{1,0:T(8,128)(2,1)S(1)} %pad.21), channel_id=1, source_target_pairs={{8,0},{16,8},{24,16},{0,24},{9,1},{17,9},{25,17},{1,25},{10,2},{18... | collective-permute-start | bytes 491528 | tf_op jit(solution)/shard_map/ppermute | solution.py:1138
  30.1 31.7 %collective-permute-start.7 = (bf16[128,640]{1,0:T(8,128)(2,1)S(1)}, bf16[128,640]{1,0:T(8,128)(2,1)}, u32[]{:S(2)}, u32[]{:S(2)}) collective-permute-start(bf16[128,640]{1,0:T(8,128)(2,1)S(1)} %pad.21), channel_id=1, source_target_pairs={{24,0},{0,8},{8,16},{16,24},{25,1},{1,9},{9,17},{17,25},{26,2},{2,... | collective-permute-start | bytes 491528 | tf_op jit(solution)/shard_map/ppermute | solution.py:1138
  30.2 32.5 %collective-permute-start = (bf16[2,64,2048]{2,1,0:T(8,128)(2,1)S(1)}, bf16[2,64,2048]{2,1,0:T(8,128)(2,1)}, u32[]{:S(2)}, u32[]{:S(2)}) collective-permute-start(bf16[2,64,2048]{2,1,0:T(8,128)(2,1)S(1)} %reverse_select_fusion.9), channel_id=1, source_target_pairs={{0,4},{4,0},{1,5},{5,1},{2,6},{6,2},{3,7},{7,3},{8,12},{12,8},{9,1... | collective-permute-start | bytes 1572872 | tf_op jit(solution)/shard_map/ppermute | solution.py:1133
  65.1 11.1 %collective-permute-start.1 = (bf16[2,2,64,2048]{3,2,0,1:T(8,128)(2,1)}, bf16[2,2,64,2048]{3,2,0,1:T(8,128)(2,1)S(1)}, u32[]{:S(2)}, u32[]{:S(2)}) collective-permute-start(bf16[2,2,64,2048]{3,2,0,1:T(8,128)(2,1)} %get-tuple-element.315), channel_id=1, source_target_pairs={{0,2},{2,0},{1,3},{3,1},{4,6},{6,4},{5,7},{7,5},{8,10},{10,8},{9,1... | collective-permute-start | bytes 3145736 | tf_op jit(solution)/shard_map/ppermute | solution.py:1133
  73.7 34.8 %collective-permute-start.20 = (bf16[512,576]{0,1:T(8,128)(2,1)}, bf16[512,576]{0,1:T(8,128)(2,1)}, u32[]{:S(2)}, u32[]{:S(2)}) collective-permute-start(bf16[512,576]{0,1:T(8,128)(2,1)} %copy.292), channel_id=1, source_target_pairs={{0,4},{4,0},{1,5},{5,1},{2,6},{6,2},{3,7},{7,3},{8,12},{12,8},{9,1... | collective-permute-start | bytes 1769480 | tf_op jit(solution)/shard_map/ppermute | solution.py:1133
  108.5 16.4 %collective-permute-start.21 = (bf16[512,576]{0,1:T(8,128)(2,1)}, bf16[512,576]{0,1:T(8,128)(2,1)}, u32[]{:S(2)}, u32[]{:S(2)}) collective-permute-start(bf16[512,576]{0,1:T(8,128)(2,1)} %copy.292), channel_id=1, source_target_pairs={{0,2},{2,0},{1,3},{3,1},{4,6},{6,4},{5,7},{7,5},{8,10},{10,8},{9,1... | collective-permute-start | bytes 1769480 | tf_op jit(solution)/shard_map/ppermute | solution.py:1133
  108.5 18.5 %collective-permute-start.22 = (bf16[512,576]{0,1:T(8,128)(2,1)}, bf16[512,576]{0,1:T(8,128)(2,1)}, u32[]{:S(2)}, u32[]{:S(2)}) collective-permute-start(bf16[512,576]{0,1:T(8,128)(2,1)} %collective-permute-done.20), channel_id=1, source_target_pairs={{0,2},{2,0},{1,3},{3,1},{4,6},{6,4},{5,7},{7,5},{8,10},{10,8},{9,1... | collective-permute-start | bytes 1769480 | tf_op jit(solution)/shard_map/ppermute | solution.py:1133
  121.9 10.7 %collective-permute-start.19 = (bf16[2,2,256,576]{2,3,1,0:T(8,128)(2,1)}, bf16[2,2,256,576]{2,3,1,0:T(8,128)(2,1)}, u32[]{:S(2)}, u32[]{:S(2)}) collective-permute-start(bf16[2,2,256,576]{2,3,1,0:T(8,128)(2,1)} %copy.291), channel_id=1, source_target_pairs={{0,2},{2,0},{1,3},{3,1},{4,6},{6,4},{5,7},{7,5},{8,10},{10,8},{9,1... | collective-permute-start | bytes 3538952 | tf_op jit(solution)/shard_map/ppermute | solution.py:1133
  152.5 11.4 %collective-permute-start.23 = (bf16[2,128,2048]{2,1,0:T(8,128)(2,1)}, bf16[2,128,2048]{2,1,0:T(8,128)(2,1)S(1)}, u32[]{:S(2)}, u32[]{:S(2)}) collective-permute-start(bf16[2,128,2048]{2,1,0:T(8,128)(2,1)} %get-tuple-element.109), channel_id=1, source_target_pairs={{0,2},{2,0},{1,3},{3,1},{4,6},{6,4},{5,7},{7,5},{8,10},{10,8},{9,1... | collective-permute-start | bytes 3145736 | tf_op jit(solution)/shard_map/ppermute | solution.py:1133
  155.7 68.3 %all-to-all-start = ((bf16[16,264,128]{2,1,0:T(8,128)(2,1)}), bf16[16,264,128]{2,1,0:T(8,128)(2,1)S(1)}, u32[]{:S(2)}, u32[]{:S(2)}) async-start(bf16[16,264,128]{2,1,0:T(8,128)(2,1)} %maximum_add_fusion), calls=%async_computation | async-start | bytes 2162688 | tf_op jit(solution)/shard_map/all_to_all | solution.py:1147
  193.3 30.8 %collective-permute-start.30 = (bf16[64,2048]{1,0:T(8,128)(2,1)S(1)}, bf16[64,2048]{1,0:T(8,128)(2,1)S(1)}, u32[]{:S(2)}, u32[]{:S(2)}) collective-permute-start(bf16[64,2048]{1,0:T(8,128)(2,1)S(1)} %multiply_convert_fusion.1.dep.refs_0_), channel_id=1, source_target_pairs={{24,0},{0,8},{8,16},{16,24},{25,1},{1,9},{9,17},{17,25},{26,2},{2,... | collective-permute-start | bytes 786440 | tf_op jit(solution)/shard_map/ppermute | solution.py:1138
  195.0 29.0 %collective-permute-start.29 = (bf16[64,2048]{1,0:T(8,128)(2,1)S(1)}, bf16[64,2048]{1,0:T(8,128)(2,1)S(1)}, u32[]{:S(2)}, u32[]{:S(2)}) collective-permute-start(bf16[64,2048]{1,0:T(8,128)(2,1)S(1)} %multiply_convert_fusion.1.dep.refs_0_), channel_id=1, source_target_pairs={{16,0},{24,8},{0,16},{8,24},{17,1},{25,9},{1,17},{9,25},{18,2},{26... | collective-permute-start | bytes 786440 | tf_op jit(solution)/shard_map/ppermute | solution.py:1138
  195.0 29.0 %collective-permute-start.28 = (bf16[64,2048]{1,0:T(8,128)(2,1)S(1)}, bf16[64,2048]{1,0:T(8,128)(2,1)S(1)}, u32[]{:S(2)}, u32[]{:S(2)}) collective-permute-start(bf16[64,2048]{1,0:T(8,128)(2,1)S(1)} %multiply_convert_fusion.1.dep.refs_0_), channel_id=1, source_target_pairs={{8,0},{16,8},{24,16},{0,24},{9,1},{17,9},{25,17},{1,25},{10,2},{18... | collective-permute-start | bytes 786440 | tf_op jit(solution)/shard_map/ppermute | solution.py:1138
  228.1 24.1 %collective-permute-start.32 = (bf16[256,2048]{1,0:T(8,128)(2,1)}, bf16[256,2048]{1,0:T(8,128)(2,1)S(1)}, u32[]{:S(2)}, u32[]{:S(2)}) collective-permute-start(bf16[256,2048]{1,0:T(8,128)(2,1)} %shard_map.297.refs_2_.refs_0_), channel_id=1, source_target_pairs={{0,4},{4,0},{1,5},{5,1},{2,6},{6,2},{3,7},{7,3},{8,12},{12,8},{9,1... | collective-permute-start | bytes 3145736 | tf_op jit(solution)/shard_map/ppermute | solution.py:1133
  230.5 23.6 %collective-permute-start.31 = (bf16[256,2048]{1,0:T(8,128)(2,1)}, bf16[256,2048]{1,0:T(8,128)(2,1)S(1)}, u32[]{:S(2)}, u32[]{:S(2)}) collective-permute-start(bf16[256,2048]{1,0:T(8,128)(2,1)} %shard_map.297.refs_2_.refs_0_), channel_id=1, source_target_pairs={{0,1},{1,0},{2,3},{3,2},{4,5},{5,4},{6,7},{7,6},{8,9},{9,8},{10,11... | collective-permute-start | bytes 3145736 | tf_op jit(solution)/shard_map/ppermute | solution.py:1133
  253.2 13.8 %collective-permute-start.34 = (bf16[128,2048]{1,0:T(8,128)(2,1)}, bf16[128,2048]{1,0:T(8,128)(2,1)}, u32[]{:S(2)}, u32[]{:S(2)}) collective-permute-start(bf16[128,2048]{1,0:T(8,128)(2,1)} %slice.364), channel_id=1, source_target_pairs={{0,1},{1,0},{2,3},{3,2},{4,5},{5,4},{6,7},{7,6},{8,9},{9,8},{10,11... | collective-permute-start | bytes 1572872 | tf_op jit(solution)/shard_map/ppermute | solution.py:1133
  254.9 12.1 %collective-permute-start.33 = (bf16[128,2048]{1,0:T(8,128)(2,1)}, bf16[128,2048]{1,0:T(8,128)(2,1)}, u32[]{:S(2)}, u32[]{:S(2)}) collective-permute-start(bf16[128,2048]{1,0:T(8,128)(2,1)} %slice.363), channel_id=1, source_target_pairs={{0,4},{4,0},{1,5},{5,1},{2,6},{6,2},{3,7},{7,3},{8,12},{12,8},{9,1... | collective-permute-start | bytes 1572872 | tf_op jit(solution)/shard_map/ppermute | solution.py:1133
  271.4 21.4 %collective-permute-start.35 = (bf16[1024,2048]{1,0:T(8,128)(2,1)}, bf16[1024,2048]{1,0:T(8,128)(2,1)}, u32[]{:S(2)}, u32[]{:S(2)}) collective-permute-start(bf16[1024,2048]{1,0:T(8,128)(2,1)} %shard_map.300.refs_0_.refs_4_), channel_id=1, source_target_pairs={{0,2},{2,0},{1,3},{3,1},{4,6},{6,4},{5,7},{7,5},{8,10},{10,8},{9,1... | collective-permute-start | bytes 12582920 | tf_op jit(solution)/shard_map/ppermute | solution.py:1133
  322.1 13.4 %collective-permute-start.36 = (bf16[1024,2176]{1,0:T(8,128)(2,1)}, bf16[1024,2176]{1,0:T(8,128)(2,1)}, u32[]{:S(2)}, u32[]{:S(2)}) collective-permute-start(bf16[1024,2176]{1,0:T(8,128)(2,1)} %shard_map.303.refs_8_), channel_id=1, source_target_pairs={{0,2},{2,0},{1,3},{3,1},{4,6},{6,4},{5,7},{7,5},{8,10},{10,8},{9,1... | collective-permute-start | bytes 13369352 | tf_op jit(solution)/shard_map/ppermute | solution.py:1133
  349.0 53.1 %collective-permute-start.37 = (bf16[1024,2048]{1,0:T(8,128)(2,1)}, bf16[1024,2048]{1,0:T(8,128)(2,1)}, u32[]{:S(2)}, u32[]{:S(2)}) collective-permute-start(bf16[1024,2048]{1,0:T(8,128)(2,1)} %shard_map.306.refs_4_), channel_id=1, source_target_pairs={{0,2},{2,0},{1,3},{3,1},{4,6},{6,4},{5,7},{7,5},{8,10},{10,8},{9,1... | collective-permute-start | bytes 12582920 | tf_op jit(solution)/shard_map/ppermute | solution.py:1133
  349.1 27.2 %collective-permute-start.38 = (bf16[2,128,2176]{2,1,0:T(8,128)(2,1)}, bf16[2,128,2176]{2,1,0:T(8,128)(2,1)S(1)}, u32[]{:S(2)}, u32[]{:S(2)}) collective-permute-start(bf16[2,128,2176]{2,1,0:T(8,128)(2,1)} %get-tuple-element.131.refs_5_), channel_id=1, source_target_pairs={{0,4},{4,0},{1,5},{5,1},{2,6},{6,2},{3,7},{7,3},{8,12},{12,8},{9,1... | collective-permute-start | bytes 3342344 | tf_op jit(solution)/shard_map/ppermute | solution.py:1133
  350.2 26.9 %collective-permute-start.39 = (bf16[2,128,2176]{2,1,0:T(8,128)(2,1)}, bf16[2,128,2176]{2,1,0:T(8,128)(2,1)S(1)}, u32[]{:S(2)}, u32[]{:S(2)}) collective-permute-start(bf16[2,128,2176]{2,1,0:T(8,128)(2,1)} %get-tuple-element.133.refs_7_), channel_id=1, source_target_pairs={{0,1},{1,0},{2,3},{3,2},{4,5},{5,4},{6,7},{7,6},{8,9},{9,8},{10,11... | collective-permute-start | bytes 3342344 | tf_op jit(solution)/shard_map/ppermute | solution.py:1133
  381.5 16.9 %collective-permute-start.40 = (bf16[128,2176]{1,0:T(8,128)(2,1)}, bf16[128,2176]{1,0:T(8,128)(2,1)S(1)}, u32[]{:S(2)}, u32[]{:S(2)}) collective-permute-start(bf16[128,2176]{1,0:T(8,128)(2,1)} %get-tuple-element.136.refs_7_), channel_id=1, source_target_pairs={{0,1},{1,0},{2,3},{3,2},{4,5},{5,4},{6,7},{7,6},{8,9},{9,8},{10,11... | collective-permute-start | bytes 1671176 | tf_op jit(solution)/shard_map/ppermute | solution.py:1133
  383.0 15.4 %collective-permute-start.41 = (bf16[128,2176]{1,0:T(8,128)(2,1)}, bf16[128,2176]{1,0:T(8,128)(2,1)S(1)}, u32[]{:S(2)}, u32[]{:S(2)}) collective-permute-start(bf16[128,2176]{1,0:T(8,128)(2,1)} %get-tuple-element.138.refs_9_), channel_id=1, source_target_pairs={{0,4},{4,0},{1,5},{5,1},{2,6},{6,2},{3,7},{7,3},{8,12},{12,8},{9,1... | collective-permute-start | bytes 1671176 | tf_op jit(solution)/shard_map/ppermute | solution.py:1133
  407.3 24.1 %collective-permute-start.42 = (bf16[2,128,2048]{2,1,0:T(8,128)(2,1)}, bf16[2,128,2048]{2,1,0:T(8,128)(2,1)S(1)}, u32[]{:S(2)}, u32[]{:S(2)}) collective-permute-start(bf16[2,128,2048]{2,1,0:T(8,128)(2,1)} %get-tuple-element.145.refs_7_), channel_id=1, source_target_pairs={{0,4},{4,0},{1,5},{5,1},{2,6},{6,2},{3,7},{7,3},{8,12},{12,8},{9,1... | collective-permute-start | bytes 3145736 | tf_op jit(solution)/shard_map/ppermute | solution.py:1133
  408.0 24.1 %collective-permute-start.43 = (bf16[2,128,2048]{2,1,0:T(8,128)(2,1)}, bf16[2,128,2048]{2,1,0:T(8,128)(2,1)S(1)}, u32[]{:S(2)}, u32[]{:S(2)}) collective-permute-start(bf16[2,128,2048]{2,1,0:T(8,128)(2,1)} %get-tuple-element.147.refs_9_), channel_id=1, source_target_pairs={{0,1},{1,0},{2,3},{3,2},{4,5},{5,4},{6,7},{7,6},{8,9},{9,8},{10,11... | collective-permute-start | bytes 3145736 | tf_op jit(solution)/shard_map/ppermute | solution.py:1133
  408.5 27.9 %collective-permute-start.46 = (bf16[64,2176]{1,0:T(8,128)(2,1)}, bf16[64,2176]{1,0:T(8,128)(2,1)}, u32[]{:S(2)}, u32[]{:S(2)}) collective-permute-start(bf16[64,2176]{1,0:T(8,128)(2,1)} %get-tuple-element.141.refs_9_), channel_id=1, source_target_pairs={{0,8},{8,16},{16,24},{24,0},{1,9},{9,17},{17,25},{25,1},{2,10},{10... | collective-permute-start | bytes 835592 | tf_op jit(solution)/shard_map/ppermute | solution.py:1143
  409.0 27.4 %collective-permute-start.47 = (bf16[64,2176]{1,0:T(8,128)(2,1)}, bf16[64,2176]{1,0:T(8,128)(2,1)}, u32[]{:S(2)}, u32[]{:S(2)}) collective-permute-start(bf16[64,2176]{1,0:T(8,128)(2,1)} %get-tuple-element.142.refs_10_), channel_id=1, source_target_pairs={{0,16},{8,24},{16,0},{24,8},{1,17},{9,25},{17,1},{25,9},{2,18},{10... | collective-permute-start | bytes 835592 | tf_op jit(solution)/shard_map/ppermute | solution.py:1143
  411.7 24.8 %collective-permute-start.48 = (bf16[64,2176]{1,0:T(8,128)(2,1)}, bf16[64,2176]{1,0:T(8,128)(2,1)}, u32[]{:S(2)}, u32[]{:S(2)}) collective-permute-start(bf16[64,2176]{1,0:T(8,128)(2,1)} %get-tuple-element.143.refs_11_), channel_id=1, source_target_pairs={{0,24},{8,0},{16,8},{24,16},{1,25},{9,1},{17,9},{25,17},{2,26},{10... | collective-permute-start | bytes 835592 | tf_op jit(solution)/shard_map/ppermute | solution.py:1143
  458.6 45.1 %all-to-all-start.1 = ((bf16[16,264,128]{2,1,0:T(8,128)(2,1)}), bf16[16,264,128]{2,1,0:T(8,128)(2,1)S(1)}, u32[]{:S(2)}, u32[]{:S(2)}) async-start(bf16[16,264,128]{2,1,0:T(8,128)(2,1)} %bitcast_bitcast_fusion), calls=%async_computation.1 | async-start | bytes 2162688 | tf_op jit(solution)/shard_map/all_to_all | solution.py:1147
  463.6 176.5 %reduce-scatter.2.cloned.1.call-start = ((), (), s32[]{:S(2)}) async-start(), calls=%async_computation.5 | async-start | bytes 3932160 | tf_op jit(solution)/shard_map/reduce_scatter | solution.py:1558
  485.5 15.7 %collective-permute-start.54 = (bf16[2,2,256,576]{2,3,1,0:T(8,128)(2,1)S(1)}, bf16[2,2,256,576]{2,3,1,0:T(8,128)(2,1)}, u32[]{:S(2)}, u32[]{:S(2)}) collective-permute-start(bf16[2,2,256,576]{2,3,1,0:T(8,128)(2,1)S(1)} %copy.311), channel_id=1, source_target_pairs={{0,2},{2,0},{1,3},{3,1},{4,6},{6,4},{5,7},{7,5},{8,10},{10,8},{9,1... | collective-permute-start | bytes 3538952 | tf_op jit(solution)/shard_map/ppermute | solution.py:1133
  545.8 35.6 %collective-permute-start.44 = (bf16[128,2048]{1,0:T(8,128)(2,1)}, bf16[128,2048]{1,0:T(8,128)(2,1)}, u32[]{:S(2)}, u32[]{:S(2)}) collective-permute-start(bf16[128,2048]{1,0:T(8,128)(2,1)} %get-tuple-element.150.refs_5_), channel_id=1, source_target_pairs={{0,1},{1,0},{2,3},{3,2},{4,5},{5,4},{6,7},{7,6},{8,9},{9,8},{10,11... | collective-permute-start | bytes 1572872 | tf_op jit(solution)/shard_map/ppermute | solution.py:1133
  547.3 34.1 %collective-permute-start.45 = (bf16[128,2048]{1,0:T(8,128)(2,1)}, bf16[128,2048]{1,0:T(8,128)(2,1)}, u32[]{:S(2)}, u32[]{:S(2)}) collective-permute-start(bf16[128,2048]{1,0:T(8,128)(2,1)} %get-tuple-element.152.refs_7_), channel_id=1, source_target_pairs={{0,4},{4,0},{1,5},{5,1},{2,6},{6,2},{3,7},{7,3},{8,12},{12,8},{9,1... | collective-permute-start | bytes 1572872 | tf_op jit(solution)/shard_map/ppermute | solution.py:1133
  552.5 17.0 %collective-permute-start.72 = (bf16[2,32,2048]{2,1,0:T(8,128)(2,1)}, bf16[2,32,2048]{2,1,0:T(8,128)(2,1)S(1)}, u32[]{:S(2)}, u32[]{:S(2)}) collective-permute-start(bf16[2,32,2048]{2,1,0:T(8,128)(2,1)} %get-tuple-element.184), channel_id=1, source_target_pairs={{0,1},{1,0},{2,3},{3,2},{4,5},{5,4},{6,7},{7,6},{8,9},{9,8},{10,11... | collective-permute-start | bytes 786440 | tf_op jit(solution)/shard_map/ppermute | solution.py:1133
  553.4 14.1 %collective-permute-start.67 = (bf16[32,576]{1,0:T(8,128)(2,1)S(1)}, bf16[32,576]{1,0:T(8,128)(2,1)S(1)}, u32[]{:S(2)}, u32[]{:S(2)}) collective-permute-start(bf16[32,576]{1,0:T(8,128)(2,1)S(1)} %slice.379), channel_id=1, source_target_pairs={{0,1},{1,0},{2,3},{3,2},{4,5},{5,4},{6,7},{7,6},{8,9},{9,8},{10,11... | collective-permute-start | bytes 110600 | tf_op jit(solution)/shard_map/ppermute | solution.py:1133
  568.5 21.2 %collective-permute-start.69 = (bf16[2,2,64,576]{3,2,1,0:T(8,128)(2,1)}, bf16[2,2,64,576]{3,2,1,0:T(8,128)(2,1)}, u32[]{:S(2)}, u32[]{:S(2)}) collective-permute-start(bf16[2,2,64,576]{3,2,1,0:T(8,128)(2,1)} %get-tuple-element.331), channel_id=1, source_target_pairs={{0,2},{2,0},{1,3},{3,1},{4,6},{6,4},{5,7},{7,5},{8,10},{10,8},{9,1... | collective-permute-start | bytes 884744 | tf_op jit(solution)/shard_map/ppermute | solution.py:1133
  584.1 24.1 %collective-permute-start.62 = (bf16[64,2048]{1,0:T(8,128)(2,1)}, bf16[64,2048]{1,0:T(8,128)(2,1)S(1)}, u32[]{:S(2)}, u32[]{:S(2)}) collective-permute-start(bf16[64,2048]{1,0:T(8,128)(2,1)} %get-tuple-element.177), channel_id=1, source_target_pairs={{0,8},{8,16},{16,24},{24,0},{1,9},{9,17},{17,25},{25,1},{2,10},{10... | collective-permute-start | bytes 786440 | tf_op jit(solution)/shard_map/ppermute | solution.py:1143
  585.5 22.7 %collective-permute-start.63 = (bf16[64,2048]{1,0:T(8,128)(2,1)}, bf16[64,2048]{1,0:T(8,128)(2,1)}, u32[]{:S(2)}, u32[]{:S(2)}) collective-permute-start(bf16[64,2048]{1,0:T(8,128)(2,1)} %get-tuple-element.178), channel_id=1, source_target_pairs={{0,16},{8,24},{16,0},{24,8},{1,17},{9,25},{17,1},{25,9},{2,18},{10... | collective-permute-start | bytes 786440 | tf_op jit(solution)/shard_map/ppermute | solution.py:1143
  587.1 25.7 %collective-permute-start.64 = (bf16[64,2048]{1,0:T(8,128)(2,1)}, bf16[64,2048]{1,0:T(8,128)(2,1)}, u32[]{:S(2)}, u32[]{:S(2)}) collective-permute-start(bf16[64,2048]{1,0:T(8,128)(2,1)} %get-tuple-element.179), channel_id=1, source_target_pairs={{0,24},{8,0},{16,8},{24,16},{1,25},{9,1},{17,9},{25,17},{2,26},{10... | collective-permute-start | bytes 786440 | tf_op jit(solution)/shard_map/ppermute | solution.py:1143
  606.7 20.7 %collective-permute-start.76 = (bf16[64,2048]{1,0:T(8,128)(2,1)S(1)}, bf16[64,2048]{1,0:T(8,128)(2,1)S(1)}, u32[]{:S(2)}, u32[]{:S(2)}) collective-permute-start(bf16[64,2048]{1,0:T(8,128)(2,1)S(1)} %add_convert_fusion), channel_id=1, source_target_pairs={{0,1},{1,0},{2,3},{3,2},{4,5},{5,4},{6,7},{7,6},{8,9},{9,8},{10,11... | collective-permute-start | bytes 786440 | tf_op jit(solution)/shard_map/ppermute | solution.py:1133
  616.1 36.5 %collective-permute-start.81 = (bf16[128,576]{1,0:T(8,128)(2,1)}, bf16[128,576]{1,0:T(8,128)(2,1)S(1)}, u32[]{:S(2)}, u32[]{:S(2)}) collective-permute-start(bf16[128,576]{1,0:T(8,128)(2,1)} %get-tuple-element.191), channel_id=1, source_target_pairs={{0,8},{8,16},{16,24},{24,0},{1,9},{9,17},{17,25},{25,1},{2,10},{10... | collective-permute-start | bytes 442376 | tf_op jit(solution)/shard_map/ppermute | solution.py:1143
  618.6 34.0 %collective-permute-start.82 = (bf16[128,576]{1,0:T(8,128)(2,1)S(1)}, bf16[128,576]{1,0:T(8,128)(2,1)S(1)}, u32[]{:S(2)}, u32[]{:S(2)}) collective-permute-start(bf16[128,576]{1,0:T(8,128)(2,1)S(1)} %copy-done.94), channel_id=1, source_target_pairs={{0,16},{8,24},{16,0},{24,8},{1,17},{9,25},{17,1},{25,9},{2,18},{10... | collective-permute-start | bytes 442376 | tf_op jit(solution)/shard_map/ppermute | solution.py:1143
  622.3 12.9 %all-to-all-start.2 = ((f32[16,19,128]{2,1,0:T(8,128)}), f32[16,19,128]{2,1,0:T(8,128)S(1)}, u32[]{:S(2)}, u32[]{:S(2)}) async-start(f32[16,19,128]{2,1,0:T(8,128)} %fusion.18), calls=%async_computation.2 | async-start | bytes 393216 | tf_op jit(solution)/shard_map/all_to_all | solution.py:1147
  (142 other events, 1151.2 us)
Sparse Core Ops, SparseCore 0:
  23.3 71.0 all-gather.5
  97.5 91.2 all-gather.3
  535.4 62.3 reduce-scatter.1

commit v6 on v5

--- a/solution.py
+++ b/solution.py
@@ -1579,7 +1579,6 @@
     grad_shared_down = shared_back[:, 2 * shared_here :].reshape(-1, rows_here)
 
 
-    output = both_halves(low(hidden_in + fold_z(routed_slab, jnp.float32, (down_grads[0],))))
     latent_input = jnp.stack([dot_nt(latent_raw_grad, down) for down in down_pieces])
     latent_input = latent_input.reshape(2, 2, block, zs, rows_here)
     latent_input = by_own(by_own(latent_input, "c", 0), "x", 1)
@@ -1599,6 +1598,7 @@
     )
     traded = by_own(by_own(traded, "x", 0), "c", 1).reshape(grad_heads.shape)
     both = traded.astype(jnp.float32)
+    output = both_halves(low(hidden_in + fold_z(routed_slab, jnp.float32, (traded,))))
     grad_down = fold_z(down_grads, jnp.float32, (traded,))
     out_at = both.shape[2] - head_rows
     grad_output = jnp.transpose(

time: 682 us -> 668 us (0.979)
    ppermute x12, waiting for transfers between devices: 6.57 us -> 14.7 us  [to_z(): lax.ppermute(value, 'z', [(i, (i + steps) % count) for i in range(count)])]
    unnamed x200 -> x176, local copies, waits for them, and re-layouts: 22.9 us -> 21.8 us
  transfers between devices with their start and end apart: 90 -> 90, of which waited for: 36 -> 34; matrix products, arithmetic and copies ran while one was open for 16% -> 16% of each run, Pallas kernels for 28% -> 30%
where the time goes in v6:
time: 668 us; the launch traced here: 656 us
  Pallas kernels  252 us (38%)
  waiting for transfers between devices  152 us (23%)
  starting transfers between devices  102 us (15%)
  local copies, waits for them, and re-layouts  75.1 us (11%)
  other arithmetic  47.2 us (7%)
  between operations  18 us (3%)
  matrix products  10.5 us (2%)
    pallas_call x41, Pallas kernels, local_call(): pl.pallas_call(run, grid=grid, in_specs=list(in_specs) + [pl.BlockSpec(me...  241 us
    ppermute x61, waiting for transfers between devices, swap(): return lax.ppermute(value, axis, [(0, 1), (1, 0)])  100 us
    ppermute x61, starting transfers between devices, swap(): return lax.ppermute(value, axis, [(0, 1), (1, 0)])  53.9 us
    ppermute x9, waiting for transfers between devices, from_z(): lax.ppermute(value, 'z', [((i + steps) % count, i) for i in range(count)])  31.7 us
    unnamed x176, local copies, waits for them, and re-layouts  21.8 us
    all_to_all x3, starting transfers between devices, trade(): return lax.all_to_all(value, axes, split_axis=0, concat_axis=0, tiled=True)  20.8 us
    ppermute x12, starting transfers between devices, to_z(): lax.ppermute(value, 'z', [(i, (i + steps) % count) for i in range(count)])  16.2 us
    ppermute x12, waiting for transfers between devices, to_z(): lax.ppermute(value, 'z', [(i, (i + steps) % count) for i in range(count)])  14.7 us
  transfers between devices with their start and end apart: 90, of which 34 were waited for; matrix products, arithmetic and copies ran while one was open for 16% of the time, Pallas kernels for 30%

profile of v6, /device:TPU:16, one launch (start us, length us, event | category | flops | bytes accessed | tf_op | source)
XLA Modules:
  0.0 656.0 jit_solution(3170632040954175302)
XLA Ops:
  12.9 9.3 %collective-permute-done.3 = bf16[128,768]{1,0:T(8,128)(2,1)S(1)} collective-permute-done((bf16[128,768]{1,0:T(8,128)(2,1)S(1)}, bf16[128,768]{1,0:T(8,128)(2,1)S(1)}, u32[]{:S(2)}, u32[]{:S(2)}) %collective-permute-start.3) | collective-permute-done | bytes 196640 | tf_op jit(solution)/shard_map/ppermute | solution.py:1133
  33.9 20.6 %collective-permute-done.5 = bf16[128,640]{1,0:T(8,128)(2,1)} collective-permute-done((bf16[128,640]{1,0:T(8,128)(2,1)S(1)}, bf16[128,640]{1,0:T(8,128)(2,1)}, u32[]{:S(2)}, u32[]{:S(2)}) %collective-permute-start.5) | collective-permute-done | bytes 163872 | tf_op jit(solution)/shard_map/ppermute | solution.py:1138
  56.5 5.3 collective-permute-done.7
  67.3 3.9 collective-permute-done.8
  84.3 7.1 %collective-permute-done.11 = bf16[64,576]{1,0:T(8,128)(2,1)S(1)} collective-permute-done((bf16[64,576]{1,0:T(8,128)(2,1)S(1)}, bf16[64,576]{1,0:T(8,128)(2,1)S(1)}, u32[]{:S(2)}, u32[]{:S(2)}) %collective-permute-start.11) | collective-permute-done | bytes 73760 | tf_op jit(solution)/shard_map/ppermute | solution.py:1133
  95.2 5.8 collective-permute-done.14
  135.6 3.8 shard_map.288
  143.6 8.9 %shard_map.289 = (bf16[2,128,2048]{2,1,0:T(8,128)(2,1)}, bf16[2,128,2048]{2,1,0:T(8,128)(2,1)}, bf16[2,512,1024]{2,1,0:T(8,128)(2,1)}, bf16[2,512,512]{2,1,0:T(8...) custom-call(bf16[512,384]{1,0:T(8,128)(2,1)} %pad_maximum_fusion.13.refs_0_.refs_1_, ...), custom_call_target="tpu_custom_call" | custom-call | flops 1 | bytes 1 | tf_op jit(solution)/shard_map/pallas_call | solution.py:503
  155.8 8.1 %all-to-all-start = ((bf16[16,264,128]{2,1,0:T(8,128)(2,1)}), bf16[16,264,128]{2,1,0:T(8,128)(2,1)S(1)}, u32[]{:S(2)}, u32[]{:S(2)}) async-start(bf16[16,264,128]{2,1,0:T(8,128)(2,1)} %maximum_add_fusion), calls=%async_computation | async-start | bytes 2162688 | tf_op jit(solution)/shard_map/all_to_all | solution.py:1147
  170.4 5.6 collective-permute-done.24.refs_1_
  183.7 5.5 collective-permute-done.26.refs_1_
  198.5 5.4 shard_map.294.refs_0_.refs_4_
  203.8 7.4 %shard_map.295.refs_2_.refs_1_ = bf16[1024,704]{1,0:T(8,128)(2,1)} custom-call(bf16[1024,2048]{1,0:T(8,128)(2,1)} %shard_map.294.refs_0_.refs_4_, bf16[704,2048]{1,0:T(8,128)(2,1)} %bitcast.299), custom_call_target="tpu_custom_call" | custom-call | flops 1 | bytes 1 | tf_op jit(solution)/shard_map/pallas_call | solution.py:503
  211.2 5.4 shard_map.293.refs_0_.refs_5_
  216.6 7.4 %shard_map.296.refs_5_.refs_1_ = bf16[1024,704]{1,0:T(8,128)(2,1)} custom-call(bf16[1024,2048]{1,0:T(8,128)(2,1)} %shard_map.293.refs_0_.refs_5_, bf16[704,2048]{1,0:T(8,128)(2,1)} %bitcast.300, bf16[1024,704]{1,0:T(8,128)(2,1)} %shard_map.295.refs_2_.refs_1_), custom_call_target="tpu_custom_call" | custom-call | flops 1 | bytes 1 | tf_op jit(solution)/shard_map/pallas_call | solution.py:503
  230.9 21.2 %collective-permute-done.32.refs_2_ = bf16[256,2048]{1,0:T(8,128)(2,1)S(1)} collective-permute-done((bf16[256,2048]{1,0:T(8,128)(2,1)}, bf16[256,2048]{1,0:T(8,128)(2,1)S(1)}, u32[]{:S(2)}, u32[]{:S(2)}) %collective-permute-start.32) | collective-permute-done | bytes 1048608 | tf_op jit(solution)/shard_map/ppermute | solution.py:1133
  257.3 4.8 shard_map.298.refs_2_
  262.0 4.8 shard_map.299.refs_5_.refs_2_
  266.8 4.4 shard_map.300.refs_0_.refs_4_
  276.5 16.1 %shard_map.301 = (bf16[1024,704]{1,0:T(8,128)(2,1)}, bf16[1024,128]{1,0:T(8,128)(2,1)}, bf16[1024,704]{1,0:T(8,128)(2,1)}, bf16[1024,704]{1,0:T(8,128)(2,1)}, bf...) custom-call(bf16[1024,2048]{1,0:T(8,128)(2,1)} %shard_map.300.refs_0_.refs_4_, bf16[1024,704]{1,0:T(8,128)(2,1)} %shard_map.295.refs_2_.refs_1_, ...), custom_call_target="tpu_custom_call" | custom-call | flops 1 | bytes 1 | tf_op jit(solution)/shard_map/pallas_call | solution.py:503
  292.7 16.2 %shard_map.302 = (bf16[1024,704]{1,0:T(8,128)(2,1)}, bf16[1024,128]{1,0:T(8,128)(2,1)}, bf16[1024,704]{1,0:T(8,128)(2,1)}, bf16[1024,704]{1,0:T(8,128)(2,1)}, bf...) custom-call(bf16[1024,2048]{1,0:T(8,128)(2,1)} %collective-permute-done.35.refs_0_.refs_5_, ...), custom_call_target="tpu_custom_call" | custom-call | flops 1 | bytes 1 | tf_op jit(solution)/shard_map/pallas_call | solution.py:503
  308.8 13.1 %shard_map.303.refs_8_ = bf16[1024,2176]{1,0:T(8,128)(2,1)} custom-call(bf16[1024,704]{1,0:T(8,128)(2,1)} %get-tuple-element.126.refs_0_.refs_1_, bf16[1024,704]{1,0:T(8,128)(2,1)} %get-tuple-element.127.refs_1_, bf16[1024,256]{1,0:T(8,128)(2,1)} %get-tuple-element.128.refs_2_.refs_3_, bf16[704,2048]{1,0:T(8,128)(2,1)} %bitcast.293, ...), custom_call_target="tpu_custom_call" | custom-call | flops 1 | bytes 1 | tf_op jit(solution)/shard_map/pallas_call | solution.py:503
  322.5 12.9 %shard_map.304 = bf16[1024,2176]{1,0:T(8,128)(2,1)} custom-call(bf16[1024,704]{1,0:T(8,128)(2,1)} %get-tuple-element.122.refs_0_, bf16[1024,704]{1,0:T(8,128)(2,1)} %get-tuple-element.123.refs_1_.refs_0_, bf16[1024,256]{1,0:T(8,128)(2,1)} %get-tuple-element.124.refs_2_, bf16[704,2048]{1,0:T(8,128)(2,1)} %bitcast.294, bf16[704,2048]{1,0:T(8,128)(2,1)} %bitcast.298, ...), custom_call_target="tpu_custom_call" | custom-call | flops 1 | bytes 1 | tf_op jit(solution)/shard_map/pallas_call | solution.py:503
  335.4 5.3 shard_map.305
  340.7 8.1 %shard_map.306.refs_4_ = bf16[1024,2048]{1,0:T(8,128)(2,1)} custom-call(bf16[1024,704]{1,0:T(8,128)(2,1)} %get-tuple-element.120.refs_0_.refs_1_, bf16[1024,128]{1,0:T(8,128)(2,1)} %get-tuple-element.121.refs_1_.refs_3_, bf16[704,2048]{1,0:T(8,128)(2,1)} %bitcast.301, bf16[128,2048]{1,0:T(8,128)(2,1)} %get-tuple-element.307.refs_1_.refs_3_, ...), custom_call_target="tpu_custom_call" | custom-call | flops 1 | bytes 1 | tf_op jit(solution)/shard_map/pallas_call | solution.py:503
  351.2 8.1 %shard_map.307.refs_6_ = bf16[1024,2048]{1,0:T(8,128)(2,1)} custom-call(bf16[1024,704]{1,0:T(8,128)(2,1)} %get-tuple-element.118.refs_8_.refs_0_, bf16[1024,128]{1,0:T(8,128)(2,1)} %get-tuple-element.119.refs_1_.refs_2_, bf16[704,2048]{1,0:T(8,128)(2,1)} %bitcast.302, bf16[128,2048]{1,0:T(8,128)(2,1)} %get-tuple-element.307.refs_1_.refs_3_, ...), custom_call_target="tpu_custom_call" | custom-call | flops 1 | bytes 1 | tf_op jit(solution)/shard_map/pallas_call | solution.py:503
  359.3 14.0 %shard_map.308 = (f32[704,2048]{1,0:T(8,128)}, bf16[128,2048]{1,0:T(8,128)(2,1)}) custom-call(bf16[1024,704]{1,0:T(8,128)(2,1)} %get-tuple-element.123.refs_1_.refs_0_, bf16[1024,704]{1,0:T(8,128)(2,1)} %get-tuple-element.127.refs_1_, bf16[1024,256]{1,0:T(8,128)(2,1)} %get-tuple-element.124.refs_2_, bf16[1024,256]{1,0:T(8,128)(2,1)} %get-tuple-element.128.refs_2_.refs_3_, ...), custom_call_target="tpu_custom_call" | custom-call | flops 1 | bytes 1 | tf_op jit(solution)/shard_map/pallas_call | solution.py:503
  377.9 3.4 shard_map.309
  384.2 14.0 %shard_map.310 = (f32[704,2048]{1,0:T(8,128)}, bf16[128,2048]{1,0:T(8,128)(2,1)}) custom-call(bf16[1024,704]{1,0:T(8,128)(2,1)} %get-tuple-element.118.refs_8_.refs_0_, bf16[1024,704]{1,0:T(8,128)(2,1)} %get-tuple-element.120.refs_0_.refs_1_, bf16[1024,128]{1,0:T(8,128)(2,1)} %get-tuple-element.119.refs_1_.refs_2_, ...), custom_call_target="tpu_custom_call" | custom-call | flops 1 | bytes 1 | tf_op jit(solution)/shard_map/pallas_call | solution.py:503
  401.9 5.3 shard_map.312
  413.4 14.3 %shard_map.313 = (f32[704,2048]{1,0:T(8,128)}, bf16[128,2048]{1,0:T(8,128)(2,1)}) custom-call(bf16[1024,704]{1,0:T(8,128)(2,1)} %get-tuple-element.122.refs_0_, bf16[1024,704]{1,0:T(8,128)(2,1)} %get-tuple-element.126.refs_0_.refs_1_, bf16[1024,256]{1,0:T(8,128)(2,1)} %get-tuple-element.124.refs_2_, bf16[1024,256]{1,0:T(8,128)(2,1)} %get-tuple-element.128.refs_2_.refs_3_, ...), custom_call_target="tpu_custom_call" | custom-call | flops 1 | bytes 1 | tf_op jit(solution)/shard_map/pallas_call | solution.py:503
  427.6 3.7 collective-permute-done.42.refs_1_
  433.0 3.3 shard_map.314
  443.1 4.7 collective-permute-done.50
  457.2 5.1 all-to-all-start.1
  465.3 3.4 shard_map.316.refs_9_.refs_3_
  468.7 13.7 %shard_map.317 = (bf16[2,2,256,576]{3,2,1,0:T(8,128)(2,1)}, bf16[2,2,256,576]{3,2,1,0:T(8,128)(2,1)}, f32[512,384]{1,0:T(8,128)}, f32[512,512]{1,0:T(8,128)}) custom-call(bf16[512,2048]{1,0:T(8,128)(2,1)} %bitcast.304, bf16[512,384]{1,0:T(8,128)(2,1)} %pad_maximum_fusion.13.refs_0_.refs_1_, bf16[2,2,256,576]{3,2,1,0:T(8,128)(2,1)} %copy-done, ...), custom_call_target="tpu_custom_call" | custom-call | flops 1 | bytes 1 | tf_op jit(solution)/shard_map/pallas_call | solution.py:503
  488.7 5.4 shard_map.318.refs_8_.refs_2_
  494.0 4.0 shard_map.325
  507.8 6.9 %collective-permute-done.55.refs_1_ = bf16[2,128,576]{2,1,0:T(8,128)(2,1)S(1)} collective-permute-done((bf16[2,128,576]{2,1,0:T(8,128)(2,1)}, bf16[2,128,576]{2,1,0:T(8,128)(2,1)S(1)}, u32[]{:S(2)}, u32[]{:S(2)}) %collective-permute-start.55) | collective-permute-done | bytes 294944 | tf_op jit(solution)/shard_map/ppermute | solution.py:1133
  520.8 3.7 collective-permute-done.57.refs_1_
  536.7 5.4 collective-permute-done.59.refs_1_
  542.1 3.3 collective-permute-done.61.refs_3_
  570.2 3.1 shard_map.329
  584.8 7.6 %all-to-all-start.2 = ((f32[16,19,128]{2,1,0:T(8,128)}), f32[16,19,128]{2,1,0:T(8,128)}, u32[]{:S(2)}, u32[]{:S(2)}) async-start(f32[16,19,128]{2,1,0:T(8,128)} %fusion.18), calls=%async_computation.3 | async-start | bytes 393216 | tf_op jit(solution)/shard_map/all_to_all | solution.py:1147
  614.4 4.8 collective-permute-done.67
  620.0 3.5 collective-permute-done.66
  634.7 3.3 collective-permute-done.82.refs_2_
  (595 shorter events, 277.7 us)
Async XLA Ops:
  7.2 128.4 %all-gather.6.cloned.1.call-start = ((), (), s32[]{:S(2)}) async-start(), calls=%async_computation.6 | async-start | bytes 3932160 | tf_op jit(solution)/shard_map/all_gather | solution.py:1352
  10.7 11.5 %collective-permute-start.4 = (bf16[128,768]{1,0:T(8,128)(2,1)S(1)}, bf16[128,768]{1,0:T(8,128)(2,1)S(1)}, u32[]{:S(2)}, u32[]{:S(2)}) collective-permute-start(bf16[128,768]{1,0:T(8,128)(2,1)S(1)} %get-tuple-element.320), channel_id=1, source_target_pairs={{0,6},{2,4},{4,2},{6,0},{1,7},{3,5},{5,3},{7,1},{8,14},{10,12},{12... | collective-permute-start | bytes 589832 | tf_op jit(solution)/shard_map/ppermute | solution.py:1317
  23.2 175.3 %all-gather.4.cloned.1.call-start = ((), (), s32[]{:S(2)}) async-start(), calls=%async_computation.4 | async-start | bytes 8650752 | tf_op jit(solution)/shard_map/all_gather | solution.py:1343
  27.0 28.5 %collective-permute-start.6 = (bf16[128,640]{1,0:T(8,128)(2,1)S(1)}, bf16[128,640]{1,0:T(8,128)(2,1)}, u32[]{:S(2)}, u32[]{:S(2)}) collective-permute-start(bf16[128,640]{1,0:T(8,128)(2,1)S(1)} %pad.21), channel_id=1, source_target_pairs={{16,0},{24,8},{0,16},{8,24},{17,1},{25,9},{1,17},{9,25},{18,2},{26... | collective-permute-start | bytes 491528 | tf_op jit(solution)/shard_map/ppermute | solution.py:1138
  27.2 27.4 %collective-permute-start.5 = (bf16[128,640]{1,0:T(8,128)(2,1)S(1)}, bf16[128,640]{1,0:T(8,128)(2,1)}, u32[]{:S(2)}, u32[]{:S(2)}) collective-permute-start(bf16[128,640]{1,0:T(8,128)(2,1)S(1)} %pad.21), channel_id=1, source_target_pairs={{8,0},{16,8},{24,16},{0,24},{9,1},{17,9},{25,17},{1,25},{10,2},{18... | collective-permute-start | bytes 491528 | tf_op jit(solution)/shard_map/ppermute | solution.py:1138
  30.1 31.7 %collective-permute-start.7 = (bf16[128,640]{1,0:T(8,128)(2,1)S(1)}, bf16[128,640]{1,0:T(8,128)(2,1)}, u32[]{:S(2)}, u32[]{:S(2)}) collective-permute-start(bf16[128,640]{1,0:T(8,128)(2,1)S(1)} %pad.21), channel_id=1, source_target_pairs={{24,0},{0,8},{8,16},{16,24},{25,1},{1,9},{9,17},{17,25},{26,2},{2,... | collective-permute-start | bytes 491528 | tf_op jit(solution)/shard_map/ppermute | solution.py:1138
  30.2 32.5 %collective-permute-start = (bf16[2,64,2048]{2,1,0:T(8,128)(2,1)S(1)}, bf16[2,64,2048]{2,1,0:T(8,128)(2,1)}, u32[]{:S(2)}, u32[]{:S(2)}) collective-permute-start(bf16[2,64,2048]{2,1,0:T(8,128)(2,1)S(1)} %reverse_select_fusion.9), channel_id=1, source_target_pairs={{0,4},{4,0},{1,5},{5,1},{2,6},{6,2},{3,7},{7,3},{8,12},{12,8},{9,1... | collective-permute-start | bytes 1572872 | tf_op jit(solution)/shard_map/ppermute | solution.py:1133
  73.7 34.8 %collective-permute-start.20 = (bf16[512,576]{0,1:T(8,128)(2,1)}, bf16[512,576]{0,1:T(8,128)(2,1)}, u32[]{:S(2)}, u32[]{:S(2)}) collective-permute-start(bf16[512,576]{0,1:T(8,128)(2,1)} %copy.292), channel_id=1, source_target_pairs={{0,4},{4,0},{1,5},{5,1},{2,6},{6,2},{3,7},{7,3},{8,12},{12,8},{9,1... | collective-permute-start | bytes 1769480 | tf_op jit(solution)/shard_map/ppermute | solution.py:1133
  108.5 16.3 %collective-permute-start.21 = (bf16[512,576]{0,1:T(8,128)(2,1)}, bf16[512,576]{0,1:T(8,128)(2,1)}, u32[]{:S(2)}, u32[]{:S(2)}) collective-permute-start(bf16[512,576]{0,1:T(8,128)(2,1)} %copy.292), channel_id=1, source_target_pairs={{0,2},{2,0},{1,3},{3,1},{4,6},{6,4},{5,7},{7,5},{8,10},{10,8},{9,1... | collective-permute-start | bytes 1769480 | tf_op jit(solution)/shard_map/ppermute | solution.py:1133
  108.5 18.5 %collective-permute-start.22 = (bf16[512,576]{0,1:T(8,128)(2,1)}, bf16[512,576]{0,1:T(8,128)(2,1)}, u32[]{:S(2)}, u32[]{:S(2)}) collective-permute-start(bf16[512,576]{0,1:T(8,128)(2,1)} %collective-permute-done.20), channel_id=1, source_target_pairs={{0,2},{2,0},{1,3},{3,1},{4,6},{6,4},{5,7},{7,5},{8,10},{10,8},{9,1... | collective-permute-start | bytes 1769480 | tf_op jit(solution)/shard_map/ppermute | solution.py:1133
  155.8 68.3 %all-to-all-start = ((bf16[16,264,128]{2,1,0:T(8,128)(2,1)}), bf16[16,264,128]{2,1,0:T(8,128)(2,1)S(1)}, u32[]{:S(2)}, u32[]{:S(2)}) async-start(bf16[16,264,128]{2,1,0:T(8,128)(2,1)} %maximum_add_fusion), calls=%async_computation | async-start | bytes 2162688 | tf_op jit(solution)/shard_map/all_to_all | solution.py:1147
  193.3 30.7 %collective-permute-start.30 = (bf16[64,2048]{1,0:T(8,128)(2,1)S(1)}, bf16[64,2048]{1,0:T(8,128)(2,1)S(1)}, u32[]{:S(2)}, u32[]{:S(2)}) collective-permute-start(bf16[64,2048]{1,0:T(8,128)(2,1)S(1)} %multiply_convert_fusion.1.dep.refs_0_), channel_id=1, source_target_pairs={{24,0},{0,8},{8,16},{16,24},{25,1},{1,9},{9,17},{17,25},{26,2},{2,... | collective-permute-start | bytes 786440 | tf_op jit(solution)/shard_map/ppermute | solution.py:1138
  195.0 29.0 %collective-permute-start.29 = (bf16[64,2048]{1,0:T(8,128)(2,1)S(1)}, bf16[64,2048]{1,0:T(8,128)(2,1)S(1)}, u32[]{:S(2)}, u32[]{:S(2)}) collective-permute-start(bf16[64,2048]{1,0:T(8,128)(2,1)S(1)} %multiply_convert_fusion.1.dep.refs_0_), channel_id=1, source_target_pairs={{16,0},{24,8},{0,16},{8,24},{17,1},{25,9},{1,17},{9,25},{18,2},{26... | collective-permute-start | bytes 786440 | tf_op jit(solution)/shard_map/ppermute | solution.py:1138
  195.0 29.0 %collective-permute-start.28 = (bf16[64,2048]{1,0:T(8,128)(2,1)S(1)}, bf16[64,2048]{1,0:T(8,128)(2,1)S(1)}, u32[]{:S(2)}, u32[]{:S(2)}) collective-permute-start(bf16[64,2048]{1,0:T(8,128)(2,1)S(1)} %multiply_convert_fusion.1.dep.refs_0_), channel_id=1, source_target_pairs={{8,0},{16,8},{24,16},{0,24},{9,1},{17,9},{25,17},{1,25},{10,2},{18... | collective-permute-start | bytes 786440 | tf_op jit(solution)/shard_map/ppermute | solution.py:1138
  228.1 24.0 %collective-permute-start.32 = (bf16[256,2048]{1,0:T(8,128)(2,1)}, bf16[256,2048]{1,0:T(8,128)(2,1)S(1)}, u32[]{:S(2)}, u32[]{:S(2)}) collective-permute-start(bf16[256,2048]{1,0:T(8,128)(2,1)} %shard_map.297.refs_2_.refs_0_), channel_id=1, source_target_pairs={{0,4},{4,0},{1,5},{5,1},{2,6},{6,2},{3,7},{7,3},{8,12},{12,8},{9,1... | collective-permute-start | bytes 3145736 | tf_op jit(solution)/shard_map/ppermute | solution.py:1133
  230.3 23.6 %collective-permute-start.31 = (bf16[256,2048]{1,0:T(8,128)(2,1)}, bf16[256,2048]{1,0:T(8,128)(2,1)S(1)}, u32[]{:S(2)}, u32[]{:S(2)}) collective-permute-start(bf16[256,2048]{1,0:T(8,128)(2,1)} %shard_map.297.refs_2_.refs_0_), channel_id=1, source_target_pairs={{0,1},{1,0},{2,3},{3,2},{4,5},{5,4},{6,7},{7,6},{8,9},{9,8},{10,11... | collective-permute-start | bytes 3145736 | tf_op jit(solution)/shard_map/ppermute | solution.py:1133
  253.0 13.8 %collective-permute-start.34 = (bf16[128,2048]{1,0:T(8,128)(2,1)}, bf16[128,2048]{1,0:T(8,128)(2,1)}, u32[]{:S(2)}, u32[]{:S(2)}) collective-permute-start(bf16[128,2048]{1,0:T(8,128)(2,1)} %slice.364), channel_id=1, source_target_pairs={{0,1},{1,0},{2,3},{3,2},{4,5},{5,4},{6,7},{7,6},{8,9},{9,8},{10,11... | collective-permute-start | bytes 1572872 | tf_op jit(solution)/shard_map/ppermute | solution.py:1133
  254.8 12.0 %collective-permute-start.33 = (bf16[128,2048]{1,0:T(8,128)(2,1)}, bf16[128,2048]{1,0:T(8,128)(2,1)}, u32[]{:S(2)}, u32[]{:S(2)}) collective-permute-start(bf16[128,2048]{1,0:T(8,128)(2,1)} %slice.363), channel_id=1, source_target_pairs={{0,4},{4,0},{1,5},{5,1},{2,6},{6,2},{3,7},{7,3},{8,12},{12,8},{9,1... | collective-permute-start | bytes 1572872 | tf_op jit(solution)/shard_map/ppermute | solution.py:1133
  271.3 21.4 %collective-permute-start.35 = (bf16[1024,2048]{1,0:T(8,128)(2,1)}, bf16[1024,2048]{1,0:T(8,128)(2,1)}, u32[]{:S(2)}, u32[]{:S(2)}) collective-permute-start(bf16[1024,2048]{1,0:T(8,128)(2,1)} %shard_map.300.refs_0_.refs_4_), channel_id=1, source_target_pairs={{0,2},{2,0},{1,3},{3,1},{4,6},{6,4},{5,7},{7,5},{8,10},{10,8},{9,1... | collective-permute-start | bytes 12582920 | tf_op jit(solution)/shard_map/ppermute | solution.py:1133
  321.9 13.4 %collective-permute-start.36 = (bf16[1024,2176]{1,0:T(8,128)(2,1)}, bf16[1024,2176]{1,0:T(8,128)(2,1)}, u32[]{:S(2)}, u32[]{:S(2)}) collective-permute-start(bf16[1024,2176]{1,0:T(8,128)(2,1)} %shard_map.303.refs_8_), channel_id=1, source_target_pairs={{0,2},{2,0},{1,3},{3,1},{4,6},{6,4},{5,7},{7,5},{8,10},{10,8},{9,1... | collective-permute-start | bytes 13369352 | tf_op jit(solution)/shard_map/ppermute | solution.py:1133
  348.8 53.1 %collective-permute-start.37 = (bf16[1024,2048]{1,0:T(8,128)(2,1)}, bf16[1024,2048]{1,0:T(8,128)(2,1)}, u32[]{:S(2)}, u32[]{:S(2)}) collective-permute-start(bf16[1024,2048]{1,0:T(8,128)(2,1)} %shard_map.306.refs_4_), channel_id=1, source_target_pairs={{0,2},{2,0},{1,3},{3,1},{4,6},{6,4},{5,7},{7,5},{8,10},{10,8},{9,1... | collective-permute-start | bytes 12582920 | tf_op jit(solution)/shard_map/ppermute | solution.py:1133
  348.9 27.2 %collective-permute-start.38 = (bf16[2,128,2176]{2,1,0:T(8,128)(2,1)}, bf16[2,128,2176]{2,1,0:T(8,128)(2,1)S(1)}, u32[]{:S(2)}, u32[]{:S(2)}) collective-permute-start(bf16[2,128,2176]{2,1,0:T(8,128)(2,1)} %get-tuple-element.131.refs_5_), channel_id=1, source_target_pairs={{0,4},{4,0},{1,5},{5,1},{2,6},{6,2},{3,7},{7,3},{8,12},{12,8},{9,1... | collective-permute-start | bytes 3342344 | tf_op jit(solution)/shard_map/ppermute | solution.py:1133
  350.0 26.9 %collective-permute-start.39 = (bf16[2,128,2176]{2,1,0:T(8,128)(2,1)}, bf16[2,128,2176]{2,1,0:T(8,128)(2,1)S(1)}, u32[]{:S(2)}, u32[]{:S(2)}) collective-permute-start(bf16[2,128,2176]{2,1,0:T(8,128)(2,1)} %get-tuple-element.133.refs_7_), channel_id=1, source_target_pairs={{0,1},{1,0},{2,3},{3,2},{4,5},{5,4},{6,7},{7,6},{8,9},{9,8},{10,11... | collective-permute-start | bytes 3342344 | tf_op jit(solution)/shard_map/ppermute | solution.py:1133
  381.3 16.9 %collective-permute-start.40 = (bf16[128,2176]{1,0:T(8,128)(2,1)}, bf16[128,2176]{1,0:T(8,128)(2,1)S(1)}, u32[]{:S(2)}, u32[]{:S(2)}) collective-permute-start(bf16[128,2176]{1,0:T(8,128)(2,1)} %get-tuple-element.136.refs_7_), channel_id=1, source_target_pairs={{0,1},{1,0},{2,3},{3,2},{4,5},{5,4},{6,7},{7,6},{8,9},{9,8},{10,11... | collective-permute-start | bytes 1671176 | tf_op jit(solution)/shard_map/ppermute | solution.py:1133
  382.8 15.4 %collective-permute-start.41 = (bf16[128,2176]{1,0:T(8,128)(2,1)}, bf16[128,2176]{1,0:T(8,128)(2,1)S(1)}, u32[]{:S(2)}, u32[]{:S(2)}) collective-permute-start(bf16[128,2176]{1,0:T(8,128)(2,1)} %get-tuple-element.138.refs_9_), channel_id=1, source_target_pairs={{0,4},{4,0},{1,5},{5,1},{2,6},{6,2},{3,7},{7,3},{8,12},{12,8},{9,1... | collective-permute-start | bytes 1671176 | tf_op jit(solution)/shard_map/ppermute | solution.py:1133
  407.2 24.2 %collective-permute-start.42 = (bf16[2,128,2048]{2,1,0:T(8,128)(2,1)}, bf16[2,128,2048]{2,1,0:T(8,128)(2,1)S(1)}, u32[]{:S(2)}, u32[]{:S(2)}) collective-permute-start(bf16[2,128,2048]{2,1,0:T(8,128)(2,1)} %get-tuple-element.145.refs_7_), channel_id=1, source_target_pairs={{0,4},{4,0},{1,5},{5,1},{2,6},{6,2},{3,7},{7,3},{8,12},{12,8},{9,1... | collective-permute-start | bytes 3145736 | tf_op jit(solution)/shard_map/ppermute | solution.py:1133
  407.9 24.1 %collective-permute-start.43 = (bf16[2,128,2048]{2,1,0:T(8,128)(2,1)}, bf16[2,128,2048]{2,1,0:T(8,128)(2,1)S(1)}, u32[]{:S(2)}, u32[]{:S(2)}) collective-permute-start(bf16[2,128,2048]{2,1,0:T(8,128)(2,1)} %get-tuple-element.147.refs_9_), channel_id=1, source_target_pairs={{0,1},{1,0},{2,3},{3,2},{4,5},{5,4},{6,7},{7,6},{8,9},{9,8},{10,11... | collective-permute-start | bytes 3145736 | tf_op jit(solution)/shard_map/ppermute | solution.py:1133
  408.4 27.8 %collective-permute-start.46 = (bf16[64,2176]{1,0:T(8,128)(2,1)}, bf16[64,2176]{1,0:T(8,128)(2,1)}, u32[]{:S(2)}, u32[]{:S(2)}) collective-permute-start(bf16[64,2176]{1,0:T(8,128)(2,1)} %get-tuple-element.141.refs_9_), channel_id=1, source_target_pairs={{0,8},{8,16},{16,24},{24,0},{1,9},{9,17},{17,25},{25,1},{2,10},{10... | collective-permute-start | bytes 835592 | tf_op jit(solution)/shard_map/ppermute | solution.py:1143
  408.9 27.4 %collective-permute-start.47 = (bf16[64,2176]{1,0:T(8,128)(2,1)}, bf16[64,2176]{1,0:T(8,128)(2,1)}, u32[]{:S(2)}, u32[]{:S(2)}) collective-permute-start(bf16[64,2176]{1,0:T(8,128)(2,1)} %get-tuple-element.142.refs_10_), channel_id=1, source_target_pairs={{0,16},{8,24},{16,0},{24,8},{1,17},{9,25},{17,1},{25,9},{2,18},{10... | collective-permute-start | bytes 835592 | tf_op jit(solution)/shard_map/ppermute | solution.py:1143
  411.5 24.7 %collective-permute-start.48 = (bf16[64,2176]{1,0:T(8,128)(2,1)}, bf16[64,2176]{1,0:T(8,128)(2,1)}, u32[]{:S(2)}, u32[]{:S(2)}) collective-permute-start(bf16[64,2176]{1,0:T(8,128)(2,1)} %get-tuple-element.143.refs_11_), channel_id=1, source_target_pairs={{0,24},{8,0},{16,8},{24,16},{1,25},{9,1},{17,9},{25,17},{2,26},{10... | collective-permute-start | bytes 835592 | tf_op jit(solution)/shard_map/ppermute | solution.py:1143
  457.2 43.7 %all-to-all-start.1 = ((bf16[16,264,128]{2,1,0:T(8,128)(2,1)}), bf16[16,264,128]{2,1,0:T(8,128)(2,1)S(1)}, u32[]{:S(2)}, u32[]{:S(2)}) async-start(bf16[16,264,128]{2,1,0:T(8,128)(2,1)} %bitcast_bitcast_fusion), calls=%async_computation.1 | async-start | bytes 2162688 | tf_op jit(solution)/shard_map/all_to_all | solution.py:1147
  462.3 147.8 %reduce-scatter.2.cloned.1.call-start = ((), (), s32[]{:S(2)}) async-start(), calls=%async_computation.5 | async-start | bytes 3932160 | tf_op jit(solution)/shard_map/reduce_scatter | solution.py:1558
  484.8 13.6 %collective-permute-start.54 = (bf16[2,2,256,576]{2,3,1,0:T(8,128)(2,1)}, bf16[2,2,256,576]{2,3,1,0:T(8,128)(2,1)}, u32[]{:S(2)}, u32[]{:S(2)}) collective-permute-start(bf16[2,2,256,576]{2,3,1,0:T(8,128)(2,1)} %copy.311), channel_id=1, source_target_pairs={{0,2},{2,0},{1,3},{3,1},{4,6},{6,4},{5,7},{7,5},{8,10},{10,8},{9,1... | collective-permute-start | bytes 3538952 | tf_op jit(solution)/shard_map/ppermute | solution.py:1133
  498.0 34.1 %collective-permute-start.69 = (bf16[2,128,2048]{2,1,0:T(8,128)(2,1)}, bf16[2,128,2048]{2,1,0:T(8,128)(2,1)S(1)}, u32[]{:S(2)}, u32[]{:S(2)}) collective-permute-start(bf16[2,128,2048]{2,1,0:T(8,128)(2,1)} %get-tuple-element.181), channel_id=1, source_target_pairs={{0,2},{2,0},{1,3},{3,1},{4,6},{6,4},{5,7},{7,5},{8,10},{10,8},{9,1... | collective-permute-start | bytes 3145736 | tf_op jit(solution)/shard_map/ppermute | solution.py:1133
  528.6 13.5 %collective-permute-start.59 = (bf16[64,576]{1,0:T(8,128)(2,1)}, bf16[64,576]{1,0:T(8,128)(2,1)S(1)}, u32[]{:S(2)}, u32[]{:S(2)}) collective-permute-start(bf16[64,576]{1,0:T(8,128)(2,1)} %get-tuple-element.173), channel_id=1, source_target_pairs={{0,8},{8,16},{16,24},{24,0},{1,9},{9,17},{17,25},{25,1},{2,10},{10... | collective-permute-start | bytes 221192 | tf_op jit(solution)/shard_map/ppermute | solution.py:1143
  530.0 12.1 %collective-permute-start.60 = (bf16[64,576]{1,0:T(8,128)(2,1)}, bf16[64,576]{1,0:T(8,128)(2,1)S(1)}, u32[]{:S(2)}, u32[]{:S(2)}) collective-permute-start(bf16[64,576]{1,0:T(8,128)(2,1)} %get-tuple-element.174), channel_id=1, source_target_pairs={{0,16},{8,24},{16,0},{24,8},{1,17},{9,25},{17,1},{25,9},{2,18},{10... | collective-permute-start | bytes 221192 | tf_op jit(solution)/shard_map/ppermute | solution.py:1143
  530.6 14.8 %collective-permute-start.61 = (bf16[64,576]{1,0:T(8,128)(2,1)}, bf16[64,576]{1,0:T(8,128)(2,1)S(1)}, u32[]{:S(2)}, u32[]{:S(2)}) collective-permute-start(bf16[64,576]{1,0:T(8,128)(2,1)} %get-tuple-element.175), channel_id=1, source_target_pairs={{0,24},{8,0},{16,8},{24,16},{1,25},{9,1},{17,9},{25,17},{2,26},{10... | collective-permute-start | bytes 221192 | tf_op jit(solution)/shard_map/ppermute | solution.py:1143
  535.9 17.0 %collective-permute-start.70 = (bf16[2,32,2048]{2,1,0:T(8,128)(2,1)}, bf16[2,32,2048]{2,1,0:T(8,128)(2,1)S(1)}, u32[]{:S(2)}, u32[]{:S(2)}) collective-permute-start(bf16[2,32,2048]{2,1,0:T(8,128)(2,1)} %get-tuple-element.183), channel_id=1, source_target_pairs={{0,1},{1,0},{2,3},{3,2},{4,5},{5,4},{6,7},{7,6},{8,9},{9,8},{10,11... | collective-permute-start | bytes 786440 | tf_op jit(solution)/shard_map/ppermute | solution.py:1133
  536.2 16.7 %collective-permute-start.71 = (bf16[2,32,2048]{2,1,0:T(8,128)(2,1)}, bf16[2,32,2048]{2,1,0:T(8,128)(2,1)S(1)}, u32[]{:S(2)}, u32[]{:S(2)}) collective-permute-start(bf16[2,32,2048]{2,1,0:T(8,128)(2,1)} %get-tuple-element.185), channel_id=1, source_target_pairs={{0,4},{4,0},{1,5},{5,1},{2,6},{6,2},{3,7},{7,3},{8,12},{12,8},{9,1... | collective-permute-start | bytes 786440 | tf_op jit(solution)/shard_map/ppermute | solution.py:1133
  563.2 36.3 %collective-permute-start.44 = (bf16[128,2048]{1,0:T(8,128)(2,1)}, bf16[128,2048]{1,0:T(8,128)(2,1)}, u32[]{:S(2)}, u32[]{:S(2)}) collective-permute-start(bf16[128,2048]{1,0:T(8,128)(2,1)} %get-tuple-element.150.refs_5_), channel_id=1, source_target_pairs={{0,1},{1,0},{2,3},{3,2},{4,5},{5,4},{6,7},{7,6},{8,9},{9,8},{10,11... | collective-permute-start | bytes 1572872 | tf_op jit(solution)/shard_map/ppermute | solution.py:1133
  564.2 35.3 %collective-permute-start.45 = (bf16[128,2048]{1,0:T(8,128)(2,1)}, bf16[128,2048]{1,0:T(8,128)(2,1)}, u32[]{:S(2)}, u32[]{:S(2)}) collective-permute-start(bf16[128,2048]{1,0:T(8,128)(2,1)} %get-tuple-element.152.refs_7_), channel_id=1, source_target_pairs={{0,4},{4,0},{1,5},{5,1},{2,6},{6,2},{3,7},{7,3},{8,12},{12,8},{9,1... | collective-permute-start | bytes 1572872 | tf_op jit(solution)/shard_map/ppermute | solution.py:1133
  584.8 19.4 %all-to-all-start.2 = ((f32[16,19,128]{2,1,0:T(8,128)}), f32[16,19,128]{2,1,0:T(8,128)}, u32[]{:S(2)}, u32[]{:S(2)}) async-start(f32[16,19,128]{2,1,0:T(8,128)} %fusion.18), calls=%async_computation.3 | async-start | bytes 393216 | tf_op jit(solution)/shard_map/all_to_all | solution.py:1147
  602.1 24.6 %collective-permute-start.62 = (bf16[64,2048]{1,0:T(8,128)(2,1)}, bf16[64,2048]{1,0:T(8,128)(2,1)S(1)}, u32[]{:S(2)}, u32[]{:S(2)}) collective-permute-start(bf16[64,2048]{1,0:T(8,128)(2,1)} %get-tuple-element.177), channel_id=1, source_target_pairs={{0,8},{8,16},{16,24},{24,0},{1,9},{9,17},{17,25},{25,1},{2,10},{10... | collective-permute-start | bytes 786440 | tf_op jit(solution)/shard_map/ppermute | solution.py:1143
  603.6 26.0 %collective-permute-start.63 = (bf16[64,2048]{1,0:T(8,128)(2,1)}, bf16[64,2048]{1,0:T(8,128)(2,1)S(1)}, u32[]{:S(2)}, u32[]{:S(2)}) collective-permute-start(bf16[64,2048]{1,0:T(8,128)(2,1)} %get-tuple-element.178), channel_id=1, source_target_pairs={{0,16},{8,24},{16,0},{24,8},{1,17},{9,25},{17,1},{25,9},{2,18},{10... | collective-permute-start | bytes 786440 | tf_op jit(solution)/shard_map/ppermute | solution.py:1143
  612.1 11.4 %collective-permute-start.66 = (bf16[128,768]{1,0:T(8,128)(2,1)S(1)}, bf16[128,768]{1,0:T(8,128)(2,1)S(1)}, u32[]{:S(2)}, u32[]{:S(2)}) collective-permute-start(bf16[128,768]{1,0:T(8,128)(2,1)S(1)} %get-tuple-element.318), channel_id=1, source_target_pairs={{0,4},{4,0},{1,5},{5,1},{2,6},{6,2},{3,7},{7,3},{8,12},{12,8},{9,1... | collective-permute-start | bytes 589832 | tf_op jit(solution)/shard_map/ppermute | solution.py:1133
  625.0 13.0 %collective-permute-start.82 = (bf16[128,576]{1,0:T(8,128)(2,1)}, bf16[128,576]{1,0:T(8,128)(2,1)}, u32[]{:S(2)}, u32[]{:S(2)}) collective-permute-start(bf16[128,576]{1,0:T(8,128)(2,1)} %get-tuple-element.192), channel_id=1, source_target_pairs={{0,16},{8,24},{16,0},{24,8},{1,17},{9,25},{17,1},{25,9},{2,18},{10... | collective-permute-start | bytes 442376 | tf_op jit(solution)/shard_map/ppermute | solution.py:1143
  626.8 13.9 %collective-permute-start.83 = (bf16[128,576]{1,0:T(8,128)(2,1)}, bf16[128,576]{1,0:T(8,128)(2,1)}, u32[]{:S(2)}, u32[]{:S(2)}) collective-permute-start(bf16[128,576]{1,0:T(8,128)(2,1)} %get-tuple-element.193), channel_id=1, source_target_pairs={{0,24},{8,0},{16,8},{24,16},{1,25},{9,1},{17,9},{25,17},{2,26},{10... | collective-permute-start | bytes 442376 | tf_op jit(solution)/shard_map/ppermute | solution.py:1143
  633.6 14.4 %collective-permute-start.68 = (bf16[64,2048]{1,0:T(8,128)(2,1)S(1)}, bf16[64,2048]{1,0:T(8,128)(2,1)S(1)}, u32[]{:S(2)}, u32[]{:S(2)}) collective-permute-start(bf16[64,2048]{1,0:T(8,128)(2,1)S(1)} %add_convert_fusion.1), channel_id=1, source_target_pairs={{0,1},{1,0},{2,3},{3,2},{4,5},{5,4},{6,7},{7,6},{8,9},{9,8},{10,11... | collective-permute-start | bytes 786440 | tf_op jit(solution)/shard_map/ppermute | solution.py:1133
  (130 other events, 1028.9 us)
Sparse Core Ops, SparseCore 0:
  23.3 71.0 all-gather.5
  97.5 91.2 all-gather.3
  498.5 66.9 reduce-scatter.1
